TPU v7x, 32 devices: a whole 2x2x4 slice. The times are simulated.
32 devices in a mesh: seq: 4 (over z), dp: 8 (over y, x, core).
Axes of the slice: x: 2, y: 2, z: 4, core: 2. Of those that a mesh axis runs over, the one named last changes fastest.
Arguments:
- queries: bfloat16 [8, 512, 1024], P('dp', 'seq'), may hold values from -16 to 16
- saved_output: bfloat16 [8, 512, 1024], P('dp', 'seq'), may hold values from -6 to 6
- grad_out: bfloat16 [8, 512, 1024], P('dp', 'seq'), may hold values from -6 to 6
- tile_kv: bfloat16 [16, 1601, 512], P('dp', None, 'seq'), may hold values from -16 to 16
- tile_count: int32 [8], replicated, may hold values from 1 to 4, 12 in all
- owner_perm: int32 [8], replicated, may hold values from 0 to 7, each once
- text_len: int32 [8], P('dp'), may hold values from 128 to 512
Outputs:
- grad_queries: bfloat16 [8, 512, 1024], P('dp', 'seq')
- grad_tile_kv: bfloat16 [16, 1601, 512], P('dp', None, 'seq')
Inputs may be any that keep to these rules, and one draw needn't show every extreme that they name: `tile_count`: the counts sum to 12, and some sample has 4 tiles.
All inputs are finite; a program needn't handle non-finite values.
Results may differ from a plain program's by a relative error of at most 0.0061.
Values may be sent and summed in bfloat16 or wider, within the bound.
No kernel may reach another device: no remote copies, remote signals or barrier semaphores. Data moves between devices by JAX's collectives and lax.ppermute only.
A program may use at most 128 MiB of HBM per device.

v0:
```python
import math

import jax
import jax.numpy as jnp
from jax import lax
from jax.sharding import PartitionSpec as P

HEAD_DIM = 128
MAX_TILES = 4


def swapped(block, axis, distance):
    count = lax.axis_size(axis)
    route = []
    for low in range(count):
        high = low | 1 << distance
        if high != low and high < count:
            route += [(low, high), (high, low)]
    return lax.ppermute(block, axis, route)


def tile_places(tile_count, owner_perm, sample, slots_owner):
    samples = tile_count.shape[0]
    offsets = jnp.cumsum(tile_count) - tile_count
    within = jnp.arange(MAX_TILES, dtype=jnp.int32)
    slot_valid = within < tile_count[sample]
    places = offsets[sample] + jnp.where(slot_valid, within, 0)
    owners = owner_perm[places % samples]
    return (owners, owners * slots_owner + places // samples, slot_valid)


def attend_backward(
    query_heads, grad_heads, delta_heads, key_tiles, value_tiles, sample_tiles, score_scale
):
    text_rows, local_heads, head_dim = query_heads.shape
    block_rows = min(512, text_rows)
    zero_slots = jnp.zeros(key_tiles.shape, jnp.float32)

    def one_block(block_index, state_all):
        grad_rows, key_grads, value_grads = state_all
        row_start = block_index * block_rows
        query_block = lax.dynamic_slice_in_dim(query_heads, row_start, block_rows, 0)
        grad_block = lax.dynamic_slice_in_dim(grad_heads, row_start, block_rows, 0)
        delta_block = jnp.transpose(
            lax.dynamic_slice_in_dim(delta_heads, row_start, block_rows, 0).astype(jnp.float32)
        )

        def block_scores(slot_index):
            key_slot = lax.dynamic_index_in_dim(key_tiles, slot_index, 0, keepdims=False)
            scores = jnp.einsum(
                "bhd,rd->hbr", query_block, key_slot, preferred_element_type=jnp.float32
            )
            return (scores * score_scale, key_slot)

        def gather_stats(slot_index, state_pair):
            row_peak, row_mass = state_pair
            scores = block_scores(slot_index)[0]
            new_peak = jnp.maximum(row_peak, jnp.max(scores, axis=2))
            row_mass = row_mass * jnp.exp(row_peak - new_peak) + jnp.sum(
                jnp.exp(scores - new_peak[:, :, None]), axis=2
            )
            return (new_peak, row_mass)

        peak_start = jnp.full((local_heads, block_rows), -jnp.inf, jnp.float32)
        mass_start = jnp.zeros((local_heads, block_rows), jnp.float32)
        row_peak, row_mass = lax.fori_loop(0, sample_tiles, gather_stats, (peak_start, mass_start))

        def slot_grads(slot_index, state_slot):
            query_grad, key_sums, value_sums = state_slot
            scores, key_slot = block_scores(slot_index)
            value_slot = lax.dynamic_index_in_dim(value_tiles, slot_index, 0, keepdims=False)
            attention = jnp.exp(scores - row_peak[:, :, None]) / row_mass[:, :, None]
            attention_half = attention.astype(jnp.bfloat16)
            grad_attention = jnp.einsum(
                "bhd,rd->hbr", grad_block, value_slot, preferred_element_type=jnp.float32
            )
            grad_scores = (attention * (grad_attention - delta_block[:, :, None])).astype(
                jnp.bfloat16
            )
            query_grad = (
                query_grad
                + jnp.einsum(
                    "hbr,rd->bhd", grad_scores, key_slot, preferred_element_type=jnp.float32
                )
                * score_scale
            )
            key_part = (
                jnp.einsum(
                    "hbr,bhd->rd", grad_scores, query_block, preferred_element_type=jnp.float32
                )
                * score_scale
            )
            value_part = jnp.einsum(
                "hbr,bhd->rd", attention_half, grad_block, preferred_element_type=jnp.float32
            )
            key_old = lax.dynamic_index_in_dim(key_sums, slot_index, 0, keepdims=False)
            value_old = lax.dynamic_index_in_dim(value_sums, slot_index, 0, keepdims=False)
            key_sums = lax.dynamic_update_index_in_dim(key_sums, key_old + key_part, slot_index, 0)
            value_sums = lax.dynamic_update_index_in_dim(
                value_sums, value_old + value_part, slot_index, 0
            )
            return (query_grad, key_sums, value_sums)

        query_start = jnp.zeros((block_rows, local_heads, head_dim), jnp.float32)
        query_grad, key_grads, value_grads = lax.fori_loop(
            0, sample_tiles, slot_grads, (query_start, key_grads, value_grads)
        )
        grad_rows = lax.dynamic_update_slice_in_dim(
            grad_rows, query_grad.astype(jnp.bfloat16), row_start, 0
        )
        return (grad_rows, key_grads, value_grads)

    grad_start = jnp.zeros(query_heads.shape, jnp.bfloat16)
    return lax.fori_loop(
        0, text_rows // block_rows, one_block, (grad_start, zero_slots, zero_slots)
    )


def shards(queries, saved_output, grad_out, tile_kv, tile_count, owner_perm, text_len):
    rows_dev = queries.shape[1]
    feature_width = queries.shape[2]
    groups = lax.axis_size("seq")
    seq_index = lax.axis_index("seq")
    sample = lax.axis_index("dp")
    head_count = feature_width // HEAD_DIM
    local_heads = head_count // groups
    slots_owner = tile_kv.shape[0]
    score_scale = 1.0 / math.sqrt(HEAD_DIM)
    position = seq_index * rows_dev + jnp.arange(rows_dev, dtype=jnp.int32)
    keep_rows = position < text_len[0]
    masked_grad = jnp.where(keep_rows[:, None], grad_out[0], jnp.zeros_like(grad_out[0]))
    products = masked_grad.astype(jnp.float32) * saved_output[0].astype(jnp.float32)
    row_delta = jnp.sum(products.reshape(rows_dev, head_count, HEAD_DIM), axis=2).astype(
        jnp.bfloat16
    )
    query_heads, grad_heads, delta_heads = (
        lax.all_to_all(queries[0], "seq", split_axis=1, concat_axis=0, tiled=True),
        lax.all_to_all(masked_grad, "seq", split_axis=1, concat_axis=0, tiled=True),
        lax.all_to_all(row_delta, "seq", split_axis=1, concat_axis=0, tiled=True),
    )
    text_rows = query_heads.shape[0]
    owners, global_slot, slot_valid = tile_places(tile_count, owner_perm, sample, slots_owner)
    empty_tiles = jnp.zeros((MAX_TILES,) + tile_kv.shape[1:], tile_kv.dtype)
    state_tiles = empty_tiles
    owner_piece = lax.all_gather(tile_kv, "dp", axis=0, tiled=True)
    piece_rows = owner_piece.shape[0]
    for slot_index in range(MAX_TILES):
        relative = global_slot[slot_index]
        inside = (relative >= 0) & (relative < piece_rows) & slot_valid[slot_index]
        one_tile = lax.dynamic_index_in_dim(
            owner_piece, jnp.clip(relative, 0, piece_rows - 1), 0, keepdims=False
        )
        state_tiles = state_tiles.at[slot_index].set(
            jnp.where(inside, one_tile, state_tiles[slot_index])
        )
    own_tiles = state_tiles
    own_tiles = jnp.where(slot_valid[:, None, None], own_tiles, jnp.zeros_like(own_tiles))
    partner_tiles = swapped(own_tiles, "seq", 0)
    is_even = seq_index % 2 == 0
    key_tiles = jnp.where(is_even, own_tiles, partner_tiles)
    value_tiles = jnp.where(is_even, partner_tiles, own_tiles)
    query_view = query_heads.reshape(text_rows, local_heads, HEAD_DIM)
    grad_view = grad_heads.reshape(text_rows, local_heads, HEAD_DIM)
    grad_rows, key_grads, value_grads = attend_backward(
        query_view, grad_view, delta_heads, key_tiles, value_tiles, tile_count[sample], score_scale
    )
    query_back = lax.all_to_all(
        grad_rows.reshape(text_rows, local_heads * HEAD_DIM),
        "seq",
        split_axis=0,
        concat_axis=1,
        tiled=True,
    )
    key_half, value_half = lax.optimization_barrier(
        (key_grads.astype(jnp.bfloat16), value_grads.astype(jnp.bfloat16))
    )
    send_part = jnp.where(is_even, value_half, key_half)
    keep_part = jnp.where(is_even, key_half, value_half)
    partner_part = swapped(send_part, "seq", 0)
    slot_total = (keep_part.astype(jnp.float32) + partner_part.astype(jnp.float32)).astype(
        jnp.bfloat16
    )
    row_ids = jnp.arange(slots_owner * lax.axis_size("dp"), dtype=jnp.int32)
    term_sum = jnp.zeros((slots_owner * lax.axis_size("dp"),) + slot_total.shape[1:], jnp.float32)
    for slot_index in range(MAX_TILES):
        slot_hit = (row_ids == global_slot[slot_index]) & slot_valid[slot_index]
        term_sum = jnp.where(
            slot_hit[:, None, None], slot_total[slot_index].astype(jnp.float32)[None], term_sum
        )
    grad_tiles = lax.psum_scatter(
        term_sum.astype(jnp.bfloat16), "dp", scatter_dimension=0, tiled=True
    )
    return (query_back[None], grad_tiles)


def solution(mesh):
    placed = (
        P("dp", "seq", None),
        P("dp", "seq", None),
        P("dp", "seq", None),
        P("dp", None, "seq"),
        P(),
        P(),
        P("dp"),
    )
    return jax.shard_map(
        shards,
        mesh=mesh,
        in_specs=placed,
        out_specs=(P("dp", "seq", None), P("dp", None, "seq")),
        check_vma=False,
    )
```

profile of v0, /device:TPU:0, one launch (start us, length us, event | category | flops | bytes accessed | tf_op | source)
XLA Modules:
  0.0 353.0 jit_solution(11258184831581632495)
XLA Ops:
  7.2 2.1 copy.46
  9.4 1.3 dynamic_slice.43
  10.7 0.8 reduce-window.9
  12.8 1.3 fusion.47
  14.8 1.3 fusion.48
  16.2 0.7 fusion.50
  24.6 0.7 iota_compare_fusion
  28.3 31.1 %all-gather.2.cloned.1.call-done = bf16[16,1601,128]{2,1,0:T(8,128)(2,1)} async-done(((bf16[2,1601,128]{2,1,0:T(8,128)(2,1)}), bf16[16,1601,128]{2,1,0:T(8,128)(2,1)}) %all-gather.2.cloned.1.call-update) | async-done | bytes 6557712 | tf_op jit(solution)/shard_map/all_gather | solution.py:145
  59.4 1.1 dynamic-slice_select_fusion
  60.7 1.1 select_dynamic-update-slice_fusion
  61.8 1.3 fusion.44
  63.1 1.3 fusion.43
  64.6 6.9 %copy.47 = bf16[4,1601,128]{2,0,1:T(4,128)(2,1)} copy(bf16[4,1601,128]{2,1,0:T(8,128)(2,1)S(1)} %broadcast_select_fusion) | data formatting | bytes 3278848 | tf_op jit(solution)/shard_map/jit(_where)/select_n | solution.py:157
  71.4 1.5 collective-permute-start
  74.9 3.7 %all-to-all-start.2 = ((bf16[128,4,2]{0,2,1:T(2,128)(2,1)}), bf16[128,4,2]{0,2,1:T(2,128)(2,1)S(1)}, u32[]{:S(2)}, u32[]{:S(2)}) async-start(bf16[128,4,2]{0,2,1:T(2,128)(2,1)} %bitcast.32), calls=%async_computation.2 | async-start | bytes 4096 | tf_op jit(solution)/shard_map/all_to_all | solution.py:139
  78.7 0.7 copy.49
  79.5 32.0 %all-to-all-done.2 = bf16[128,4,2]{0,2,1:T(2,128)(2,1)S(1)} async-done(((bf16[128,4,2]{0,2,1:T(2,128)(2,1)}), bf16[128,4,2]{0,2,1:T(2,128)(2,1)S(1)}, u32[]{:S(2)}, u32[]{:S(2)}) %all-to-all-start.2) | async-done | bytes 2080 | tf_op jit(solution)/shard_map/all_to_all | solution.py:139
  111.5 3.4 all-to-all-start
  115.1 0.8 copy_select_fusion
  115.9 7.4 %all-to-all-done = bf16[128,4,256]{2,0,1:T(8,128)(2,1)S(1)} async-done(((bf16[128,4,256]{2,0,1:T(8,128)(2,1)}), bf16[128,4,256]{2,0,1:T(8,128)(2,1)S(1)}, u32[]{:S(2)}, u32[]{:S(2)}) %all-to-all-start) | async-done | bytes 262176 | tf_op jit(solution)/shard_map/all_to_all | solution.py:137
  123.3 3.4 all-to-all-start.1
  126.9 6.7 %all-to-all-done.1 = bf16[128,4,256]{2,0,1:T(8,128)(2,1)S(1)} async-done(((bf16[128,4,256]{2,0,1:T(8,128)(2,1)}), bf16[128,4,256]{2,0,1:T(8,128)(2,1)S(1)}, u32[]{:S(2)}, u32[]{:S(2)}) %all-to-all-start.1) | async-done | bytes 262176 | tf_op jit(solution)/shard_map/all_to_all | solution.py:138
  133.8 3.6 %broadcast_select_fusion.2 = (bf16[4,1601,128]{2,1,0:T(8,128)(2,1)}, bf16[4,1601,128]{2,1,0:T(8,128)(2,1)}) fusion(pred[]{:T(512)S(6)} %eq.47, bf16[4,1601,128]{2,0,1:T(4,128)(2,1)} %collective-permute-done, bf16[4,1601,128]{2,1,0:T(8,128)(2,1)S(1)} %fusion.43, pred[4]{0:T(512)(128)(4,1)S(1)} %iota_compare_fusion), kind=kLoop, calls=%fused_computation.45 | loop fusion | flops 2459136 | bytes 6557701 | tf_op jit(solution)/shard_map/jit(_where)/select_n | solution.py:161
  137.4 4.6 %while.46 = (s32[]{:T(128)}, f32[2,512]{1,0:T(2,128)S(1)}, f32[2,512]{1,0:T(2,128)S(1)}, s32[]{:T(128)}, bf16[4,1601,128]{2,1,0:T(8,128)(2,1)}, /*index=5*/bf16[...) while((s32[]{:T(128)}, f32[2,512]{1,0:T(2,128)S(1)}, f32[2,512]{1,0:T(2,128)S(1)}, s32[]{:T(128)}, ...), condition=%wide.region_4.5_spmd, body=%wide.region_1.4_spmd.sunk | while | flops 427891712 | bytes 13842571 | solution.py:66
  138.1 2.1 bitcast_reduce_fusion.2
  140.2 1.1 fusion.76
  142.1 2.0 broadcast_in_dim.127.clone
  144.0 1.9 broadcast_in_dim.127
  145.9 11.3 %while.47 = (s32[]{:T(128)}, f32[512,2,128]{0,2,1:T(8,128)S(1)}, f32[4,1601,128]{2,1,0:T(8,128)}, f32[4,1601,128]{2,1,0:T(8,128)}, s32[]{:T(128)}, /*index=5*/bf...) while((s32[]{:T(128)}, f32[512,2,128]{0,2,1:T(8,128)S(1)}, ...), condition=%wide.region_7.8_spmd, body=%wide.region_6.7_spmd.sunk | while | flops 2110815616 | bytes 39433424 | solution.py:105
  146.8 1.5 constant_dynamic-slice_fusion.4
  148.3 1.4 fusion.87
  149.7 2.0 fusion.91
  151.8 2.1 fusion.88
  153.9 0.7 fusion.89
  154.6 2.0 fusion.90
  157.3 2.3 convert_element_type.79
  160.6 6.0 %copy.58 = bf16[4,1601,128]{2,0,1:T(4,128)(2,1)S(1)} copy(bf16[4,1601,128]{2,1,0:T(8,128)(2,1)S(1)} %broadcast_select_fusion.1) | data formatting | bytes 3278848 | tf_op jit(solution)/shard_map/jit(_where)/select_n | solution.py:177
  166.6 1.4 collective-permute-start.1
  167.9 2.5 compare_and_fusion.2
  170.4 2.4 compare_and_fusion
  172.9 28.3 %collective-permute-done.1 = bf16[4,1601,128]{2,0,1:T(4,128)(2,1)S(1)} collective-permute-done((bf16[4,1601,128]{2,0,1:T(4,128)(2,1)S(1)}, bf16[4,1601,128]{2,0,1:T(4,128)(2,1)S(1)}, u32[]{:S(2)}, u32[]{:S(2)}) %collective-permute-start.1) | collective-permute-done | bytes 1639456 | tf_op jit(solution)/shard_map/ppermute | solution.py:19
  201.9 9.7 %select_convert_fusion = bf16[16,1601,128]{2,0,1:T(8,128)(2,1)} fusion(bf16[1601,128]{1,0:T(8,128)(2,1)S(1)} %get-tuple-element.310, bf16[1601,128]{1,0:T(8,128)(2,1)S(1)} %get-tuple-element.311, bf16[1601,128]{1,0:T(8,128)(2,1)S(1)} %get-tuple-element.312, bf16[1601,128]{1,0:T(8,128)(2,1)S(1)} %get-tuple-element.309, ...), kind=kLoop, calls=%fused_computation.41 | loop fusion | flops 13115392 | bytes 8197184 | tf_op jit(solution)/shard_map/convert_element_type | solution.py:191
  211.7 0.9 copy.61
  212.6 3.4 all-to-all-start.3
  217.3 5.5 %all-to-all-done.3 = bf16[4,128,256]{2,1,0:T(8,128)(2,1)S(1)} async-done(((bf16[4,128,256]{2,1,0:T(8,128)(2,1)}), bf16[4,128,256]{2,1,0:T(8,128)(2,1)S(1)}, u32[]{:S(2)}, u32[]{:S(2)}) %all-to-all-start.3) | async-done | bytes 262176 | tf_op jit(solution)/shard_map/all_to_all | solution.py:167
  223.0 0.9 copy.60
  223.8 119.2 %all-reduce.4.cloned.1.call-done = bf16[16,1601,128]{2,0,1:T(8,128)(2,1)} async-done(((bf16[16,1601,128]{2,0,1:T(8,128)(2,1)}), bf16[16,1601,128]{2,0,1:T(8,128)(2,1)}) %all-reduce.4.cloned.1.call-update) | async-done | bytes 6557712
  343.0 3.1 constant_dynamic-slice_fusion.2
  (55 shorter events, 7.5 us)
Async XLA Ops:
  7.2 7.0 %copy-start = (s32[8]{0:T(128)S(1)}, s32[8]{0:T(128)}, u32[]{:S(2)}) copy-start(s32[8]{0:T(128)} %param.24) | copy-start | bytes 100
  7.2 52.2 %all-gather.2.cloned.1.call-start = ((), (), s32[]{:S(2)}) async-start(), calls=%async_computation.4 | async-start | bytes 7409664 | tf_op jit(solution)/shard_map/all_gather | solution.py:145
  64.4 9.2 %copy-start.4 = (bf16[1,128,1024]{2,1,0:T(8,128)(2,1)S(1)}, bf16[1,128,1024]{2,1,0:T(8,128)(2,1)}, u32[]{:S(2)}) copy-start(bf16[1,128,1024]{2,1,0:T(8,128)(2,1)} %param.21) | copy-start | bytes 786436
  64.4 9.3 %copy-start.5 = (bf16[1,128,1024]{2,1,0:T(8,128)(2,1)S(1)}, bf16[1,128,1024]{2,1,0:T(8,128)(2,1)}, u32[]{:S(2)}) copy-start(bf16[1,128,1024]{2,1,0:T(8,128)(2,1)} %param.20) | copy-start | bytes 786436
  64.6 14.0 %copy-start.6 = (bf16[1,128,1024]{2,1,0:T(8,128)(2,1)S(1)}, bf16[1,128,1024]{2,1,0:T(8,128)(2,1)}, u32[]{:S(2)}) copy-start(bf16[1,128,1024]{2,1,0:T(8,128)(2,1)} %param.19) | copy-start | bytes 786436
  71.4 62.3 %collective-permute-start = (bf16[4,1601,128]{2,0,1:T(4,128)(2,1)}, bf16[4,1601,128]{2,0,1:T(4,128)(2,1)}, u32[]{:S(2)}, u32[]{:S(2)}) collective-permute-start(bf16[4,1601,128]{2,0,1:T(4,128)(2,1)} %copy.47), channel_id=1, source_target_pairs={{0,8},{8,0},{16,24},{24,16},{1,9},{9,1},{17,25},{25,17},{2,10},{10... | collective-permute-start | bytes 4918280 | tf_op jit(solution)/shard_map/ppermute | solution.py:19
  74.9 36.6 %all-to-all-start.2 = ((bf16[128,4,2]{0,2,1:T(2,128)(2,1)}), bf16[128,4,2]{0,2,1:T(2,128)(2,1)S(1)}, u32[]{:S(2)}, u32[]{:S(2)}) async-start(bf16[128,4,2]{0,2,1:T(2,128)(2,1)} %bitcast.32), calls=%async_computation.2 | async-start | bytes 4096 | tf_op jit(solution)/shard_map/all_to_all | solution.py:139
  111.5 11.8 %all-to-all-start = ((bf16[128,4,256]{2,0,1:T(8,128)(2,1)}), bf16[128,4,256]{2,0,1:T(8,128)(2,1)S(1)}, u32[]{:S(2)}, u32[]{:S(2)}) async-start(bf16[128,4,256]{2,0,1:T(8,128)(2,1)} %copy.49), calls=%async_computation | async-start | bytes 524288 | tf_op jit(solution)/shard_map/all_to_all | solution.py:137
  123.3 10.3 %all-to-all-start.1 = ((bf16[128,4,256]{2,0,1:T(8,128)(2,1)}), bf16[128,4,256]{2,0,1:T(8,128)(2,1)S(1)}, u32[]{:S(2)}, u32[]{:S(2)}) async-start(bf16[128,4,256]{2,0,1:T(8,128)(2,1)} %copy_select_fusion), calls=%async_computation.1 | async-start | bytes 524288 | tf_op jit(solution)/shard_map/all_to_all | solution.py:138
  126.7 216.3 %all-reduce.4.cloned.1.call-start = ((), (), s32[]{:S(2)}) async-start(), calls=%async_computation.5 | async-start | bytes 13115392
  142.1 3.9 %copy-start.3 = (bf16[4,1601,128]{2,1,0:T(8,128)(2,1)S(1)}, bf16[4,1601,128]{2,1,0:T(8,128)(2,1)}, u32[]{:S(2)}) copy-start(bf16[4,1601,128]{2,1,0:T(8,128)(2,1)} %get-tuple-element.522) | copy-start | bytes 4918276
  157.3 2.9 copy-start.2
  166.6 34.6 %collective-permute-start.1 = (bf16[4,1601,128]{2,0,1:T(4,128)(2,1)S(1)}, bf16[4,1601,128]{2,0,1:T(4,128)(2,1)S(1)}, u32[]{:S(2)}, u32[]{:S(2)}) collective-permute-start(bf16[4,1601,128]{2,0,1:T(4,128)(2,1)S(1)} %copy.58), channel_id=1, source_target_pairs={{0,8},{8,0},{16,24},{24,16},{1,9},{9,1},{17,25},{25,17},{2,10},{10... | collective-permute-start | bytes 4918280 | tf_op jit(solution)/shard_map/ppermute | solution.py:19
  211.6 4.5 %copy-start.7 = (u32[32]{0:T(128)S(1)}, u32[32]{0:T(128)}, u32[]{:S(2)}) copy-start(u32[32]{0:T(128)} %constant.250) | copy-start | bytes 388
  211.6 134.5 %copy-start.1 = (s32[8]{0:T(128)S(1)}, s32[8]{0:T(128)}, u32[]{:S(2)}) copy-start(s32[8]{0:T(128)} %param.24) | copy-start | bytes 100
  212.6 10.2 %all-to-all-start.3 = ((bf16[4,128,256]{2,1,0:T(8,128)(2,1)}), bf16[4,128,256]{2,1,0:T(8,128)(2,1)S(1)}, u32[]{:S(2)}, u32[]{:S(2)}) async-start(bf16[4,128,256]{2,1,0:T(8,128)(2,1)} %copy.61), calls=%async_computation.3 | async-start | bytes 524288 | tf_op jit(solution)/shard_map/all_to_all | solution.py:167
Sparse Core Ops, SparseCore 0:
  9.9 49.4 all-gather.1
  211.7 131.2 all-reduce.3
where the time goes:
time: 357 us; the launch traced here: 353 us
  waiting for transfers between devices  230 us (64%)
  other arithmetic  33.7 us (9%)
  local copies, waits for them, and re-layouts  32.9 us (9%)
  between operations  25.8 us (7%)
  starting transfers between devices  16.8 us (5%)
  matrix products  10.3 us (3%)
    unnamed x3, waiting for transfers between devices  119 us
    all_to_all x1, waiting for transfers between devices, shards(): lax.all_to_all(row_delta, 'seq', split_axis=1, concat_axis=0, tiled=True)  32 us
    all_gather x1, waiting for transfers between devices, shards(): owner_piece = lax.all_gather(tile_kv, 'dp', axis=0, tiled=True)  31.1 us
    ppermute x2, waiting for transfers between devices, swapped(): return lax.ppermute(block, axis, route)  28.3 us
    convert_element_type x1, other arithmetic, shards(): term_sum.astype(jnp.bfloat16)  9.7 us
    unnamed x22, local copies, waits for them, and re-layouts  7.49 us
    all_to_all x1, waiting for transfers between devices, shards(): lax.all_to_all(queries[0], 'seq', split_axis=1, concat_axis=0, tiled=True)  7.44 us
  transfers between devices with their start and end apart: 8, of which 7 were waited for; matrix products, arithmetic and copies ran while one was open for 5% of the time, Pallas kernels for 0%

commit v1 on v0

v1 whole, which is shorter than its diff:
```python
import functools
import math

import jax
import jax.numpy as jnp
from jax import lax
from jax.experimental import pallas as pl
from jax.experimental.pallas import tpu as pltpu
from jax.sharding import PartitionSpec as P

HEAD_DIM = 128
MAX_TILES = 4
KEY_ROWS = 256
TEXT_CHUNKS = 4
DELTA_ROWS = 16
SCALE = 1.0 / math.sqrt(HEAD_DIM)
SCALE_LOG2 = SCALE / math.log(2.0)
BF16 = jnp.bfloat16
F32 = jnp.float32

SMEM = pl.BlockSpec(memory_space=pltpu.SMEM)
VMEM = pl.BlockSpec(memory_space=pltpu.VMEM)
ANY = pl.BlockSpec(memory_space=pl.ANY)


def exchange(block, axis, distance):
    count = lax.axis_size(axis)
    return lax.ppermute(block, axis, [(i, i ^ distance) for i in range(count)])


def call(kernel, out_shape, in_specs, scratch, args, out_specs=None, megabytes=16, flops=0, moved=0):
    many = isinstance(out_shape, (list, tuple))
    if out_specs is None:
        out_specs = [VMEM] * len(out_shape) if many else VMEM
    return pl.pallas_call(
        kernel,
        out_shape=out_shape,
        in_specs=in_specs,
        out_specs=out_specs,
        scratch_shapes=scratch,
        compiler_params=pltpu.CompilerParams(vmem_limit_bytes=megabytes << 20),
        cost_estimate=pl.CostEstimate(flops=flops, bytes_accessed=moved, transcendentals=0),
    )(*args)


def place_of(perm_ref, owner, owners):
    first = jnp.int32(0)
    for index in range(owners):
        first = first + jnp.where(perm_ref[index] == owner, index, 0)
    return first


def sample_at(count_ref, place, samples):
    end, sample, start = jnp.int32(0), jnp.int32(0), jnp.int32(0)
    for index in range(samples):
        end = end + count_ref[index]
        passed = place >= end
        sample = sample + passed.astype(jnp.int32)
        start = jnp.where(passed, end, start)
    return sample, start


def pack_kernel(groups, heads, who, length, q_ref, o_ref, g_ref, *outs):
    rows = q_ref.shape[0]
    seq = who[0]
    position = seq * rows + lax.broadcasted_iota(jnp.int32, (rows, HEAD_DIM), 0)
    keep = position < length[0]
    half = heads // 2
    for j in range(groups):
        q_out, g_out = outs[j], outs[groups + j]
        for h in range(heads):
            start = pl.multiple_of(((seq ^ j) * heads + h) * HEAD_DIM, HEAD_DIM)
            columns = pl.ds(start, HEAD_DIM)
            q_out[h // half, h % half] = q_ref[:, columns]
            grad = jnp.where(keep, g_ref[:, columns].astype(F32), 0.0)
            product = grad * o_ref[:, columns].astype(F32)
            delta = jnp.sum(jnp.transpose(product), axis=0, keepdims=True)
            g_out[h // half, h % half, :rows] = grad.astype(BF16)
            g_out[h // half, h % half, rows:] = jnp.broadcast_to(
                delta, (DELTA_ROWS, HEAD_DIM)
            ).astype(BF16)


def fetch(pieces, relative, target, sem):
    for index, piece in enumerate(pieces):
        @pl.when(relative == index)
        def _(piece=piece):
            pltpu.make_async_copy(piece, target, sem).start()


def chunks_of(rows):
    full = rows // KEY_ROWS
    tail = rows - full * KEY_ROWS
    return full, tail, -(-tail // 16) * 16


def dot_nt(a, b):
    return lax.dot_general(a, b, (((1,), (1,)), ((), ())), preferred_element_type=F32)


def dot_nn(a, b):
    return jnp.dot(a, b, preferred_element_type=F32)


def stats_kernel(owners, heads, slots, who, counts, perm, own_kv, partner_kv, *refs):
    q_pieces = (refs[:owners], refs[owners:2 * owners])
    out, q_buf, k_buf, k_tail, q_sem, k_sem = refs[2 * owners:]
    seq, me = who[0], who[1]
    groups = q_buf.shape[2]
    half = heads // 2
    rows = k_buf.shape[1]
    full, tail, tail_pad = chunks_of(rows)
    first = place_of(perm, me, owners)
    samples = [sample_at(counts, first + slot * owners, owners)[0] for slot in range(slots)]
    for slot in range(slots):
        @pl.when(samples[slot] < owners)
        def _(slot=slot):
            @pl.when(seq % 2 == 0)
            def _():
                pltpu.make_async_copy(own_kv.at[slot], k_buf.at[slot], k_sem.at[slot]).start()

            @pl.when(seq % 2 == 1)
            def _():
                pltpu.make_async_copy(partner_kv.at[slot], k_buf.at[slot], k_sem.at[slot]).start()

            for side in range(2):
                fetch(q_pieces[side], samples[slot] ^ me, q_buf.at[slot, side], q_sem.at[slot, side])
    k_tail[...] = jnp.zeros(k_tail.shape, BF16)
    text_chunks = min(TEXT_CHUNKS, groups)
    width = text_chunks * HEAD_DIM

    for slot in range(slots):
        @pl.when(samples[slot] < owners)
        def _(slot=slot):
            pltpu.make_async_copy(own_kv.at[slot], k_buf.at[slot], k_sem.at[slot]).wait()
            for side in range(2):
                pltpu.make_async_copy(q_pieces[side][0], q_buf.at[slot, side], q_sem.at[slot, side]).wait()
            k_tail[:tail] = k_buf[slot, full * KEY_ROWS:]

            def one_block(step, carry):
                head, block = step // (groups // text_chunks), step % (groups // text_chunks)
                query = q_buf[slot, head // half, pl.ds(block * text_chunks, text_chunks), head % half]
                query = query.reshape(width, HEAD_DIM)
                peak = jnp.full((8, width), -jnp.inf, F32)
                mass = jnp.zeros((8, width), F32)
                for chunk in range(full + 1):
                    if chunk < full:
                        scores = dot_nt(k_buf[slot, chunk * KEY_ROWS:(chunk + 1) * KEY_ROWS], query)
                    else:
                        scores = dot_nt(k_tail[...], query)
                        row = lax.broadcasted_iota(jnp.int32, scores.shape, 0)
                        scores = jnp.where(row < tail, scores, -jnp.inf)
                    scores = scores.reshape(-1, 8, width)
                    new_peak = jnp.maximum(peak, jnp.max(scores, axis=0))
                    shift = new_peak * SCALE_LOG2
                    mass = mass * jnp.exp2(peak * SCALE_LOG2 - shift) + jnp.sum(
                        jnp.exp2(scores * SCALE_LOG2 - shift[None]), axis=0
                    )
                    peak = new_peak
                peak = peak * SCALE_LOG2
                top = jnp.max(peak, axis=0, keepdims=True)
                total = jnp.sum(mass * jnp.exp2(peak - top), axis=0, keepdims=True)
                for piece in range(text_chunks):
                    lanes = slice(piece * HEAD_DIM, (piece + 1) * HEAD_DIM)
                    place = block * text_chunks + piece
                    out[slot, 0, head, pl.ds(place, 1)] = top[:, lanes]
                    out[slot, 1, head, pl.ds(place, 1)] = total[:, lanes]
                return carry

            lax.fori_loop(0, heads * (groups // text_chunks), one_block, 0)


def grads_kernel(owners, heads, slots, who, counts, perm, stats, own_kv, partner_kv, *refs):
    q_pieces = (refs[:owners], refs[owners:2 * owners])
    g_pieces = (refs[2 * owners:3 * owners], refs[3 * owners:4 * owners])
    (dq_out, keep_out, send_out, q_buf, g_buf, kv_buf, kv_tail, k_turn, sums, q_sem, g_sem, kv_sem) = refs[4 * owners:]
    seq, me = who[0], who[1]
    parity = seq % 2
    groups = q_buf.shape[2]
    half = heads // 2
    rows = kv_buf.shape[2]
    full, tail, tail_pad = chunks_of(rows)
    first = place_of(perm, me, owners)
    placed = [sample_at(counts, first + slot * owners, owners) for slot in range(slots)]
    for slot in range(slots):
        sample = placed[slot][0]

        @pl.when(sample < owners)
        def _(slot=slot, sample=sample):
            pltpu.make_async_copy(own_kv.at[slot], kv_buf.at[slot, parity], kv_sem.at[slot, 0]).start()
            pltpu.make_async_copy(partner_kv.at[slot], kv_buf.at[slot, 1 - parity], kv_sem.at[slot, 1]).start()
            for side in range(2):
                fetch(q_pieces[side], sample ^ me, q_buf.at[slot, side], q_sem.at[slot, side])
                fetch(g_pieces[side], sample ^ me, g_buf.at[slot, side], g_sem.at[slot, side])
    kv_tail[...] = jnp.zeros(kv_tail.shape, BF16)
    text_chunks = min(TEXT_CHUNKS, groups)
    width = text_chunks * HEAD_DIM
    spans = [(index * KEY_ROWS, KEY_ROWS) for index in range(full)] + [(full * KEY_ROWS, tail_pad)]

    for slot in range(slots):
        sample, start = placed[slot]

        @pl.when(sample >= owners)
        def _(slot=slot):
            keep_out[slot] = jnp.zeros(keep_out.shape[1:], BF16)
            send_out[slot] = jnp.zeros(send_out.shape[1:], BF16)

        @pl.when(sample < owners)
        def _(slot=slot, sample=sample, start=start):
            pltpu.make_async_copy(own_kv.at[slot], kv_buf.at[slot, parity], kv_sem.at[slot, 0]).wait()
            pltpu.make_async_copy(partner_kv.at[slot], kv_buf.at[slot, 1 - parity], kv_sem.at[slot, 1]).wait()
            for side in range(2):
                pltpu.make_async_copy(q_pieces[side][0], q_buf.at[slot, side], q_sem.at[slot, side]).wait()
                pltpu.make_async_copy(g_pieces[side][0], g_buf.at[slot, side], g_sem.at[slot, side]).wait()
            kv_tail[0, :tail] = kv_buf[slot, 0, full * KEY_ROWS:]
            kv_tail[1, :tail] = kv_buf[slot, 1, full * KEY_ROWS:]

            def rows_of(which, index):
                if index < full:
                    return kv_buf[slot, which, index * KEY_ROWS:(index + 1) * KEY_ROWS]
                return kv_tail[which]

            for index, (low, size) in enumerate(spans):
                k_turn[:, low:low + size] = jnp.transpose(rows_of(0, index).astype(F32)).astype(BF16)
            sums[...] = jnp.zeros(sums.shape, F32)
            tiles = counts[jnp.minimum(sample, owners - 1)]

            def normaliser(head, piece):
                found = []
                for index in range(MAX_TILES):
                    live = index < tiles
                    place = jnp.where(live, start + index, start)
                    other = perm[place % owners] ^ me
                    top = stats[other, place // owners, 0, head, pl.ds(piece, 1)]
                    mass = stats[other, place // owners, 1, head, pl.ds(piece, 1)]
                    found.append((jnp.where(live, top, -jnp.inf), jnp.where(live, mass, 0.0)))
                top = functools.reduce(jnp.maximum, [peak for peak, _ in found])
                total = sum(mass * jnp.exp2(peak - top) for peak, mass in found)
                return top + jnp.log2(total)

            def one_block(step, carry):
                head, block = step // (groups // text_chunks), step % (groups // text_chunks)
                side, inner = head // half, head % half
                pieces = pl.ds(block * text_chunks, text_chunks)
                query = q_buf[slot, side, pieces, inner].reshape(width, HEAD_DIM)
                grad = g_buf[slot, side, pieces, inner, :HEAD_DIM].reshape(width, HEAD_DIM)
                delta = jnp.concatenate(
                    [
                        g_buf[slot, side, block * text_chunks + piece, inner, HEAD_DIM:].astype(F32)[:1]
                        for piece in range(text_chunks)
                    ],
                    axis=1,
                )
                level = jnp.concatenate(
                    [normaliser(head, block * text_chunks + piece) for piece in range(text_chunks)], axis=1
                )
                turned = jnp.zeros((HEAD_DIM, width), F32)
                for index, (low, size) in enumerate(spans):
                    scores = dot_nt(rows_of(0, index), query)
                    weights = jnp.exp2(scores * SCALE_LOG2 - level)
                    if index == full:
                        row = lax.broadcasted_iota(jnp.int32, scores.shape, 0)
                        weights = jnp.where(row < tail, weights, 0.0)
                    slope = dot_nt(rows_of(1, index), grad)
                    bent = (weights * (slope - delta)).astype(BF16)
                    turned = turned + dot_nn(k_turn[:, low:low + size], bent)
                    sums[0, low:low + size] += dot_nn(bent, query)
                    sums[1, low:low + size] += dot_nn(weights.astype(BF16), grad)
                result = (jnp.transpose(turned) * SCALE).astype(BF16)
                start_row = pl.multiple_of(block * width, width)
                start_col = pl.multiple_of(head * HEAD_DIM, HEAD_DIM)
                dq_out[slot, pl.ds(start_row, width), pl.ds(start_col, HEAD_DIM)] = result
                return carry

            lax.fori_loop(0, heads * (groups // text_chunks), one_block, 0)
            keep_scale = jnp.where(parity == 0, SCALE, 1.0)
            send_scale = jnp.where(parity == 0, 1.0, SCALE)
            keep_out[slot] = (sums[parity, :rows] * keep_scale).astype(BF16)
            send_out[slot] = (sums[1 - parity, :rows] * send_scale).astype(BF16)


def route_kernel(owners, slots, who, counts, perm, own, other, *outs):
    me = who[1]
    found = []
    for near, source in ((me, own), (me ^ 1, other)):
        first = place_of(perm, near, owners)
        for slot in range(slots):
            found.append((sample_at(counts, first + slot * owners, owners)[0], source, slot))
    block = 128
    for distance, out in enumerate(outs):
        target = me ^ (2 * distance)

        def one(step, carry):
            rows = pl.ds(pl.multiple_of(step * block, block), block)
            total = jnp.zeros((block, out.shape[1]), F32)
            for sample, source, slot in found:
                total = total + jnp.where(sample == target, source[slot, rows].astype(F32), 0.0)
            out[rows] = total.astype(BF16)
            return carry

        lax.fori_loop(0, out.shape[0] // block, one, 0)


def gather_kernel(parts, *refs):
    outs = refs[parts:]
    rows = outs[0].shape[0]
    for piece, out in enumerate(outs):
        span = slice(piece * rows, (piece + 1) * rows)
        out[...] = sum(ref[span].astype(F32) for ref in refs[:parts]).astype(BF16)


def place_kernel(who, *refs):
    out = refs[-1]
    for distance, ref in enumerate(refs[:-1]):
        width = ref.shape[1]
        start = pl.multiple_of((who[0] ^ distance) * width, width)
        out[:, pl.ds(start, width)] = ref[...]


def gather_pieces(block, turn):
    count = lax.axis_size("dp")
    near = {0: block}
    for distance in sorted(range(2, count, 2), key=lambda d: (bin(d).count("1"), d)):
        last = 1 << (distance.bit_length() - 1) if turn == 0 else distance & -distance
        near[distance] = exchange(near[distance ^ last], "dp", last)
    result = [None] * count
    for distance, piece in near.items():
        result[distance] = piece
        result[distance ^ 1] = exchange(piece, "dp", 1)
    return result


def shards(queries, saved_output, grad_out, tile_kv, tile_count, owner_perm, text_len):
    rows_dev, features = queries.shape[1], queries.shape[2]
    groups, owners = lax.axis_size("seq"), lax.axis_size("dp")
    heads = features // HEAD_DIM // groups
    half = heads // 2
    width = heads * HEAD_DIM
    text_rows = groups * rows_dev
    slots, tile_rows = tile_kv.shape[0], tile_kv.shape[1]
    full, tail, tail_pad = chunks_of(tile_rows)
    padded = full * KEY_ROWS + tail_pad
    who = jnp.stack([lax.axis_index("seq"), lax.axis_index("dp")]).astype(jnp.int32)

    q_shape = jax.ShapeDtypeStruct((2, half, rows_dev, HEAD_DIM), BF16)
    g_shape = jax.ShapeDtypeStruct((2, half, rows_dev + DELTA_ROWS, HEAD_DIM), BF16)
    packed = call(
        functools.partial(pack_kernel, groups, heads),
        [q_shape] * groups + [g_shape] * groups,
        [SMEM, SMEM] + [VMEM] * 3,
        [],
        (who, text_len, queries[0], saved_output[0], grad_out[0]),
    )

    def over_seq(pieces):
        got = [pieces[0]] + [exchange(pieces[j], "seq", j) for j in range(1, groups)]
        return [jnp.stack([piece[side] for piece in got]) for side in range(2)]

    q_sides = [gather_pieces(block, side) for side, block in enumerate(over_seq(packed[:groups]))]
    g_sides = [gather_pieces(block, side) for side, block in enumerate(over_seq(packed[groups:]))]
    partner_kv = exchange(tile_kv, "seq", 1)

    stats = call(
        functools.partial(stats_kernel, owners, heads, slots),
        jax.ShapeDtypeStruct((slots, 2, heads, groups, rows_dev), F32),
        [SMEM] * 3 + [ANY] * (2 + 2 * owners),
        [
            pltpu.VMEM((slots, 2, groups, half, rows_dev, HEAD_DIM), BF16),
            pltpu.VMEM((slots, tile_rows, HEAD_DIM), BF16),
            pltpu.VMEM((tail_pad, HEAD_DIM), BF16),
            pltpu.SemaphoreType.DMA((slots, 2)),
            pltpu.SemaphoreType.DMA((slots,)),
        ],
        (who, tile_count, owner_perm, tile_kv, partner_kv, *q_sides[0], *q_sides[1]),
        megabytes=32,
        flops=slots * 2 * width * text_rows * tile_rows,
    )
    pair = jnp.stack([stats, exchange(stats, "dp", 1)])
    all_stats = jnp.concatenate([pair] + [exchange(pair, "dp", d) for d in range(2, owners, 2)])

    kv_shape = jax.ShapeDtypeStruct(tile_kv.shape, BF16)
    grads_q, kv_keep, kv_send = call(
        functools.partial(grads_kernel, owners, heads, slots),
        [jax.ShapeDtypeStruct((slots, text_rows, width), BF16), kv_shape, kv_shape],
        [SMEM] * 3 + [VMEM] + [ANY] * (2 + 4 * owners),
        [
            pltpu.VMEM((slots, 2, groups, half, rows_dev, HEAD_DIM), BF16),
            pltpu.VMEM((slots, 2, groups, half, rows_dev + DELTA_ROWS, HEAD_DIM), BF16),
            pltpu.VMEM((slots, 2, tile_rows, HEAD_DIM), BF16),
            pltpu.VMEM((2, tail_pad, HEAD_DIM), BF16),
            pltpu.VMEM((HEAD_DIM, -(-padded // HEAD_DIM) * HEAD_DIM), BF16),
            pltpu.VMEM((2, padded, HEAD_DIM), F32),
            pltpu.SemaphoreType.DMA((slots, 2)),
            pltpu.SemaphoreType.DMA((slots, 2)),
            pltpu.SemaphoreType.DMA((slots, 2)),
        ],
        (who, tile_count, owner_perm, all_stats, tile_kv, partner_kv, *q_sides[0], *q_sides[1], *g_sides[0], *g_sides[1]),
        megabytes=48,
        flops=slots * 10 * width * text_rows * tile_rows,
    )
    kv_got = exchange(kv_send, "seq", 1)
    grad_tiles = (kv_keep.astype(F32) + kv_got.astype(F32)).astype(BF16)

    sums = call(
        functools.partial(route_kernel, owners, slots),
        [jax.ShapeDtypeStruct((text_rows, width), BF16)] * (owners // 2),
        [SMEM] * 3 + [VMEM] * 2,
        [],
        (who, tile_count, owner_perm, grads_q, exchange(grads_q, "dp", 1)),
        megabytes=32,
    )
    sums = [sums[0]] + [exchange(sums[d], "dp", 2 * d) for d in range(1, owners // 2)]
    cut = call(
        functools.partial(gather_kernel, len(sums)),
        [jax.ShapeDtypeStruct((rows_dev, width), BF16)] * groups,
        [VMEM] * len(sums),
        [],
        sums,
        megabytes=32,
    )
    back = [cut[0]] + [exchange(cut[j], "seq", j) for j in range(1, groups)]
    grad_queries = call(
        place_kernel,
        jax.ShapeDtypeStruct((rows_dev, features), BF16),
        [SMEM] + [VMEM] * groups,
        [],
        (who, *back),
    )
    return (grad_queries[None], grad_tiles)


def solution(mesh):
    placed = (
        P("dp", "seq", None),
        P("dp", "seq", None),
        P("dp", "seq", None),
        P("dp", None, "seq"),
        P(),
        P(),
        P("dp"),
    )
    return jax.shard_map(
        shards,
        mesh=mesh,
        in_specs=placed,
        out_specs=(P("dp", "seq", None), P("dp", None, "seq")),
        check_vma=False,
    )
```

time: 357 us -> 120 us (0.34); the launches traced: 353 us -> 120 us
  waiting for transfers between devices: 230 us -> 31.7 us
  starting transfers between devices: 16.8 us -> 53 us
  other arithmetic: 33.7 us -> 0.33 us
  between operations: 25.8 us -> 1.63 us
  Pallas kernels: 0 us -> 16.9 us
  local copies, waits for them, and re-layouts: 32.9 us -> 16.4 us
  matrix products: 10.3 us -> 0 us
    unnamed x3 -> x0, waiting for transfers between devices: 119 us -> none
    all_to_all x4 -> x0, waiting for transfers between devices: 51.7 us -> none  [the longest x1 32 us: shards(): lax.all_to_all(row_delta, 'seq', split_axis=1, concat_axis=0, tiled=True)]
    ppermute x2 -> x47, starting transfers between devices: 2.84 us -> 53 us  [exchange(): return lax.ppermute(block, axis, [(i, i ^ distance) for i in range(count)])]
    all_gather x1 -> x0, waiting for transfers between devices: 31.1 us -> none  [shards(): owner_piece = lax.all_gather(tile_kv, 'dp', axis=0, tiled=True)]
    pallas_call x0 -> x6, Pallas kernels: none -> 16.9 us  [call(): pl.pallas_call(kernel, out_shape=out_shape, in_specs=in_specs, out_specs=...]
    all_to_all x4 -> x0, starting transfers between devices: 13.9 us -> none  [the longest x1 3.68 us: shards(): lax.all_to_all(row_delta, 'seq', split_axis=1, concat_axis=0, tiled=True)]
    select_n x2 -> x0, local copies, waits for them, and re-layouts: 12.8 us -> none  [the longest x1 6.85 us: shards(): jnp.where(slot_valid[:, None, None], own_tiles, jnp.zeros_like(own_tiles))]
    convert_element_type x5 -> x1, other arithmetic: 12.8 us -> 0.16 us  [shards(): grad_tiles = (kv_keep.astype(F32) + kv_got.astype(F32)).astype(BF16)]
  transfers between devices with their start and end apart: 8 -> 47, of which waited for: 7 -> 14; matrix products, arithmetic and copies ran while one was open for 5% -> 6% of each run, Pallas kernels for 0% -> 4%
where the time goes in v1:
time: 120 us
  starting transfers between devices  53 us (44%)
  waiting for transfers between devices  31.7 us (26%)
  Pallas kernels  16.9 us (14%)
  local copies, waits for them, and re-layouts  16.4 us (14%)
  between operations  1.63 us (1%)
    ppermute x47, starting transfers between devices, exchange(): return lax.ppermute(block, axis, [(i, i ^ distance) for i in range(count)])  53 us
    ppermute x47, waiting for transfers between devices, exchange(): return lax.ppermute(block, axis, [(i, i ^ distance) for i in range(count)])  31.7 us
    pallas_call x6, Pallas kernels, call(): pl.pallas_call(kernel, out_shape=out_shape, in_specs=in_specs, out_specs=...  16.9 us
    unnamed x22, local copies, waits for them, and re-layouts  9.71 us
    pallas_call x1, local copies, waits for them, and re-layouts, call(): pl.pallas_call(kernel, out_shape=out_shape, in_specs=in_specs, out_specs=...  6.53 us
  transfers between devices with their start and end apart: 47, of which 14 were waited for; matrix products, arithmetic and copies ran while one was open for 6% of the time, Pallas kernels for 4%

profile of v1, /device:TPU:0, one launch (start us, length us, event | category | flops | bytes accessed | tf_op | source)
XLA Modules:
  0.0 120.0 jit_solution(8424432954838970071)
XLA Ops:
  1.4 0.9 copy-done.2
  2.3 0.9 copy-done.3
  3.3 0.9 copy-done.4
  4.2 0.9 shard_map.86
  5.1 3.1 %collective-permute-start.1 = (bf16[2,1,128,128]{3,2,1,0:T(8,128)(2,1)S(1)}, bf16[2,1,128,128]{3,2,1,0:T(8,128)(2,1)S(1)}, u32[]{:S(2)}, u32[]{:S(2)}) collective-permute-start(bf16[2,1,128,128]{3,2,1,0:T(8,128)(2,1)S(1)} %get-tuple-element.22), channel_id=1, source_target_pairs={{0,8},{8,0},{16,24},{24,16},{1,9},{9,1},{17,25},{25,17},{2,10},{10... | collective-permute-start | bytes 196616 | tf_op jit(solution)/shard_map/ppermute | solution.py:28
  8.2 2.6 %collective-permute-start.2 = (bf16[2,1,128,128]{3,2,1,0:T(8,128)(2,1)S(1)}, bf16[2,1,128,128]{3,2,1,0:T(8,128)(2,1)S(1)}, u32[]{:S(2)}, u32[]{:S(2)}) collective-permute-start(bf16[2,1,128,128]{3,2,1,0:T(8,128)(2,1)S(1)} %get-tuple-element.23), channel_id=1, source_target_pairs={{0,16},{8,24},{16,0},{24,8},{1,17},{9,25},{17,1},{25,9},{2,18},{10... | collective-permute-start | bytes 196616 | tf_op jit(solution)/shard_map/ppermute | solution.py:28
  10.8 0.9 collective-permute-start.22
  11.7 3.5 %collective-permute-start.23 = (bf16[2,1,144,128]{3,2,1,0:T(8,128)(2,1)S(1)}, bf16[2,1,144,128]{3,2,1,0:T(8,128)(2,1)S(1)}, u32[]{:S(2)}, u32[]{:S(2)}) collective-permute-start(bf16[2,1,144,128]{3,2,1,0:T(8,128)(2,1)S(1)} %get-tuple-element.27), channel_id=1, source_target_pairs={{0,16},{8,24},{16,0},{24,8},{1,17},{9,25},{17,1},{25,9},{2,18},{10... | collective-permute-start | bytes 221192 | tf_op jit(solution)/shard_map/ppermute | solution.py:28
  15.6 0.9 collective-permute-start
  16.5 1.0 collective-permute-done.3
  17.6 1.6 %collective-permute-start.7 = (bf16[4,1,128,128]{3,2,1,0:T(8,128)(2,1)S(1)}, bf16[4,1,128,128]{3,2,1,0:T(8,128)(2,1)S(1)}, u32[]{:S(2)}, u32[]{:S(2)}) collective-permute-start(bf16[4,1,128,128]{3,2,1,0:T(8,128)(2,1)S(1)} %pad_maximum_fusion.2.refs_0_), channel_id=1, source_target_pairs={{0,4},{1,5},{2,6},{3,7},{4,0},{5,1},{6,2},{7,3},{8,12},{9,13},{10,... | collective-permute-start | bytes 393224 | tf_op jit(solution)/shard_map/ppermute | solution.py:28
  19.3 1.6 %collective-permute-start.5 = (bf16[4,1,128,128]{3,2,1,0:T(8,128)(2,1)S(1)}, bf16[4,1,128,128]{3,2,1,0:T(8,128)(2,1)S(1)}, u32[]{:S(2)}, u32[]{:S(2)}) collective-permute-start(bf16[4,1,128,128]{3,2,1,0:T(8,128)(2,1)S(1)} %pad_maximum_fusion.2.refs_0_), channel_id=1, source_target_pairs={{0,2},{1,3},{2,0},{3,1},{4,6},{5,7},{6,4},{7,5},{8,10},{9,11},{10,... | collective-permute-start | bytes 393224 | tf_op jit(solution)/shard_map/ppermute | solution.py:28
  20.9 1.5 %collective-permute-done.23 = bf16[2,1,144,128]{3,2,1,0:T(8,128)(2,1)S(1)} collective-permute-done((bf16[2,1,144,128]{3,2,1,0:T(8,128)(2,1)S(1)}, bf16[2,1,144,128]{3,2,1,0:T(8,128)(2,1)S(1)}, u32[]{:S(2)}, u32[]{:S(2)}) %collective-permute-start.23) | collective-permute-done | bytes 73760 | tf_op jit(solution)/shard_map/ppermute | solution.py:28
  22.4 1.5 %collective-permute-start.14 = (bf16[4,1,128,128]{3,2,1,0:T(8,128)(2,1)S(1)}, bf16[4,1,128,128]{3,2,1,0:T(8,128)(2,1)S(1)}, u32[]{:S(2)}, u32[]{:S(2)}) collective-permute-start(bf16[4,1,128,128]{3,2,1,0:T(8,128)(2,1)S(1)} %pad_maximum_fusion.3.refs_8_), channel_id=1, source_target_pairs={{0,4},{1,5},{2,6},{3,7},{4,0},{5,1},{6,2},{7,3},{8,12},{9,13},{10,... | collective-permute-start | bytes 393224 | tf_op jit(solution)/shard_map/ppermute | solution.py:28
  23.9 1.5 %collective-permute-start.12 = (bf16[4,1,128,128]{3,2,1,0:T(8,128)(2,1)S(1)}, bf16[4,1,128,128]{3,2,1,0:T(8,128)(2,1)S(1)}, u32[]{:S(2)}, u32[]{:S(2)}) collective-permute-start(bf16[4,1,128,128]{3,2,1,0:T(8,128)(2,1)S(1)} %pad_maximum_fusion.3.refs_8_), channel_id=1, source_target_pairs={{0,2},{1,3},{2,0},{3,1},{4,6},{5,7},{6,4},{7,5},{8,10},{9,11},{10,... | collective-permute-start | bytes 393224 | tf_op jit(solution)/shard_map/ppermute | solution.py:28
  26.0 2.3 %collective-permute-done.14.refs_12_ = bf16[4,1,128,128]{3,2,1,0:T(8,128)(2,1)S(1)} collective-permute-done((bf16[4,1,128,128]{3,2,1,0:T(8,128)(2,1)S(1)}, bf16[4,1,128,128]{3,2,1,0:T(8,128)(2,1)S(1)}, u32[]{:S(2)}, u32[]{:S(2)}) %collective-permute-start.14) | collective-permute-done | bytes 131104 | tf_op jit(solution)/shard_map/ppermute | solution.py:28
  28.3 1.5 %collective-permute-start.9 = (bf16[4,1,128,128]{3,2,1,0:T(8,128)(2,1)S(1)}, bf16[4,1,128,128]{3,2,1,0:T(8,128)(2,1)S(1)}, u32[]{:S(2)}, u32[]{:S(2)}) collective-permute-start(bf16[4,1,128,128]{3,2,1,0:T(8,128)(2,1)S(1)} %collective-permute-done.5.refs_2_), channel_id=1, source_target_pairs={{0,4},{1,5},{2,6},{3,7},{4,0},{5,1},{6,2},{7,3},{8,12},{9,13},{10,... | collective-permute-start | bytes 393224 | tf_op jit(solution)/shard_map/ppermute | solution.py:28
  29.8 1.5 %collective-permute-start.16 = (bf16[4,1,128,128]{3,2,1,0:T(8,128)(2,1)S(1)}, bf16[4,1,128,128]{3,2,1,0:T(8,128)(2,1)S(1)}, u32[]{:S(2)}, u32[]{:S(2)}) collective-permute-start(bf16[4,1,128,128]{3,2,1,0:T(8,128)(2,1)S(1)} %collective-permute-done.14.refs_12_), channel_id=1, source_target_pairs={{0,2},{1,3},{2,0},{3,1},{4,6},{5,7},{6,4},{7,5},{8,10},{9,11},{10,... | collective-permute-start | bytes 393224 | tf_op jit(solution)/shard_map/ppermute | solution.py:28
  31.9 1.5 %collective-permute-done.9.refs_6_ = bf16[4,1,128,128]{3,2,1,0:T(8,128)(2,1)S(1)} collective-permute-done((bf16[4,1,128,128]{3,2,1,0:T(8,128)(2,1)S(1)}, bf16[4,1,128,128]{3,2,1,0:T(8,128)(2,1)S(1)}, u32[]{:S(2)}, u32[]{:S(2)}) %collective-permute-start.9) | collective-permute-done | bytes 131104 | tf_op jit(solution)/shard_map/ppermute | solution.py:28
  33.4 1.4 %collective-permute-done.16.refs_14_ = bf16[4,1,128,128]{3,2,1,0:T(8,128)(2,1)S(1)} collective-permute-done((bf16[4,1,128,128]{3,2,1,0:T(8,128)(2,1)S(1)}, bf16[4,1,128,128]{3,2,1,0:T(8,128)(2,1)S(1)}, u32[]{:S(2)}, u32[]{:S(2)}) %collective-permute-start.16) | collective-permute-done | bytes 131104 | tf_op jit(solution)/shard_map/ppermute | solution.py:28
  34.8 2.7 %collective-permute-done = bf16[2,1601,128]{2,0,1:T(2,128)(2,1)S(1)} collective-permute-done((bf16[2,1601,128]{2,0,1:T(2,128)(2,1)S(1)}, bf16[2,1601,128]{2,0,1:T(2,128)(2,1)S(1)}, u32[]{:S(2)}, u32[]{:S(2)}) %collective-permute-start) | collective-permute-done | bytes 819744 | tf_op jit(solution)/shard_map/ppermute | solution.py:28
  37.7 1.7 %collective-permute-start.28 = (bf16[4,1,144,128]{3,2,1,0:T(8,128)(2,1)S(1)}, bf16[4,1,144,128]{3,2,1,0:T(8,128)(2,1)S(1)}, u32[]{:S(2)}, u32[]{:S(2)}) collective-permute-start(bf16[4,1,144,128]{3,2,1,0:T(8,128)(2,1)S(1)} %pad_maximum_fusion.refs_16_), channel_id=1, source_target_pairs={{0,4},{1,5},{2,6},{3,7},{4,0},{5,1},{6,2},{7,3},{8,12},{9,13},{10,... | collective-permute-start | bytes 442376 | tf_op jit(solution)/shard_map/ppermute | solution.py:28
  39.4 1.5 %collective-permute-start.26 = (bf16[4,1,144,128]{3,2,1,0:T(8,128)(2,1)S(1)}, bf16[4,1,144,128]{3,2,1,0:T(8,128)(2,1)S(1)}, u32[]{:S(2)}, u32[]{:S(2)}) collective-permute-start(bf16[4,1,144,128]{3,2,1,0:T(8,128)(2,1)S(1)} %pad_maximum_fusion.refs_16_), channel_id=1, source_target_pairs={{0,2},{1,3},{2,0},{3,1},{4,6},{5,7},{6,4},{7,5},{8,10},{9,11},{10,... | collective-permute-start | bytes 442376 | tf_op jit(solution)/shard_map/ppermute | solution.py:28
  40.9 3.5 %shard_map.87 = f32[2,2,2,4,128]{4,3,2,1,0:T(4,128)S(1)} custom-call(s32[2]{0:T(128)S(1)} %pad_add_fusion.who, s32[8]{0:T(128)S(1)} %copy-done.5, s32[8]{0:T(128)S(1)} %copy-done.6, bf16[2,1601,128]{2,1,0:T(8,128)(2,1)S(1)} %copy.13.own_kv, bf16[2,1601,128]{2,1,0:T(8,128)(2,1)S(1)} %copy.14.partner_kv, ...), custom_call_target="tpu_custom_call" | custom-call | flops 839385088 | tf_op jit(solution)/shard_map/pallas_call | solution.py:35
  44.5 0.6 collective-permute-start.18
  45.0 3.4 %collective-permute-start.35 = (bf16[4,1,144,128]{3,2,1,0:T(8,128)(2,1)S(1)}, bf16[4,1,144,128]{3,2,1,0:T(8,128)(2,1)S(1)}, u32[]{:S(2)}, u32[]{:S(2)}) collective-permute-start(bf16[4,1,144,128]{3,2,1,0:T(8,128)(2,1)S(1)} %pad_maximum_fusion.1.refs_24_), channel_id=1, source_target_pairs={{0,4},{1,5},{2,6},{3,7},{4,0},{5,1},{6,2},{7,3},{8,12},{9,13},{10,... | collective-permute-start | bytes 442376 | tf_op jit(solution)/shard_map/ppermute | solution.py:28
  48.4 0.7 collective-permute-start.33
  49.7 1.0 collective-permute-start.30
  50.7 1.9 %collective-permute-done.35.refs_28_ = bf16[4,1,144,128]{3,2,1,0:T(8,128)(2,1)S(1)} collective-permute-done((bf16[4,1,144,128]{3,2,1,0:T(8,128)(2,1)S(1)}, bf16[4,1,144,128]{3,2,1,0:T(8,128)(2,1)S(1)}, u32[]{:S(2)}, u32[]{:S(2)}) %collective-permute-start.35) | collective-permute-done | bytes 147488 | tf_op jit(solution)/shard_map/ppermute | solution.py:28
  52.6 2.1 %collective-permute-start.37 = (bf16[4,1,144,128]{3,2,1,0:T(8,128)(2,1)S(1)}, bf16[4,1,144,128]{3,2,1,0:T(8,128)(2,1)S(1)}, u32[]{:S(2)}, u32[]{:S(2)}) collective-permute-start(bf16[4,1,144,128]{3,2,1,0:T(8,128)(2,1)S(1)} %collective-permute-done.35.refs_28_), channel_id=1, source_target_pairs={{0,2},{1,3},{2,0},{3,1},{4,6},{5,7},{6,4},{7,5},{8,10},{9,11},{10,... | collective-permute-start | bytes 442376 | tf_op jit(solution)/shard_map/ppermute | solution.py:28
  55.0 1.7 %collective-permute-start.21 = (f32[2,2,2,2,4,128]{5,4,3,2,1,0:T(4,128)S(1)}, f32[2,2,2,2,4,128]{5,4,3,2,1,0:T(4,128)S(1)}, u32[]{:S(2)}, u32[]{:S(2)}) collective-permute-start(f32[2,2,2,2,4,128]{5,4,3,2,1,0:T(4,128)S(1)} %pad_maximum_fusion.4), channel_id=1, source_target_pairs={{0,6},{1,7},{2,4},{3,5},{4,2},{5,3},{6,0},{7,1},{8,14},{9,15},{10,... | collective-permute-start | bytes 98312 | tf_op jit(solution)/shard_map/ppermute | solution.py:28
  56.8 2.3 %collective-permute-done.19 = f32[2,2,2,2,4,128]{5,4,3,2,1,0:T(4,128)S(1)} collective-permute-done((f32[2,2,2,2,4,128]{5,4,3,2,1,0:T(4,128)S(1)}, f32[2,2,2,2,4,128]{5,4,3,2,1,0:T(4,128)S(1)}, u32[]{:S(2)}, u32[]{:S(2)}) %collective-permute-start.19) | collective-permute-done | bytes 32800 | tf_op jit(solution)/shard_map/ppermute | solution.py:28
  59.0 1.5 %collective-permute-start.20 = (f32[2,2,2,2,4,128]{5,4,3,2,1,0:T(4,128)S(1)}, f32[2,2,2,2,4,128]{5,4,3,2,1,0:T(4,128)S(1)}, u32[]{:S(2)}, u32[]{:S(2)}) collective-permute-start(f32[2,2,2,2,4,128]{5,4,3,2,1,0:T(4,128)S(1)} %pad_maximum_fusion.4), channel_id=1, source_target_pairs={{0,4},{1,5},{2,6},{3,7},{4,0},{5,1},{6,2},{7,3},{8,12},{9,13},{10,... | collective-permute-start | bytes 98312 | tf_op jit(solution)/shard_map/ppermute | solution.py:28
  61.6 1.3 %collective-permute-done.20 = f32[2,2,2,2,4,128]{5,4,3,2,1,0:T(4,128)S(1)} collective-permute-done((f32[2,2,2,2,4,128]{5,4,3,2,1,0:T(4,128)S(1)}, f32[2,2,2,2,4,128]{5,4,3,2,1,0:T(4,128)S(1)}, u32[]{:S(2)}, u32[]{:S(2)}) %collective-permute-start.20) | collective-permute-done | bytes 32800 | tf_op jit(solution)/shard_map/ppermute | solution.py:28
  63.0 1.3 %collective-permute-done.38.refs_31_ = bf16[4,1,144,128]{3,2,1,0:T(8,128)(2,1)S(1)} collective-permute-done((bf16[4,1,144,128]{3,2,1,0:T(8,128)(2,1)S(1)}, bf16[4,1,144,128]{3,2,1,0:T(8,128)(2,1)S(1)}, u32[]{:S(2)}, u32[]{:S(2)}) %collective-permute-start.38) | collective-permute-done | bytes 147488 | tf_op jit(solution)/shard_map/ppermute | solution.py:28
  64.3 9.6 %shard_map.88 = (bf16[2,512,256]{2,1,0:T(8,128)(2,1)S(1)}, bf16[2,1601,128]{2,1,0:T(8,128)(2,1)S(1)}, bf16[2,1601,128]{2,1,0:T(8,128)(2,1)}) custom-call(s32[2]{0:T(128)S(1)} %pad_add_fusion.who, s32[8]{0:T(128)S(1)} %copy-done.5, s32[8]{0:T(128)S(1)} %copy-done.6, f32[8,2,2,2,4,128]{5,4,3,2,1,0:T(4,128)S(1)} %constant_dynamic-update-slice_fusion.stats, ...), custom_call_target="tpu_custom_call" | custom-call | flops 4196925440 | tf_op jit(solution)/shard_map/pallas_call | solution.py:35
  74.0 6.5 %copy.17 = bf16[2,1601,128]{2,0,1:T(2,128)(2,1)S(1)} copy(bf16[2,1601,128]{2,1,0:T(8,128)(2,1)} %get-tuple-element.39) | data formatting | bytes 1639424 | tf_op jit(solution)/shard_map/pallas_call | solution.py:35
  81.0 1.9 %collective-permute-done.39.other = bf16[2,512,256]{2,1,0:T(8,128)(2,1)S(1)} collective-permute-done((bf16[2,512,256]{2,1,0:T(8,128)(2,1)S(1)}, bf16[2,512,256]{2,1,0:T(8,128)(2,1)S(1)}, u32[]{:S(2)}, u32[]{:S(2)}) %collective-permute-start.39) | collective-permute-done | bytes 524320 | tf_op jit(solution)/shard_map/ppermute | solution.py:28
  82.9 1.5 %shard_map.89 = (bf16[512,256]{1,0:T(8,128)(2,1)S(1)}, bf16[512,256]{1,0:T(8,128)(2,1)S(1)}, bf16[512,256]{1,0:T(8,128)(2,1)S(1)}, bf16[512,256]{1,0:T(8,128)(2,1)S(1)}) custom-call(s32[2]{0:T(128)S(1)} %pad_add_fusion.who, s32[8]{0:T(128)S(1)} %copy-done.5, s32[8]{0:T(128)S(1)} %copy-done.6, bf16[2,512,256]{2,1,0:T(8,128)(2,1)S(1)} %get-tuple-element.29.own, ...), custom_call_target="tpu_custom_call" | custom-call | tf_op jit(solution)/shard_map/pallas_call | solution.py:35
  84.5 9.1 %collective-permute-start.40 = (bf16[512,256]{1,0:T(8,128)(2,1)S(1)}, bf16[512,256]{1,0:T(8,128)(2,1)S(1)}, u32[]{:S(2)}, u32[]{:S(2)}) collective-permute-start(bf16[512,256]{1,0:T(8,128)(2,1)S(1)} %get-tuple-element.31), channel_id=1, source_target_pairs={{0,2},{1,3},{2,0},{3,1},{4,6},{5,7},{6,4},{7,5},{8,10},{9,11},{10,... | collective-permute-start | bytes 786440 | tf_op jit(solution)/shard_map/ppermute | solution.py:28
  93.7 1.4 %collective-permute-start.42 = (bf16[512,256]{1,0:T(8,128)(2,1)S(1)}, bf16[512,256]{1,0:T(8,128)(2,1)S(1)}, u32[]{:S(2)}, u32[]{:S(2)}) collective-permute-start(bf16[512,256]{1,0:T(8,128)(2,1)S(1)} %get-tuple-element.33), channel_id=1, source_target_pairs={{0,6},{1,7},{2,4},{3,5},{4,2},{5,3},{6,0},{7,1},{8,14},{9,15},{10,... | collective-permute-start | bytes 786440 | tf_op jit(solution)/shard_map/ppermute | solution.py:28
  95.1 5.5 %collective-permute-done.40.refs_1_ = bf16[512,256]{1,0:T(8,128)(2,1)S(1)} collective-permute-done((bf16[512,256]{1,0:T(8,128)(2,1)S(1)}, bf16[512,256]{1,0:T(8,128)(2,1)S(1)}, u32[]{:S(2)}, u32[]{:S(2)}) %collective-permute-start.40) | collective-permute-done | bytes 262176 | tf_op jit(solution)/shard_map/ppermute | solution.py:28
  100.6 6.6 %collective-permute-done.41.refs_2_ = bf16[512,256]{1,0:T(8,128)(2,1)S(1)} collective-permute-done((bf16[512,256]{1,0:T(8,128)(2,1)S(1)}, bf16[512,256]{1,0:T(8,128)(2,1)S(1)}, u32[]{:S(2)}, u32[]{:S(2)}) %collective-permute-start.41) | collective-permute-done | bytes 262176 | tf_op jit(solution)/shard_map/ppermute | solution.py:28
  107.4 1.6 %collective-permute-start.43 = (bf16[128,256]{1,0:T(8,128)(2,1)S(1)}, bf16[128,256]{1,0:T(8,128)(2,1)S(1)}, u32[]{:S(2)}, u32[]{:S(2)}) collective-permute-start(bf16[128,256]{1,0:T(8,128)(2,1)S(1)} %get-tuple-element.35), channel_id=1, source_target_pairs={{0,8},{8,0},{16,24},{24,16},{1,9},{9,1},{17,25},{25,17},{2,10},{10... | collective-permute-start | bytes 196616 | tf_op jit(solution)/shard_map/ppermute | solution.py:28
  109.0 1.2 collective-permute-start.44
  110.2 1.6 %collective-permute-start.45 = (bf16[128,256]{1,0:T(8,128)(2,1)S(1)}, bf16[128,256]{1,0:T(8,128)(2,1)S(1)}, u32[]{:S(2)}, u32[]{:S(2)}) collective-permute-start(bf16[128,256]{1,0:T(8,128)(2,1)S(1)} %get-tuple-element.37), channel_id=1, source_target_pairs={{0,24},{8,16},{16,8},{24,0},{1,25},{9,17},{17,9},{25,1},{2,26},{10... | collective-permute-start | bytes 196616 | tf_op jit(solution)/shard_map/ppermute | solution.py:28
  112.0 6.7 %copy.19 = bf16[2,1601,128]{2,0,1:T(2,128)(2,1)} copy(bf16[2,1601,128]{2,1,0:T(8,128)(2,1)S(1)} %add_convert_fusion) | data formatting | bytes 1639424
  118.7 1.3 %shard_map.91 = bf16[128,1024]{1,0:T(8,128)(2,1)} custom-call(s32[2]{0:T(128)S(1)} %pad_add_fusion.who, bf16[128,256]{1,0:T(8,128)(2,1)S(1)} %get-tuple-element.34.refs_0_, bf16[128,256]{1,0:T(8,128)(2,1)S(1)} %collective-permute-done.43.refs_1_, bf16[128,256]{1,0:T(8,128)(2,1)S(1)} %collective-permute-done.44.refs_2_, ...), custom_call_target="tpu_custom_call" | custom-call | tf_op jit(solution)/shard_map/pallas_call | solution.py:35
  (92 shorter events, 5.1 us)
Async XLA Ops:
  5.1 10.1 %collective-permute-start.1 = (bf16[2,1,128,128]{3,2,1,0:T(8,128)(2,1)S(1)}, bf16[2,1,128,128]{3,2,1,0:T(8,128)(2,1)S(1)}, u32[]{:S(2)}, u32[]{:S(2)}) collective-permute-start(bf16[2,1,128,128]{3,2,1,0:T(8,128)(2,1)S(1)} %get-tuple-element.22), channel_id=1, source_target_pairs={{0,8},{8,0},{16,24},{24,16},{1,9},{9,1},{17,25},{25,17},{2,10},{10... | collective-permute-start | bytes 196616 | tf_op jit(solution)/shard_map/ppermute | solution.py:28
  8.2 7.4 %collective-permute-start.2 = (bf16[2,1,128,128]{3,2,1,0:T(8,128)(2,1)S(1)}, bf16[2,1,128,128]{3,2,1,0:T(8,128)(2,1)S(1)}, u32[]{:S(2)}, u32[]{:S(2)}) collective-permute-start(bf16[2,1,128,128]{3,2,1,0:T(8,128)(2,1)S(1)} %get-tuple-element.23), channel_id=1, source_target_pairs={{0,16},{8,24},{16,0},{24,8},{1,17},{9,25},{17,1},{25,9},{2,18},{10... | collective-permute-start | bytes 196616 | tf_op jit(solution)/shard_map/ppermute | solution.py:28
  10.8 6.8 %collective-permute-start.3 = (bf16[2,1,128,128]{3,2,1,0:T(8,128)(2,1)S(1)}, bf16[2,1,128,128]{3,2,1,0:T(8,128)(2,1)S(1)}, u32[]{:S(2)}, u32[]{:S(2)}) collective-permute-start(bf16[2,1,128,128]{3,2,1,0:T(8,128)(2,1)S(1)} %get-tuple-element.24), channel_id=1, source_target_pairs={{0,24},{8,16},{16,8},{24,0},{1,25},{9,17},{17,9},{25,1},{2,26},{10... | collective-permute-start | bytes 196616 | tf_op jit(solution)/shard_map/ppermute | solution.py:28
  10.8 8.5 %collective-permute-start.22 = (bf16[2,1,144,128]{3,2,1,0:T(8,128)(2,1)S(1)}, bf16[2,1,144,128]{3,2,1,0:T(8,128)(2,1)S(1)}, u32[]{:S(2)}, u32[]{:S(2)}) collective-permute-start(bf16[2,1,144,128]{3,2,1,0:T(8,128)(2,1)S(1)} %get-tuple-element.26), channel_id=1, source_target_pairs={{0,8},{8,0},{16,24},{24,16},{1,9},{9,1},{17,25},{25,17},{2,10},{10... | collective-permute-start | bytes 221192 | tf_op jit(solution)/shard_map/ppermute | solution.py:28
  11.7 10.7 %collective-permute-start.23 = (bf16[2,1,144,128]{3,2,1,0:T(8,128)(2,1)S(1)}, bf16[2,1,144,128]{3,2,1,0:T(8,128)(2,1)S(1)}, u32[]{:S(2)}, u32[]{:S(2)}) collective-permute-start(bf16[2,1,144,128]{3,2,1,0:T(8,128)(2,1)S(1)} %get-tuple-element.27), channel_id=1, source_target_pairs={{0,16},{8,24},{16,0},{24,8},{1,17},{9,25},{17,1},{25,9},{2,18},{10... | collective-permute-start | bytes 221192 | tf_op jit(solution)/shard_map/ppermute | solution.py:28
  15.2 7.2 %collective-permute-start.24 = (bf16[2,1,144,128]{3,2,1,0:T(8,128)(2,1)S(1)}, bf16[2,1,144,128]{3,2,1,0:T(8,128)(2,1)S(1)}, u32[]{:S(2)}, u32[]{:S(2)}) collective-permute-start(bf16[2,1,144,128]{3,2,1,0:T(8,128)(2,1)S(1)} %get-tuple-element.28), channel_id=1, source_target_pairs={{0,24},{8,16},{16,8},{24,0},{1,25},{9,17},{17,9},{25,1},{2,26},{10... | collective-permute-start | bytes 221192 | tf_op jit(solution)/shard_map/ppermute | solution.py:28
  15.6 21.9 %collective-permute-start = (bf16[2,1601,128]{2,0,1:T(2,128)(2,1)S(1)}, bf16[2,1601,128]{2,0,1:T(2,128)(2,1)S(1)}, u32[]{:S(2)}, u32[]{:S(2)}) collective-permute-start(bf16[2,1601,128]{2,0,1:T(2,128)(2,1)S(1)} %copy-done.7), channel_id=1, source_target_pairs={{0,8},{8,0},{16,24},{24,16},{1,9},{9,1},{17,25},{25,17},{2,10},{10... | collective-permute-start | bytes 2459144 | tf_op jit(solution)/shard_map/ppermute | solution.py:28
  17.6 6.3 %collective-permute-start.7 = (bf16[4,1,128,128]{3,2,1,0:T(8,128)(2,1)S(1)}, bf16[4,1,128,128]{3,2,1,0:T(8,128)(2,1)S(1)}, u32[]{:S(2)}, u32[]{:S(2)}) collective-permute-start(bf16[4,1,128,128]{3,2,1,0:T(8,128)(2,1)S(1)} %pad_maximum_fusion.2.refs_0_), channel_id=1, source_target_pairs={{0,4},{1,5},{2,6},{3,7},{4,0},{5,1},{6,2},{7,3},{8,12},{9,13},{10,... | collective-permute-start | bytes 393224 | tf_op jit(solution)/shard_map/ppermute | solution.py:28
  19.3 21.7 %copy-start = (bf16[2,1601,128]{2,1,0:T(8,128)(2,1)}, bf16[2,1601,128]{2,1,0:T(8,128)(2,1)S(1)}, u32[]{:S(2)}) copy-start(bf16[2,1601,128]{2,1,0:T(8,128)(2,1)S(1)} %copy.13.own_kv) | copy-start | bytes 2459140
  19.3 6.1 %collective-permute-start.5 = (bf16[4,1,128,128]{3,2,1,0:T(8,128)(2,1)S(1)}, bf16[4,1,128,128]{3,2,1,0:T(8,128)(2,1)S(1)}, u32[]{:S(2)}, u32[]{:S(2)}) collective-permute-start(bf16[4,1,128,128]{3,2,1,0:T(8,128)(2,1)S(1)} %pad_maximum_fusion.2.refs_0_), channel_id=1, source_target_pairs={{0,2},{1,3},{2,0},{3,1},{4,6},{5,7},{6,4},{7,5},{8,10},{9,11},{10,... | collective-permute-start | bytes 393224 | tf_op jit(solution)/shard_map/ppermute | solution.py:28
  22.4 3.1 %collective-permute-start.4 = (bf16[4,1,128,128]{3,2,1,0:T(8,128)(2,1)S(1)}, bf16[4,1,128,128]{3,2,1,0:T(8,128)(2,1)S(1)}, u32[]{:S(2)}, u32[]{:S(2)}) collective-permute-start(bf16[4,1,128,128]{3,2,1,0:T(8,128)(2,1)S(1)} %pad_maximum_fusion.2.refs_0_), channel_id=1, source_target_pairs={{0,1},{1,0},{2,3},{3,2},{4,5},{5,4},{6,7},{7,6},{8,9},{9,8},{10,11... | collective-permute-start | bytes 393224 | tf_op jit(solution)/shard_map/ppermute | solution.py:28
  22.4 5.9 %collective-permute-start.14 = (bf16[4,1,128,128]{3,2,1,0:T(8,128)(2,1)S(1)}, bf16[4,1,128,128]{3,2,1,0:T(8,128)(2,1)S(1)}, u32[]{:S(2)}, u32[]{:S(2)}) collective-permute-start(bf16[4,1,128,128]{3,2,1,0:T(8,128)(2,1)S(1)} %pad_maximum_fusion.3.refs_8_), channel_id=1, source_target_pairs={{0,4},{1,5},{2,6},{3,7},{4,0},{5,1},{6,2},{7,3},{8,12},{9,13},{10,... | collective-permute-start | bytes 393224 | tf_op jit(solution)/shard_map/ppermute | solution.py:28
  23.9 5.9 %collective-permute-start.12 = (bf16[4,1,128,128]{3,2,1,0:T(8,128)(2,1)S(1)}, bf16[4,1,128,128]{3,2,1,0:T(8,128)(2,1)S(1)}, u32[]{:S(2)}, u32[]{:S(2)}) collective-permute-start(bf16[4,1,128,128]{3,2,1,0:T(8,128)(2,1)S(1)} %pad_maximum_fusion.3.refs_8_), channel_id=1, source_target_pairs={{0,2},{1,3},{2,0},{3,1},{4,6},{5,7},{6,4},{7,5},{8,10},{9,11},{10,... | collective-permute-start | bytes 393224 | tf_op jit(solution)/shard_map/ppermute | solution.py:28
  25.4 5.9 %collective-permute-start.11 = (bf16[4,1,128,128]{3,2,1,0:T(8,128)(2,1)S(1)}, bf16[4,1,128,128]{3,2,1,0:T(8,128)(2,1)S(1)}, u32[]{:S(2)}, u32[]{:S(2)}) collective-permute-start(bf16[4,1,128,128]{3,2,1,0:T(8,128)(2,1)S(1)} %pad_maximum_fusion.3.refs_8_), channel_id=1, source_target_pairs={{0,1},{1,0},{2,3},{3,2},{4,5},{5,4},{6,7},{7,6},{8,9},{9,8},{10,11... | collective-permute-start | bytes 393224 | tf_op jit(solution)/shard_map/ppermute | solution.py:28
  25.5 5.9 %collective-permute-start.8 = (bf16[4,1,128,128]{3,2,1,0:T(8,128)(2,1)S(1)}, bf16[4,1,128,128]{3,2,1,0:T(8,128)(2,1)S(1)}, u32[]{:S(2)}, u32[]{:S(2)}) collective-permute-start(bf16[4,1,128,128]{3,2,1,0:T(8,128)(2,1)S(1)} %collective-permute-done.7.refs_4_), channel_id=1, source_target_pairs={{0,1},{1,0},{2,3},{3,2},{4,5},{5,4},{6,7},{7,6},{8,9},{9,8},{10,11... | collective-permute-start | bytes 393224 | tf_op jit(solution)/shard_map/ppermute | solution.py:28
  28.3 5.1 %collective-permute-start.9 = (bf16[4,1,128,128]{3,2,1,0:T(8,128)(2,1)S(1)}, bf16[4,1,128,128]{3,2,1,0:T(8,128)(2,1)S(1)}, u32[]{:S(2)}, u32[]{:S(2)}) collective-permute-start(bf16[4,1,128,128]{3,2,1,0:T(8,128)(2,1)S(1)} %collective-permute-done.5.refs_2_), channel_id=1, source_target_pairs={{0,4},{1,5},{2,6},{3,7},{4,0},{5,1},{6,2},{7,3},{8,12},{9,13},{10,... | collective-permute-start | bytes 393224 | tf_op jit(solution)/shard_map/ppermute | solution.py:28
  29.8 5.0 %collective-permute-start.16 = (bf16[4,1,128,128]{3,2,1,0:T(8,128)(2,1)S(1)}, bf16[4,1,128,128]{3,2,1,0:T(8,128)(2,1)S(1)}, u32[]{:S(2)}, u32[]{:S(2)}) collective-permute-start(bf16[4,1,128,128]{3,2,1,0:T(8,128)(2,1)S(1)} %collective-permute-done.14.refs_12_), channel_id=1, source_target_pairs={{0,2},{1,3},{2,0},{3,1},{4,6},{5,7},{6,4},{7,5},{8,10},{9,11},{10,... | collective-permute-start | bytes 393224 | tf_op jit(solution)/shard_map/ppermute | solution.py:28
  31.3 6.4 %collective-permute-start.6 = (bf16[4,1,128,128]{3,2,1,0:T(8,128)(2,1)S(1)}, bf16[4,1,128,128]{3,2,1,0:T(8,128)(2,1)S(1)}, u32[]{:S(2)}, u32[]{:S(2)}) collective-permute-start(bf16[4,1,128,128]{3,2,1,0:T(8,128)(2,1)S(1)} %collective-permute-done.5.refs_2_), channel_id=1, source_target_pairs={{0,1},{1,0},{2,3},{3,2},{4,5},{5,4},{6,7},{7,6},{8,9},{9,8},{10,11... | collective-permute-start | bytes 393224 | tf_op jit(solution)/shard_map/ppermute | solution.py:28
  31.4 8.0 %collective-permute-start.15 = (bf16[4,1,128,128]{3,2,1,0:T(8,128)(2,1)S(1)}, bf16[4,1,128,128]{3,2,1,0:T(8,128)(2,1)S(1)}, u32[]{:S(2)}, u32[]{:S(2)}) collective-permute-start(bf16[4,1,128,128]{3,2,1,0:T(8,128)(2,1)S(1)} %collective-permute-done.14.refs_12_), channel_id=1, source_target_pairs={{0,1},{1,0},{2,3},{3,2},{4,5},{5,4},{6,7},{7,6},{8,9},{9,8},{10,11... | collective-permute-start | bytes 393224 | tf_op jit(solution)/shard_map/ppermute | solution.py:28
  33.4 7.5 %collective-permute-start.13 = (bf16[4,1,128,128]{3,2,1,0:T(8,128)(2,1)S(1)}, bf16[4,1,128,128]{3,2,1,0:T(8,128)(2,1)S(1)}, u32[]{:S(2)}, u32[]{:S(2)}) collective-permute-start(bf16[4,1,128,128]{3,2,1,0:T(8,128)(2,1)S(1)} %collective-permute-done.12.refs_10_), channel_id=1, source_target_pairs={{0,1},{1,0},{2,3},{3,2},{4,5},{5,4},{6,7},{7,6},{8,9},{9,8},{10,11... | collective-permute-start | bytes 393224 | tf_op jit(solution)/shard_map/ppermute | solution.py:28
  34.8 6.1 %collective-permute-start.10 = (bf16[4,1,128,128]{3,2,1,0:T(8,128)(2,1)S(1)}, bf16[4,1,128,128]{3,2,1,0:T(8,128)(2,1)S(1)}, u32[]{:S(2)}, u32[]{:S(2)}) collective-permute-start(bf16[4,1,128,128]{3,2,1,0:T(8,128)(2,1)S(1)} %collective-permute-done.9.refs_6_), channel_id=1, source_target_pairs={{0,1},{1,0},{2,3},{3,2},{4,5},{5,4},{6,7},{7,6},{8,9},{9,8},{10,11... | collective-permute-start | bytes 393224 | tf_op jit(solution)/shard_map/ppermute | solution.py:28
  37.5 3.4 %collective-permute-start.17 = (bf16[4,1,128,128]{3,2,1,0:T(8,128)(2,1)S(1)}, bf16[4,1,128,128]{3,2,1,0:T(8,128)(2,1)S(1)}, u32[]{:S(2)}, u32[]{:S(2)}) collective-permute-start(bf16[4,1,128,128]{3,2,1,0:T(8,128)(2,1)S(1)} %collective-permute-done.16.refs_14_), channel_id=1, source_target_pairs={{0,1},{1,0},{2,3},{3,2},{4,5},{5,4},{6,7},{7,6},{8,9},{9,8},{10,11... | collective-permute-start | bytes 393224 | tf_op jit(solution)/shard_map/ppermute | solution.py:28
  37.7 11.4 %collective-permute-start.28 = (bf16[4,1,144,128]{3,2,1,0:T(8,128)(2,1)S(1)}, bf16[4,1,144,128]{3,2,1,0:T(8,128)(2,1)S(1)}, u32[]{:S(2)}, u32[]{:S(2)}) collective-permute-start(bf16[4,1,144,128]{3,2,1,0:T(8,128)(2,1)S(1)} %pad_maximum_fusion.refs_16_), channel_id=1, source_target_pairs={{0,4},{1,5},{2,6},{3,7},{4,0},{5,1},{6,2},{7,3},{8,12},{9,13},{10,... | collective-permute-start | bytes 442376 | tf_op jit(solution)/shard_map/ppermute | solution.py:28
  39.4 9.8 %collective-permute-start.26 = (bf16[4,1,144,128]{3,2,1,0:T(8,128)(2,1)S(1)}, bf16[4,1,144,128]{3,2,1,0:T(8,128)(2,1)S(1)}, u32[]{:S(2)}, u32[]{:S(2)}) collective-permute-start(bf16[4,1,144,128]{3,2,1,0:T(8,128)(2,1)S(1)} %pad_maximum_fusion.refs_16_), channel_id=1, source_target_pairs={{0,2},{1,3},{2,0},{3,1},{4,6},{5,7},{6,4},{7,5},{8,10},{9,11},{10,... | collective-permute-start | bytes 442376 | tf_op jit(solution)/shard_map/ppermute | solution.py:28
  40.9 8.8 %collective-permute-start.25 = (bf16[4,1,144,128]{3,2,1,0:T(8,128)(2,1)S(1)}, bf16[4,1,144,128]{3,2,1,0:T(8,128)(2,1)S(1)}, u32[]{:S(2)}, u32[]{:S(2)}) collective-permute-start(bf16[4,1,144,128]{3,2,1,0:T(8,128)(2,1)S(1)} %pad_maximum_fusion.refs_16_), channel_id=1, source_target_pairs={{0,1},{1,0},{2,3},{3,2},{4,5},{5,4},{6,7},{7,6},{8,9},{9,8},{10,11... | collective-permute-start | bytes 442376 | tf_op jit(solution)/shard_map/ppermute | solution.py:28
  44.5 4.0 %collective-permute-start.18 = (f32[2,2,2,4,128]{4,3,2,1,0:T(4,128)S(1)}, f32[2,2,2,4,128]{4,3,2,1,0:T(4,128)S(1)}, u32[]{:S(2)}, u32[]{:S(2)}) collective-permute-start(f32[2,2,2,4,128]{4,3,2,1,0:T(4,128)S(1)} %shard_map.87), channel_id=1, source_target_pairs={{0,1},{1,0},{2,3},{3,2},{4,5},{5,4},{6,7},{7,6},{8,9},{9,8},{10,11... | collective-permute-start | bytes 49160 | tf_op jit(solution)/shard_map/ppermute | solution.py:28
  45.0 7.5 %collective-permute-start.35 = (bf16[4,1,144,128]{3,2,1,0:T(8,128)(2,1)S(1)}, bf16[4,1,144,128]{3,2,1,0:T(8,128)(2,1)S(1)}, u32[]{:S(2)}, u32[]{:S(2)}) collective-permute-start(bf16[4,1,144,128]{3,2,1,0:T(8,128)(2,1)S(1)} %pad_maximum_fusion.1.refs_24_), channel_id=1, source_target_pairs={{0,4},{1,5},{2,6},{3,7},{4,0},{5,1},{6,2},{7,3},{8,12},{9,13},{10,... | collective-permute-start | bytes 442376 | tf_op jit(solution)/shard_map/ppermute | solution.py:28
  48.4 6.2 %collective-permute-start.33 = (bf16[4,1,144,128]{3,2,1,0:T(8,128)(2,1)S(1)}, bf16[4,1,144,128]{3,2,1,0:T(8,128)(2,1)S(1)}, u32[]{:S(2)}, u32[]{:S(2)}) collective-permute-start(bf16[4,1,144,128]{3,2,1,0:T(8,128)(2,1)S(1)} %pad_maximum_fusion.1.refs_24_), channel_id=1, source_target_pairs={{0,2},{1,3},{2,0},{3,1},{4,6},{5,7},{6,4},{7,5},{8,10},{9,11},{10,... | collective-permute-start | bytes 442376 | tf_op jit(solution)/shard_map/ppermute | solution.py:28
  49.1 5.9 %collective-permute-start.32 = (bf16[4,1,144,128]{3,2,1,0:T(8,128)(2,1)S(1)}, bf16[4,1,144,128]{3,2,1,0:T(8,128)(2,1)S(1)}, u32[]{:S(2)}, u32[]{:S(2)}) collective-permute-start(bf16[4,1,144,128]{3,2,1,0:T(8,128)(2,1)S(1)} %pad_maximum_fusion.1.refs_24_), channel_id=1, source_target_pairs={{0,1},{1,0},{2,3},{3,2},{4,5},{5,4},{6,7},{7,6},{8,9},{9,8},{10,11... | collective-permute-start | bytes 442376 | tf_op jit(solution)/shard_map/ppermute | solution.py:28
  49.2 11.3 %collective-permute-start.29 = (bf16[4,1,144,128]{3,2,1,0:T(8,128)(2,1)S(1)}, bf16[4,1,144,128]{3,2,1,0:T(8,128)(2,1)S(1)}, u32[]{:S(2)}, u32[]{:S(2)}) collective-permute-start(bf16[4,1,144,128]{3,2,1,0:T(8,128)(2,1)S(1)} %collective-permute-done.28.refs_20_), channel_id=1, source_target_pairs={{0,1},{1,0},{2,3},{3,2},{4,5},{5,4},{6,7},{7,6},{8,9},{9,8},{10,11... | collective-permute-start | bytes 442376 | tf_op jit(solution)/shard_map/ppermute | solution.py:28
  49.7 10.9 %collective-permute-start.30 = (bf16[4,1,144,128]{3,2,1,0:T(8,128)(2,1)S(1)}, bf16[4,1,144,128]{3,2,1,0:T(8,128)(2,1)S(1)}, u32[]{:S(2)}, u32[]{:S(2)}) collective-permute-start(bf16[4,1,144,128]{3,2,1,0:T(8,128)(2,1)S(1)} %collective-permute-done.26.refs_18_), channel_id=1, source_target_pairs={{0,4},{1,5},{2,6},{3,7},{4,0},{5,1},{6,2},{7,3},{8,12},{9,13},{10,... | collective-permute-start | bytes 442376 | tf_op jit(solution)/shard_map/ppermute | solution.py:28
  52.6 8.6 %collective-permute-start.37 = (bf16[4,1,144,128]{3,2,1,0:T(8,128)(2,1)S(1)}, bf16[4,1,144,128]{3,2,1,0:T(8,128)(2,1)S(1)}, u32[]{:S(2)}, u32[]{:S(2)}) collective-permute-start(bf16[4,1,144,128]{3,2,1,0:T(8,128)(2,1)S(1)} %collective-permute-done.35.refs_28_), channel_id=1, source_target_pairs={{0,2},{1,3},{2,0},{3,1},{4,6},{5,7},{6,4},{7,5},{8,10},{9,11},{10,... | collective-permute-start | bytes 442376 | tf_op jit(solution)/shard_map/ppermute | solution.py:28
  54.7 4.4 %collective-permute-start.19 = (f32[2,2,2,2,4,128]{5,4,3,2,1,0:T(4,128)S(1)}, f32[2,2,2,2,4,128]{5,4,3,2,1,0:T(4,128)S(1)}, u32[]{:S(2)}, u32[]{:S(2)}) collective-permute-start(f32[2,2,2,2,4,128]{5,4,3,2,1,0:T(4,128)S(1)} %pad_maximum_fusion.4), channel_id=1, source_target_pairs={{0,2},{1,3},{2,0},{3,1},{4,6},{5,7},{6,4},{7,5},{8,10},{9,11},{10,... | collective-permute-start | bytes 98312 | tf_op jit(solution)/shard_map/ppermute | solution.py:28
  55.0 6.2 %collective-permute-start.21 = (f32[2,2,2,2,4,128]{5,4,3,2,1,0:T(4,128)S(1)}, f32[2,2,2,2,4,128]{5,4,3,2,1,0:T(4,128)S(1)}, u32[]{:S(2)}, u32[]{:S(2)}) collective-permute-start(f32[2,2,2,2,4,128]{5,4,3,2,1,0:T(4,128)S(1)} %pad_maximum_fusion.4), channel_id=1, source_target_pairs={{0,6},{1,7},{2,4},{3,5},{4,2},{5,3},{6,0},{7,1},{8,14},{9,15},{10,... | collective-permute-start | bytes 98312 | tf_op jit(solution)/shard_map/ppermute | solution.py:28
  59.0 3.9 %collective-permute-start.20 = (f32[2,2,2,2,4,128]{5,4,3,2,1,0:T(4,128)S(1)}, f32[2,2,2,2,4,128]{5,4,3,2,1,0:T(4,128)S(1)}, u32[]{:S(2)}, u32[]{:S(2)}) collective-permute-start(f32[2,2,2,2,4,128]{5,4,3,2,1,0:T(4,128)S(1)} %pad_maximum_fusion.4), channel_id=1, source_target_pairs={{0,4},{1,5},{2,6},{3,7},{4,0},{5,1},{6,2},{7,3},{8,12},{9,13},{10,... | collective-permute-start | bytes 98312 | tf_op jit(solution)/shard_map/ppermute | solution.py:28
  60.5 2.5 %collective-permute-start.27 = (bf16[4,1,144,128]{3,2,1,0:T(8,128)(2,1)S(1)}, bf16[4,1,144,128]{3,2,1,0:T(8,128)(2,1)S(1)}, u32[]{:S(2)}, u32[]{:S(2)}) collective-permute-start(bf16[4,1,144,128]{3,2,1,0:T(8,128)(2,1)S(1)} %collective-permute-done.26.refs_18_), channel_id=1, source_target_pairs={{0,1},{1,0},{2,3},{3,2},{4,5},{5,4},{6,7},{7,6},{8,9},{9,8},{10,11... | collective-permute-start | bytes 442376 | tf_op jit(solution)/shard_map/ppermute | solution.py:28
  60.6 2.4 %collective-permute-start.36 = (bf16[4,1,144,128]{3,2,1,0:T(8,128)(2,1)S(1)}, bf16[4,1,144,128]{3,2,1,0:T(8,128)(2,1)S(1)}, u32[]{:S(2)}, u32[]{:S(2)}) collective-permute-start(bf16[4,1,144,128]{3,2,1,0:T(8,128)(2,1)S(1)} %collective-permute-done.35.refs_28_), channel_id=1, source_target_pairs={{0,1},{1,0},{2,3},{3,2},{4,5},{5,4},{6,7},{7,6},{8,9},{9,8},{10,11... | collective-permute-start | bytes 442376 | tf_op jit(solution)/shard_map/ppermute | solution.py:28
  61.1 1.9 %collective-permute-start.34 = (bf16[4,1,144,128]{3,2,1,0:T(8,128)(2,1)S(1)}, bf16[4,1,144,128]{3,2,1,0:T(8,128)(2,1)S(1)}, u32[]{:S(2)}, u32[]{:S(2)}) collective-permute-start(bf16[4,1,144,128]{3,2,1,0:T(8,128)(2,1)S(1)} %collective-permute-done.33.refs_26_), channel_id=1, source_target_pairs={{0,1},{1,0},{2,3},{3,2},{4,5},{5,4},{6,7},{7,6},{8,9},{9,8},{10,11... | collective-permute-start | bytes 442376 | tf_op jit(solution)/shard_map/ppermute | solution.py:28
  61.2 1.8 %collective-permute-start.31 = (bf16[4,1,144,128]{3,2,1,0:T(8,128)(2,1)S(1)}, bf16[4,1,144,128]{3,2,1,0:T(8,128)(2,1)S(1)}, u32[]{:S(2)}, u32[]{:S(2)}) collective-permute-start(bf16[4,1,144,128]{3,2,1,0:T(8,128)(2,1)S(1)} %collective-permute-done.30.refs_22_), channel_id=1, source_target_pairs={{0,1},{1,0},{2,3},{3,2},{4,5},{5,4},{6,7},{7,6},{8,9},{9,8},{10,11... | collective-permute-start | bytes 442376 | tf_op jit(solution)/shard_map/ppermute | solution.py:28
  63.0 1.4 %collective-permute-start.38 = (bf16[4,1,144,128]{3,2,1,0:T(8,128)(2,1)S(1)}, bf16[4,1,144,128]{3,2,1,0:T(8,128)(2,1)S(1)}, u32[]{:S(2)}, u32[]{:S(2)}) collective-permute-start(bf16[4,1,144,128]{3,2,1,0:T(8,128)(2,1)S(1)} %collective-permute-done.37.refs_30_), channel_id=1, source_target_pairs={{0,1},{1,0},{2,3},{3,2},{4,5},{5,4},{6,7},{7,6},{8,9},{9,8},{10,11... | collective-permute-start | bytes 442376 | tf_op jit(solution)/shard_map/ppermute | solution.py:28
  80.5 31.4 %collective-permute-start.46 = (bf16[2,1601,128]{2,0,1:T(2,128)(2,1)S(1)}, bf16[2,1601,128]{2,0,1:T(2,128)(2,1)S(1)}, u32[]{:S(2)}, u32[]{:S(2)}) collective-permute-start(bf16[2,1601,128]{2,0,1:T(2,128)(2,1)S(1)} %copy.17), channel_id=1, source_target_pairs={{0,8},{8,0},{16,24},{24,16},{1,9},{9,1},{17,25},{25,17},{2,10},{10... | collective-permute-start | bytes 2459144 | tf_op jit(solution)/shard_map/ppermute | solution.py:28
  81.0 1.9 %collective-permute-start.39 = (bf16[2,512,256]{2,1,0:T(8,128)(2,1)S(1)}, bf16[2,512,256]{2,1,0:T(8,128)(2,1)S(1)}, u32[]{:S(2)}, u32[]{:S(2)}) collective-permute-start(bf16[2,512,256]{2,1,0:T(8,128)(2,1)S(1)} %get-tuple-element.29.own), channel_id=1, source_target_pairs={{0,1},{1,0},{2,3},{3,2},{4,5},{5,4},{6,7},{7,6},{8,9},{9,8},{10,11... | collective-permute-start | bytes 1572872 | tf_op jit(solution)/shard_map/ppermute | solution.py:28
  84.5 16.2 %collective-permute-start.40 = (bf16[512,256]{1,0:T(8,128)(2,1)S(1)}, bf16[512,256]{1,0:T(8,128)(2,1)S(1)}, u32[]{:S(2)}, u32[]{:S(2)}) collective-permute-start(bf16[512,256]{1,0:T(8,128)(2,1)S(1)} %get-tuple-element.31), channel_id=1, source_target_pairs={{0,2},{1,3},{2,0},{3,1},{4,6},{5,7},{6,4},{7,5},{8,10},{9,11},{10,... | collective-permute-start | bytes 786440 | tf_op jit(solution)/shard_map/ppermute | solution.py:28
  93.6 13.7 %collective-permute-start.41 = (bf16[512,256]{1,0:T(8,128)(2,1)S(1)}, bf16[512,256]{1,0:T(8,128)(2,1)S(1)}, u32[]{:S(2)}, u32[]{:S(2)}) collective-permute-start(bf16[512,256]{1,0:T(8,128)(2,1)S(1)} %get-tuple-element.32), channel_id=1, source_target_pairs={{0,4},{1,5},{2,6},{3,7},{4,0},{5,1},{6,2},{7,3},{8,12},{9,13},{10,... | collective-permute-start | bytes 786440 | tf_op jit(solution)/shard_map/ppermute | solution.py:28
  93.7 13.5 %collective-permute-start.42 = (bf16[512,256]{1,0:T(8,128)(2,1)S(1)}, bf16[512,256]{1,0:T(8,128)(2,1)S(1)}, u32[]{:S(2)}, u32[]{:S(2)}) collective-permute-start(bf16[512,256]{1,0:T(8,128)(2,1)S(1)} %get-tuple-element.33), channel_id=1, source_target_pairs={{0,6},{1,7},{2,4},{3,5},{4,2},{5,3},{6,0},{7,1},{8,14},{9,15},{10,... | collective-permute-start | bytes 786440 | tf_op jit(solution)/shard_map/ppermute | solution.py:28
  107.4 11.3 %collective-permute-start.43 = (bf16[128,256]{1,0:T(8,128)(2,1)S(1)}, bf16[128,256]{1,0:T(8,128)(2,1)S(1)}, u32[]{:S(2)}, u32[]{:S(2)}) collective-permute-start(bf16[128,256]{1,0:T(8,128)(2,1)S(1)} %get-tuple-element.35), channel_id=1, source_target_pairs={{0,8},{8,0},{16,24},{24,16},{1,9},{9,1},{17,25},{25,17},{2,10},{10... | collective-permute-start | bytes 196616 | tf_op jit(solution)/shard_map/ppermute | solution.py:28
  109.0 9.7 %collective-permute-start.44 = (bf16[128,256]{1,0:T(8,128)(2,1)S(1)}, bf16[128,256]{1,0:T(8,128)(2,1)S(1)}, u32[]{:S(2)}, u32[]{:S(2)}) collective-permute-start(bf16[128,256]{1,0:T(8,128)(2,1)S(1)} %get-tuple-element.36), channel_id=1, source_target_pairs={{0,16},{8,24},{16,0},{24,8},{1,17},{9,25},{17,1},{25,9},{2,18},{10... | collective-permute-start | bytes 196616 | tf_op jit(solution)/shard_map/ppermute | solution.py:28
  110.2 8.5 %collective-permute-start.45 = (bf16[128,256]{1,0:T(8,128)(2,1)S(1)}, bf16[128,256]{1,0:T(8,128)(2,1)S(1)}, u32[]{:S(2)}, u32[]{:S(2)}) collective-permute-start(bf16[128,256]{1,0:T(8,128)(2,1)S(1)} %get-tuple-element.37), channel_id=1, source_target_pairs={{0,24},{8,16},{16,8},{24,0},{1,25},{9,17},{17,9},{25,1},{2,26},{10... | collective-permute-start | bytes 196616 | tf_op jit(solution)/shard_map/ppermute | solution.py:28
  (7 other events, 27.7 us)

commit v2 on v1

v2 whole, which is shorter than its diff:
```python
import functools
import math

import jax
import jax.numpy as jnp
from jax import lax
from jax.experimental import pallas as pl
from jax.experimental.pallas import tpu as pltpu
from jax.sharding import PartitionSpec as P

HEAD_DIM = 128
MAX_TILES = 4
KEY_ROWS = 256
TEXT_CHUNKS = 4
DELTA_ROWS = 16
SCALE = 1.0 / math.sqrt(HEAD_DIM)
SCALE_LOG2 = SCALE / math.log(2.0)
BF16 = jnp.bfloat16
F32 = jnp.float32

SMEM = pl.BlockSpec(memory_space=pltpu.SMEM)
VMEM = pl.BlockSpec(memory_space=pltpu.VMEM)
ANY = pl.BlockSpec(memory_space=pl.ANY)


def exchange(block, axis, distance):
    count = lax.axis_size(axis)
    return lax.ppermute(block, axis, [(i, i ^ distance) for i in range(count)])


def call(kernel, out_shape, in_specs, scratch, args, out_specs=None, grid=(), megabytes=16, flops=0, moved=0):
    many = isinstance(out_shape, (list, tuple))
    if out_specs is None:
        out_specs = [VMEM] * len(out_shape) if many else VMEM
    return pl.pallas_call(
        kernel,
        out_shape=out_shape,
        in_specs=in_specs,
        out_specs=out_specs,
        grid=grid,
        scratch_shapes=scratch,
        compiler_params=pltpu.CompilerParams(vmem_limit_bytes=megabytes << 20),
        cost_estimate=pl.CostEstimate(flops=flops, bytes_accessed=moved, transcendentals=0),
    )(*args)


def place_of(perm_ref, owner, owners):
    first = jnp.int32(0)
    for index in range(owners):
        first = first + jnp.where(perm_ref[index] == owner, index, 0)
    return first


def sample_at(count_ref, place, samples):
    end, sample, start = jnp.int32(0), jnp.int32(0), jnp.int32(0)
    for index in range(samples):
        end = end + count_ref[index]
        passed = place >= end
        sample = sample + passed.astype(jnp.int32)
        start = jnp.where(passed, end, start)
    return sample, start


def pack_queries(groups, heads, who, q_ref, *refs):
    outs, sem = refs[:-1], refs[-1]
    copies = []
    for j, out in enumerate(outs):
        for h in range(heads):
            start = pl.multiple_of(((who[0] ^ j) * heads + h) * HEAD_DIM, HEAD_DIM)
            copy = pltpu.make_async_copy(q_ref.at[:, pl.ds(start, HEAD_DIM)], out.at[h], sem.at[j, h])
            copy.start()
            copies.append(copy)
    for copy in copies:
        copy.wait()


def pack_grads(groups, heads, who, length, o_hbm, g_hbm, *refs):
    outs, o_ref, g_ref, sem = refs[:groups], refs[-3], refs[-2], refs[-1]
    first = pltpu.make_async_copy(o_hbm, o_ref, sem.at[0])
    second = pltpu.make_async_copy(g_hbm, g_ref, sem.at[1])
    first.start()
    second.start()
    first.wait()
    second.wait()
    rows = g_ref.shape[0]
    seq = who[0]
    position = seq * rows + lax.broadcasted_iota(jnp.int32, (rows, HEAD_DIM), 0)
    keep = position < length[0]
    for j, out in enumerate(outs):
        for h in range(heads):
            columns = pl.ds(pl.multiple_of(((seq ^ j) * heads + h) * HEAD_DIM, HEAD_DIM), HEAD_DIM)
            grad = jnp.where(keep, g_ref[:, columns].astype(F32), 0.0)
            product = grad * o_ref[:, columns].astype(F32)
            delta = jnp.sum(jnp.transpose(product), axis=0, keepdims=True)
            out[h, :rows] = grad.astype(BF16)
            out[h, rows:] = jnp.broadcast_to(delta, (DELTA_ROWS, HEAD_DIM)).astype(BF16)


def fetch(pieces, relative, target, sem):
    for index, piece in enumerate(pieces):
        @pl.when(relative == index)
        def _(piece=piece):
            pltpu.make_async_copy(piece, target, sem).start()


def spans_of(rows):
    full = rows // KEY_ROWS
    tail = rows - full * KEY_ROWS
    return [(i * KEY_ROWS, KEY_ROWS, KEY_ROWS) for i in range(full)] + [(full * KEY_ROWS, -(-tail // 16) * 16, tail)]


def dot_nt(a, b):
    return lax.dot_general(a, b, (((1,), (1,)), ((), ())), preferred_element_type=F32)


def dot_nn(a, b):
    return jnp.dot(a, b, preferred_element_type=F32)


def own_tiles(owners, slots, who, counts, perm):
    first = place_of(perm, who[1], owners)
    return [sample_at(counts, first + slot * owners, owners) for slot in range(slots)]


def weights_kernel(owners, heads, blocks, slots, who, counts, perm, own_kv, partner_kv, *refs):
    q_pieces = refs[:owners]
    stats, weights, q_buf, k_buf, k_tail, scores_buf, q_sem, k_sem = refs[owners:]
    step = pl.program_id(0)
    odd = who[0] & 1
    rows = k_buf.shape[1]
    spans = spans_of(rows)
    chunks = q_buf.shape[1] // blocks
    width = chunks * HEAD_DIM
    tiles = own_tiles(owners, slots, who, counts, perm)

    @pl.when(step == 0)
    def _():
        k_tail[...] = jnp.zeros(k_tail.shape, BF16)
        for slot in range(slots):
            @pl.when(tiles[slot][0] < owners)
            def _(slot=slot):
                fetch([own_kv.at[slot], partner_kv.at[slot]], odd, k_buf.at[slot], k_sem.at[slot])
                fetch(q_pieces, tiles[slot][0] ^ who[1], q_buf.at[slot], q_sem.at[slot])

    for slot in range(slots):
        base = slot * heads * blocks

        @pl.when((step == base) & (tiles[slot][0] < owners))
        def _(slot=slot):
            pltpu.make_async_copy(own_kv.at[slot], k_buf.at[slot], k_sem.at[slot]).wait()
            pltpu.make_async_copy(q_pieces[0], q_buf.at[slot], q_sem.at[slot]).wait()
            k_tail[:spans[-1][2]] = k_buf[slot, spans[-1][0]:]

        @pl.when((step >= base) & (step < base + heads * blocks) & (tiles[slot][0] < owners))
        def _(slot=slot, base=base):
            head, block = (step - base) // blocks, (step - base) % blocks
            query = q_buf[slot, pl.ds(block * chunks, chunks), head].reshape(width, HEAD_DIM)
            peak = jnp.full((8, width), -jnp.inf, F32)
            for low, size, used in spans:
                if size == used:
                    scores = dot_nt(k_buf[slot, low:low + size], query)
                else:
                    scores = dot_nt(k_tail[...], query)
                    row = lax.broadcasted_iota(jnp.int32, scores.shape, 0)
                    scores = jnp.where(row < used, scores, -jnp.inf)
                scores_buf[low:low + size] = scores
                peak = jnp.maximum(peak, jnp.max(scores.reshape(-1, 8, width), axis=0))
            top = jnp.max(peak, axis=0, keepdims=True) * SCALE_LOG2
            mass = jnp.zeros((8, width), F32)
            for low, size, used in spans:
                part = jnp.exp2(scores_buf[low:low + size] * SCALE_LOG2 - top)
                mass = mass + jnp.sum(part.reshape(-1, 8, width), axis=0)
                weights[0, low:low + size] = part.astype(BF16)
            total = jnp.sum(mass, axis=0, keepdims=True)
            stats[slot, 0, head, pl.ds(block, 1)] = top
            stats[slot, 1, head, pl.ds(block, 1)] = total


def slopes_kernel(owners, heads, blocks, slots, who, counts, perm, weights, own_kv, partner_kv, *refs):
    g_pieces = refs[:owners]
    slopes, turned, g_buf, kv_buf, kv_tail, k_turn, g_sem, kv_sem = refs[owners:]
    step = pl.program_id(0)
    odd = who[0] & 1
    rows = kv_buf.shape[2]
    spans = spans_of(rows)
    chunks = g_buf.shape[1] // blocks
    width = chunks * HEAD_DIM
    tiles = own_tiles(owners, slots, who, counts, perm)

    @pl.when(step == 0)
    def _():
        kv_tail[...] = jnp.zeros(kv_tail.shape, BF16)
        for slot in range(slots):
            @pl.when(tiles[slot][0] < owners)
            def _(slot=slot):
                pltpu.make_async_copy(own_kv.at[slot], kv_buf.at[slot, odd], kv_sem.at[slot, 0]).start()
                pltpu.make_async_copy(partner_kv.at[slot], kv_buf.at[slot, 1 - odd], kv_sem.at[slot, 1]).start()
                fetch(g_pieces, tiles[slot][0] ^ who[1], g_buf.at[slot], g_sem.at[slot])

    for slot in range(slots):
        base = slot * heads * blocks

        @pl.when((step == base) & (tiles[slot][0] < owners))
        def _(slot=slot):
            pltpu.make_async_copy(own_kv.at[slot], kv_buf.at[slot, odd], kv_sem.at[slot, 0]).wait()
            pltpu.make_async_copy(partner_kv.at[slot], kv_buf.at[slot, 1 - odd], kv_sem.at[slot, 1]).wait()
            pltpu.make_async_copy(g_pieces[0], g_buf.at[slot], g_sem.at[slot]).wait()
            for which in range(2):
                kv_tail[which, :spans[-1][2]] = kv_buf[slot, which, spans[-1][0]:]
            for low, size, used in spans:
                keys = kv_buf[slot, 0, low:low + size] if size == used else kv_tail[0]
                k_turn[:, low:low + size] = jnp.transpose(keys.astype(F32)).astype(BF16)

        @pl.when((step >= base) & (step < base + heads * blocks) & (tiles[slot][0] < owners))
        def _(slot=slot, base=base):
            head, block = (step - base) // blocks, (step - base) % blocks
            pieces = pl.ds(block * chunks, chunks)
            grad = g_buf[slot, pieces, head, :HEAD_DIM].reshape(width, HEAD_DIM)
            delta = jnp.concatenate(
                [g_buf[slot, block * chunks + piece, head, HEAD_DIM:].astype(F32)[:1] for piece in range(chunks)], axis=1
            )
            total = jnp.zeros((HEAD_DIM, width), F32)
            for low, size, used in spans:
                values = kv_buf[slot, 1, low:low + size] if size == used else kv_tail[1]
                slope = dot_nt(values, grad)
                bent = (weights[0, low:low + size].astype(F32) * (slope - delta)).astype(BF16)
                slopes[0, low:low + size] = bent
                total = total + dot_nn(k_turn[:, low:low + size], bent)
            turned[slot, head, :, pl.ds(pl.multiple_of(block * width, width), width)] = total.astype(BF16)


def load_stats(stats, stats_buf):
    for index, ref in enumerate(stats):
        stats_buf[2 * index:2 * index + 2] = ref[...]


def peak_and_mass(stats_buf, owners, me, perm, start, tiles, head, block):
    found = []
    for index in range(MAX_TILES):
        live = index < tiles
        place = jnp.where(live, start + index, start)
        other = perm[place & (owners - 1)] ^ me
        slot = lax.div(place, owners)
        top = stats_buf[other, slot, 0, head, pl.ds(block, 1)]
        mass = stats_buf[other, slot, 1, head, pl.ds(block, 1)]
        found.append((jnp.where(live, top, -jnp.inf), jnp.where(live, mass, 0.0)))
    top = functools.reduce(jnp.maximum, [peak for peak, _ in found])
    return top, sum(mass * jnp.exp2(peak - top) for peak, mass in found)


def sums_kernel(owners, heads, blocks, slots, slot, who, counts, perm, weights, slopes, *refs):
    stats = refs[:owners // 2]
    q_pieces, g_pieces = refs[owners // 2:owners // 2 + owners], refs[owners // 2 + owners:owners // 2 + 2 * owners]
    keep_out, send_out, stats_buf, q_buf, g_buf, sums, q_sem, g_sem = refs[owners // 2 + 2 * owners:]
    step = pl.program_id(0)
    odd, me = who[0] & 1, who[1]
    spans = spans_of(sums.shape[1])
    chunks = q_buf.shape[0] // blocks
    width = chunks * HEAD_DIM
    sample, start = own_tiles(owners, slots, who, counts, perm)[slot]
    used = sample < owners

    @pl.when((step == 0) & used)
    def _():
        fetch(q_pieces, sample ^ me, q_buf, q_sem)
        fetch(g_pieces, sample ^ me, g_buf, g_sem)
        load_stats(stats, stats_buf)
        pltpu.make_async_copy(q_pieces[0], q_buf, q_sem).wait()
        pltpu.make_async_copy(g_pieces[0], g_buf, g_sem).wait()

    @pl.when(jnp.logical_not(used))
    def _():
        keep_out[...] = jnp.zeros(keep_out.shape, BF16)
        send_out[...] = jnp.zeros(send_out.shape, BF16)

    @pl.when(used)
    def _():
        head, block = step // blocks, step % blocks
        top, mass = peak_and_mass(stats_buf, owners, me, perm, start, counts[jnp.minimum(sample, owners - 1)], head, block)
        factor = jnp.exp2(stats_buf[0, slot, 0, head, pl.ds(block, 1)] - top) / mass
        factor = jnp.transpose(jnp.broadcast_to(factor, (HEAD_DIM, width)))
        pieces = pl.ds(block * chunks, chunks)
        query = q_buf[pieces, head].reshape(width, HEAD_DIM)
        grad = g_buf[pieces, head, :HEAD_DIM].reshape(width, HEAD_DIM)
        query = (query.astype(F32) * factor * SCALE).astype(BF16)
        grad = (grad.astype(F32) * factor).astype(BF16)

        def add(which, source, right, fresh):
            for low in range(0, sums.shape[1], 2 * KEY_ROWS):
                span = slice(low, min(low + 2 * KEY_ROWS, sums.shape[1]))
                part = dot_nn(source[0, span], right)
                sums[which, span] = part if fresh else sums[which, span] + part

        for fresh in (True, False):
            @pl.when((step == 0) == fresh)
            def _(fresh=fresh):
                add(0, slopes, query, fresh)
                add(1, weights, grad, fresh)

        @pl.when(step == heads * blocks - 1)
        def _():
            keep_out[...] = sums[odd].astype(BF16)
            send_out[...] = sums[1 - odd].astype(BF16)


def route_kernel(owners, heads, blocks, slots, who, counts, perm, own, other, *refs):
    stats = refs[:owners // 2]
    outs, stats_buf = refs[owners // 2:-1], refs[-1]
    load_stats(stats, stats_buf)
    me = who[1]
    width = own.shape[3] // blocks
    found = []
    for near in range(2):
        first = place_of(perm, me ^ near, owners)
        for slot in range(slots):
            sample, start = sample_at(counts, first + slot * owners, owners)
            found.append((near, slot, sample, start, counts[jnp.minimum(sample, owners - 1)]))

    def one(step, carry):
        head, block = step // blocks, step % blocks
        columns = pl.ds(pl.multiple_of(block * width, width), width)
        scaled = []
        for near, slot, sample, start, tiles in found:
            top, mass = peak_and_mass(stats_buf, owners, me, perm, start, tiles, head, block)
            factor = jnp.exp2(stats_buf[near, slot, 0, head, pl.ds(block, 1)] - top) / mass * SCALE
            scaled.append((own, other)[near][slot, head, :, columns].astype(F32) * factor)
        for distance, out in enumerate(outs):
            target = me ^ (2 * distance)
            total = sum(jnp.where(item[2] == target, part, 0.0) for item, part in zip(found, scaled))
            out[head, :, columns] = total.astype(BF16)
        return carry

    lax.fori_loop(0, heads * blocks, one, 0)


def gather_kernel(parts, *refs):
    outs = refs[parts:]
    rows = outs[0].shape[0]
    for piece, out in enumerate(outs):
        span = slice(piece * rows, (piece + 1) * rows)
        for head in range(refs[0].shape[0]):
            total = sum(ref[head, :, span].astype(F32) for ref in refs[:parts])
            out[:, head * HEAD_DIM:(head + 1) * HEAD_DIM] = jnp.transpose(total).astype(BF16)


def place_kernel(who, *refs):
    out = refs[-1]
    for distance, ref in enumerate(refs[:-1]):
        width = ref.shape[1]
        start = pl.multiple_of((who[0] ^ distance) * width, width)
        out[:, pl.ds(start, width)] = ref[...]


def merge_kernel(slots, *refs):
    keep, got, out = refs[:slots], refs[slots:-1], refs[-1]
    for low, size, used in spans_of(out.shape[0]):
        row = lax.broadcasted_iota(jnp.int32, (slots * size, slots * size), 0)
        column = lax.broadcasted_iota(jnp.int32, (slots * size, slots * size), 1)
        source = lax.rem(row, slots) * size + lax.div(row, slots)
        order = (source == column).astype(BF16)
        total = [
            (keep[slot][low:low + size].astype(F32) + got[slot][low:low + size].astype(F32)).astype(BF16)
            for slot in range(slots)
        ]
        mixed = dot_nn(order, jnp.concatenate(total, axis=0)).astype(BF16).reshape(size, slots, HEAD_DIM)
        out[low:low + used] = mixed[:used]


def gather_pieces(block):
    count = lax.axis_size("dp")
    near = [block] + [exchange(block, "dp", distance) for distance in range(2, count, 2)]
    result = []
    for piece in near:
        result += [piece, exchange(piece, "dp", 1)]
    return result


def shards(queries, saved_output, grad_out, tile_kv, tile_count, owner_perm, text_len):
    rows_dev, features = queries.shape[1], queries.shape[2]
    groups, owners = lax.axis_size("seq"), lax.axis_size("dp")
    heads = features // HEAD_DIM // groups
    width = heads * HEAD_DIM
    text_rows = groups * rows_dev
    chunks = min(TEXT_CHUNKS, groups)
    blocks = groups // chunks
    block_rows = chunks * rows_dev
    steps = heads * blocks
    slots, tile_rows = tile_kv.shape[0], tile_kv.shape[1]
    low, tail_rows, _ = spans_of(tile_rows)[-1]
    padded = low + tail_rows
    who = jnp.stack([lax.axis_index("seq"), lax.axis_index("dp")]).astype(jnp.int32)
    work = 2 * width * text_rows * tile_rows

    q_packed = call(
        functools.partial(pack_queries, groups, heads),
        [jax.ShapeDtypeStruct((heads, rows_dev, HEAD_DIM), BF16)] * groups,
        [SMEM, ANY],
        [pltpu.SemaphoreType.DMA((groups, heads))],
        (who, queries[0]),
    )
    g_packed = call(
        functools.partial(pack_grads, groups, heads),
        [jax.ShapeDtypeStruct((heads, rows_dev + DELTA_ROWS, HEAD_DIM), BF16)] * groups,
        [SMEM, SMEM, ANY, ANY],
        [pltpu.VMEM((rows_dev, features), BF16)] * 2 + [pltpu.SemaphoreType.DMA((2,))],
        (who, text_len, saved_output[0], grad_out[0]),
    )

    def over_seq(pieces):
        return jnp.stack([pieces[0]] + [exchange(pieces[j], "seq", j) for j in range(1, groups)])

    q_all = gather_pieces(over_seq(q_packed))
    partner_kv = exchange(tile_kv, "seq", 1)
    g_all = gather_pieces(over_seq(g_packed))

    known = (who, tile_count, owner_perm)
    q_scratch = pltpu.VMEM((slots,) + q_all[0].shape, BF16)
    g_scratch = pltpu.VMEM((slots,) + g_all[0].shape, BF16)
    stack_shape = jax.ShapeDtypeStruct((slots * steps, padded, block_rows), BF16)
    stack_spec = pl.BlockSpec((1, padded, block_rows), lambda i: (i, 0, 0))
    stats_shape = (slots, 2, heads, blocks, block_rows)

    stats, weights = call(
        functools.partial(weights_kernel, owners, heads, blocks, slots),
        [jax.ShapeDtypeStruct(stats_shape, F32), stack_shape],
        [SMEM] * 3 + [ANY] * (2 + owners),
        [
            q_scratch,
            pltpu.VMEM((slots, tile_rows, HEAD_DIM), BF16),
            pltpu.VMEM((tail_rows, HEAD_DIM), BF16),
            pltpu.VMEM((padded, block_rows), F32),
            pltpu.SemaphoreType.DMA((slots,)),
            pltpu.SemaphoreType.DMA((slots,)),
        ],
        (*known, tile_kv, partner_kv, *q_all),
        out_specs=[VMEM, stack_spec],
        grid=(slots * steps,),
        megabytes=32,
        flops=slots * work,
    )
    pair = jnp.stack([stats, exchange(stats, "dp", 1)])
    all_stats = [pair] + [exchange(pair, "dp", d) for d in range(2, owners, 2)]

    slopes, turned = call(
        functools.partial(slopes_kernel, owners, heads, blocks, slots),
        [stack_shape, jax.ShapeDtypeStruct((slots, heads, HEAD_DIM, text_rows), BF16)],
        [SMEM] * 3 + [stack_spec] + [ANY] * (2 + owners),
        [
            g_scratch,
            pltpu.VMEM((slots, 2, tile_rows, HEAD_DIM), BF16),
            pltpu.VMEM((2, tail_rows, HEAD_DIM), BF16),
            pltpu.VMEM((HEAD_DIM, -(-padded // HEAD_DIM) * HEAD_DIM), BF16),
            pltpu.SemaphoreType.DMA((slots,)),
            pltpu.SemaphoreType.DMA((slots, 2)),
        ],
        (*known, weights, tile_kv, partner_kv, *g_all),
        out_specs=[stack_spec, VMEM],
        grid=(slots * steps,),
        megabytes=32,
        flops=2 * slots * work,
    )

    stats_scratch = pltpu.VMEM((owners,) + stats_shape, F32)
    routed = call(
        functools.partial(route_kernel, owners, heads, blocks, slots),
        [jax.ShapeDtypeStruct((heads, HEAD_DIM, text_rows), BF16)] * (owners // 2),
        [SMEM] * 3 + [VMEM] * (2 + owners // 2),
        [stats_scratch],
        (*known, turned, exchange(turned, "dp", 1), *all_stats),
        megabytes=32,
    )

    kept, got = [], []
    for slot in range(slots):
        part_spec = pl.BlockSpec((1, padded, block_rows), lambda i, slot=slot: (slot * steps + i, 0, 0))
        keep, send = call(
            functools.partial(sums_kernel, owners, heads, blocks, slots, slot),
            [jax.ShapeDtypeStruct((padded, HEAD_DIM), BF16)] * 2,
            [SMEM] * 3 + [part_spec] * 2 + [VMEM] * (owners // 2) + [ANY] * (2 * owners),
            [
                stats_scratch,
                pltpu.VMEM(q_all[0].shape, BF16),
                pltpu.VMEM(g_all[0].shape, BF16),
                pltpu.VMEM((2, padded, HEAD_DIM), F32),
                pltpu.SemaphoreType.DMA(()),
                pltpu.SemaphoreType.DMA(()),
            ],
            (*known, weights, slopes, *all_stats, *q_all, *g_all),
            out_specs=[VMEM, VMEM],
            grid=(steps,),
            megabytes=32,
            flops=2 * work,
        )
        kept.append(keep)
        got.append(exchange(send, "seq", 1))

    sums = [routed[0]] + [exchange(routed[d], "dp", 2 * d) for d in range(1, owners // 2)]
    cut = call(
        functools.partial(gather_kernel, len(sums)),
        [jax.ShapeDtypeStruct((rows_dev, width), BF16)] * groups,
        [VMEM] * len(sums),
        [],
        sums,
        megabytes=32,
    )
    back = [cut[0]] + [exchange(cut[j], "seq", j) for j in range(1, groups)]
    grad_queries = call(
        place_kernel,
        jax.ShapeDtypeStruct((rows_dev, features), BF16),
        [SMEM] + [VMEM] * groups,
        [],
        (who, *back),
    )
    grad_tiles = call(
        functools.partial(merge_kernel, slots),
        jax.ShapeDtypeStruct((tile_rows, slots, HEAD_DIM), BF16),
        [VMEM] * (2 * slots),
        [],
        (*kept, *got),
    )
    return (grad_queries[None], jnp.transpose(grad_tiles, (1, 0, 2)))


def solution(mesh):
    placed = (
        P("dp", "seq", None),
        P("dp", "seq", None),
        P("dp", "seq", None),
        P("dp", None, "seq"),
        P(),
        P(),
        P("dp"),
    )
    return jax.shard_map(
        shards,
        mesh=mesh,
        in_specs=placed,
        out_specs=(P("dp", "seq", None), P("dp", None, "seq")),
        check_vma=False,
    )
```

time: 120 us -> 122 us (1.017)
  waiting for transfers between devices: 31.7 us -> 51.2 us
  local copies, waits for them, and re-layouts: 16.4 us -> 5.51 us
  starting transfers between devices: 53 us -> 44.4 us
  Pallas kernels: 16.9 us -> 19.8 us
    ppermute x47 -> x34, waiting for transfers between devices: 31.7 us -> 51.2 us  [exchange(): return lax.ppermute(block, axis, [(i, i ^ distance) for i in range(count)])]
    ppermute x47 -> x34, starting transfers between devices: 53 us -> 44.4 us  [exchange(): return lax.ppermute(block, axis, [(i, i ^ distance) for i in range(count)])]
    pallas_call x1 -> x0, local copies, waits for them, and re-layouts: 6.53 us -> none  [call(): pl.pallas_call(kernel, out_shape=out_shape, in_specs=in_specs, out_specs=...]
    unnamed x22 -> x11, local copies, waits for them, and re-layouts: 9.71 us -> 5.4 us
    pallas_call x6 -> x10, Pallas kernels: 16.9 us -> 19.8 us  [call(): pl.pallas_call(kernel, out_shape=out_shape, in_specs=in_specs, out_specs=...]
  transfers between devices with their start and end apart: 47 -> 34, of which waited for: 14 -> 15; matrix products, arithmetic and copies ran while one was open for 6% -> 1% of each run, Pallas kernels for 4% -> 10%
where the time goes in v2:
time: 122 us; the launch traced here: 123 us
  waiting for transfers between devices  51.2 us (42%)
  starting transfers between devices  44.4 us (36%)
  Pallas kernels  19.8 us (16%)
  local copies, waits for them, and re-layouts  5.51 us (5%)
  between operations  1.47 us (1%)
    ppermute x34, waiting for transfers between devices, exchange(): return lax.ppermute(block, axis, [(i, i ^ distance) for i in range(count)])  51.2 us
    ppermute x34, starting transfers between devices, exchange(): return lax.ppermute(block, axis, [(i, i ^ distance) for i in range(count)])  44.4 us
    pallas_call x10, Pallas kernels, call(): pl.pallas_call(kernel, out_shape=out_shape, in_specs=in_specs, out_specs=...  19.8 us
    unnamed x11, local copies, waits for them, and re-layouts  5.4 us
  transfers between devices with their start and end apart: 34, of which 15 were waited for; matrix products, arithmetic and copies ran while one was open for 1% of the time, Pallas kernels for 10%

profile of v2, /device:TPU:0, one launch (start us, length us, event | category | flops | bytes accessed | tf_op | source)
XLA Modules:
  0.0 122.5 jit_solution(7124967259337989066)
XLA Ops:
  0.7 0.9 copy-done
  1.7 0.7 shard_map.86
  2.4 5.1 %collective-permute-start.3 = (bf16[2,128,128]{2,1,0:T(8,128)(2,1)S(1)}, bf16[2,128,128]{2,1,0:T(8,128)(2,1)S(1)}, u32[]{:S(2)}, u32[]{:S(2)}) collective-permute-start(bf16[2,128,128]{2,1,0:T(8,128)(2,1)S(1)} %get-tuple-element.29), channel_id=1, source_target_pairs={{0,24},{8,16},{16,8},{24,0},{1,25},{9,17},{17,9},{25,1},{2,26},{10... | collective-permute-start | bytes 196616 | tf_op jit(solution)/shard_map/ppermute | solution.py:28
  7.5 0.6 collective-permute-start.1
  8.2 1.4 %collective-permute-start = (bf16[2,1601,128]{2,0,1:T(2,128)(2,1)}, bf16[2,1601,128]{2,0,1:T(2,128)(2,1)S(1)}, u32[]{:S(2)}, u32[]{:S(2)}) collective-permute-start(bf16[2,1601,128]{2,0,1:T(2,128)(2,1)} %param.10), channel_id=1, source_target_pairs={{0,8},{8,0},{16,24},{24,16},{1,9},{9,1},{17,25},{25,17},{2,10},{10... | collective-permute-start | bytes 2459144 | tf_op jit(solution)/shard_map/ppermute | solution.py:28
  9.6 0.5 collective-permute-done.3
  10.1 3.1 %collective-permute-done.2 = bf16[2,128,128]{2,1,0:T(8,128)(2,1)S(1)} collective-permute-done((bf16[2,128,128]{2,1,0:T(8,128)(2,1)S(1)}, bf16[2,128,128]{2,1,0:T(8,128)(2,1)S(1)}, u32[]{:S(2)}, u32[]{:S(2)}) %collective-permute-start.2) | collective-permute-done | bytes 65568 | tf_op jit(solution)/shard_map/ppermute | solution.py:28
  14.5 0.9 copy-done.1
  15.4 0.9 copy-done.2
  16.4 0.9 shard_map.88
  17.2 2.6 %collective-permute-start.13 = (bf16[2,144,128]{2,1,0:T(8,128)(2,1)S(1)}, bf16[2,144,128]{2,1,0:T(8,128)(2,1)S(1)}, u32[]{:S(2)}, u32[]{:S(2)}) collective-permute-start(bf16[2,144,128]{2,1,0:T(8,128)(2,1)S(1)} %get-tuple-element.34), channel_id=1, source_target_pairs={{0,24},{8,16},{16,8},{24,0},{1,25},{9,17},{17,9},{25,1},{2,26},{10... | collective-permute-start | bytes 221192 | tf_op jit(solution)/shard_map/ppermute | solution.py:28
  20.4 1.3 %collective-permute-start.11 = (bf16[2,144,128]{2,1,0:T(8,128)(2,1)S(1)}, bf16[2,144,128]{2,1,0:T(8,128)(2,1)S(1)}, u32[]{:S(2)}, u32[]{:S(2)}) collective-permute-start(bf16[2,144,128]{2,1,0:T(8,128)(2,1)S(1)} %get-tuple-element.32), channel_id=1, source_target_pairs={{0,8},{8,0},{16,24},{24,16},{1,9},{9,1},{17,25},{25,17},{2,10},{10... | collective-permute-start | bytes 221192 | tf_op jit(solution)/shard_map/ppermute | solution.py:28
  21.7 12.3 %collective-permute-done.13 = bf16[2,144,128]{2,1,0:T(8,128)(2,1)S(1)} collective-permute-done((bf16[2,144,128]{2,1,0:T(8,128)(2,1)S(1)}, bf16[2,144,128]{2,1,0:T(8,128)(2,1)S(1)}, u32[]{:S(2)}, u32[]{:S(2)}) %collective-permute-start.13) | collective-permute-done | bytes 73760 | tf_op jit(solution)/shard_map/ppermute | solution.py:28
  34.0 1.5 %collective-permute-start.5 = (bf16[4,2,128,128]{3,2,1,0:T(8,128)(2,1)S(1)}, bf16[4,2,128,128]{3,2,1,0:T(8,128)(2,1)S(1)}, u32[]{:S(2)}, u32[]{:S(2)}) collective-permute-start(bf16[4,2,128,128]{3,2,1,0:T(8,128)(2,1)S(1)} %pad_maximum_fusion.1.refs_0_.refs_4_), channel_id=1, source_target_pairs={{0,2},{1,3},{2,0},{3,1},{4,6},{5,7},{6,4},{7,5},{8,10},{9,11},{10,... | collective-permute-start | bytes 786440 | tf_op jit(solution)/shard_map/ppermute | solution.py:28
  35.5 1.5 %collective-permute-start.7 = (bf16[4,2,128,128]{3,2,1,0:T(8,128)(2,1)S(1)}, bf16[4,2,128,128]{3,2,1,0:T(8,128)(2,1)S(1)}, u32[]{:S(2)}, u32[]{:S(2)}) collective-permute-start(bf16[4,2,128,128]{3,2,1,0:T(8,128)(2,1)S(1)} %pad_maximum_fusion.1.refs_0_.refs_4_), channel_id=1, source_target_pairs={{0,4},{1,5},{2,6},{3,7},{4,0},{5,1},{6,2},{7,3},{8,12},{9,13},{10,... | collective-permute-start | bytes 786440 | tf_op jit(solution)/shard_map/ppermute | solution.py:28
  37.1 0.6 collective-permute-start.15
  37.7 1.4 %collective-permute-start.9 = (bf16[4,2,128,128]{3,2,1,0:T(8,128)(2,1)S(1)}, bf16[4,2,128,128]{3,2,1,0:T(8,128)(2,1)S(1)}, u32[]{:S(2)}, u32[]{:S(2)}) collective-permute-start(bf16[4,2,128,128]{3,2,1,0:T(8,128)(2,1)S(1)} %pad_maximum_fusion.1.refs_0_.refs_4_), channel_id=1, source_target_pairs={{0,6},{1,7},{2,4},{3,5},{4,2},{5,3},{6,0},{7,1},{8,14},{9,15},{10,... | collective-permute-start | bytes 786440 | tf_op jit(solution)/shard_map/ppermute | solution.py:28
  39.1 4.0 %collective-permute-done.5.refs_2_.refs_6_ = bf16[4,2,128,128]{3,2,1,0:T(8,128)(2,1)S(1)} collective-permute-done((bf16[4,2,128,128]{3,2,1,0:T(8,128)(2,1)S(1)}, bf16[4,2,128,128]{3,2,1,0:T(8,128)(2,1)S(1)}, u32[]{:S(2)}, u32[]{:S(2)}) %collective-permute-start.5) | collective-permute-done | bytes 262176 | tf_op jit(solution)/shard_map/ppermute | solution.py:28
  43.1 1.5 %collective-permute-start.17 = (bf16[4,2,144,128]{3,2,1,0:T(8,128)(2,1)S(1)}, bf16[4,2,144,128]{3,2,1,0:T(8,128)(2,1)S(1)}, u32[]{:S(2)}, u32[]{:S(2)}) collective-permute-start(bf16[4,2,144,128]{3,2,1,0:T(8,128)(2,1)S(1)} %pad_maximum_fusion.refs_0_.refs_12_), channel_id=1, source_target_pairs={{0,4},{1,5},{2,6},{3,7},{4,0},{5,1},{6,2},{7,3},{8,12},{9,13},{10,... | collective-permute-start | bytes 884744 | tf_op jit(solution)/shard_map/ppermute | solution.py:28
  45.1 1.3 %collective-permute-start.19 = (bf16[4,2,144,128]{3,2,1,0:T(8,128)(2,1)S(1)}, bf16[4,2,144,128]{3,2,1,0:T(8,128)(2,1)S(1)}, u32[]{:S(2)}, u32[]{:S(2)}) collective-permute-start(bf16[4,2,144,128]{3,2,1,0:T(8,128)(2,1)S(1)} %pad_maximum_fusion.refs_0_.refs_12_), channel_id=1, source_target_pairs={{0,6},{1,7},{2,4},{3,5},{4,2},{5,3},{6,0},{7,1},{8,14},{9,15},{10,... | collective-permute-start | bytes 884744 | tf_op jit(solution)/shard_map/ppermute | solution.py:28
  46.4 9.6 %collective-permute-done.9.refs_6_.refs_10_ = bf16[4,2,128,128]{3,2,1,0:T(8,128)(2,1)S(1)} collective-permute-done((bf16[4,2,128,128]{3,2,1,0:T(8,128)(2,1)S(1)}, bf16[4,2,128,128]{3,2,1,0:T(8,128)(2,1)S(1)}, u32[]{:S(2)}, u32[]{:S(2)}) %collective-permute-start.9) | collective-permute-done | bytes 262176 | tf_op jit(solution)/shard_map/ppermute | solution.py:28
  56.5 3.9 %collective-permute-done.17.refs_4_.refs_16_ = bf16[4,2,144,128]{3,2,1,0:T(8,128)(2,1)S(1)} collective-permute-done((bf16[4,2,144,128]{3,2,1,0:T(8,128)(2,1)S(1)}, bf16[4,2,144,128]{3,2,1,0:T(8,128)(2,1)S(1)}, u32[]{:S(2)}, u32[]{:S(2)}) %collective-permute-start.17) | collective-permute-done | bytes 294944 | tf_op jit(solution)/shard_map/ppermute | solution.py:28
  61.5 1.3 %copy.12.own_kv = bf16[2,1601,128]{2,1,0:T(8,128)(2,1)S(1)} copy(bf16[2,1601,128]{2,0,1:T(2,128)(2,1)} %param.10) | data formatting | bytes 1639424 | tf_op args[3]
  62.9 0.6 copy-done.3
  63.5 0.7 copy-done.4
  64.2 3.6 %shard_map.87 = (f32[2,2,2,1,512]{4,3,2,1,0:T(1,128)S(1)}, bf16[4,1616,512]{2,1,0:T(8,128)(2,1)S(1)}) custom-call(s32[2]{0:T(128)S(1)} %pad_add_fusion.who, s32[8]{0:T(128)S(1)} %copy-done.3, s32[8]{0:T(128)S(1)} %copy-done.4, bf16[2,1601,128]{2,1,0:T(8,128)(2,1)S(1)} %copy.12.own_kv, bf16[2,1601,128]{2,1,0:T(8,128)(2,1)S(1)} %copy.13.partner_kv, ...), custom_call_target="tpu_custom_call" | custom-call | flops 839385088 | tf_op jit(solution)/shard_map/pallas_call | solution.py:35
  67.9 5.0 %shard_map.89 = (bf16[4,1616,512]{2,1,0:T(8,128)(2,1)S(1)}, bf16[2,2,128,512]{3,2,1,0:T(8,128)(2,1)S(1)}) custom-call(s32[2]{0:T(128)S(1)} %pad_add_fusion.who, s32[8]{0:T(128)S(1)} %copy-done.3, s32[8]{0:T(128)S(1)} %copy-done.4, bf16[4,1616,512]{2,1,0:T(8,128)(2,1)S(1)} %get-tuple-element.30.weights, bf16[2,1601,128]{2,1,0:T(8,128)(2,1)S(1)} %copy.12.own_kv, ...), custom_call_target="tpu_custom_call" | custom-call | flops 1678770176 | tf_op jit(solution)/shard_map/pallas_call | solution.py:35
  72.9 7.2 %collective-permute-start.21 = (bf16[2,2,128,512]{3,2,1,0:T(8,128)(2,1)S(1)}, bf16[2,2,128,512]{3,2,1,0:T(8,128)(2,1)S(1)}, u32[]{:S(2)}, u32[]{:S(2)}) collective-permute-start(bf16[2,2,128,512]{3,2,1,0:T(8,128)(2,1)S(1)} %get-tuple-element.35.own), channel_id=1, source_target_pairs={{0,1},{1,0},{2,3},{3,2},{4,5},{5,4},{6,7},{7,6},{8,9},{9,8},{10,11... | collective-permute-start | bytes 1572872 | tf_op jit(solution)/shard_map/ppermute | solution.py:28
  80.2 1.5 %collective-permute-done.22 = f32[2,2,2,1,512]{4,3,2,1,0:T(1,128)S(1)} collective-permute-done((f32[2,2,2,1,512]{4,3,2,1,0:T(1,128)S(1)}, f32[2,2,2,1,512]{4,3,2,1,0:T(1,128)S(1)}, u32[]{:S(2)}, u32[]{:S(2)}) %collective-permute-start.22) | collective-permute-done | bytes 16416 | tf_op jit(solution)/shard_map/ppermute | solution.py:28
  81.7 1.6 %collective-permute-start.23 = (f32[2,2,2,2,1,512]{5,4,3,2,1,0:T(1,128)S(1)}, f32[2,2,2,2,1,512]{5,4,3,2,1,0:T(1,128)S(1)}, u32[]{:S(2)}, u32[]{:S(2)}) collective-permute-start(f32[2,2,2,2,1,512]{5,4,3,2,1,0:T(1,128)S(1)} %pad_maximum_fusion.2.refs_0_), channel_id=1, source_target_pairs={{0,2},{1,3},{2,0},{3,1},{4,6},{5,7},{6,4},{7,5},{8,10},{9,11},{10,... | collective-permute-start | bytes 98312 | tf_op jit(solution)/shard_map/ppermute | solution.py:28
  83.3 2.0 %collective-permute-start.25 = (f32[2,2,2,2,1,512]{5,4,3,2,1,0:T(1,128)S(1)}, f32[2,2,2,2,1,512]{5,4,3,2,1,0:T(1,128)S(1)}, u32[]{:S(2)}, u32[]{:S(2)}) collective-permute-start(f32[2,2,2,2,1,512]{5,4,3,2,1,0:T(1,128)S(1)} %pad_maximum_fusion.2.refs_0_), channel_id=1, source_target_pairs={{0,6},{1,7},{2,4},{3,5},{4,2},{5,3},{6,0},{7,1},{8,14},{9,15},{10,... | collective-permute-start | bytes 98312 | tf_op jit(solution)/shard_map/ppermute | solution.py:28
  85.7 1.8 %collective-permute-done.24.refs_2_ = f32[2,2,2,2,1,512]{5,4,3,2,1,0:T(1,128)S(1)} collective-permute-done((f32[2,2,2,2,1,512]{5,4,3,2,1,0:T(1,128)S(1)}, f32[2,2,2,2,1,512]{5,4,3,2,1,0:T(1,128)S(1)}, u32[]{:S(2)}, u32[]{:S(2)}) %collective-permute-start.24) | collective-permute-done | bytes 32800 | tf_op jit(solution)/shard_map/ppermute | solution.py:28
  87.5 0.6 collective-permute-done.25.refs_3_
  88.1 3.4 %shard_map.93 = (bf16[1616,128]{1,0:T(8,128)(2,1)S(1)}, bf16[1616,128]{1,0:T(8,128)(2,1)S(1)}) custom-call(s32[2]{0:T(128)S(1)} %pad_add_fusion.who, s32[8]{0:T(128)S(1)} %copy-done.3, s32[8]{0:T(128)S(1)} %copy-done.4, bf16[4,1616,512]{2,1,0:T(8,128)(2,1)S(1)} %get-tuple-element.30.weights, bf16[4,1616,512]{2,1,0:T(8,128)(2,1)S(1)} %get-tuple-element.45.slopes, ...), custom_call_target="tpu_custom_call" | custom-call | flops 839385088 | tf_op jit(solution)/shard_map/pallas_call | solution.py:35
  91.6 1.1 shard_map.94
  92.8 1.9 %collective-permute-start.33 = (bf16[1616,128]{1,0:T(8,128)(2,1)S(1)}, bf16[1616,128]{1,0:T(8,128)(2,1)S(1)}, u32[]{:S(2)}, u32[]{:S(2)}) collective-permute-start(bf16[1616,128]{1,0:T(8,128)(2,1)S(1)} %get-tuple-element.49), channel_id=1, source_target_pairs={{0,8},{8,0},{16,24},{24,16},{1,9},{9,1},{17,25},{25,17},{2,10},{10... | collective-permute-start | bytes 1241096 | tf_op jit(solution)/shard_map/ppermute | solution.py:28
  94.6 1.5 %shard_map.90 = (bf16[2,128,512]{2,1,0:T(8,128)(2,1)S(1)}, bf16[2,128,512]{2,1,0:T(8,128)(2,1)S(1)}, bf16[2,128,512]{2,1,0:T(8,128)(2,1)S(1)}, bf16[2,128,512]{2,1,0:T(8,128)(2,1)S(1)}) custom-call(s32[2]{0:T(128)S(1)} %pad_add_fusion.who, s32[8]{0:T(128)S(1)} %copy-done.3, s32[8]{0:T(128)S(1)} %copy-done.4, ...), custom_call_target="tpu_custom_call" | custom-call | tf_op jit(solution)/shard_map/pallas_call | solution.py:35
  96.1 3.8 %collective-permute-start.26 = (bf16[2,128,512]{2,1,0:T(8,128)(2,1)S(1)}, bf16[2,128,512]{2,1,0:T(8,128)(2,1)S(1)}, u32[]{:S(2)}, u32[]{:S(2)}) collective-permute-start(bf16[2,128,512]{2,1,0:T(8,128)(2,1)S(1)} %get-tuple-element.38), channel_id=1, source_target_pairs={{0,2},{1,3},{2,0},{3,1},{4,6},{5,7},{6,4},{7,5},{8,10},{9,11},{10,... | collective-permute-start | bytes 786440 | tf_op jit(solution)/shard_map/ppermute | solution.py:28
  99.9 0.9 collective-permute-start.27
  100.8 1.4 %collective-permute-start.28 = (bf16[2,128,512]{2,1,0:T(8,128)(2,1)S(1)}, bf16[2,128,512]{2,1,0:T(8,128)(2,1)S(1)}, u32[]{:S(2)}, u32[]{:S(2)}) collective-permute-start(bf16[2,128,512]{2,1,0:T(8,128)(2,1)S(1)} %get-tuple-element.40), channel_id=1, source_target_pairs={{0,6},{1,7},{2,4},{3,5},{4,2},{5,3},{6,0},{7,1},{8,14},{9,15},{10,... | collective-permute-start | bytes 786440 | tf_op jit(solution)/shard_map/ppermute | solution.py:28
  102.2 5.0 %collective-permute-done.26.refs_1_ = bf16[2,128,512]{2,1,0:T(8,128)(2,1)S(1)} collective-permute-done((bf16[2,128,512]{2,1,0:T(8,128)(2,1)S(1)}, bf16[2,128,512]{2,1,0:T(8,128)(2,1)S(1)}, u32[]{:S(2)}, u32[]{:S(2)}) %collective-permute-start.26) | collective-permute-done | bytes 262176 | tf_op jit(solution)/shard_map/ppermute | solution.py:28
  107.1 4.3 %collective-permute-done.27.refs_2_ = bf16[2,128,512]{2,1,0:T(8,128)(2,1)S(1)} collective-permute-done((bf16[2,128,512]{2,1,0:T(8,128)(2,1)S(1)}, bf16[2,128,512]{2,1,0:T(8,128)(2,1)S(1)}, u32[]{:S(2)}, u32[]{:S(2)}) %collective-permute-start.27) | collective-permute-done | bytes 262176 | tf_op jit(solution)/shard_map/ppermute | solution.py:28
  111.6 0.6 collective-permute-start.29
  112.2 3.0 %collective-permute-start.30 = (bf16[128,256]{1,0:T(8,128)(2,1)S(1)}, bf16[128,256]{1,0:T(8,128)(2,1)S(1)}, u32[]{:S(2)}, u32[]{:S(2)}) collective-permute-start(bf16[128,256]{1,0:T(8,128)(2,1)S(1)} %get-tuple-element.43), channel_id=1, source_target_pairs={{0,16},{8,24},{16,0},{24,8},{1,17},{9,25},{17,1},{25,9},{2,18},{10... | collective-permute-start | bytes 196616 | tf_op jit(solution)/shard_map/ppermute | solution.py:28
  115.2 0.9 collective-permute-start.31
  116.1 2.0 %shard_map.95 = bf16[1601,2,128]{2,1,0:T(2,128)(2,1)} custom-call(bf16[1616,128]{1,0:T(8,128)(2,1)S(1)} %get-tuple-element.46.refs_0_, bf16[1616,128]{1,0:T(8,128)(2,1)S(1)} %get-tuple-element.47.refs_1_, bf16[1616,128]{1,0:T(8,128)(2,1)S(1)} %collective-permute-done.32.refs_2_, bf16[1616,128]{1,0:T(8,128)(2,1)S(1)} %collective-permute-done.33.refs_3_), custom_call_target="tpu_custom_call" | custom-call | tf_op jit(solution)/shard_map/pallas_call | solution.py:35
  118.1 3.1 %collective-permute-done.31.refs_3_ = bf16[128,256]{1,0:T(8,128)(2,1)S(1)} collective-permute-done((bf16[128,256]{1,0:T(8,128)(2,1)S(1)}, bf16[128,256]{1,0:T(8,128)(2,1)S(1)}, u32[]{:S(2)}, u32[]{:S(2)}) %collective-permute-start.31) | collective-permute-done | bytes 65568 | tf_op jit(solution)/shard_map/ppermute | solution.py:28
  121.3 1.3 %shard_map.92 = bf16[128,1024]{1,0:T(8,128)(2,1)} custom-call(s32[2]{0:T(128)S(1)} %pad_add_fusion.who, bf16[128,256]{1,0:T(8,128)(2,1)S(1)} %get-tuple-element.41.refs_0_, bf16[128,256]{1,0:T(8,128)(2,1)S(1)} %collective-permute-done.29.refs_1_, bf16[128,256]{1,0:T(8,128)(2,1)S(1)} %collective-permute-done.30.refs_2_, ...), custom_call_target="tpu_custom_call" | custom-call | tf_op jit(solution)/shard_map/pallas_call | solution.py:35
  (46 shorter events, 4.3 us)
Async XLA Ops:
  0.7 1.0 copy-start
  2.4 7.7 %collective-permute-start.3 = (bf16[2,128,128]{2,1,0:T(8,128)(2,1)S(1)}, bf16[2,128,128]{2,1,0:T(8,128)(2,1)S(1)}, u32[]{:S(2)}, u32[]{:S(2)}) collective-permute-start(bf16[2,128,128]{2,1,0:T(8,128)(2,1)S(1)} %get-tuple-element.29), channel_id=1, source_target_pairs={{0,24},{8,16},{16,8},{24,0},{1,25},{9,17},{17,9},{25,1},{2,26},{10... | collective-permute-start | bytes 196616 | tf_op jit(solution)/shard_map/ppermute | solution.py:28
  7.5 5.7 %collective-permute-start.2 = (bf16[2,128,128]{2,1,0:T(8,128)(2,1)S(1)}, bf16[2,128,128]{2,1,0:T(8,128)(2,1)S(1)}, u32[]{:S(2)}, u32[]{:S(2)}) collective-permute-start(bf16[2,128,128]{2,1,0:T(8,128)(2,1)S(1)} %get-tuple-element.28), channel_id=1, source_target_pairs={{0,16},{8,24},{16,0},{24,8},{1,17},{9,25},{17,1},{25,9},{2,18},{10... | collective-permute-start | bytes 196616 | tf_op jit(solution)/shard_map/ppermute | solution.py:28
  7.5 6.2 %collective-permute-start.1 = (bf16[2,128,128]{2,1,0:T(8,128)(2,1)S(1)}, bf16[2,128,128]{2,1,0:T(8,128)(2,1)S(1)}, u32[]{:S(2)}, u32[]{:S(2)}) collective-permute-start(bf16[2,128,128]{2,1,0:T(8,128)(2,1)S(1)} %get-tuple-element.27), channel_id=1, source_target_pairs={{0,8},{8,0},{16,24},{24,16},{1,9},{9,1},{17,25},{25,17},{2,10},{10... | collective-permute-start | bytes 196616 | tf_op jit(solution)/shard_map/ppermute | solution.py:28
  8.2 53.2 %collective-permute-start = (bf16[2,1601,128]{2,0,1:T(2,128)(2,1)}, bf16[2,1601,128]{2,0,1:T(2,128)(2,1)S(1)}, u32[]{:S(2)}, u32[]{:S(2)}) collective-permute-start(bf16[2,1601,128]{2,0,1:T(2,128)(2,1)} %param.10), channel_id=1, source_target_pairs={{0,8},{8,0},{16,24},{24,16},{1,9},{9,1},{17,25},{25,17},{2,10},{10... | collective-permute-start | bytes 2459144 | tf_op jit(solution)/shard_map/ppermute | solution.py:28
  13.7 23.9 %collective-permute-start.4 = (bf16[4,2,128,128]{3,2,1,0:T(8,128)(2,1)S(1)}, bf16[4,2,128,128]{3,2,1,0:T(8,128)(2,1)S(1)}, u32[]{:S(2)}, u32[]{:S(2)}) collective-permute-start(bf16[4,2,128,128]{3,2,1,0:T(8,128)(2,1)S(1)} %pad_maximum_fusion.1.refs_0_.refs_4_), channel_id=1, source_target_pairs={{0,1},{1,0},{2,3},{3,2},{4,5},{5,4},{6,7},{7,6},{8,9},{9,8},{10,11... | collective-permute-start | bytes 786440 | tf_op jit(solution)/shard_map/ppermute | solution.py:28
  14.5 1.0 copy-start.1
  15.4 0.9 copy-start.2
  17.2 16.8 %collective-permute-start.13 = (bf16[2,144,128]{2,1,0:T(8,128)(2,1)S(1)}, bf16[2,144,128]{2,1,0:T(8,128)(2,1)S(1)}, u32[]{:S(2)}, u32[]{:S(2)}) collective-permute-start(bf16[2,144,128]{2,1,0:T(8,128)(2,1)S(1)} %get-tuple-element.34), channel_id=1, source_target_pairs={{0,24},{8,16},{16,8},{24,0},{1,25},{9,17},{17,9},{25,1},{2,26},{10... | collective-permute-start | bytes 221192 | tf_op jit(solution)/shard_map/ppermute | solution.py:28
  19.9 15.6 %collective-permute-start.12 = (bf16[2,144,128]{2,1,0:T(8,128)(2,1)S(1)}, bf16[2,144,128]{2,1,0:T(8,128)(2,1)S(1)}, u32[]{:S(2)}, u32[]{:S(2)}) collective-permute-start(bf16[2,144,128]{2,1,0:T(8,128)(2,1)S(1)} %get-tuple-element.33), channel_id=1, source_target_pairs={{0,16},{8,24},{16,0},{24,8},{1,17},{9,25},{17,1},{25,9},{2,18},{10... | collective-permute-start | bytes 221192 | tf_op jit(solution)/shard_map/ppermute | solution.py:28
  20.4 16.6 %collective-permute-start.11 = (bf16[2,144,128]{2,1,0:T(8,128)(2,1)S(1)}, bf16[2,144,128]{2,1,0:T(8,128)(2,1)S(1)}, u32[]{:S(2)}, u32[]{:S(2)}) collective-permute-start(bf16[2,144,128]{2,1,0:T(8,128)(2,1)S(1)} %get-tuple-element.32), channel_id=1, source_target_pairs={{0,8},{8,0},{16,24},{24,16},{1,9},{9,1},{17,25},{25,17},{2,10},{10... | collective-permute-start | bytes 221192 | tf_op jit(solution)/shard_map/ppermute | solution.py:28
  34.0 9.1 %collective-permute-start.5 = (bf16[4,2,128,128]{3,2,1,0:T(8,128)(2,1)S(1)}, bf16[4,2,128,128]{3,2,1,0:T(8,128)(2,1)S(1)}, u32[]{:S(2)}, u32[]{:S(2)}) collective-permute-start(bf16[4,2,128,128]{3,2,1,0:T(8,128)(2,1)S(1)} %pad_maximum_fusion.1.refs_0_.refs_4_), channel_id=1, source_target_pairs={{0,2},{1,3},{2,0},{3,1},{4,6},{5,7},{6,4},{7,5},{8,10},{9,11},{10,... | collective-permute-start | bytes 786440 | tf_op jit(solution)/shard_map/ppermute | solution.py:28
  35.5 9.6 %collective-permute-start.7 = (bf16[4,2,128,128]{3,2,1,0:T(8,128)(2,1)S(1)}, bf16[4,2,128,128]{3,2,1,0:T(8,128)(2,1)S(1)}, u32[]{:S(2)}, u32[]{:S(2)}) collective-permute-start(bf16[4,2,128,128]{3,2,1,0:T(8,128)(2,1)S(1)} %pad_maximum_fusion.1.refs_0_.refs_4_), channel_id=1, source_target_pairs={{0,4},{1,5},{2,6},{3,7},{4,0},{5,1},{6,2},{7,3},{8,12},{9,13},{10,... | collective-permute-start | bytes 786440 | tf_op jit(solution)/shard_map/ppermute | solution.py:28
  37.1 18.9 %collective-permute-start.15 = (bf16[4,2,144,128]{3,2,1,0:T(8,128)(2,1)S(1)}, bf16[4,2,144,128]{3,2,1,0:T(8,128)(2,1)S(1)}, u32[]{:S(2)}, u32[]{:S(2)}) collective-permute-start(bf16[4,2,144,128]{3,2,1,0:T(8,128)(2,1)S(1)} %pad_maximum_fusion.refs_0_.refs_12_), channel_id=1, source_target_pairs={{0,2},{1,3},{2,0},{3,1},{4,6},{5,7},{6,4},{7,5},{8,10},{9,11},{10,... | collective-permute-start | bytes 884744 | tf_op jit(solution)/shard_map/ppermute | solution.py:28
  37.7 18.3 %collective-permute-start.9 = (bf16[4,2,128,128]{3,2,1,0:T(8,128)(2,1)S(1)}, bf16[4,2,128,128]{3,2,1,0:T(8,128)(2,1)S(1)}, u32[]{:S(2)}, u32[]{:S(2)}) collective-permute-start(bf16[4,2,128,128]{3,2,1,0:T(8,128)(2,1)S(1)} %pad_maximum_fusion.1.refs_0_.refs_4_), channel_id=1, source_target_pairs={{0,6},{1,7},{2,4},{3,5},{4,2},{5,3},{6,0},{7,1},{8,14},{9,15},{10,... | collective-permute-start | bytes 786440 | tf_op jit(solution)/shard_map/ppermute | solution.py:28
  43.1 17.2 %collective-permute-start.17 = (bf16[4,2,144,128]{3,2,1,0:T(8,128)(2,1)S(1)}, bf16[4,2,144,128]{3,2,1,0:T(8,128)(2,1)S(1)}, u32[]{:S(2)}, u32[]{:S(2)}) collective-permute-start(bf16[4,2,144,128]{3,2,1,0:T(8,128)(2,1)S(1)} %pad_maximum_fusion.refs_0_.refs_12_), channel_id=1, source_target_pairs={{0,4},{1,5},{2,6},{3,7},{4,0},{5,1},{6,2},{7,3},{8,12},{9,13},{10,... | collective-permute-start | bytes 884744 | tf_op jit(solution)/shard_map/ppermute | solution.py:28
  45.1 15.3 %collective-permute-start.19 = (bf16[4,2,144,128]{3,2,1,0:T(8,128)(2,1)S(1)}, bf16[4,2,144,128]{3,2,1,0:T(8,128)(2,1)S(1)}, u32[]{:S(2)}, u32[]{:S(2)}) collective-permute-start(bf16[4,2,144,128]{3,2,1,0:T(8,128)(2,1)S(1)} %pad_maximum_fusion.refs_0_.refs_12_), channel_id=1, source_target_pairs={{0,6},{1,7},{2,4},{3,5},{4,2},{5,3},{6,0},{7,1},{8,14},{9,15},{10,... | collective-permute-start | bytes 884744 | tf_op jit(solution)/shard_map/ppermute | solution.py:28
  56.0 4.9 %collective-permute-start.6 = (bf16[4,2,128,128]{3,2,1,0:T(8,128)(2,1)S(1)}, bf16[4,2,128,128]{3,2,1,0:T(8,128)(2,1)S(1)}, u32[]{:S(2)}, u32[]{:S(2)}) collective-permute-start(bf16[4,2,128,128]{3,2,1,0:T(8,128)(2,1)S(1)} %collective-permute-done.5.refs_2_.refs_6_), channel_id=1, source_target_pairs={{0,1},{1,0},{2,3},{3,2},{4,5},{5,4},{6,7},{7,6},{8,9},{9,8},{10,11... | collective-permute-start | bytes 786440 | tf_op jit(solution)/shard_map/ppermute | solution.py:28
  56.0 5.0 %collective-permute-start.8 = (bf16[4,2,128,128]{3,2,1,0:T(8,128)(2,1)S(1)}, bf16[4,2,128,128]{3,2,1,0:T(8,128)(2,1)S(1)}, u32[]{:S(2)}, u32[]{:S(2)}) collective-permute-start(bf16[4,2,128,128]{3,2,1,0:T(8,128)(2,1)S(1)} %collective-permute-done.7.refs_4_.refs_8_), channel_id=1, source_target_pairs={{0,1},{1,0},{2,3},{3,2},{4,5},{5,4},{6,7},{7,6},{8,9},{9,8},{10,11... | collective-permute-start | bytes 786440 | tf_op jit(solution)/shard_map/ppermute | solution.py:28
  60.4 2.5 %collective-permute-start.10 = (bf16[4,2,128,128]{3,2,1,0:T(8,128)(2,1)S(1)}, bf16[4,2,128,128]{3,2,1,0:T(8,128)(2,1)S(1)}, u32[]{:S(2)}, u32[]{:S(2)}) collective-permute-start(bf16[4,2,128,128]{3,2,1,0:T(8,128)(2,1)S(1)} %collective-permute-done.9.refs_6_.refs_10_), channel_id=1, source_target_pairs={{0,1},{1,0},{2,3},{3,2},{4,5},{5,4},{6,7},{7,6},{8,9},{9,8},{10,11... | collective-permute-start | bytes 786440 | tf_op jit(solution)/shard_map/ppermute | solution.py:28
  60.4 7.4 %collective-permute-start.14 = (bf16[4,2,144,128]{3,2,1,0:T(8,128)(2,1)S(1)}, bf16[4,2,144,128]{3,2,1,0:T(8,128)(2,1)S(1)}, u32[]{:S(2)}, u32[]{:S(2)}) collective-permute-start(bf16[4,2,144,128]{3,2,1,0:T(8,128)(2,1)S(1)} %pad_maximum_fusion.refs_0_.refs_12_), channel_id=1, source_target_pairs={{0,1},{1,0},{2,3},{3,2},{4,5},{5,4},{6,7},{7,6},{8,9},{9,8},{10,11... | collective-permute-start | bytes 884744 | tf_op jit(solution)/shard_map/ppermute | solution.py:28
  60.9 6.9 %collective-permute-start.16 = (bf16[4,2,144,128]{3,2,1,0:T(8,128)(2,1)S(1)}, bf16[4,2,144,128]{3,2,1,0:T(8,128)(2,1)S(1)}, u32[]{:S(2)}, u32[]{:S(2)}) collective-permute-start(bf16[4,2,144,128]{3,2,1,0:T(8,128)(2,1)S(1)} %collective-permute-done.15.refs_2_.refs_14_), channel_id=1, source_target_pairs={{0,1},{1,0},{2,3},{3,2},{4,5},{5,4},{6,7},{7,6},{8,9},{9,8},{10,11... | collective-permute-start | bytes 884744 | tf_op jit(solution)/shard_map/ppermute | solution.py:28
  61.0 6.9 %collective-permute-start.18 = (bf16[4,2,144,128]{3,2,1,0:T(8,128)(2,1)S(1)}, bf16[4,2,144,128]{3,2,1,0:T(8,128)(2,1)S(1)}, u32[]{:S(2)}, u32[]{:S(2)}) collective-permute-start(bf16[4,2,144,128]{3,2,1,0:T(8,128)(2,1)S(1)} %collective-permute-done.17.refs_4_.refs_16_), channel_id=1, source_target_pairs={{0,1},{1,0},{2,3},{3,2},{4,5},{5,4},{6,7},{7,6},{8,9},{9,8},{10,11... | collective-permute-start | bytes 884744 | tf_op jit(solution)/shard_map/ppermute | solution.py:28
  61.4 6.4 %collective-permute-start.20 = (bf16[4,2,144,128]{3,2,1,0:T(8,128)(2,1)S(1)}, bf16[4,2,144,128]{3,2,1,0:T(8,128)(2,1)S(1)}, u32[]{:S(2)}, u32[]{:S(2)}) collective-permute-start(bf16[4,2,144,128]{3,2,1,0:T(8,128)(2,1)S(1)} %collective-permute-done.19.refs_6_.refs_18_), channel_id=1, source_target_pairs={{0,1},{1,0},{2,3},{3,2},{4,5},{5,4},{6,7},{7,6},{8,9},{9,8},{10,11... | collective-permute-start | bytes 884744 | tf_op jit(solution)/shard_map/ppermute | solution.py:28
  62.8 0.7 copy-start.3
  63.5 0.7 copy-start.4
  72.9 21.7 %collective-permute-start.21 = (bf16[2,2,128,512]{3,2,1,0:T(8,128)(2,1)S(1)}, bf16[2,2,128,512]{3,2,1,0:T(8,128)(2,1)S(1)}, u32[]{:S(2)}, u32[]{:S(2)}) collective-permute-start(bf16[2,2,128,512]{3,2,1,0:T(8,128)(2,1)S(1)} %get-tuple-element.35.own), channel_id=1, source_target_pairs={{0,1},{1,0},{2,3},{3,2},{4,5},{5,4},{6,7},{7,6},{8,9},{9,8},{10,11... | collective-permute-start | bytes 1572872 | tf_op jit(solution)/shard_map/ppermute | solution.py:28
  80.1 1.6 %collective-permute-start.22 = (f32[2,2,2,1,512]{4,3,2,1,0:T(1,128)S(1)}, f32[2,2,2,1,512]{4,3,2,1,0:T(1,128)S(1)}, u32[]{:S(2)}, u32[]{:S(2)}) collective-permute-start(f32[2,2,2,1,512]{4,3,2,1,0:T(1,128)S(1)} %get-tuple-element.36), channel_id=1, source_target_pairs={{0,1},{1,0},{2,3},{3,2},{4,5},{5,4},{6,7},{7,6},{8,9},{9,8},{10,11... | collective-permute-start | bytes 49160 | tf_op jit(solution)/shard_map/ppermute | solution.py:28
  81.7 4.0 %collective-permute-start.23 = (f32[2,2,2,2,1,512]{5,4,3,2,1,0:T(1,128)S(1)}, f32[2,2,2,2,1,512]{5,4,3,2,1,0:T(1,128)S(1)}, u32[]{:S(2)}, u32[]{:S(2)}) collective-permute-start(f32[2,2,2,2,1,512]{5,4,3,2,1,0:T(1,128)S(1)} %pad_maximum_fusion.2.refs_0_), channel_id=1, source_target_pairs={{0,2},{1,3},{2,0},{3,1},{4,6},{5,7},{6,4},{7,5},{8,10},{9,11},{10,... | collective-permute-start | bytes 98312 | tf_op jit(solution)/shard_map/ppermute | solution.py:28
  83.3 4.3 %collective-permute-start.24 = (f32[2,2,2,2,1,512]{5,4,3,2,1,0:T(1,128)S(1)}, f32[2,2,2,2,1,512]{5,4,3,2,1,0:T(1,128)S(1)}, u32[]{:S(2)}, u32[]{:S(2)}) collective-permute-start(f32[2,2,2,2,1,512]{5,4,3,2,1,0:T(1,128)S(1)} %pad_maximum_fusion.2.refs_0_), channel_id=1, source_target_pairs={{0,4},{1,5},{2,6},{3,7},{4,0},{5,1},{6,2},{7,3},{8,12},{9,13},{10,... | collective-permute-start | bytes 98312 | tf_op jit(solution)/shard_map/ppermute | solution.py:28
  83.3 4.8 %collective-permute-start.25 = (f32[2,2,2,2,1,512]{5,4,3,2,1,0:T(1,128)S(1)}, f32[2,2,2,2,1,512]{5,4,3,2,1,0:T(1,128)S(1)}, u32[]{:S(2)}, u32[]{:S(2)}) collective-permute-start(f32[2,2,2,2,1,512]{5,4,3,2,1,0:T(1,128)S(1)} %pad_maximum_fusion.2.refs_0_), channel_id=1, source_target_pairs={{0,6},{1,7},{2,4},{3,5},{4,2},{5,3},{6,0},{7,1},{8,14},{9,15},{10,... | collective-permute-start | bytes 98312 | tf_op jit(solution)/shard_map/ppermute | solution.py:28
  91.5 24.6 %collective-permute-start.32 = (bf16[1616,128]{1,0:T(8,128)(2,1)S(1)}, bf16[1616,128]{1,0:T(8,128)(2,1)S(1)}, u32[]{:S(2)}, u32[]{:S(2)}) collective-permute-start(bf16[1616,128]{1,0:T(8,128)(2,1)S(1)} %get-tuple-element.48), channel_id=1, source_target_pairs={{0,8},{8,0},{16,24},{24,16},{1,9},{9,1},{17,25},{25,17},{2,10},{10... | collective-permute-start | bytes 1241096 | tf_op jit(solution)/shard_map/ppermute | solution.py:28
  92.8 23.3 %collective-permute-start.33 = (bf16[1616,128]{1,0:T(8,128)(2,1)S(1)}, bf16[1616,128]{1,0:T(8,128)(2,1)S(1)}, u32[]{:S(2)}, u32[]{:S(2)}) collective-permute-start(bf16[1616,128]{1,0:T(8,128)(2,1)S(1)} %get-tuple-element.49), channel_id=1, source_target_pairs={{0,8},{8,0},{16,24},{24,16},{1,9},{9,1},{17,25},{25,17},{2,10},{10... | collective-permute-start | bytes 1241096 | tf_op jit(solution)/shard_map/ppermute | solution.py:28
  96.1 11.0 %collective-permute-start.26 = (bf16[2,128,512]{2,1,0:T(8,128)(2,1)S(1)}, bf16[2,128,512]{2,1,0:T(8,128)(2,1)S(1)}, u32[]{:S(2)}, u32[]{:S(2)}) collective-permute-start(bf16[2,128,512]{2,1,0:T(8,128)(2,1)S(1)} %get-tuple-element.38), channel_id=1, source_target_pairs={{0,2},{1,3},{2,0},{3,1},{4,6},{5,7},{6,4},{7,5},{8,10},{9,11},{10,... | collective-permute-start | bytes 786440 | tf_op jit(solution)/shard_map/ppermute | solution.py:28
  99.9 11.5 %collective-permute-start.27 = (bf16[2,128,512]{2,1,0:T(8,128)(2,1)S(1)}, bf16[2,128,512]{2,1,0:T(8,128)(2,1)S(1)}, u32[]{:S(2)}, u32[]{:S(2)}) collective-permute-start(bf16[2,128,512]{2,1,0:T(8,128)(2,1)S(1)} %get-tuple-element.39), channel_id=1, source_target_pairs={{0,4},{1,5},{2,6},{3,7},{4,0},{5,1},{6,2},{7,3},{8,12},{9,13},{10,... | collective-permute-start | bytes 786440 | tf_op jit(solution)/shard_map/ppermute | solution.py:28
  100.8 10.7 %collective-permute-start.28 = (bf16[2,128,512]{2,1,0:T(8,128)(2,1)S(1)}, bf16[2,128,512]{2,1,0:T(8,128)(2,1)S(1)}, u32[]{:S(2)}, u32[]{:S(2)}) collective-permute-start(bf16[2,128,512]{2,1,0:T(8,128)(2,1)S(1)} %get-tuple-element.40), channel_id=1, source_target_pairs={{0,6},{1,7},{2,4},{3,5},{4,2},{5,3},{6,0},{7,1},{8,14},{9,15},{10,... | collective-permute-start | bytes 786440 | tf_op jit(solution)/shard_map/ppermute | solution.py:28
  111.6 6.5 %collective-permute-start.29 = (bf16[128,256]{1,0:T(8,128)(2,1)S(1)}, bf16[128,256]{1,0:T(8,128)(2,1)S(1)}, u32[]{:S(2)}, u32[]{:S(2)}) collective-permute-start(bf16[128,256]{1,0:T(8,128)(2,1)S(1)} %get-tuple-element.42), channel_id=1, source_target_pairs={{0,8},{8,0},{16,24},{24,16},{1,9},{9,1},{17,25},{25,17},{2,10},{10... | collective-permute-start | bytes 196616 | tf_op jit(solution)/shard_map/ppermute | solution.py:28
  112.2 5.9 %collective-permute-start.30 = (bf16[128,256]{1,0:T(8,128)(2,1)S(1)}, bf16[128,256]{1,0:T(8,128)(2,1)S(1)}, u32[]{:S(2)}, u32[]{:S(2)}) collective-permute-start(bf16[128,256]{1,0:T(8,128)(2,1)S(1)} %get-tuple-element.43), channel_id=1, source_target_pairs={{0,16},{8,24},{16,0},{24,8},{1,17},{9,25},{17,1},{25,9},{2,18},{10... | collective-permute-start | bytes 196616 | tf_op jit(solution)/shard_map/ppermute | solution.py:28
  115.2 6.1 %collective-permute-start.31 = (bf16[128,256]{1,0:T(8,128)(2,1)S(1)}, bf16[128,256]{1,0:T(8,128)(2,1)S(1)}, u32[]{:S(2)}, u32[]{:S(2)}) collective-permute-start(bf16[128,256]{1,0:T(8,128)(2,1)S(1)} %get-tuple-element.44), channel_id=1, source_target_pairs={{0,24},{8,16},{16,8},{24,0},{1,25},{9,17},{17,9},{25,1},{2,26},{10... | collective-permute-start | bytes 196616 | tf_op jit(solution)/shard_map/ppermute | solution.py:28

commit v3 on v2

v3 whole, which is shorter than its diff:
```python
import functools
import math

import jax
import jax.numpy as jnp
from jax import lax
from jax.experimental import pallas as pl
from jax.experimental.pallas import tpu as pltpu
from jax.sharding import PartitionSpec as P

HEAD_DIM = 128
MAX_TILES = 4
KEY_ROWS = 256
TEXT_CHUNKS = 4
DELTA_ROWS = 16
SCALE = 1.0 / math.sqrt(HEAD_DIM)
SCALE_LOG2 = SCALE / math.log(2.0)
BF16 = jnp.bfloat16
F32 = jnp.float32

SMEM = pl.BlockSpec(memory_space=pltpu.SMEM)
VMEM = pl.BlockSpec(memory_space=pltpu.VMEM)
ANY = pl.BlockSpec(memory_space=pl.ANY)
HBM = pl.BlockSpec(memory_space=pltpu.HBM)


def exchange(block, axis, distance):
    count = lax.axis_size(axis)
    return lax.ppermute(block, axis, [(i, i ^ distance) for i in range(count)])


def call(kernel, out_shape, in_specs, scratch, args, out_specs=None, grid=(), megabytes=16, flops=0, moved=0):
    many = isinstance(out_shape, (list, tuple))
    if out_specs is None:
        out_specs = [VMEM] * len(out_shape) if many else VMEM
    return pl.pallas_call(
        kernel,
        out_shape=out_shape,
        in_specs=in_specs,
        out_specs=out_specs,
        grid=grid,
        scratch_shapes=scratch,
        compiler_params=pltpu.CompilerParams(vmem_limit_bytes=megabytes << 20),
        cost_estimate=pl.CostEstimate(flops=flops, bytes_accessed=moved, transcendentals=0),
    )(*args)


def place_of(perm_ref, owner, owners):
    first = jnp.int32(0)
    for index in range(owners):
        first = first + jnp.where(perm_ref[index] == owner, index, 0)
    return first


def sample_at(count_ref, place, samples):
    end, sample, start = jnp.int32(0), jnp.int32(0), jnp.int32(0)
    for index in range(samples):
        end = end + count_ref[index]
        passed = place >= end
        sample = sample + passed.astype(jnp.int32)
        start = jnp.where(passed, end, start)
    return sample, start


def pack_kernel(heads, who, length, *refs):
    inputs, outs, buffers, sem = refs[:3], refs[3:-4], refs[-4:-1], refs[-1]
    copies = [pltpu.make_async_copy(a, b, sem.at[i]) for i, (a, b) in enumerate(zip(inputs, buffers))]
    for copy in copies:
        copy.start()
    for copy in copies:
        copy.wait()
    q_ref, o_ref, g_ref = buffers
    rows = q_ref.shape[0]
    seq = who[0]
    position = seq * rows + lax.broadcasted_iota(jnp.int32, (rows, HEAD_DIM), 0)
    keep = position < length[0]
    for j, out in enumerate(outs):
        for h in range(heads):
            columns = pl.ds(pl.multiple_of(((seq ^ j) * heads + h) * HEAD_DIM, HEAD_DIM), HEAD_DIM)
            grad = jnp.where(keep, g_ref[:, columns].astype(F32), 0.0)
            product = grad * o_ref[:, columns].astype(F32)
            delta = jnp.sum(jnp.transpose(product), axis=0, keepdims=True)
            out[h, :rows] = q_ref[:, columns]
            out[h, rows:2 * rows] = grad.astype(BF16)
            out[h, 2 * rows:] = jnp.broadcast_to(delta, (DELTA_ROWS, HEAD_DIM)).astype(BF16)


def stack_kernel(count, *refs):
    out, sem = refs[-2], refs[-1]
    copies = [pltpu.make_async_copy(refs[i], out.at[i], sem.at[i]) for i in range(count)]
    for copy in copies:
        copy.start()
    for copy in copies:
        copy.wait()


def fetch(pieces, relative, target, sem):
    for index, piece in enumerate(pieces):
        @pl.when(relative == index)
        def _(piece=piece):
            pltpu.make_async_copy(piece, target, sem).start()


def spans_of(rows):
    full = rows // KEY_ROWS
    tail = rows - full * KEY_ROWS
    return [(i * KEY_ROWS, KEY_ROWS, KEY_ROWS) for i in range(full)] + [(full * KEY_ROWS, -(-tail // 16) * 16, tail)]


def dot_nt(a, b):
    return lax.dot_general(a, b, (((1,), (1,)), ((), ())), preferred_element_type=F32)


def dot_nn(a, b):
    return jnp.dot(a, b, preferred_element_type=F32)


def own_tiles(owners, slots, who, counts, perm):
    first = place_of(perm, who[1], owners)
    return [sample_at(counts, first + slot * owners, owners) for slot in range(slots)]


def tiles_kernel(slots, who, own, partner, keys, values, turned):
    for odd in range(2):
        @pl.when((who[0] & 1) == odd)
        def _(odd=odd):
            for slot in range(slots):
                for source, target in (((own, partner)[odd], keys), ((own, partner)[1 - odd], values)):
                    for low, size, used in spans_of(own.shape[1]):
                        if size != used:
                            target[slot, low:] = jnp.zeros((size, HEAD_DIM), BF16)
                        target[slot, low:low + used] = source[slot, low:low + used]
    for slot in range(slots):
        for low, size, _ in spans_of(own.shape[1]):
            turned[slot, :, low:low + size] = jnp.transpose(keys[slot, low:low + size].astype(F32)).astype(BF16)


def weights_kernel(owners, heads, blocks, slots, rows, who, counts, perm, keys, *refs):
    pieces = refs[:owners]
    stats, weights, text_buf, scores_buf, sem = refs[owners:]
    step = pl.program_id(0)
    spans = spans_of(rows)
    chunks = text_buf.shape[1] // blocks
    width = chunks * HEAD_DIM
    tiles = own_tiles(owners, slots, who, counts, perm)

    @pl.when(step == 0)
    def _():
        for slot in range(slots):
            @pl.when(tiles[slot][0] < owners)
            def _(slot=slot):
                fetch(pieces, tiles[slot][0] ^ who[1], text_buf.at[slot], sem.at[slot])

    for slot in range(slots):
        base = slot * heads * blocks

        @pl.when((step == base) & (tiles[slot][0] < owners))
        def _(slot=slot):
            pltpu.make_async_copy(pieces[0], text_buf.at[slot], sem.at[slot]).wait()

        @pl.when((step >= base) & (step < base + heads * blocks) & (tiles[slot][0] < owners))
        def _(slot=slot, base=base):
            head, block = (step - base) // blocks, (step - base) % blocks
            query = text_buf[slot, pl.ds(block * chunks, chunks), head, :HEAD_DIM].reshape(width, HEAD_DIM)
            peak = jnp.full((8, width), -jnp.inf, F32)
            for low, size, used in spans:
                scores = dot_nt(keys[slot, low:low + size], query)
                if size != used:
                    row = lax.broadcasted_iota(jnp.int32, scores.shape, 0)
                    scores = jnp.where(row < used, scores, -jnp.inf)
                scores_buf[low:low + size] = scores
                peak = jnp.maximum(peak, jnp.max(scores.reshape(-1, 8, width), axis=0))
            top = jnp.max(peak, axis=0, keepdims=True) * SCALE_LOG2
            mass = jnp.zeros((8, width), F32)
            for low, size, used in spans:
                part = jnp.exp2(scores_buf[low:low + size] * SCALE_LOG2 - top)
                mass = mass + jnp.sum(part.reshape(-1, 8, width), axis=0)
                weights[0, low:low + size] = part.astype(BF16)
            stats[slot, 0, head, pl.ds(block, 1)] = top
            stats[slot, 1, head, pl.ds(block, 1)] = jnp.sum(mass, axis=0, keepdims=True)


def slopes_kernel(owners, heads, blocks, slots, slot, rows, who, counts, perm, weights, values, keys_turned, *refs):
    pieces = refs[:owners]
    slopes, turned, text_buf, sem = refs[-4:]
    step = pl.program_id(0)
    spans = spans_of(rows)
    chunks = text_buf.shape[0] // blocks
    width = chunks * HEAD_DIM
    sample = own_tiles(owners, slots, who, counts, perm)[slot][0]

    @pl.when((step == 0) & (sample < owners))
    def _():
        fetch(pieces, sample ^ who[1], text_buf, sem)
        pltpu.make_async_copy(pieces[0], text_buf, sem).wait()

    @pl.when(sample < owners)
    def _():
        head, block = step // blocks, step % blocks
        grad = text_buf[pl.ds(block * chunks, chunks), head, HEAD_DIM:2 * HEAD_DIM].reshape(width, HEAD_DIM)
        delta = jnp.concatenate(
            [text_buf[block * chunks + piece, head, 2 * HEAD_DIM:].astype(F32)[:1] for piece in range(chunks)], axis=1
        )
        for low, size, used in spans:
            slope = dot_nt(values[slot, low:low + size], grad)
            slopes[0, low:low + size] = (weights[0, low:low + size].astype(F32) * (slope - delta)).astype(BF16)
        total = dot_nn(keys_turned[slot, :, :slopes.shape[1]], slopes[0])
        turned[head, :, pl.ds(pl.multiple_of(block * width, width), width)] = total.astype(BF16)


def load_stats(stats, stats_buf):
    for index, ref in enumerate(stats):
        stats_buf[2 * index:2 * index + 2] = ref[...]


def peak_and_mass(stats_buf, owners, me, perm, start, tiles, head, block):
    found = []
    for index in range(MAX_TILES):
        live = index < tiles
        place = jnp.where(live, start + index, start)
        other = perm[place & (owners - 1)] ^ me
        slot = lax.div(place, owners)
        top = stats_buf[other, slot, 0, head, pl.ds(block, 1)]
        mass = stats_buf[other, slot, 1, head, pl.ds(block, 1)]
        found.append((jnp.where(live, top, -jnp.inf), jnp.where(live, mass, 0.0)))
    top = functools.reduce(jnp.maximum, [peak for peak, _ in found])
    return top, sum(mass * jnp.exp2(peak - top) for peak, mass in found)


def sums_kernel(owners, heads, blocks, slots, slot, who, counts, perm, *refs):
    weights, slopes, refs = refs[:2], refs[2:4], refs[4:]
    chips = owners // 2
    stats, refs = (refs[:chips], refs[chips:2 * chips]), refs[2 * chips:]
    pieces, refs = (refs[:owners], refs[owners:2 * owners]), refs[2 * owners:]
    keep_out, send_out, stats_buf, text_buf, sums, sem = refs
    step = pl.program_id(0)
    odd, me = who[0] & 1, who[1]
    steps = heads * blocks
    chunks = text_buf.shape[1] // blocks
    width = chunks * HEAD_DIM
    sample, start = own_tiles(owners, slots, who, counts, perm)[slot]
    used = sample < owners

    @pl.when((step == 0) & used)
    def _():
        for half in range(2):
            fetch(pieces[half], sample ^ me, text_buf.at[half], sem.at[half])
            load_stats(stats[half], stats_buf.at[half])
        for half in range(2):
            pltpu.make_async_copy(pieces[half][0], text_buf.at[half], sem.at[half]).wait()

    @pl.when(jnp.logical_not(used))
    def _():
        keep_out[...] = jnp.zeros(keep_out.shape, BF16)
        send_out[...] = jnp.zeros(send_out.shape, BF16)

    for half in range(2):
        @pl.when(used & (step >= half * steps) & (step < (half + 1) * steps))
        def _(half=half):
            inner = step - half * steps
            head, block = inner // blocks, inner % blocks
            tiles = counts[jnp.minimum(sample, owners - 1)]
            top, mass = peak_and_mass(stats_buf.at[half], owners, me, perm, start, tiles, head, block)
            factor = jnp.exp2(stats_buf[half, 0, slot, 0, head, pl.ds(block, 1)] - top) / mass
            factor = jnp.transpose(jnp.broadcast_to(factor, (HEAD_DIM, width)))
            where = pl.ds(block * chunks, chunks)
            query = text_buf[half, where, head, :HEAD_DIM].reshape(width, HEAD_DIM)
            grad = text_buf[half, where, head, HEAD_DIM:2 * HEAD_DIM].reshape(width, HEAD_DIM)
            query = (query.astype(F32) * factor * SCALE).astype(BF16)
            grad = (grad.astype(F32) * factor).astype(BF16)

            def add(which, source, right, fresh):
                for low in range(0, sums.shape[1], 2 * KEY_ROWS):
                    span = slice(low, min(low + 2 * KEY_ROWS, sums.shape[1]))
                    part = dot_nn(source[0, span], right)
                    sums[which, span] = part if fresh else sums[which, span] + part

            for fresh in (True, False):
                if half and fresh:
                    continue

                @pl.when((step == 0) == fresh)
                def _(fresh=fresh):
                    add(0, slopes[half], query, fresh)
                    add(1, weights[half], grad, fresh)

    @pl.when(used & (step == 2 * steps - 1))
    def _():
        keep_out[...] = sums[odd].astype(BF16)
        send_out[...] = sums[1 - odd].astype(BF16)


def route_kernel(owners, heads, blocks, slots, who, counts, perm, *refs):
    parts, refs = (refs[:slots], refs[slots:2 * slots]), refs[2 * slots:]
    stats = refs[:owners // 2]
    outs, stats_buf = refs[owners // 2:-1], refs[-1]
    load_stats(stats, stats_buf)
    me = who[1]
    width = parts[0][0].shape[2] // blocks
    found = []
    for near in range(2):
        first = place_of(perm, me ^ near, owners)
        for slot in range(slots):
            sample, start = sample_at(counts, first + slot * owners, owners)
            found.append((near, slot, sample, start, counts[jnp.minimum(sample, owners - 1)]))

    def one(step, carry):
        head, block = step // blocks, step % blocks
        columns = pl.ds(pl.multiple_of(block * width, width), width)
        scaled = []
        for near, slot, sample, start, tiles in found:
            top, mass = peak_and_mass(stats_buf, owners, me, perm, start, tiles, head, block)
            factor = jnp.exp2(stats_buf[near, slot, 0, head, pl.ds(block, 1)] - top) / mass * SCALE
            scaled.append(parts[near][slot][head, :, columns].astype(F32) * factor)
        for distance, out in enumerate(outs):
            target = me ^ (2 * distance)
            total = sum(jnp.where(item[2] == target, part, 0.0) for item, part in zip(found, scaled))
            out[head, :, columns] = total.astype(BF16)
        return carry

    lax.fori_loop(0, heads * blocks, one, 0)


def gather_kernel(parts, *refs):
    outs = refs[parts:]
    rows = outs[0].shape[0]
    for piece, out in enumerate(outs):
        span = slice(piece * rows, (piece + 1) * rows)
        for head in range(refs[0].shape[0]):
            total = sum(ref[head, :, span].astype(F32) for ref in refs[:parts])
            out[:, head * HEAD_DIM:(head + 1) * HEAD_DIM] = jnp.transpose(total).astype(BF16)


def place_kernel(who, *refs):
    out = refs[-1]
    for distance, ref in enumerate(refs[:-1]):
        width = ref.shape[1]
        start = pl.multiple_of((who[0] ^ distance) * width, width)
        out[:, pl.ds(start, width)] = ref[...]


def merge_kernel(slots, *refs):
    keep, got, out = refs[:slots], refs[slots:-1], refs[-1]
    for low, size, used in spans_of(out.shape[0]):
        row = lax.broadcasted_iota(jnp.int32, (slots * size, slots * size), 0)
        column = lax.broadcasted_iota(jnp.int32, (slots * size, slots * size), 1)
        source = lax.rem(row, slots) * size + lax.div(row, slots)
        order = (source == column).astype(BF16)
        total = [
            (keep[slot][low:low + size].astype(F32) + got[slot][low:low + size].astype(F32)).astype(BF16)
            for slot in range(slots)
        ]
        mixed = dot_nn(order, jnp.concatenate(total, axis=0)).astype(BF16).reshape(size, slots, HEAD_DIM)
        out[low:low + used] = mixed[:used]


def shards(queries, saved_output, grad_out, tile_kv, tile_count, owner_perm, text_len):
    rows_dev, features = queries.shape[1], queries.shape[2]
    groups, owners = lax.axis_size("seq"), lax.axis_size("dp")
    heads = features // HEAD_DIM // groups
    width = heads * HEAD_DIM
    each = groups // 2
    chunks = min(TEXT_CHUNKS, each)
    blocks = each // chunks
    half_rows, block_rows = each * rows_dev, chunks * rows_dev
    steps = heads * blocks
    slots, tile_rows = tile_kv.shape[0], tile_kv.shape[1]
    low, tail_rows, _ = spans_of(tile_rows)[-1]
    padded = low + tail_rows
    who = jnp.stack([lax.axis_index("seq"), lax.axis_index("dp")]).astype(jnp.int32)
    known = (who, tile_count, owner_perm)
    cost = 10**9

    piece_shape = (heads, 2 * rows_dev + DELTA_ROWS, HEAD_DIM)
    packed = call(
        functools.partial(pack_kernel, heads),
        [jax.ShapeDtypeStruct(piece_shape, BF16)] * groups,
        [SMEM, SMEM] + [HBM] * 3,
        [pltpu.VMEM((rows_dev, features), BF16)] * 3 + [pltpu.SemaphoreType.DMA((3,))],
        (who, text_len, queries[0], saved_output[0], grad_out[0]),
        flops=2 * cost,
    )
    pieces = [packed[0]] + [exchange(packed[j], "seq", j) for j in range(1, groups)]
    partner_kv = exchange(tile_kv, "seq", 1)

    text, first = [], ()
    for half in range(2):
        mine = call(
            functools.partial(stack_kernel, each),
            jax.ShapeDtypeStruct((each,) + piece_shape, BF16),
            [ANY] * (each + len(first)),
            [pltpu.SemaphoreType.DMA((each,))],
            (*pieces[half * each:(half + 1) * each], *first),
        )
        near = [mine] + [exchange(mine, "dp", d) for d in range(2, owners, 2)]
        all_near = []
        for piece in near:
            all_near += [piece, exchange(piece, "dp", 1)]
        first = (all_near[1],)
        text.append(all_near)

    tile_shape = jax.ShapeDtypeStruct((slots, padded, HEAD_DIM), BF16)
    turn_shape = jax.ShapeDtypeStruct((slots, HEAD_DIM, -(-padded // HEAD_DIM) * HEAD_DIM), BF16)
    keys, values, keys_turned = call(
        functools.partial(tiles_kernel, slots),
        [tile_shape, tile_shape, turn_shape],
        [SMEM] + [VMEM] * 2,
        [],
        (who, tile_kv, partner_kv),
        flops=cost,
    )

    stats_shape = (slots, 2, heads, blocks, block_rows)
    text_shape = (each,) + piece_shape
    all_stats, weights = [], []
    slopes, routed = [[None, None] for _ in range(slots)], []

    def stack_spec(first_block, count):
        return pl.BlockSpec((1, padded, block_rows), lambda i: (first_block + jnp.clip(i, 0, count - 1), 0, 0))

    for half in range(2):
        stats, weight = call(
            functools.partial(weights_kernel, owners, heads, blocks, slots, tile_rows),
            [
                jax.ShapeDtypeStruct(stats_shape, F32),
                jax.ShapeDtypeStruct((slots * steps, padded, block_rows), BF16),
            ],
            [SMEM] * 3 + [VMEM] + [ANY] * owners,
            [
                pltpu.VMEM((slots,) + text_shape, BF16),
                pltpu.VMEM((padded, block_rows), F32),
                pltpu.SemaphoreType.DMA((slots,)),
            ],
            (*known, keys, *text[half]),
            out_specs=[VMEM, stack_spec(0, slots * steps)],
            grid=(slots * steps,),
            megabytes=32,
            flops=3 * cost,
        )
        weights.append(weight)
        pair = jnp.stack([stats, exchange(stats, "dp", 1)])
        shared = [pair] + [exchange(pair, "dp", d) for d in range(2, owners, 2)]
        all_stats.append(shared)

        parts, others = [], []
        for slot in range(slots):
            order = shared[1:] if slot else shared[:1]
            slope, part = call(
                functools.partial(slopes_kernel, owners, heads, blocks, slots, slot, tile_rows),
                [
                    jax.ShapeDtypeStruct((steps, padded, block_rows), BF16),
                    jax.ShapeDtypeStruct((heads, HEAD_DIM, half_rows), BF16),
                ],
                [SMEM] * 3 + [stack_spec(slot * steps, steps)] + [VMEM] * 2 + [ANY] * (owners + len(order)),
                [pltpu.VMEM(text_shape, BF16), pltpu.SemaphoreType.DMA(())],
                (*known, weight, values, keys_turned, *text[half], *order),
                out_specs=[stack_spec(0, steps), VMEM],
                grid=(steps,),
                megabytes=32,
                flops=2 * cost,
            )
            slopes[slot][half] = slope
            parts.append(part)
            others.append(exchange(part, "dp", 1))

        routed.append(
            call(
                functools.partial(route_kernel, owners, heads, blocks, slots),
                [jax.ShapeDtypeStruct((heads, HEAD_DIM, half_rows), BF16)] * (owners // 2),
                [SMEM] * 3 + [VMEM] * (2 * slots + owners // 2),
                [pltpu.VMEM((owners,) + stats_shape, F32)],
                (*known, *parts, *others, *shared),
                megabytes=32,
                flops=cost,
            )
        )

    kept, got = [], []
    for slot in range(slots):
        weight_specs = [
            pl.BlockSpec(
                (1, padded, block_rows),
                lambda i, half=half: (slot * steps + jnp.clip(i - half * steps, 0, steps - 1), 0, 0),
            )
            for half in range(2)
        ]
        slope_specs = [
            pl.BlockSpec(
                (1, padded, block_rows), lambda i, half=half: (jnp.clip(i - half * steps, 0, steps - 1), 0, 0)
            )
            for half in range(2)
        ]
        keep, send = call(
            functools.partial(sums_kernel, owners, heads, blocks, slots, slot),
            [jax.ShapeDtypeStruct((padded, HEAD_DIM), BF16)] * 2,
            [SMEM] * 3 + weight_specs + slope_specs + [VMEM] * owners + [ANY] * (2 * owners),
            [
                pltpu.VMEM((2, owners) + stats_shape, F32),
                pltpu.VMEM((2,) + text_shape, BF16),
                pltpu.VMEM((2, padded, HEAD_DIM), F32),
                pltpu.SemaphoreType.DMA((2,)),
            ],
            (*known, *weights, *slopes[slot], *all_stats[0], *all_stats[1], *text[0], *text[1]),
            grid=(2 * steps,),
            megabytes=32,
            flops=4 * cost,
        )
        kept.append(keep)
        got.append(exchange(send, "seq", 1))

    back = []
    for half in range(2):
        sums = [routed[half][0]] + [exchange(routed[half][d], "dp", 2 * d) for d in range(1, owners // 2)]
        cut = call(
            functools.partial(gather_kernel, len(sums)),
            [jax.ShapeDtypeStruct((rows_dev, width), BF16)] * each,
            [VMEM] * len(sums),
            [],
            sums,
            megabytes=32,
        )
        for index, piece in enumerate(cut):
            j = half * each + index
            back.append(exchange(piece, "seq", j) if j else piece)
    grad_queries = call(
        place_kernel,
        jax.ShapeDtypeStruct((rows_dev, features), BF16),
        [SMEM] + [VMEM] * groups,
        [],
        (who, *back),
    )
    grad_tiles = call(
        functools.partial(merge_kernel, slots),
        jax.ShapeDtypeStruct((tile_rows, slots, HEAD_DIM), BF16),
        [VMEM] * (2 * slots),
        [],
        (*kept, *got),
        flops=2 * cost,
    )
    return (grad_queries[None], jnp.transpose(grad_tiles, (1, 0, 2)))


def solution(mesh):
    placed = (
        P("dp", "seq", None),
        P("dp", "seq", None),
        P("dp", "seq", None),
        P("dp", None, "seq"),
        P(),
        P(),
        P("dp"),
    )
    return jax.shard_map(
        shards,
        mesh=mesh,
        in_specs=placed,
        out_specs=(P("dp", "seq", None), P("dp", None, "seq")),
        check_vma=False,
    )
```

time: 122 us -> 122 us (level)
  waiting for transfers between devices: 51.2 us -> 44.8 us
  Pallas kernels: 19.8 us -> 24.6 us
  starting transfers between devices: 44.4 us -> 47.4 us
  local copies, waits for them, and re-layouts: 5.51 us -> 3.08 us
    ppermute x34 -> x41, waiting for transfers between devices: 51.2 us -> 44.8 us  [exchange(): return lax.ppermute(block, axis, [(i, i ^ distance) for i in range(count)])]
    pallas_call x10 -> x18, Pallas kernels: 19.8 us -> 24.6 us  [call(): pl.pallas_call(kernel, out_shape=out_shape, in_specs=in_specs, out_specs=...]
    ppermute x34 -> x41, starting transfers between devices: 44.4 us -> 47.4 us  [exchange(): return lax.ppermute(block, axis, [(i, i ^ distance) for i in range(count)])]
    unnamed x11 -> x13, local copies, waits for them, and re-layouts: 5.4 us -> 2.97 us
  transfers between devices with their start and end apart: 34 -> 41, of which waited for: 15 -> 13; matrix products, arithmetic and copies ran while one was open for 1% -> 0% of each run, Pallas kernels for 10% -> 19%
where the time goes in v3:
time: 122 us
  starting transfers between devices  47.4 us (39%)
  waiting for transfers between devices  44.8 us (37%)
  Pallas kernels  24.6 us (20%)
  local copies, waits for them, and re-layouts  3.08 us (3%)
  between operations  1.56 us (1%)
    ppermute x41, starting transfers between devices, exchange(): return lax.ppermute(block, axis, [(i, i ^ distance) for i in range(count)])  47.4 us
    ppermute x41, waiting for transfers between devices, exchange(): return lax.ppermute(block, axis, [(i, i ^ distance) for i in range(count)])  44.8 us
    pallas_call x18, Pallas kernels, call(): pl.pallas_call(kernel, out_shape=out_shape, in_specs=in_specs, out_specs=...  24.6 us
    unnamed x13, local copies, waits for them, and re-layouts  2.97 us
  transfers between devices with their start and end apart: 41, of which 13 were waited for; matrix products, arithmetic and copies ran while one was open for 0% of the time, Pallas kernels for 19%

profile of v3, /device:TPU:0, one launch (start us, length us, event | category | flops | bytes accessed | tf_op | source)
XLA Modules:
  0.0 121.5 jit_solution(12616492062126365400)
XLA Ops:
  0.6 3.1 %collective-permute-start = (bf16[2,1601,128]{2,0,1:T(2,128)(2,1)}, bf16[2,1601,128]{2,0,1:T(2,128)(2,1)S(1)}, u32[]{:S(2)}, u32[]{:S(2)}) collective-permute-start(bf16[2,1601,128]{2,0,1:T(2,128)(2,1)} %param.10), channel_id=1, source_target_pairs={{0,8},{8,0},{16,24},{24,16},{1,9},{9,1},{17,25},{25,17},{2,10},{10... | collective-permute-start | bytes 2459144 | tf_op jit(solution)/shard_map/ppermute | solution.py:29
  5.4 0.9 copy-done.1
  6.4 0.9 copy-done.2
  7.3 1.0 shard_map.87
  8.4 3.0 %collective-permute-start.19 = (bf16[2,272,128]{2,1,0:T(8,128)(2,1)S(1)}, bf16[2,272,128]{2,1,0:T(8,128)(2,1)S(1)}, u32[]{:S(2)}, u32[]{:S(2)}) collective-permute-start(bf16[2,272,128]{2,1,0:T(8,128)(2,1)S(1)} %get-tuple-element.52), channel_id=1, source_target_pairs={{0,16},{8,24},{16,0},{24,8},{1,17},{9,25},{17,1},{25,9},{2,18},{10... | collective-permute-start | bytes 417800 | tf_op jit(solution)/shard_map/ppermute | solution.py:29
  11.4 16.8 %collective-permute-done.1.refs_1_ = bf16[2,272,128]{2,1,0:T(8,128)(2,1)S(1)} collective-permute-done((bf16[2,272,128]{2,1,0:T(8,128)(2,1)S(1)}, bf16[2,272,128]{2,1,0:T(8,128)(2,1)S(1)}, u32[]{:S(2)}, u32[]{:S(2)}) %collective-permute-start.1) | collective-permute-done | bytes 139296 | tf_op jit(solution)/shard_map/ppermute | solution.py:29
  28.5 1.7 %collective-permute-start.3 = (bf16[2,2,272,128]{3,2,1,0:T(8,128)(2,1)S(1)}, bf16[2,2,272,128]{3,2,1,0:T(8,128)(2,1)S(1)}, u32[]{:S(2)}, u32[]{:S(2)}) collective-permute-start(bf16[2,2,272,128]{3,2,1,0:T(8,128)(2,1)S(1)} %shard_map.88.refs_0_.refs_12_), channel_id=1, source_target_pairs={{0,2},{1,3},{2,0},{3,1},{4,6},{5,7},{6,4},{7,5},{8,10},{9,11},{10,... | collective-permute-start | bytes 835592 | tf_op jit(solution)/shard_map/ppermute | solution.py:29
  30.2 1.5 %collective-permute-start.5 = (bf16[2,2,272,128]{3,2,1,0:T(8,128)(2,1)S(1)}, bf16[2,2,272,128]{3,2,1,0:T(8,128)(2,1)S(1)}, u32[]{:S(2)}, u32[]{:S(2)}) collective-permute-start(bf16[2,2,272,128]{3,2,1,0:T(8,128)(2,1)S(1)} %shard_map.88.refs_0_.refs_12_), channel_id=1, source_target_pairs={{0,4},{1,5},{2,6},{3,7},{4,0},{5,1},{6,2},{7,3},{8,12},{9,13},{10,... | collective-permute-start | bytes 835592 | tf_op jit(solution)/shard_map/ppermute | solution.py:29
  32.1 3.8 %collective-permute-start.20 = (bf16[2,272,128]{2,1,0:T(8,128)(2,1)S(1)}, bf16[2,272,128]{2,1,0:T(8,128)(2,1)S(1)}, u32[]{:S(2)}, u32[]{:S(2)}) collective-permute-start(bf16[2,272,128]{2,1,0:T(8,128)(2,1)S(1)} %get-tuple-element.53), channel_id=1, source_target_pairs={{0,24},{8,16},{16,8},{24,0},{1,25},{9,17},{17,9},{25,1},{2,26},{10... | collective-permute-start | bytes 417800 | tf_op jit(solution)/shard_map/ppermute | solution.py:29
  35.8 3.2 %collective-permute-done.20.refs_1_ = bf16[2,272,128]{2,1,0:T(8,128)(2,1)S(1)} collective-permute-done((bf16[2,272,128]{2,1,0:T(8,128)(2,1)S(1)}, bf16[2,272,128]{2,1,0:T(8,128)(2,1)S(1)}, u32[]{:S(2)}, u32[]{:S(2)}) %collective-permute-start.20) | collective-permute-done | bytes 139296 | tf_op jit(solution)/shard_map/ppermute | solution.py:29
  39.5 3.9 %collective-permute-done.5.refs_4_.refs_16_ = bf16[2,2,272,128]{3,2,1,0:T(8,128)(2,1)S(1)} collective-permute-done((bf16[2,2,272,128]{3,2,1,0:T(8,128)(2,1)S(1)}, bf16[2,2,272,128]{3,2,1,0:T(8,128)(2,1)S(1)}, u32[]{:S(2)}, u32[]{:S(2)}) %collective-permute-start.5) | collective-permute-done | bytes 278560 | tf_op jit(solution)/shard_map/ppermute | solution.py:29
  45.3 1.3 %collective-permute-start.24 = (bf16[2,2,272,128]{3,2,1,0:T(8,128)(2,1)S(1)}, bf16[2,2,272,128]{3,2,1,0:T(8,128)(2,1)S(1)}, u32[]{:S(2)}, u32[]{:S(2)}) collective-permute-start(bf16[2,2,272,128]{3,2,1,0:T(8,128)(2,1)S(1)} %shard_map.94.refs_0_.refs_20_), channel_id=1, source_target_pairs={{0,4},{1,5},{2,6},{3,7},{4,0},{5,1},{6,2},{7,3},{8,12},{9,13},{10,... | collective-permute-start | bytes 835592 | tf_op jit(solution)/shard_map/ppermute | solution.py:29
  46.7 1.0 shard_map.86
  47.7 1.5 %collective-permute-start.26 = (bf16[2,2,272,128]{3,2,1,0:T(8,128)(2,1)S(1)}, bf16[2,2,272,128]{3,2,1,0:T(8,128)(2,1)S(1)}, u32[]{:S(2)}, u32[]{:S(2)}) collective-permute-start(bf16[2,2,272,128]{3,2,1,0:T(8,128)(2,1)S(1)} %shard_map.94.refs_0_.refs_20_), channel_id=1, source_target_pairs={{0,6},{1,7},{2,4},{3,5},{4,2},{5,3},{6,0},{7,1},{8,14},{9,15},{10,... | collective-permute-start | bytes 835592 | tf_op jit(solution)/shard_map/ppermute | solution.py:29
  49.2 2.4 %shard_map.89 = (f32[2,2,2,1,256]{4,3,2,1,0:T(1,128)S(1)}, bf16[4,1616,256]{2,1,0:T(8,128)(2,1)S(1)}) custom-call(s32[2]{0:T(128)S(1)} %pad_add_fusion.who, s32[8]{0:T(128)S(1)} %copy-done.3, s32[8]{0:T(128)S(1)} %copy-done.4, bf16[2,1616,128]{2,1,0:T(8,128)(2,1)S(1)} %get-tuple-element.37.keys, bf16[2,2,272,128]{3,2,1,0:T(8,128)(2,1)S(1)} %shard_map.88.refs_0_.refs_12_, ...), custom_call_target="tpu_custom_call" | custom-call | flops 3000000000 | tf_op jit(solution)/shard_map/pallas_call | solution.py:36
  52.4 1.7 %collective-permute-done.22.refs_2_.refs_22_ = bf16[2,2,272,128]{3,2,1,0:T(8,128)(2,1)S(1)} collective-permute-done((bf16[2,2,272,128]{3,2,1,0:T(8,128)(2,1)S(1)}, bf16[2,2,272,128]{3,2,1,0:T(8,128)(2,1)S(1)}, u32[]{:S(2)}, u32[]{:S(2)}) %collective-permute-start.22) | collective-permute-done | bytes 278560 | tf_op jit(solution)/shard_map/ppermute | solution.py:29
  54.1 4.3 %collective-permute-done.24.refs_4_.refs_24_ = bf16[2,2,272,128]{3,2,1,0:T(8,128)(2,1)S(1)} collective-permute-done((bf16[2,2,272,128]{3,2,1,0:T(8,128)(2,1)S(1)}, bf16[2,2,272,128]{3,2,1,0:T(8,128)(2,1)S(1)}, u32[]{:S(2)}, u32[]{:S(2)}) %collective-permute-start.24) | collective-permute-done | bytes 278560 | tf_op jit(solution)/shard_map/ppermute | solution.py:29
  58.4 1.6 %collective-permute-done.26.refs_6_.refs_26_ = bf16[2,2,272,128]{3,2,1,0:T(8,128)(2,1)S(1)} collective-permute-done((bf16[2,2,272,128]{3,2,1,0:T(8,128)(2,1)S(1)}, bf16[2,2,272,128]{3,2,1,0:T(8,128)(2,1)S(1)}, u32[]{:S(2)}, u32[]{:S(2)}) %collective-permute-start.26) | collective-permute-done | bytes 278560 | tf_op jit(solution)/shard_map/ppermute | solution.py:29
  60.1 1.4 %collective-permute-start.10 = (f32[2,2,2,2,1,256]{5,4,3,2,1,0:T(1,128)S(1)}, f32[2,2,2,2,1,256]{5,4,3,2,1,0:T(1,128)S(1)}, u32[]{:S(2)}, u32[]{:S(2)}) collective-permute-start(f32[2,2,2,2,1,256]{5,4,3,2,1,0:T(1,128)S(1)} %pad_maximum_fusion.refs_8_.refs_4_), channel_id=1, source_target_pairs={{0,2},{1,3},{2,0},{3,1},{4,6},{5,7},{6,4},{7,5},{8,10},{9,11},{10,... | collective-permute-start | bytes 49160 | tf_op jit(solution)/shard_map/ppermute | solution.py:29
  61.4 2.1 %shard_map.90 = (bf16[2,1616,256]{2,1,0:T(8,128)(2,1)S(1)}, bf16[2,128,256]{2,1,0:T(8,128)(2,1)S(1)}) custom-call(s32[2]{0:T(128)S(1)} %pad_add_fusion.who, s32[8]{0:T(128)S(1)} %copy-done.3, s32[8]{0:T(128)S(1)} %copy-done.4, bf16[4,1616,256]{2,1,0:T(8,128)(2,1)S(1)} %get-tuple-element.40.weights.refs_0_, ...), custom_call_target="tpu_custom_call" | custom-call | flops 2000000000 | tf_op jit(solution)/shard_map/pallas_call | solution.py:36
  63.6 1.6 %collective-permute-start.11 = (f32[2,2,2,2,1,256]{5,4,3,2,1,0:T(1,128)S(1)}, f32[2,2,2,2,1,256]{5,4,3,2,1,0:T(1,128)S(1)}, u32[]{:S(2)}, u32[]{:S(2)}) collective-permute-start(f32[2,2,2,2,1,256]{5,4,3,2,1,0:T(1,128)S(1)} %pad_maximum_fusion.refs_8_.refs_4_), channel_id=1, source_target_pairs={{0,4},{1,5},{2,6},{3,7},{4,0},{5,1},{6,2},{7,3},{8,12},{9,13},{10,... | collective-permute-start | bytes 49160 | tf_op jit(solution)/shard_map/ppermute | solution.py:29
  65.9 2.4 %shard_map.95 = (f32[2,2,2,1,256]{4,3,2,1,0:T(1,128)S(1)}, bf16[4,1616,256]{2,1,0:T(8,128)(2,1)S(1)}) custom-call(s32[2]{0:T(128)S(1)} %pad_add_fusion.who, s32[8]{0:T(128)S(1)} %copy-done.3, s32[8]{0:T(128)S(1)} %copy-done.4, bf16[2,1616,128]{2,1,0:T(8,128)(2,1)S(1)} %get-tuple-element.37.keys, bf16[2,2,272,128]{3,2,1,0:T(8,128)(2,1)S(1)} %shard_map.94.refs_0_.refs_20_, ...), custom_call_target="tpu_custom_call" | custom-call | flops 3000000000 | tf_op jit(solution)/shard_map/pallas_call | solution.py:36
  68.2 2.0 %collective-permute-start.28 = (f32[2,2,2,1,256]{4,3,2,1,0:T(1,128)S(1)}, f32[2,2,2,1,256]{4,3,2,1,0:T(1,128)S(1)}, u32[]{:S(2)}, u32[]{:S(2)}) collective-permute-start(f32[2,2,2,1,256]{4,3,2,1,0:T(1,128)S(1)} %get-tuple-element.55), channel_id=1, source_target_pairs={{0,1},{1,0},{2,3},{3,2},{4,5},{5,4},{6,7},{7,6},{8,9},{9,8},{10,11... | collective-permute-start | bytes 24584 | tf_op jit(solution)/shard_map/ppermute | solution.py:29
  70.9 1.6 %collective-permute-start.14 = (bf16[2,128,256]{2,1,0:T(8,128)(2,1)S(1)}, bf16[2,128,256]{2,1,0:T(8,128)(2,1)S(1)}, u32[]{:S(2)}, u32[]{:S(2)}) collective-permute-start(bf16[2,128,256]{2,1,0:T(8,128)(2,1)S(1)} %get-tuple-element.45.refs_1_), channel_id=1, source_target_pairs={{0,1},{1,0},{2,3},{3,2},{4,5},{5,4},{6,7},{7,6},{8,9},{9,8},{10,11... | collective-permute-start | bytes 393224 | tf_op jit(solution)/shard_map/ppermute | solution.py:29
  72.5 1.4 %collective-permute-start.29 = (f32[2,2,2,2,1,256]{5,4,3,2,1,0:T(1,128)S(1)}, f32[2,2,2,2,1,256]{5,4,3,2,1,0:T(1,128)S(1)}, u32[]{:S(2)}, u32[]{:S(2)}) collective-permute-start(f32[2,2,2,2,1,256]{5,4,3,2,1,0:T(1,128)S(1)} %pad_maximum_fusion.1.refs_8_.refs_4_), channel_id=1, source_target_pairs={{0,2},{1,3},{2,0},{3,1},{4,6},{5,7},{6,4},{7,5},{8,10},{9,11},{10,... | collective-permute-start | bytes 49160 | tf_op jit(solution)/shard_map/ppermute | solution.py:29
  73.9 1.1 collective-permute-start.30
  75.0 1.1 collective-permute-start.31
  76.1 2.2 %shard_map.96 = (bf16[2,1616,256]{2,1,0:T(8,128)(2,1)S(1)}, bf16[2,128,256]{2,1,0:T(8,128)(2,1)S(1)}) custom-call(s32[2]{0:T(128)S(1)} %pad_add_fusion.who, s32[8]{0:T(128)S(1)} %copy-done.3, s32[8]{0:T(128)S(1)} %copy-done.4, bf16[4,1616,256]{2,1,0:T(8,128)(2,1)S(1)} %get-tuple-element.54.weights.refs_1_, ...), custom_call_target="tpu_custom_call" | custom-call | flops 2000000000 | tf_op jit(solution)/shard_map/pallas_call | solution.py:36
  78.4 1.3 %collective-permute-done.31.refs_10_.refs_7_.refs_11_ = f32[2,2,2,2,1,256]{5,4,3,2,1,0:T(1,128)S(1)} collective-permute-done((f32[2,2,2,2,1,256]{5,4,3,2,1,0:T(1,128)S(1)}, f32[2,2,2,2,1,256]{5,4,3,2,1,0:T(1,128)S(1)}, u32[]{:S(2)}, u32[]{:S(2)}) %collective-permute-start.31) | collective-permute-done | bytes 16416 | tf_op jit(solution)/shard_map/ppermute | solution.py:29
  80.3 1.4 %shard_map.102 = (bf16[1616,128]{1,0:T(8,128)(2,1)S(1)}, bf16[1616,128]{1,0:T(8,128)(2,1)S(1)}) custom-call(s32[2]{0:T(128)S(1)} %pad_add_fusion.who, s32[8]{0:T(128)S(1)} %copy-done.3, s32[8]{0:T(128)S(1)} %copy-done.4, bf16[4,1616,256]{2,1,0:T(8,128)(2,1)S(1)} %get-tuple-element.40.weights.refs_0_, ...), custom_call_target="tpu_custom_call" | custom-call | flops 4000000000 | tf_op jit(solution)/shard_map/pallas_call | solution.py:36
  81.8 3.6 %collective-permute-start.33 = (bf16[2,128,256]{2,1,0:T(8,128)(2,1)S(1)}, bf16[2,128,256]{2,1,0:T(8,128)(2,1)S(1)}, u32[]{:S(2)}, u32[]{:S(2)}) collective-permute-start(bf16[2,128,256]{2,1,0:T(8,128)(2,1)S(1)} %get-tuple-element.57.refs_1_), channel_id=1, source_target_pairs={{0,1},{1,0},{2,3},{3,2},{4,5},{5,4},{6,7},{7,6},{8,9},{9,8},{10,11... | collective-permute-start | bytes 393224 | tf_op jit(solution)/shard_map/ppermute | solution.py:29
  85.5 4.2 %shard_map.101 = (bf16[1616,128]{1,0:T(8,128)(2,1)S(1)}, bf16[1616,128]{1,0:T(8,128)(2,1)S(1)}) custom-call(s32[2]{0:T(128)S(1)} %pad_add_fusion.who, s32[8]{0:T(128)S(1)} %copy-done.3, s32[8]{0:T(128)S(1)} %copy-done.4, bf16[4,1616,256]{2,1,0:T(8,128)(2,1)S(1)} %get-tuple-element.40.weights.refs_0_, ...), custom_call_target="tpu_custom_call" | custom-call | flops 4000000000 | tf_op jit(solution)/shard_map/pallas_call | solution.py:36
  89.7 1.7 %collective-permute-start.39 = (bf16[1616,128]{1,0:T(8,128)(2,1)S(1)}, bf16[1616,128]{1,0:T(8,128)(2,1)S(1)}, u32[]{:S(2)}, u32[]{:S(2)}) collective-permute-start(bf16[1616,128]{1,0:T(8,128)(2,1)S(1)} %get-tuple-element.70), channel_id=1, source_target_pairs={{0,8},{8,0},{16,24},{24,16},{1,9},{9,1},{17,25},{25,17},{2,10},{10... | collective-permute-start | bytes 1241096 | tf_op jit(solution)/shard_map/ppermute | solution.py:29
  91.4 1.1 shard_map.92
  92.6 1.4 %collective-permute-start.15 = (bf16[2,128,256]{2,1,0:T(8,128)(2,1)S(1)}, bf16[2,128,256]{2,1,0:T(8,128)(2,1)S(1)}, u32[]{:S(2)}, u32[]{:S(2)}) collective-permute-start(bf16[2,128,256]{2,1,0:T(8,128)(2,1)S(1)} %get-tuple-element.47), channel_id=1, source_target_pairs={{0,2},{1,3},{2,0},{3,1},{4,6},{5,7},{6,4},{7,5},{8,10},{9,11},{10,... | collective-permute-start | bytes 393224 | tf_op jit(solution)/shard_map/ppermute | solution.py:29
  93.9 1.4 %collective-permute-start.16 = (bf16[2,128,256]{2,1,0:T(8,128)(2,1)S(1)}, bf16[2,128,256]{2,1,0:T(8,128)(2,1)S(1)}, u32[]{:S(2)}, u32[]{:S(2)}) collective-permute-start(bf16[2,128,256]{2,1,0:T(8,128)(2,1)S(1)} %get-tuple-element.48), channel_id=1, source_target_pairs={{0,4},{1,5},{2,6},{3,7},{4,0},{5,1},{6,2},{7,3},{8,12},{9,13},{10,... | collective-permute-start | bytes 393224 | tf_op jit(solution)/shard_map/ppermute | solution.py:29
  96.2 1.1 shard_map.98
  98.1 1.3 %collective-permute-start.34 = (bf16[2,128,256]{2,1,0:T(8,128)(2,1)S(1)}, bf16[2,128,256]{2,1,0:T(8,128)(2,1)S(1)}, u32[]{:S(2)}, u32[]{:S(2)}) collective-permute-start(bf16[2,128,256]{2,1,0:T(8,128)(2,1)S(1)} %get-tuple-element.59), channel_id=1, source_target_pairs={{0,2},{1,3},{2,0},{3,1},{4,6},{5,7},{6,4},{7,5},{8,10},{9,11},{10,... | collective-permute-start | bytes 393224 | tf_op jit(solution)/shard_map/ppermute | solution.py:29
  99.4 1.7 %collective-permute-done.16.refs_2_ = bf16[2,128,256]{2,1,0:T(8,128)(2,1)S(1)} collective-permute-done((bf16[2,128,256]{2,1,0:T(8,128)(2,1)S(1)}, bf16[2,128,256]{2,1,0:T(8,128)(2,1)S(1)}, u32[]{:S(2)}, u32[]{:S(2)}) %collective-permute-start.16) | collective-permute-done | bytes 131104 | tf_op jit(solution)/shard_map/ppermute | solution.py:29
  101.1 2.4 %collective-permute-start.35 = (bf16[2,128,256]{2,1,0:T(8,128)(2,1)S(1)}, bf16[2,128,256]{2,1,0:T(8,128)(2,1)S(1)}, u32[]{:S(2)}, u32[]{:S(2)}) collective-permute-start(bf16[2,128,256]{2,1,0:T(8,128)(2,1)S(1)} %get-tuple-element.60), channel_id=1, source_target_pairs={{0,4},{1,5},{2,6},{3,7},{4,0},{5,1},{6,2},{7,3},{8,12},{9,13},{10,... | collective-permute-start | bytes 393224 | tf_op jit(solution)/shard_map/ppermute | solution.py:29
  104.8 3.1 %collective-permute-done.35.refs_2_ = bf16[2,128,256]{2,1,0:T(8,128)(2,1)S(1)} collective-permute-done((bf16[2,128,256]{2,1,0:T(8,128)(2,1)S(1)}, bf16[2,128,256]{2,1,0:T(8,128)(2,1)S(1)}, u32[]{:S(2)}, u32[]{:S(2)}) %collective-permute-start.35) | collective-permute-done | bytes 131104 | tf_op jit(solution)/shard_map/ppermute | solution.py:29
  107.9 1.5 %collective-permute-done.36.refs_3_ = bf16[2,128,256]{2,1,0:T(8,128)(2,1)S(1)} collective-permute-done((bf16[2,128,256]{2,1,0:T(8,128)(2,1)S(1)}, bf16[2,128,256]{2,1,0:T(8,128)(2,1)S(1)}, u32[]{:S(2)}, u32[]{:S(2)}) %collective-permute-start.36) | collective-permute-done | bytes 131104 | tf_op jit(solution)/shard_map/ppermute | solution.py:29
  109.6 2.5 %collective-permute-start.37 = (bf16[128,256]{1,0:T(8,128)(2,1)S(1)}, bf16[128,256]{1,0:T(8,128)(2,1)S(1)}, u32[]{:S(2)}, u32[]{:S(2)}) collective-permute-start(bf16[128,256]{1,0:T(8,128)(2,1)S(1)} %get-tuple-element.62), channel_id=1, source_target_pairs={{0,16},{8,24},{16,0},{24,8},{1,17},{9,25},{17,1},{25,9},{2,18},{10... | collective-permute-start | bytes 196616 | tf_op jit(solution)/shard_map/ppermute | solution.py:29
  112.1 1.2 %collective-permute-start.38 = (bf16[128,256]{1,0:T(8,128)(2,1)S(1)}, bf16[128,256]{1,0:T(8,128)(2,1)S(1)}, u32[]{:S(2)}, u32[]{:S(2)}) collective-permute-start(bf16[128,256]{1,0:T(8,128)(2,1)S(1)} %get-tuple-element.63), channel_id=1, source_target_pairs={{0,24},{8,16},{16,8},{24,0},{1,25},{9,17},{17,9},{25,1},{2,26},{10... | collective-permute-start | bytes 196616 | tf_op jit(solution)/shard_map/ppermute | solution.py:29
  113.3 2.4 %collective-permute-done.37.refs_2_ = bf16[128,256]{1,0:T(8,128)(2,1)S(1)} collective-permute-done((bf16[128,256]{1,0:T(8,128)(2,1)S(1)}, bf16[128,256]{1,0:T(8,128)(2,1)S(1)}, u32[]{:S(2)}, u32[]{:S(2)}) %collective-permute-start.37) | collective-permute-done | bytes 65568 | tf_op jit(solution)/shard_map/ppermute | solution.py:29
  115.7 2.5 %collective-permute-done.38.refs_3_ = bf16[128,256]{1,0:T(8,128)(2,1)S(1)} collective-permute-done((bf16[128,256]{1,0:T(8,128)(2,1)S(1)}, bf16[128,256]{1,0:T(8,128)(2,1)S(1)}, u32[]{:S(2)}, u32[]{:S(2)}) %collective-permute-start.38) | collective-permute-done | bytes 65568 | tf_op jit(solution)/shard_map/ppermute | solution.py:29
  118.2 1.3 %shard_map.100 = bf16[128,1024]{1,0:T(8,128)(2,1)} custom-call(s32[2]{0:T(128)S(1)} %pad_add_fusion.who, bf16[128,256]{1,0:T(8,128)(2,1)S(1)} %get-tuple-element.50.refs_0_, bf16[128,256]{1,0:T(8,128)(2,1)S(1)} %collective-permute-done.18.refs_1_, bf16[128,256]{1,0:T(8,128)(2,1)S(1)} %collective-permute-done.37.refs_2_, ...), custom_call_target="tpu_custom_call" | custom-call | tf_op jit(solution)/shard_map/pallas_call | solution.py:36
  119.5 2.0 %shard_map.103 = bf16[1601,2,128]{2,1,0:T(2,128)(2,1)} custom-call(bf16[1616,128]{1,0:T(8,128)(2,1)S(1)} %get-tuple-element.66.refs_0_, bf16[1616,128]{1,0:T(8,128)(2,1)S(1)} %get-tuple-element.69.refs_1_, bf16[1616,128]{1,0:T(8,128)(2,1)S(1)} %collective-permute-done.39.refs_2_, bf16[1616,128]{1,0:T(8,128)(2,1)S(1)} %collective-permute-done.40.refs_3_), custom_call_target="tpu_custom_call" | custom-call | flops 2000000000 | tf_op jit(solution)/shard_map/pallas_call | solution.py:36
  (69 shorter events, 10.2 us)
Async XLA Ops:
  0.6 44.6 %collective-permute-start = (bf16[2,1601,128]{2,0,1:T(2,128)(2,1)}, bf16[2,1601,128]{2,0,1:T(2,128)(2,1)S(1)}, u32[]{:S(2)}, u32[]{:S(2)}) collective-permute-start(bf16[2,1601,128]{2,0,1:T(2,128)(2,1)} %param.10), channel_id=1, source_target_pairs={{0,8},{8,0},{16,24},{24,16},{1,9},{9,1},{17,25},{25,17},{2,10},{10... | collective-permute-start | bytes 2459144 | tf_op jit(solution)/shard_map/ppermute | solution.py:29
  4.4 1.0 copy-start
  5.4 0.9 copy-start.1
  6.3 0.9 copy-start.2
  7.3 36.7 %copy-start.5 = (bf16[2,1601,128]{2,0,1:T(2,128)(2,1)S(1)}, bf16[2,1601,128]{2,0,1:T(2,128)(2,1)}, u32[]{:S(2)}) copy-start(bf16[2,1601,128]{2,0,1:T(2,128)(2,1)} %param.10) | copy-start | bytes 2459140
  8.3 19.9 %collective-permute-start.1 = (bf16[2,272,128]{2,1,0:T(8,128)(2,1)S(1)}, bf16[2,272,128]{2,1,0:T(8,128)(2,1)S(1)}, u32[]{:S(2)}, u32[]{:S(2)}) collective-permute-start(bf16[2,272,128]{2,1,0:T(8,128)(2,1)S(1)} %get-tuple-element.39), channel_id=1, source_target_pairs={{0,8},{8,0},{16,24},{24,16},{1,9},{9,1},{17,25},{25,17},{2,10},{10... | collective-permute-start | bytes 417800 | tf_op jit(solution)/shard_map/ppermute | solution.py:29
  8.4 23.7 %collective-permute-start.19 = (bf16[2,272,128]{2,1,0:T(8,128)(2,1)S(1)}, bf16[2,272,128]{2,1,0:T(8,128)(2,1)S(1)}, u32[]{:S(2)}, u32[]{:S(2)}) collective-permute-start(bf16[2,272,128]{2,1,0:T(8,128)(2,1)S(1)} %get-tuple-element.52), channel_id=1, source_target_pairs={{0,16},{8,24},{16,0},{24,8},{1,17},{9,25},{17,1},{25,9},{2,18},{10... | collective-permute-start | bytes 417800 | tf_op jit(solution)/shard_map/ppermute | solution.py:29
  28.5 10.5 %collective-permute-start.3 = (bf16[2,2,272,128]{3,2,1,0:T(8,128)(2,1)S(1)}, bf16[2,2,272,128]{3,2,1,0:T(8,128)(2,1)S(1)}, u32[]{:S(2)}, u32[]{:S(2)}) collective-permute-start(bf16[2,2,272,128]{3,2,1,0:T(8,128)(2,1)S(1)} %shard_map.88.refs_0_.refs_12_), channel_id=1, source_target_pairs={{0,2},{1,3},{2,0},{3,1},{4,6},{5,7},{6,4},{7,5},{8,10},{9,11},{10,... | collective-permute-start | bytes 835592 | tf_op jit(solution)/shard_map/ppermute | solution.py:29
  30.2 13.2 %collective-permute-start.5 = (bf16[2,2,272,128]{3,2,1,0:T(8,128)(2,1)S(1)}, bf16[2,2,272,128]{3,2,1,0:T(8,128)(2,1)S(1)}, u32[]{:S(2)}, u32[]{:S(2)}) collective-permute-start(bf16[2,2,272,128]{3,2,1,0:T(8,128)(2,1)S(1)} %shard_map.88.refs_0_.refs_12_), channel_id=1, source_target_pairs={{0,4},{1,5},{2,6},{3,7},{4,0},{5,1},{6,2},{7,3},{8,12},{9,13},{10,... | collective-permute-start | bytes 835592 | tf_op jit(solution)/shard_map/ppermute | solution.py:29
  31.7 11.7 %collective-permute-start.7 = (bf16[2,2,272,128]{3,2,1,0:T(8,128)(2,1)S(1)}, bf16[2,2,272,128]{3,2,1,0:T(8,128)(2,1)S(1)}, u32[]{:S(2)}, u32[]{:S(2)}) collective-permute-start(bf16[2,2,272,128]{3,2,1,0:T(8,128)(2,1)S(1)} %shard_map.88.refs_0_.refs_12_), channel_id=1, source_target_pairs={{0,6},{1,7},{2,4},{3,5},{4,2},{5,3},{6,0},{7,1},{8,14},{9,15},{10,... | collective-permute-start | bytes 835592 | tf_op jit(solution)/shard_map/ppermute | solution.py:29
  32.1 7.0 %collective-permute-start.20 = (bf16[2,272,128]{2,1,0:T(8,128)(2,1)S(1)}, bf16[2,272,128]{2,1,0:T(8,128)(2,1)S(1)}, u32[]{:S(2)}, u32[]{:S(2)}) collective-permute-start(bf16[2,272,128]{2,1,0:T(8,128)(2,1)S(1)} %get-tuple-element.53), channel_id=1, source_target_pairs={{0,24},{8,16},{16,8},{24,0},{1,25},{9,17},{17,9},{25,1},{2,26},{10... | collective-permute-start | bytes 417800 | tf_op jit(solution)/shard_map/ppermute | solution.py:29
  39.0 5.0 %collective-permute-start.2 = (bf16[2,2,272,128]{3,2,1,0:T(8,128)(2,1)S(1)}, bf16[2,2,272,128]{3,2,1,0:T(8,128)(2,1)S(1)}, u32[]{:S(2)}, u32[]{:S(2)}) collective-permute-start(bf16[2,2,272,128]{3,2,1,0:T(8,128)(2,1)S(1)} %shard_map.88.refs_0_.refs_12_), channel_id=1, source_target_pairs={{0,1},{1,0},{2,3},{3,2},{4,5},{5,4},{6,7},{7,6},{8,9},{9,8},{10,11... | collective-permute-start | bytes 835592 | tf_op jit(solution)/shard_map/ppermute | solution.py:29
  39.0 8.7 %collective-permute-start.4 = (bf16[2,2,272,128]{3,2,1,0:T(8,128)(2,1)S(1)}, bf16[2,2,272,128]{3,2,1,0:T(8,128)(2,1)S(1)}, u32[]{:S(2)}, u32[]{:S(2)}) collective-permute-start(bf16[2,2,272,128]{3,2,1,0:T(8,128)(2,1)S(1)} %collective-permute-done.3.refs_2_.refs_14_), channel_id=1, source_target_pairs={{0,1},{1,0},{2,3},{3,2},{4,5},{5,4},{6,7},{7,6},{8,9},{9,8},{10,11... | collective-permute-start | bytes 835592 | tf_op jit(solution)/shard_map/ppermute | solution.py:29
  43.4 5.8 %collective-permute-start.6 = (bf16[2,2,272,128]{3,2,1,0:T(8,128)(2,1)S(1)}, bf16[2,2,272,128]{3,2,1,0:T(8,128)(2,1)S(1)}, u32[]{:S(2)}, u32[]{:S(2)}) collective-permute-start(bf16[2,2,272,128]{3,2,1,0:T(8,128)(2,1)S(1)} %collective-permute-done.5.refs_4_.refs_16_), channel_id=1, source_target_pairs={{0,1},{1,0},{2,3},{3,2},{4,5},{5,4},{6,7},{7,6},{8,9},{9,8},{10,11... | collective-permute-start | bytes 835592 | tf_op jit(solution)/shard_map/ppermute | solution.py:29
  43.5 5.8 %collective-permute-start.8 = (bf16[2,2,272,128]{3,2,1,0:T(8,128)(2,1)S(1)}, bf16[2,2,272,128]{3,2,1,0:T(8,128)(2,1)S(1)}, u32[]{:S(2)}, u32[]{:S(2)}) collective-permute-start(bf16[2,2,272,128]{3,2,1,0:T(8,128)(2,1)S(1)} %collective-permute-done.7.refs_6_.refs_18_), channel_id=1, source_target_pairs={{0,1},{1,0},{2,3},{3,2},{4,5},{5,4},{6,7},{7,6},{8,9},{9,8},{10,11... | collective-permute-start | bytes 835592 | tf_op jit(solution)/shard_map/ppermute | solution.py:29
  44.5 9.6 %collective-permute-start.22 = (bf16[2,2,272,128]{3,2,1,0:T(8,128)(2,1)S(1)}, bf16[2,2,272,128]{3,2,1,0:T(8,128)(2,1)S(1)}, u32[]{:S(2)}, u32[]{:S(2)}) collective-permute-start(bf16[2,2,272,128]{3,2,1,0:T(8,128)(2,1)S(1)} %shard_map.94.refs_0_.refs_20_), channel_id=1, source_target_pairs={{0,2},{1,3},{2,0},{3,1},{4,6},{5,7},{6,4},{7,5},{8,10},{9,11},{10,... | collective-permute-start | bytes 835592 | tf_op jit(solution)/shard_map/ppermute | solution.py:29
  45.3 13.1 %collective-permute-start.24 = (bf16[2,2,272,128]{3,2,1,0:T(8,128)(2,1)S(1)}, bf16[2,2,272,128]{3,2,1,0:T(8,128)(2,1)S(1)}, u32[]{:S(2)}, u32[]{:S(2)}) collective-permute-start(bf16[2,2,272,128]{3,2,1,0:T(8,128)(2,1)S(1)} %shard_map.94.refs_0_.refs_20_), channel_id=1, source_target_pairs={{0,4},{1,5},{2,6},{3,7},{4,0},{5,1},{6,2},{7,3},{8,12},{9,13},{10,... | collective-permute-start | bytes 835592 | tf_op jit(solution)/shard_map/ppermute | solution.py:29
  46.7 2.5 %copy-start.3 = (s32[8]{0:T(128)S(1)}, s32[8]{0:T(128)}, u32[]{:S(2)}) copy-start(s32[8]{0:T(128)} %counts.19) | copy-start | bytes 100
  46.7 2.5 %copy-start.4 = (s32[8]{0:T(128)S(1)}, s32[8]{0:T(128)}, u32[]{:S(2)}) copy-start(s32[8]{0:T(128)} %perm.19) | copy-start | bytes 100
  47.7 12.3 %collective-permute-start.26 = (bf16[2,2,272,128]{3,2,1,0:T(8,128)(2,1)S(1)}, bf16[2,2,272,128]{3,2,1,0:T(8,128)(2,1)S(1)}, u32[]{:S(2)}, u32[]{:S(2)}) collective-permute-start(bf16[2,2,272,128]{3,2,1,0:T(8,128)(2,1)S(1)} %shard_map.94.refs_0_.refs_20_), channel_id=1, source_target_pairs={{0,6},{1,7},{2,4},{3,5},{4,2},{5,3},{6,0},{7,1},{8,14},{9,15},{10,... | collective-permute-start | bytes 835592 | tf_op jit(solution)/shard_map/ppermute | solution.py:29
  51.6 8.4 %collective-permute-start.9 = (f32[2,2,2,1,256]{4,3,2,1,0:T(1,128)S(1)}, f32[2,2,2,1,256]{4,3,2,1,0:T(1,128)S(1)}, u32[]{:S(2)}, u32[]{:S(2)}) collective-permute-start(f32[2,2,2,1,256]{4,3,2,1,0:T(1,128)S(1)} %get-tuple-element.43), channel_id=1, source_target_pairs={{0,1},{1,0},{2,3},{3,2},{4,5},{5,4},{6,7},{7,6},{8,9},{9,8},{10,11... | collective-permute-start | bytes 24584 | tf_op jit(solution)/shard_map/ppermute | solution.py:29
  52.3 11.3 %collective-permute-start.21 = (bf16[2,2,272,128]{3,2,1,0:T(8,128)(2,1)S(1)}, bf16[2,2,272,128]{3,2,1,0:T(8,128)(2,1)S(1)}, u32[]{:S(2)}, u32[]{:S(2)}) collective-permute-start(bf16[2,2,272,128]{3,2,1,0:T(8,128)(2,1)S(1)} %shard_map.94.refs_0_.refs_20_), channel_id=1, source_target_pairs={{0,1},{1,0},{2,3},{3,2},{4,5},{5,4},{6,7},{7,6},{8,9},{9,8},{10,11... | collective-permute-start | bytes 835592 | tf_op jit(solution)/shard_map/ppermute | solution.py:29
  54.1 11.1 %collective-permute-start.23 = (bf16[2,2,272,128]{3,2,1,0:T(8,128)(2,1)S(1)}, bf16[2,2,272,128]{3,2,1,0:T(8,128)(2,1)S(1)}, u32[]{:S(2)}, u32[]{:S(2)}) collective-permute-start(bf16[2,2,272,128]{3,2,1,0:T(8,128)(2,1)S(1)} %collective-permute-done.22.refs_2_.refs_22_), channel_id=1, source_target_pairs={{0,1},{1,0},{2,3},{3,2},{4,5},{5,4},{6,7},{7,6},{8,9},{9,8},{10,11... | collective-permute-start | bytes 835592 | tf_op jit(solution)/shard_map/ppermute | solution.py:29
  58.4 7.4 %collective-permute-start.25 = (bf16[2,2,272,128]{3,2,1,0:T(8,128)(2,1)S(1)}, bf16[2,2,272,128]{3,2,1,0:T(8,128)(2,1)S(1)}, u32[]{:S(2)}, u32[]{:S(2)}) collective-permute-start(bf16[2,2,272,128]{3,2,1,0:T(8,128)(2,1)S(1)} %collective-permute-done.24.refs_4_.refs_24_), channel_id=1, source_target_pairs={{0,1},{1,0},{2,3},{3,2},{4,5},{5,4},{6,7},{7,6},{8,9},{9,8},{10,11... | collective-permute-start | bytes 835592 | tf_op jit(solution)/shard_map/ppermute | solution.py:29
  60.0 5.8 %collective-permute-start.27 = (bf16[2,2,272,128]{3,2,1,0:T(8,128)(2,1)S(1)}, bf16[2,2,272,128]{3,2,1,0:T(8,128)(2,1)S(1)}, u32[]{:S(2)}, u32[]{:S(2)}) collective-permute-start(bf16[2,2,272,128]{3,2,1,0:T(8,128)(2,1)S(1)} %collective-permute-done.26.refs_6_.refs_26_), channel_id=1, source_target_pairs={{0,1},{1,0},{2,3},{3,2},{4,5},{5,4},{6,7},{7,6},{8,9},{9,8},{10,11... | collective-permute-start | bytes 835592 | tf_op jit(solution)/shard_map/ppermute | solution.py:29
  60.1 10.2 %collective-permute-start.10 = (f32[2,2,2,2,1,256]{5,4,3,2,1,0:T(1,128)S(1)}, f32[2,2,2,2,1,256]{5,4,3,2,1,0:T(1,128)S(1)}, u32[]{:S(2)}, u32[]{:S(2)}) collective-permute-start(f32[2,2,2,2,1,256]{5,4,3,2,1,0:T(1,128)S(1)} %pad_maximum_fusion.refs_8_.refs_4_), channel_id=1, source_target_pairs={{0,2},{1,3},{2,0},{3,1},{4,6},{5,7},{6,4},{7,5},{8,10},{9,11},{10,... | collective-permute-start | bytes 49160 | tf_op jit(solution)/shard_map/ppermute | solution.py:29
  63.6 6.6 %collective-permute-start.11 = (f32[2,2,2,2,1,256]{5,4,3,2,1,0:T(1,128)S(1)}, f32[2,2,2,2,1,256]{5,4,3,2,1,0:T(1,128)S(1)}, u32[]{:S(2)}, u32[]{:S(2)}) collective-permute-start(f32[2,2,2,2,1,256]{5,4,3,2,1,0:T(1,128)S(1)} %pad_maximum_fusion.refs_8_.refs_4_), channel_id=1, source_target_pairs={{0,4},{1,5},{2,6},{3,7},{4,0},{5,1},{6,2},{7,3},{8,12},{9,13},{10,... | collective-permute-start | bytes 49160 | tf_op jit(solution)/shard_map/ppermute | solution.py:29
  65.2 5.0 %collective-permute-start.12 = (f32[2,2,2,2,1,256]{5,4,3,2,1,0:T(1,128)S(1)}, f32[2,2,2,2,1,256]{5,4,3,2,1,0:T(1,128)S(1)}, u32[]{:S(2)}, u32[]{:S(2)}) collective-permute-start(f32[2,2,2,2,1,256]{5,4,3,2,1,0:T(1,128)S(1)} %pad_maximum_fusion.refs_8_.refs_4_), channel_id=1, source_target_pairs={{0,6},{1,7},{2,4},{3,5},{4,2},{5,3},{6,0},{7,1},{8,14},{9,15},{10,... | collective-permute-start | bytes 49160 | tf_op jit(solution)/shard_map/ppermute | solution.py:29
  65.9 23.8 %collective-permute-start.13 = (bf16[2,128,256]{2,1,0:T(8,128)(2,1)S(1)}, bf16[2,128,256]{2,1,0:T(8,128)(2,1)S(1)}, u32[]{:S(2)}, u32[]{:S(2)}) collective-permute-start(bf16[2,128,256]{2,1,0:T(8,128)(2,1)S(1)} %get-tuple-element.44.refs_0_), channel_id=1, source_target_pairs={{0,1},{1,0},{2,3},{3,2},{4,5},{5,4},{6,7},{7,6},{8,9},{9,8},{10,11... | collective-permute-start | bytes 393224 | tf_op jit(solution)/shard_map/ppermute | solution.py:29
  68.2 4.3 %collective-permute-start.28 = (f32[2,2,2,1,256]{4,3,2,1,0:T(1,128)S(1)}, f32[2,2,2,1,256]{4,3,2,1,0:T(1,128)S(1)}, u32[]{:S(2)}, u32[]{:S(2)}) collective-permute-start(f32[2,2,2,1,256]{4,3,2,1,0:T(1,128)S(1)} %get-tuple-element.55), channel_id=1, source_target_pairs={{0,1},{1,0},{2,3},{3,2},{4,5},{5,4},{6,7},{7,6},{8,9},{9,8},{10,11... | collective-permute-start | bytes 24584 | tf_op jit(solution)/shard_map/ppermute | solution.py:29
  70.9 20.5 %collective-permute-start.14 = (bf16[2,128,256]{2,1,0:T(8,128)(2,1)S(1)}, bf16[2,128,256]{2,1,0:T(8,128)(2,1)S(1)}, u32[]{:S(2)}, u32[]{:S(2)}) collective-permute-start(bf16[2,128,256]{2,1,0:T(8,128)(2,1)S(1)} %get-tuple-element.45.refs_1_), channel_id=1, source_target_pairs={{0,1},{1,0},{2,3},{3,2},{4,5},{5,4},{6,7},{7,6},{8,9},{9,8},{10,11... | collective-permute-start | bytes 393224 | tf_op jit(solution)/shard_map/ppermute | solution.py:29
  72.5 5.7 %collective-permute-start.29 = (f32[2,2,2,2,1,256]{5,4,3,2,1,0:T(1,128)S(1)}, f32[2,2,2,2,1,256]{5,4,3,2,1,0:T(1,128)S(1)}, u32[]{:S(2)}, u32[]{:S(2)}) collective-permute-start(f32[2,2,2,2,1,256]{5,4,3,2,1,0:T(1,128)S(1)} %pad_maximum_fusion.1.refs_8_.refs_4_), channel_id=1, source_target_pairs={{0,2},{1,3},{2,0},{3,1},{4,6},{5,7},{6,4},{7,5},{8,10},{9,11},{10,... | collective-permute-start | bytes 49160 | tf_op jit(solution)/shard_map/ppermute | solution.py:29
  73.9 4.4 %collective-permute-start.30 = (f32[2,2,2,2,1,256]{5,4,3,2,1,0:T(1,128)S(1)}, f32[2,2,2,2,1,256]{5,4,3,2,1,0:T(1,128)S(1)}, u32[]{:S(2)}, u32[]{:S(2)}) collective-permute-start(f32[2,2,2,2,1,256]{5,4,3,2,1,0:T(1,128)S(1)} %pad_maximum_fusion.1.refs_8_.refs_4_), channel_id=1, source_target_pairs={{0,4},{1,5},{2,6},{3,7},{4,0},{5,1},{6,2},{7,3},{8,12},{9,13},{10,... | collective-permute-start | bytes 49160 | tf_op jit(solution)/shard_map/ppermute | solution.py:29
  75.0 4.6 %collective-permute-start.31 = (f32[2,2,2,2,1,256]{5,4,3,2,1,0:T(1,128)S(1)}, f32[2,2,2,2,1,256]{5,4,3,2,1,0:T(1,128)S(1)}, u32[]{:S(2)}, u32[]{:S(2)}) collective-permute-start(f32[2,2,2,2,1,256]{5,4,3,2,1,0:T(1,128)S(1)} %pad_maximum_fusion.1.refs_8_.refs_4_), channel_id=1, source_target_pairs={{0,6},{1,7},{2,4},{3,5},{4,2},{5,3},{6,0},{7,1},{8,14},{9,15},{10,... | collective-permute-start | bytes 49160 | tf_op jit(solution)/shard_map/ppermute | solution.py:29
  78.3 15.7 %collective-permute-start.32 = (bf16[2,128,256]{2,1,0:T(8,128)(2,1)S(1)}, bf16[2,128,256]{2,1,0:T(8,128)(2,1)S(1)}, u32[]{:S(2)}, u32[]{:S(2)}) collective-permute-start(bf16[2,128,256]{2,1,0:T(8,128)(2,1)S(1)} %get-tuple-element.56.refs_0_), channel_id=1, source_target_pairs={{0,1},{1,0},{2,3},{3,2},{4,5},{5,4},{6,7},{7,6},{8,9},{9,8},{10,11... | collective-permute-start | bytes 393224 | tf_op jit(solution)/shard_map/ppermute | solution.py:29
  81.8 37.7 %collective-permute-start.40 = (bf16[1616,128]{1,0:T(8,128)(2,1)S(1)}, bf16[1616,128]{1,0:T(8,128)(2,1)S(1)}, u32[]{:S(2)}, u32[]{:S(2)}) collective-permute-start(bf16[1616,128]{1,0:T(8,128)(2,1)S(1)} %get-tuple-element.71), channel_id=1, source_target_pairs={{0,8},{8,0},{16,24},{24,16},{1,9},{9,1},{17,25},{25,17},{2,10},{10... | collective-permute-start | bytes 1241096 | tf_op jit(solution)/shard_map/ppermute | solution.py:29
  81.8 13.6 %collective-permute-start.33 = (bf16[2,128,256]{2,1,0:T(8,128)(2,1)S(1)}, bf16[2,128,256]{2,1,0:T(8,128)(2,1)S(1)}, u32[]{:S(2)}, u32[]{:S(2)}) collective-permute-start(bf16[2,128,256]{2,1,0:T(8,128)(2,1)S(1)} %get-tuple-element.57.refs_1_), channel_id=1, source_target_pairs={{0,1},{1,0},{2,3},{3,2},{4,5},{5,4},{6,7},{7,6},{8,9},{9,8},{10,11... | collective-permute-start | bytes 393224 | tf_op jit(solution)/shard_map/ppermute | solution.py:29
  89.7 29.8 %collective-permute-start.39 = (bf16[1616,128]{1,0:T(8,128)(2,1)S(1)}, bf16[1616,128]{1,0:T(8,128)(2,1)S(1)}, u32[]{:S(2)}, u32[]{:S(2)}) collective-permute-start(bf16[1616,128]{1,0:T(8,128)(2,1)S(1)} %get-tuple-element.70), channel_id=1, source_target_pairs={{0,8},{8,0},{16,24},{24,16},{1,9},{9,1},{17,25},{25,17},{2,10},{10... | collective-permute-start | bytes 1241096 | tf_op jit(solution)/shard_map/ppermute | solution.py:29
  92.6 5.5 %collective-permute-start.15 = (bf16[2,128,256]{2,1,0:T(8,128)(2,1)S(1)}, bf16[2,128,256]{2,1,0:T(8,128)(2,1)S(1)}, u32[]{:S(2)}, u32[]{:S(2)}) collective-permute-start(bf16[2,128,256]{2,1,0:T(8,128)(2,1)S(1)} %get-tuple-element.47), channel_id=1, source_target_pairs={{0,2},{1,3},{2,0},{3,1},{4,6},{5,7},{6,4},{7,5},{8,10},{9,11},{10,... | collective-permute-start | bytes 393224 | tf_op jit(solution)/shard_map/ppermute | solution.py:29
  93.9 7.1 %collective-permute-start.16 = (bf16[2,128,256]{2,1,0:T(8,128)(2,1)S(1)}, bf16[2,128,256]{2,1,0:T(8,128)(2,1)S(1)}, u32[]{:S(2)}, u32[]{:S(2)}) collective-permute-start(bf16[2,128,256]{2,1,0:T(8,128)(2,1)S(1)} %get-tuple-element.48), channel_id=1, source_target_pairs={{0,4},{1,5},{2,6},{3,7},{4,0},{5,1},{6,2},{7,3},{8,12},{9,13},{10,... | collective-permute-start | bytes 393224 | tf_op jit(solution)/shard_map/ppermute | solution.py:29
  95.4 8.2 %collective-permute-start.17 = (bf16[2,128,256]{2,1,0:T(8,128)(2,1)S(1)}, bf16[2,128,256]{2,1,0:T(8,128)(2,1)S(1)}, u32[]{:S(2)}, u32[]{:S(2)}) collective-permute-start(bf16[2,128,256]{2,1,0:T(8,128)(2,1)S(1)} %get-tuple-element.49), channel_id=1, source_target_pairs={{0,6},{1,7},{2,4},{3,5},{4,2},{5,3},{6,0},{7,1},{8,14},{9,15},{10,... | collective-permute-start | bytes 393224 | tf_op jit(solution)/shard_map/ppermute | solution.py:29
  98.1 6.4 %collective-permute-start.34 = (bf16[2,128,256]{2,1,0:T(8,128)(2,1)S(1)}, bf16[2,128,256]{2,1,0:T(8,128)(2,1)S(1)}, u32[]{:S(2)}, u32[]{:S(2)}) collective-permute-start(bf16[2,128,256]{2,1,0:T(8,128)(2,1)S(1)} %get-tuple-element.59), channel_id=1, source_target_pairs={{0,2},{1,3},{2,0},{3,1},{4,6},{5,7},{6,4},{7,5},{8,10},{9,11},{10,... | collective-permute-start | bytes 393224 | tf_op jit(solution)/shard_map/ppermute | solution.py:29
  101.1 6.8 %collective-permute-start.35 = (bf16[2,128,256]{2,1,0:T(8,128)(2,1)S(1)}, bf16[2,128,256]{2,1,0:T(8,128)(2,1)S(1)}, u32[]{:S(2)}, u32[]{:S(2)}) collective-permute-start(bf16[2,128,256]{2,1,0:T(8,128)(2,1)S(1)} %get-tuple-element.60), channel_id=1, source_target_pairs={{0,4},{1,5},{2,6},{3,7},{4,0},{5,1},{6,2},{7,3},{8,12},{9,13},{10,... | collective-permute-start | bytes 393224 | tf_op jit(solution)/shard_map/ppermute | solution.py:29
  103.5 5.9 %collective-permute-start.36 = (bf16[2,128,256]{2,1,0:T(8,128)(2,1)S(1)}, bf16[2,128,256]{2,1,0:T(8,128)(2,1)S(1)}, u32[]{:S(2)}, u32[]{:S(2)}) collective-permute-start(bf16[2,128,256]{2,1,0:T(8,128)(2,1)S(1)} %get-tuple-element.61), channel_id=1, source_target_pairs={{0,6},{1,7},{2,4},{3,5},{4,2},{5,3},{6,0},{7,1},{8,14},{9,15},{10,... | collective-permute-start | bytes 393224 | tf_op jit(solution)/shard_map/ppermute | solution.py:29
  104.4 8.9 %collective-permute-start.18 = (bf16[128,256]{1,0:T(8,128)(2,1)S(1)}, bf16[128,256]{1,0:T(8,128)(2,1)S(1)}, u32[]{:S(2)}, u32[]{:S(2)}) collective-permute-start(bf16[128,256]{1,0:T(8,128)(2,1)S(1)} %get-tuple-element.51), channel_id=1, source_target_pairs={{0,8},{8,0},{16,24},{24,16},{1,9},{9,1},{17,25},{25,17},{2,10},{10... | collective-permute-start | bytes 196616 | tf_op jit(solution)/shard_map/ppermute | solution.py:29
  109.6 6.1 %collective-permute-start.37 = (bf16[128,256]{1,0:T(8,128)(2,1)S(1)}, bf16[128,256]{1,0:T(8,128)(2,1)S(1)}, u32[]{:S(2)}, u32[]{:S(2)}) collective-permute-start(bf16[128,256]{1,0:T(8,128)(2,1)S(1)} %get-tuple-element.62), channel_id=1, source_target_pairs={{0,16},{8,24},{16,0},{24,8},{1,17},{9,25},{17,1},{25,9},{2,18},{10... | collective-permute-start | bytes 196616 | tf_op jit(solution)/shard_map/ppermute | solution.py:29
  112.1 6.1 %collective-permute-start.38 = (bf16[128,256]{1,0:T(8,128)(2,1)S(1)}, bf16[128,256]{1,0:T(8,128)(2,1)S(1)}, u32[]{:S(2)}, u32[]{:S(2)}) collective-permute-start(bf16[128,256]{1,0:T(8,128)(2,1)S(1)} %get-tuple-element.63), channel_id=1, source_target_pairs={{0,24},{8,16},{16,8},{24,0},{1,25},{9,17},{17,9},{25,1},{2,26},{10... | collective-permute-start | bytes 196616 | tf_op jit(solution)/shard_map/ppermute | solution.py:29

commit v4 on v2

v4 whole, which is shorter than its diff:
```python
import functools
import math

import jax
import jax.numpy as jnp
from jax import lax
from jax.experimental import pallas as pl
from jax.experimental.pallas import tpu as pltpu
from jax.sharding import PartitionSpec as P

HEAD_DIM = 128
MAX_TILES = 4
KEY_ROWS = 256
TEXT_CHUNKS = 4
DELTA_ROWS = 16
NOTE_ROWS = 16
LOWEST = -1e30
SCALE = 1.0 / math.sqrt(HEAD_DIM)
SCALE_LOG2 = SCALE / math.log(2.0)
BF16 = jnp.bfloat16
F32 = jnp.float32

SMEM = pl.BlockSpec(memory_space=pltpu.SMEM)
VMEM = pl.BlockSpec(memory_space=pltpu.VMEM)
ANY = pl.BlockSpec(memory_space=pl.ANY)
HBM = pl.BlockSpec(memory_space=pltpu.HBM)


def exchange(block, axis, distance):
    count = lax.axis_size(axis)
    return lax.ppermute(block, axis, [(i, i ^ distance) for i in range(count)])


def call(kernel, out_shape, in_specs, scratch, args, out_specs=None, grid=(), megabytes=16, cost=0):
    many = isinstance(out_shape, (list, tuple))
    if out_specs is None:
        out_specs = [VMEM] * len(out_shape) if many else VMEM
    return pl.pallas_call(
        kernel,
        out_shape=out_shape,
        in_specs=in_specs,
        out_specs=out_specs,
        grid=grid,
        name=getattr(kernel, "func", kernel).__name__,
        scratch_shapes=scratch,
        compiler_params=pltpu.CompilerParams(vmem_limit_bytes=megabytes << 20),
        cost_estimate=pl.CostEstimate(flops=cost * 10**9, bytes_accessed=0, transcendentals=0),
    )(*args)


def place_of(perm_ref, owner, owners):
    first = jnp.int32(0)
    for index in range(owners):
        first = first + jnp.where(perm_ref[index] == owner, index, 0)
    return first


def sample_at(count_ref, place, samples):
    end, sample, start = jnp.int32(0), jnp.int32(0), jnp.int32(0)
    for index in range(samples):
        end = end + count_ref[index]
        passed = place >= end
        sample = sample + passed.astype(jnp.int32)
        start = jnp.where(passed, end, start)
    return sample, start


def pack_kernel(heads, who, length, *refs):
    inputs, outs, buffers, sem = refs[:3], refs[3:-4], refs[-4:-1], refs[-1]
    copies = [pltpu.make_async_copy(a, b, sem.at[i]) for i, (a, b) in enumerate(zip(inputs, buffers))]
    for copy in copies:
        copy.start()
    for copy in copies:
        copy.wait()
    q_ref, o_ref, g_ref = buffers
    rows = q_ref.shape[0]
    seq = who[0]
    position = seq * rows + lax.broadcasted_iota(jnp.int32, (rows, HEAD_DIM), 0)
    keep = position < length[0]
    for j, out in enumerate(outs):
        for h in range(heads):
            columns = pl.ds(pl.multiple_of(((seq ^ j) * heads + h) * HEAD_DIM, HEAD_DIM), HEAD_DIM)
            grad = jnp.where(keep, g_ref[:, columns].astype(F32), 0.0)
            product = grad * o_ref[:, columns].astype(F32)
            delta = jnp.sum(jnp.transpose(product), axis=0, keepdims=True)
            out[h, :rows] = q_ref[:, columns]
            out[h, rows:2 * rows] = grad.astype(BF16)
            out[h, 2 * rows:] = jnp.broadcast_to(delta, (DELTA_ROWS, HEAD_DIM)).astype(BF16)


def stack_kernel(count, rows, *refs):
    out, sem = refs[-2], refs[-1]
    copies = [pltpu.make_async_copy(refs[i].at[:, rows], out.at[i], sem.at[i]) for i in range(count)]
    for copy in copies:
        copy.start()
    for copy in copies:
        copy.wait()


def join_kernel(count, *refs):
    out, sem = refs[-2], refs[-1]
    copies = [pltpu.make_async_copy(refs[i], out.at[i], sem.at[i]) for i in range(count)]
    for copy in copies:
        copy.start()
    for copy in copies:
        copy.wait()


def fetch(pieces, relative, target, sem):
    for core, piece in enumerate(pieces):
        @pl.when((relative & 1) == core)
        def _(piece=piece):
            pltpu.make_async_copy(piece.at[lax.shift_right_logical(relative, 1)], target, sem).start()


def spans_of(rows):
    full = rows // KEY_ROWS
    tail = rows - full * KEY_ROWS
    return [(i * KEY_ROWS, KEY_ROWS, KEY_ROWS) for i in range(full)] + [(full * KEY_ROWS, -(-tail // 16) * 16, tail)]


def dot_nt(a, b):
    return lax.dot_general(a, b, (((1,), (1,)), ((), ())), preferred_element_type=F32)


def dot_nn(a, b):
    return jnp.dot(a, b, preferred_element_type=F32)


def own_tiles(owners, slots, who, counts, perm):
    first = place_of(perm, who[1], owners)
    return [sample_at(counts, first + slot * owners, owners) for slot in range(slots)]


def pad_kernel(tiles, *refs):
    out = refs[-1]
    for slot in range(tiles.shape[0]):
        for low, size, used in spans_of(tiles.shape[1]):
            if size != used:
                out[slot, low:] = jnp.zeros((size, HEAD_DIM), BF16)
            out[slot, low:low + used] = tiles[slot, low:low + used]


def tiles_kernel(slots, rows, who, own, partner, keys, values, turned):
    for odd in range(2):
        @pl.when((who[0] & 1) == odd)
        def _(odd=odd):
            keys[...] = (own, partner)[odd][...]
            values[...] = (own, partner)[1 - odd][...]
    for slot in range(slots):
        for low, size, _ in spans_of(rows):
            turned[slot, :, low:low + size] = jnp.transpose(keys[slot, low:low + size].astype(F32)).astype(BF16)


def weights_kernel(owners, heads, blocks, slots, rows, who, counts, perm, keys, *refs):
    pieces = refs[:2]
    stats, weights, text_buf, scores_buf, sem = refs[2:]
    step = pl.program_id(0)
    spans = spans_of(rows)
    chunks = text_buf.shape[1] // blocks
    width = chunks * HEAD_DIM
    tiles = own_tiles(owners, slots, who, counts, perm)

    @pl.when(step == 0)
    def _():
        for slot in range(slots):
            @pl.when(tiles[slot][0] < owners)
            def _(slot=slot):
                fetch(pieces, tiles[slot][0] ^ who[1], text_buf.at[slot], sem.at[slot])

    for slot in range(slots):
        base = slot * heads * blocks

        @pl.when((step == base) & (tiles[slot][0] < owners))
        def _(slot=slot):
            pltpu.make_async_copy(pieces[0].at[0], text_buf.at[slot], sem.at[slot]).wait()

        @pl.when((step >= base) & (step < base + heads * blocks) & (tiles[slot][0] < owners))
        def _(slot=slot, base=base):
            head, block = (step - base) // blocks, (step - base) % blocks
            query = text_buf[slot, pl.ds(block * chunks, chunks), head].reshape(width, HEAD_DIM)
            peak = jnp.full((8, width), -jnp.inf, F32)
            for low, size, used in spans:
                scores = dot_nt(keys[slot, low:low + size], query)
                if size != used:
                    row = lax.broadcasted_iota(jnp.int32, scores.shape, 0)
                    scores = jnp.where(row < used, scores, -jnp.inf)
                scores_buf[low:low + size] = scores
                peak = jnp.maximum(peak, jnp.max(scores.reshape(-1, 8, width), axis=0))
            top = jnp.max(peak, axis=0, keepdims=True) * SCALE_LOG2
            mass = jnp.zeros((8, width), F32)
            for low, size, used in spans:
                part = jnp.exp2(scores_buf[low:low + size] * SCALE_LOG2 - top)
                mass = mass + jnp.sum(part.reshape(-1, 8, width), axis=0)
                weights[0, low:low + size] = part.astype(BF16)
            stats[slot, 0, head, pl.ds(block, 1)] = top
            stats[slot, 1, head, pl.ds(block, 1)] = jnp.sum(mass, axis=0, keepdims=True)


def in_parts(value):
    high = value.astype(BF16).astype(F32)
    middle = (value - high).astype(BF16).astype(F32)
    return [high, middle, value - high - middle]


def note_rows(peak, mass):
    rows = in_parts(peak) + in_parts(mass)
    index = lax.broadcasted_iota(jnp.int32, (NOTE_ROWS, peak.shape[1]), 0)
    result = jnp.zeros(index.shape, F32)
    for place, row in enumerate(rows):
        result = jnp.where(index == place, row, result)
    return result.astype(BF16)


def read_notes(notes):
    notes = notes.astype(F32)
    rows = [notes[place:place + 1] for place in range(6)]
    return rows[0] + rows[1] + rows[2], rows[3] + rows[4] + rows[5]


def slopes_kernel(owners, heads, blocks, slots, rows, who, counts, perm, stats, weights, values, keys_turned, *refs):
    pieces = refs[:2]
    slopes, turned, text_buf, sem = refs[-4:]
    step = pl.program_id(0)
    spans = spans_of(rows)
    chunks = text_buf.shape[1] // blocks
    width = chunks * HEAD_DIM
    tiles = own_tiles(owners, slots, who, counts, perm)

    @pl.when(step == 0)
    def _():
        for slot in range(slots):
            @pl.when(tiles[slot][0] < owners)
            def _(slot=slot):
                fetch(pieces, tiles[slot][0] ^ who[1], text_buf.at[slot], sem.at[slot])

    for slot in range(slots):
        base = slot * heads * blocks

        @pl.when((step == base) & (tiles[slot][0] < owners))
        def _(slot=slot):
            pltpu.make_async_copy(pieces[0].at[0], text_buf.at[slot], sem.at[slot]).wait()

        @pl.when((step >= base) & (step < base + heads * blocks) & (tiles[slot][0] < owners))
        def _(slot=slot, base=base):
            head, block = (step - base) // blocks, (step - base) % blocks
            grad = text_buf[slot, pl.ds(block * chunks, chunks), head, :HEAD_DIM].reshape(width, HEAD_DIM)
            delta = jnp.concatenate(
                [
                    text_buf[slot, block * chunks + piece, head, HEAD_DIM:].astype(F32)[:1]
                    for piece in range(chunks)
                ],
                axis=1,
            )
            for low, size, used in spans:
                slope = dot_nt(values[slot, low:low + size], grad)
                slopes[0, low:low + size] = (weights[0, low:low + size].astype(F32) * (slope - delta)).astype(BF16)
            total = dot_nn(keys_turned[slot, :, :slopes.shape[1]], slopes[0])
            columns = pl.ds(pl.multiple_of(block * width, width), width)
            turned[slot, head, :HEAD_DIM, columns] = total.astype(BF16)
            turned[slot, head, HEAD_DIM:, columns] = note_rows(
                stats[slot, 0, head, pl.ds(block, 1)], stats[slot, 1, head, pl.ds(block, 1)]
            )


def peak_and_mass(stats, owners, me, perm, start, tiles, head, block):
    found = []
    for index in range(MAX_TILES):
        live = index < tiles
        place = jnp.where(live, start + index, start)
        other, slot = perm[place & (owners - 1)] ^ me, lax.div(place, owners)
        top = stats[other, slot, 0, head, pl.ds(block, 1)]
        mass = stats[other, slot, 1, head, pl.ds(block, 1)]
        found.append((jnp.where(live, top, -jnp.inf), jnp.where(live, mass, 0.0)))
    top = functools.reduce(jnp.maximum, [peak for peak, _ in found])
    return top, sum(mass * jnp.exp2(peak - top) for peak, mass in found)


def factors_kernel(owners, heads, blocks, slots, who, counts, perm, *refs):
    out, stats = refs[-2:]
    for index, ref in enumerate(refs[:-2]):
        stats[2 * index:2 * index + 2] = ref[...]
    for slot, (sample, start) in enumerate(own_tiles(owners, slots, who, counts, perm)):
        @pl.when(sample < owners)
        def _(slot=slot, sample=sample, start=start):
            tiles = counts[jnp.minimum(sample, owners - 1)]
            for head in range(heads):
                for block in range(blocks):
                    top, mass = peak_and_mass(stats, owners, who[1], perm, start, tiles, head, block)
                    peak = stats[0, slot, 0, head, pl.ds(block, 1)]
                    out[slot, head, pl.ds(block, 1)] = jnp.exp2(peak - top) / mass


def sums_kernel(owners, heads, blocks, slots, slot, who, counts, perm, *refs):
    weights, slopes, factors = refs[:3]
    q_pieces, g_pieces = refs[3:5], refs[5:7]
    keep_out, send_out, q_buf, g_buf, sums, sem = refs[-6:]
    step = pl.program_id(0)
    odd, me = who[0] & 1, who[1]
    chunks = q_buf.shape[0] // blocks
    width = chunks * HEAD_DIM
    sample = own_tiles(owners, slots, who, counts, perm)[slot][0]
    used = sample < owners

    @pl.when((step == 0) & used)
    def _():
        fetch(q_pieces, sample ^ me, q_buf, sem.at[0])
        fetch(g_pieces, sample ^ me, g_buf, sem.at[1])
        pltpu.make_async_copy(q_pieces[0].at[0], q_buf, sem.at[0]).wait()
        pltpu.make_async_copy(g_pieces[0].at[0], g_buf, sem.at[1]).wait()

    @pl.when(jnp.logical_not(used))
    def _():
        keep_out[...] = jnp.zeros(keep_out.shape, BF16)
        send_out[...] = jnp.zeros(send_out.shape, BF16)

    @pl.when(used)
    def _():
        head, block = step // blocks, step % blocks
        factor = jnp.transpose(jnp.broadcast_to(factors[slot, head, pl.ds(block, 1)], (HEAD_DIM, width)))
        where = pl.ds(block * chunks, chunks)
        query = q_buf[where, head].reshape(width, HEAD_DIM)
        grad = g_buf[where, head, :HEAD_DIM].reshape(width, HEAD_DIM)
        query = (query.astype(F32) * factor * SCALE).astype(BF16)
        grad = (grad.astype(F32) * factor).astype(BF16)

        def add(which, source, right, fresh):
            for low in range(0, sums.shape[1], 2 * KEY_ROWS):
                span = slice(low, min(low + 2 * KEY_ROWS, sums.shape[1]))
                part = dot_nn(source[0, span], right)
                sums[which, span] = part if fresh else sums[which, span] + part

        for fresh in (True, False):
            @pl.when((step == 0) == fresh)
            def _(fresh=fresh):
                add(0, slopes, query, fresh)
                add(1, weights, grad, fresh)

        @pl.when(step == heads * blocks - 1)
        def _():
            keep_out[...] = sums[odd].astype(BF16)
            send_out[...] = sums[1 - odd].astype(BF16)


def route_kernel(owners, heads, blocks, slots, who, counts, perm, own, other, *refs):
    outs = refs[-(owners // 2):]
    me = who[1]
    width = own.shape[3] // blocks
    found = []
    for near in range(2):
        first = place_of(perm, me ^ near, owners)
        for slot in range(slots):
            found.append((near, slot, sample_at(counts, first + slot * owners, owners)[0]))

    def one(step, carry):
        head, block = step // blocks, step % blocks
        columns = pl.ds(pl.multiple_of(block * width, width), width)
        notes = [read_notes((own, other)[near][slot, head, HEAD_DIM:, columns]) for near, slot, _ in found]
        for distance, out in enumerate(outs):
            live = [sample == me ^ (2 * distance) for _, _, sample in found]
            top = functools.reduce(
                jnp.maximum, [jnp.where(hit, note[0], LOWEST) for hit, note in zip(live, notes)]
            )
            mass = jnp.zeros(top.shape, F32)
            total = jnp.zeros((HEAD_DIM, width), F32)
            for hit, note, (near, slot, _) in zip(live, notes, found):
                factor = jnp.exp2(jnp.where(hit, note[0] - top, -jnp.inf))
                mass = mass + jnp.where(hit, note[1] * factor, 0.0)
                part = (own, other)[near][slot, head, :HEAD_DIM, columns].astype(F32)
                total = total + jnp.where(hit, part * factor, 0.0)
            out[head, :HEAD_DIM, columns] = total.astype(BF16)
            out[head, HEAD_DIM:, columns] = note_rows(top, mass)
        return carry

    lax.fori_loop(0, heads * blocks, one, 0)


def gather_kernel(parts, *refs):
    outs = refs[parts:]
    rows = outs[0].shape[0]
    for piece, out in enumerate(outs):
        span = slice(piece * rows, (piece + 1) * rows)
        for head in range(refs[0].shape[0]):
            notes = [read_notes(ref[head, HEAD_DIM:, span]) for ref in refs[:parts]]
            top = functools.reduce(jnp.maximum, [note[0] for note in notes])
            factors = [jnp.exp2(note[0] - top) for note in notes]
            mass = sum(note[1] * factor for note, factor in zip(notes, factors))
            total = sum(ref[head, :HEAD_DIM, span].astype(F32) * factor for ref, factor in zip(refs[:parts], factors))
            total = total * (SCALE / mass)
            out[:, head * HEAD_DIM:(head + 1) * HEAD_DIM] = jnp.transpose(total).astype(BF16)


def place_kernel(who, *refs):
    out = refs[-1]
    for distance, ref in enumerate(refs[:-1]):
        width = ref.shape[1]
        start = pl.multiple_of((who[0] ^ distance) * width, width)
        out[:, pl.ds(start, width)] = ref[...]


def merge_kernel(slots, *refs):
    keep, got, out = refs[:slots], refs[slots:-1], refs[-1]
    for low, size, used in spans_of(out.shape[0]):
        row = lax.broadcasted_iota(jnp.int32, (slots * size, slots * size), 0)
        column = lax.broadcasted_iota(jnp.int32, (slots * size, slots * size), 1)
        source = lax.rem(row, slots) * size + lax.div(row, slots)
        order = (source == column).astype(BF16)
        total = [
            (keep[slot][low:low + size].astype(F32) + got[slot][low:low + size].astype(F32)).astype(BF16)
            for slot in range(slots)
        ]
        mixed = dot_nn(order, jnp.concatenate(total, axis=0)).astype(BF16).reshape(size, slots, HEAD_DIM)
        out[low:low + used] = mixed[:used]


def shards(queries, saved_output, grad_out, tile_kv, tile_count, owner_perm, text_len):
    rows_dev, features = queries.shape[1], queries.shape[2]
    groups, owners = lax.axis_size("seq"), lax.axis_size("dp")
    heads = features // HEAD_DIM // groups
    width = heads * HEAD_DIM
    chunks = min(TEXT_CHUNKS, groups)
    blocks = groups // chunks
    text_rows, block_rows = groups * rows_dev, chunks * rows_dev
    steps = heads * blocks
    slots, tile_rows = tile_kv.shape[0], tile_kv.shape[1]
    low, tail_rows, _ = spans_of(tile_rows)[-1]
    padded = low + tail_rows
    who = jnp.stack([lax.axis_index("seq"), lax.axis_index("dp")]).astype(jnp.int32)
    known = (who, tile_count, owner_perm)
    scale = blocks

    piece_rows = 2 * rows_dev + DELTA_ROWS
    packed = call(
        functools.partial(pack_kernel, heads),
        [jax.ShapeDtypeStruct((heads, piece_rows, HEAD_DIM), BF16)] * groups,
        [SMEM, SMEM] + [HBM] * 3,
        [pltpu.VMEM((rows_dev, features), BF16)] * 3 + [pltpu.SemaphoreType.DMA((3,))],
        (who, text_len, queries[0], saved_output[0], grad_out[0]),
        megabytes=60,
        cost=1,
    )
    pieces = [packed[0]] + [exchange(packed[j], "seq", j) for j in range(1, groups)]
    tile_shape = jax.ShapeDtypeStruct((slots, padded, HEAD_DIM), BF16)
    own_tile = call(pad_kernel, tile_shape, [VMEM] + [ANY] * (groups - 1), [], (tile_kv, *pieces[1:]), cost=1)
    partner_tile = exchange(own_tile, "seq", 1)

    def near_of(first, count, order):
        block = call(
            functools.partial(stack_kernel, groups, slice(first, first + count)),
            jax.ShapeDtypeStruct((groups, heads, count, HEAD_DIM), BF16),
            [ANY] * (groups + len(order)),
            [pltpu.SemaphoreType.DMA((groups,))],
            (*pieces, *order),
            megabytes=8,
        )
        return [block] + [exchange(block, "dp", d) for d in range(2, owners, 2)]

    def over_core(near, order):
        joined = call(
            functools.partial(join_kernel, len(near)),
            jax.ShapeDtypeStruct((len(near),) + near[0].shape, BF16),
            [ANY] * (len(near) + len(order)),
            [pltpu.SemaphoreType.DMA((len(near),))],
            (*near, *order),
            megabytes=12 * scale,
        )
        return joined, exchange(joined, "dp", 1)

    q_near = near_of(0, rows_dev, [own_tile])
    g_near = near_of(rows_dev, rows_dev + DELTA_ROWS, q_near[1:2])
    q_pair = over_core(q_near, [partner_tile])

    turn_shape = jax.ShapeDtypeStruct((slots, HEAD_DIM, -(-padded // HEAD_DIM) * HEAD_DIM), BF16)
    keys, values, keys_turned = call(
        functools.partial(tiles_kernel, slots, tile_rows),
        [tile_shape, tile_shape, turn_shape],
        [SMEM] + [VMEM] * 2,
        [],
        (who, own_tile, partner_tile),
        cost=1,
    )
    stats_shape = (slots, 2, heads, blocks, block_rows)
    stack_shape = jax.ShapeDtypeStruct((slots * steps, padded, block_rows), BF16)
    stack_spec = pl.BlockSpec((1, padded, block_rows), lambda i: (i, 0, 0))
    stats, weights = call(
        functools.partial(weights_kernel, owners, heads, blocks, slots, tile_rows),
        [jax.ShapeDtypeStruct(stats_shape, F32), stack_shape],
        [SMEM] * 3 + [VMEM] + [ANY] * 2,
        [
            pltpu.VMEM((slots,) + q_near[0].shape, BF16),
            pltpu.VMEM((padded, block_rows), F32),
            pltpu.SemaphoreType.DMA((slots,)),
        ],
        (*known, keys, *q_pair),
        out_specs=[VMEM, stack_spec],
        grid=(slots * steps,),
        megabytes=16,
        cost=6,
    )
    pair = jnp.stack([stats, exchange(stats, "dp", 1)])
    shared = [pair] + [exchange(pair, "dp", d) for d in range(2, owners, 2)]
    g_pair = over_core(g_near, [stats])
    slopes, part = call(
        functools.partial(slopes_kernel, owners, heads, blocks, slots, tile_rows),
        [stack_shape, jax.ShapeDtypeStruct((slots, heads, HEAD_DIM + NOTE_ROWS, text_rows), BF16)],
        [SMEM] * 3 + [VMEM, stack_spec] + [VMEM] * 2 + [ANY] * 3,
        [pltpu.VMEM((slots,) + g_near[0].shape, BF16), pltpu.SemaphoreType.DMA((slots,))],
        (*known, stats, weights, values, keys_turned, *g_pair, pair),
        out_specs=[stack_spec, VMEM],
        grid=(slots * steps,),
        megabytes=20,
        cost=6,
    )
    factors = call(
        functools.partial(factors_kernel, owners, heads, blocks, slots),
        jax.ShapeDtypeStruct((slots, heads, blocks, block_rows), F32),
        [SMEM] * 3 + [VMEM] * len(shared),
        [pltpu.VMEM((owners,) + stats_shape, F32)],
        (*known, *shared),
        cost=30,
    )
    routed = call(
        functools.partial(route_kernel, owners, heads, blocks, slots),
        [jax.ShapeDtypeStruct((heads, HEAD_DIM + NOTE_ROWS, text_rows), BF16)] * (owners // 2),
        [SMEM] * 3 + [VMEM] * 2 + [ANY],
        [],
        (*known, part, exchange(part, "dp", 1), factors),
        megabytes=14,
        cost=30,
    )

    kept, got = [], []
    for slot in range(slots):
        left_spec = pl.BlockSpec((1, padded, block_rows), lambda i, slot=slot: (slot * steps + i, 0, 0))
        keep, send = call(
            functools.partial(sums_kernel, owners, heads, blocks, slots, slot),
            [jax.ShapeDtypeStruct((padded, HEAD_DIM), BF16)] * 2,
            [SMEM] * 3 + [left_spec] * 2 + [VMEM] + [ANY] * 5,
            [
                pltpu.VMEM(q_near[0].shape, BF16),
                pltpu.VMEM(g_near[0].shape, BF16),
                pltpu.VMEM((2, padded, HEAD_DIM), F32),
                pltpu.SemaphoreType.DMA((2,)),
            ],
            (*known, weights, slopes, factors, *q_pair, *g_pair, routed[0]),
            out_specs=[VMEM] * 2,
            grid=(steps,),
            megabytes=8 * scale,
            cost=4,
        )
        kept.append(keep)
        got.append(exchange(send, "seq", 1))

    sums = [routed[0]] + [exchange(routed[d], "dp", 2 * d) for d in range(1, owners // 2)]
    cut = call(
        functools.partial(gather_kernel, len(sums)),
        [jax.ShapeDtypeStruct((rows_dev, width), BF16)] * groups,
        [VMEM] * len(sums),
        [],
        sums,
        megabytes=8 * scale,
        cost=30,
    )
    back = [cut[0]] + [exchange(cut[j], "seq", j) for j in range(1, groups)]
    grad_queries = call(
        place_kernel,
        jax.ShapeDtypeStruct((rows_dev, features), BF16),
        [SMEM] + [VMEM] * groups,
        [],
        (who, *back),
        cost=1,
    )
    grad_tiles = call(
        functools.partial(merge_kernel, slots),
        jax.ShapeDtypeStruct((tile_rows, slots, HEAD_DIM), BF16),
        [VMEM] * (2 * slots),
        [],
        (*kept, *got),
        cost=2,
    )
    return (grad_queries[None], jnp.transpose(grad_tiles, (1, 0, 2)))


def solution(mesh):
    placed = (
        P("dp", "seq", None),
        P("dp", "seq", None),
        P("dp", "seq", None),
        P("dp", None, "seq"),
        P(),
        P(),
        P("dp"),
    )
    return jax.shard_map(
        shards,
        mesh=mesh,
        in_specs=placed,
        out_specs=(P("dp", "seq", None), P("dp", None, "seq")),
        check_vma=False,
    )
```

time: 122 us -> 109 us (0.89); the launches traced: 123 us -> 108 us
  starting transfers between devices: 44.4 us -> 31 us
  local copies, waits for them, and re-layouts: 5.51 us -> 2.18 us
  Pallas kernels: 19.8 us -> 21.4 us
    ppermute x34 -> x25, starting transfers between devices: 44.4 us -> 31 us  [exchange(): return lax.ppermute(block, axis, [(i, i ^ distance) for i in range(count)])]
    unnamed x11, local copies, waits for them, and re-layouts: 5.4 us -> 2.18 us
    pallas_call x10 -> x16, Pallas kernels: 19.8 us -> 21.4 us  [call(): pl.pallas_call(kernel, out_shape=out_shape, in_specs=in_specs, out_specs=...]
    ppermute x34 -> x25, waiting for transfers between devices: 51.2 us -> 51.2 us  [exchange(): return lax.ppermute(block, axis, [(i, i ^ distance) for i in range(count)])]
  transfers between devices with their start and end apart: 34 -> 25, of which waited for: 15 -> 15; matrix products, arithmetic and copies ran while one was open for 1% -> 1% of each run, Pallas kernels for 10% -> 13%
where the time goes in v4:
time: 109 us; the launch traced here: 108 us
  waiting for transfers between devices  51.2 us (47%)
  starting transfers between devices  31 us (28%)
  Pallas kernels  21.4 us (20%)
  local copies, waits for them, and re-layouts  2.18 us (2%)
  between operations  1.48 us (1%)
    ppermute x25, waiting for transfers between devices, exchange(): return lax.ppermute(block, axis, [(i, i ^ distance) for i in range(count)])  51.2 us
    ppermute x25, starting transfers between devices, exchange(): return lax.ppermute(block, axis, [(i, i ^ distance) for i in range(count)])  31 us
    pallas_call x16, Pallas kernels, call(): pl.pallas_call(kernel, out_shape=out_shape, in_specs=in_specs, out_specs=...  21.4 us
    unnamed x11, local copies, waits for them, and re-layouts  2.18 us
  transfers between devices with their start and end apart: 25, of which 15 were waited for; matrix products, arithmetic and copies ran while one was open for 1% of the time, Pallas kernels for 13%

profile of v4, /device:TPU:0, one launch (start us, length us, event | category | flops | bytes accessed | tf_op | source)
XLA Modules:
  0.0 107.8 jit_solution(7079832857776781142)
XLA Ops:
  1.3 0.6 pad_add_fusion.who
  1.9 2.9 %pack_kernel.1 = (bf16[2,272,128]{2,1,0:T(8,128)(2,1)}, bf16[2,272,128]{2,1,0:T(8,128)(2,1)}, bf16[2,272,128]{2,1,0:T(8,128)(2,1)}, bf16[2,272,128]{2,1,0:T(8,128)(2,1)}) custom-call(s32[2]{0:T(128)} %pad_add_fusion.who, s32[1]{0:T(128)S(6)} %copy.10.length, bf16[128,1024]{1,0:T(8,128)(2,1)} %bitcast.11, bf16[128,1024]{1,0:T(8,128)(2,1)} %bitcast.12, ...), custom_call_target="tpu_custom_call" | custom-call | flops 1000000000 | tf_op jit(solution)/shard_map/pack_kernel/pallas_call | solution.py:38
  4.8 3.1 %collective-permute-start = (bf16[2,272,128]{2,1,0:T(8,128)(2,1)}, bf16[2,272,128]{2,1,0:T(8,128)(2,1)S(1)}, u32[]{:S(2)}, u32[]{:S(2)}) collective-permute-start(bf16[2,272,128]{2,1,0:T(8,128)(2,1)} %get-tuple-element.25), channel_id=1, source_target_pairs={{0,8},{8,0},{16,24},{24,16},{1,9},{9,1},{17,25},{25,17},{2,10},{10... | collective-permute-start | bytes 417800 | tf_op jit(solution)/shard_map/ppermute | solution.py:31
  7.9 2.6 %collective-permute-start.1 = (bf16[2,272,128]{2,1,0:T(8,128)(2,1)}, bf16[2,272,128]{2,1,0:T(8,128)(2,1)S(1)}, u32[]{:S(2)}, u32[]{:S(2)}) collective-permute-start(bf16[2,272,128]{2,1,0:T(8,128)(2,1)} %get-tuple-element.26), channel_id=1, source_target_pairs={{0,16},{8,24},{16,0},{24,8},{1,17},{9,25},{17,1},{25,9},{2,18},{10... | collective-permute-start | bytes 417800 | tf_op jit(solution)/shard_map/ppermute | solution.py:31
  10.5 1.3 %copy.9.tiles = bf16[2,1601,128]{2,1,0:T(8,128)(2,1)S(1)} copy(bf16[2,1601,128]{2,0,1:T(2,128)(2,1)} %param.10) | data formatting | bytes 1639424 | tf_op args[3]
  11.8 1.8 %collective-permute-done.refs_0_.refs_1_ = bf16[2,272,128]{2,1,0:T(8,128)(2,1)S(1)} collective-permute-done((bf16[2,272,128]{2,1,0:T(8,128)(2,1)}, bf16[2,272,128]{2,1,0:T(8,128)(2,1)S(1)}, u32[]{:S(2)}, u32[]{:S(2)}) %collective-permute-start) | collective-permute-done | bytes 139296 | tf_op jit(solution)/shard_map/ppermute | solution.py:31
  13.5 8.0 %collective-permute-done.1.refs_1_.refs_2_ = bf16[2,272,128]{2,1,0:T(8,128)(2,1)S(1)} collective-permute-done((bf16[2,272,128]{2,1,0:T(8,128)(2,1)}, bf16[2,272,128]{2,1,0:T(8,128)(2,1)S(1)}, u32[]{:S(2)}, u32[]{:S(2)}) %collective-permute-start.1) | collective-permute-done | bytes 139296 | tf_op jit(solution)/shard_map/ppermute | solution.py:31
  21.6 2.2 %collective-permute-start.3 = (bf16[2,1616,128]{2,1,0:T(8,128)(2,1)S(1)}, bf16[2,1616,128]{2,1,0:T(8,128)(2,1)S(1)}, u32[]{:S(2)}, u32[]{:S(2)}) collective-permute-start(bf16[2,1616,128]{2,1,0:T(8,128)(2,1)S(1)} %pad_kernel.1.own.refs_4_), channel_id=1, source_target_pairs={{0,8},{8,0},{16,24},{24,16},{1,9},{9,1},{17,25},{25,17},{2,10},{10... | collective-permute-start | bytes 2482184 | tf_op jit(solution)/shard_map/ppermute | solution.py:31
  23.8 0.9 copy-done
  24.9 2.5 %collective-permute-start.6 = (bf16[4,2,128,128]{3,2,1,0:T(8,128)(2,1)S(1)}, bf16[4,2,128,128]{3,2,1,0:T(8,128)(2,1)S(1)}, u32[]{:S(2)}, u32[]{:S(2)}) collective-permute-start(bf16[4,2,128,128]{3,2,1,0:T(8,128)(2,1)S(1)} %stack_kernel.2.refs_0_), channel_id=1, source_target_pairs={{0,6},{1,7},{2,4},{3,5},{4,2},{5,3},{6,0},{7,1},{8,14},{9,15},{10,... | collective-permute-start | bytes 786440 | tf_op jit(solution)/shard_map/ppermute | solution.py:31
  27.4 0.5 collective-permute-start.5
  27.9 0.5 collective-permute-start.4
  28.5 6.7 %collective-permute-done.6.refs_3_ = bf16[4,2,128,128]{3,2,1,0:T(8,128)(2,1)S(1)} collective-permute-done((bf16[4,2,128,128]{3,2,1,0:T(8,128)(2,1)S(1)}, bf16[4,2,128,128]{3,2,1,0:T(8,128)(2,1)S(1)}, u32[]{:S(2)}, u32[]{:S(2)}) %collective-permute-start.6) | collective-permute-done | bytes 262176 | tf_op jit(solution)/shard_map/ppermute | solution.py:31
  35.2 3.0 %collective-permute-done.5.refs_2_ = bf16[4,2,128,128]{3,2,1,0:T(8,128)(2,1)S(1)} collective-permute-done((bf16[4,2,128,128]{3,2,1,0:T(8,128)(2,1)S(1)}, bf16[4,2,128,128]{3,2,1,0:T(8,128)(2,1)S(1)}, u32[]{:S(2)}, u32[]{:S(2)}) %collective-permute-start.5) | collective-permute-done | bytes 262176 | tf_op jit(solution)/shard_map/ppermute | solution.py:31
  38.2 2.9 %collective-permute-done.3.partner.refs_4_ = bf16[2,1616,128]{2,1,0:T(8,128)(2,1)S(1)} collective-permute-done((bf16[2,1616,128]{2,1,0:T(8,128)(2,1)S(1)}, bf16[2,1616,128]{2,1,0:T(8,128)(2,1)S(1)}, u32[]{:S(2)}, u32[]{:S(2)}) %collective-permute-start.3) | collective-permute-done | bytes 827424 | tf_op jit(solution)/shard_map/ppermute | solution.py:31
  41.6 2.5 %collective-permute-start.10 = (bf16[4,2,144,128]{3,2,1,0:T(8,128)(2,1)S(1)}, bf16[4,2,144,128]{3,2,1,0:T(8,128)(2,1)S(1)}, u32[]{:S(2)}, u32[]{:S(2)}) collective-permute-start(bf16[4,2,144,128]{3,2,1,0:T(8,128)(2,1)S(1)} %stack_kernel.3.refs_0_), channel_id=1, source_target_pairs={{0,6},{1,7},{2,4},{3,5},{4,2},{5,3},{6,0},{7,1},{8,14},{9,15},{10,... | collective-permute-start | bytes 884744 | tf_op jit(solution)/shard_map/ppermute | solution.py:31
  44.1 0.5 collective-permute-start.9
  44.6 0.5 collective-permute-start.8
  45.1 1.0 tiles_kernel.1
  46.1 3.3 %weights_kernel.1 = (f32[2,2,2,1,512]{4,3,2,1,0:T(1,128)S(1)}, bf16[4,1616,512]{2,1,0:T(8,128)(2,1)S(1)}) custom-call(s32[2]{0:T(128)S(1)} %copy-done.4, s32[8]{0:T(128)S(1)} %copy-done.2, s32[8]{0:T(128)S(1)} %copy-done.3, bf16[2,1616,128]{2,1,0:T(8,128)(2,1)S(1)} %get-tuple-element.28.keys, bf16[4,4,2,128,128]{4,3,2,1,0:T(8,128)(2,1)S(1)} %join_kernel.2.refs_0_.refs_3_, ...), custom_call_target="tpu_custom_call" | custom-call | flops 6000000000 | tf_op jit(solution)/shard_map/weights_kernel/pallas_call | solution.py:38
  49.5 2.9 %collective-permute-done.10.refs_3_ = bf16[4,2,144,128]{3,2,1,0:T(8,128)(2,1)S(1)} collective-permute-done((bf16[4,2,144,128]{3,2,1,0:T(8,128)(2,1)S(1)}, bf16[4,2,144,128]{3,2,1,0:T(8,128)(2,1)S(1)}, u32[]{:S(2)}, u32[]{:S(2)}) %collective-permute-start.10) | collective-permute-done | bytes 294944 | tf_op jit(solution)/shard_map/ppermute | solution.py:31
  52.4 5.8 %collective-permute-done.9.refs_2_ = bf16[4,2,144,128]{3,2,1,0:T(8,128)(2,1)S(1)} collective-permute-done((bf16[4,2,144,128]{3,2,1,0:T(8,128)(2,1)S(1)}, bf16[4,2,144,128]{3,2,1,0:T(8,128)(2,1)S(1)}, u32[]{:S(2)}, u32[]{:S(2)}) %collective-permute-start.9) | collective-permute-done | bytes 294944 | tf_op jit(solution)/shard_map/ppermute | solution.py:31
  58.7 0.5 collective-permute-start.12
  59.2 2.4 %collective-permute-done.12 = f32[2,2,2,1,512]{4,3,2,1,0:T(1,128)S(1)} collective-permute-done((f32[2,2,2,1,512]{4,3,2,1,0:T(1,128)S(1)}, f32[2,2,2,1,512]{4,3,2,1,0:T(1,128)S(1)}, u32[]{:S(2)}, u32[]{:S(2)}) %collective-permute-start.12) | collective-permute-done | bytes 16416 | tf_op jit(solution)/shard_map/ppermute | solution.py:31
  61.6 1.7 %collective-permute-start.16 = (f32[2,2,2,2,1,512]{5,4,3,2,1,0:T(1,128)S(1)}, f32[2,2,2,2,1,512]{5,4,3,2,1,0:T(1,128)S(1)}, u32[]{:S(2)}, u32[]{:S(2)}) collective-permute-start(f32[2,2,2,2,1,512]{5,4,3,2,1,0:T(1,128)S(1)} %pad_maximum_fusion.refs_2_.refs_0_), channel_id=1, source_target_pairs={{0,6},{1,7},{2,4},{3,5},{4,2},{5,3},{6,0},{7,1},{8,14},{9,15},{10,... | collective-permute-start | bytes 98312 | tf_op jit(solution)/shard_map/ppermute | solution.py:31
  63.3 1.3 %collective-permute-start.15 = (f32[2,2,2,2,1,512]{5,4,3,2,1,0:T(1,128)S(1)}, f32[2,2,2,2,1,512]{5,4,3,2,1,0:T(1,128)S(1)}, u32[]{:S(2)}, u32[]{:S(2)}) collective-permute-start(f32[2,2,2,2,1,512]{5,4,3,2,1,0:T(1,128)S(1)} %pad_maximum_fusion.refs_2_.refs_0_), channel_id=1, source_target_pairs={{0,4},{1,5},{2,6},{3,7},{4,0},{5,1},{6,2},{7,3},{8,12},{9,13},{10,... | collective-permute-start | bytes 98312 | tf_op jit(solution)/shard_map/ppermute | solution.py:31
  64.6 0.5 collective-permute-start.14
  65.1 2.7 %slopes_kernel.1 = (bf16[4,1616,512]{2,1,0:T(8,128)(2,1)S(1)}, bf16[2,2,144,512]{3,2,1,0:T(8,128)(2,1)S(1)}) custom-call(s32[2]{0:T(128)S(1)} %copy-done.4, s32[8]{0:T(128)S(1)} %copy-done.2, s32[8]{0:T(128)S(1)} %copy-done.3, f32[2,2,2,1,512]{4,3,2,1,0:T(1,128)S(1)} %get-tuple-element.30.refs_4_.stats, ...), custom_call_target="tpu_custom_call" | custom-call | flops 6000000000 | tf_op jit(solution)/shard_map/slopes_kernel/pallas_call | solution.py:38
  67.8 1.2 %collective-permute-start.13 = (bf16[2,2,144,512]{3,2,1,0:T(8,128)(2,1)S(1)}, bf16[2,2,144,512]{3,2,1,0:T(8,128)(2,1)S(1)}, u32[]{:S(2)}, u32[]{:S(2)}) collective-permute-start(bf16[2,2,144,512]{3,2,1,0:T(8,128)(2,1)S(1)} %get-tuple-element.34.own), channel_id=1, source_target_pairs={{0,1},{1,0},{2,3},{3,2},{4,5},{5,4},{6,7},{7,6},{8,9},{9,8},{10,11... | collective-permute-start | bytes 1769480 | tf_op jit(solution)/shard_map/ppermute | solution.py:31
  69.0 0.8 factors_kernel.1.refs_0_.refs_2_
  69.8 0.8 collective-permute-done.13.other
  70.6 2.0 %route_kernel.1 = (bf16[2,144,512]{2,1,0:T(8,128)(2,1)S(1)}, bf16[2,144,512]{2,1,0:T(8,128)(2,1)S(1)}, bf16[2,144,512]{2,1,0:T(8,128)(2,1)S(1)}, bf16[2,144,512]{2,1,0:T(8,128)(2,1)S(1)}) custom-call(s32[2]{0:T(128)S(1)} %copy-done.4, s32[8]{0:T(128)S(1)} %copy-done.2, s32[8]{0:T(128)S(1)} %copy-done.3, bf16[2,2,144,512]{3,2,1,0:T(8,128)(2,1)S(1)} %get-tuple-element.34.own, ...), custom_call_target="tpu_custom_call" | custom-call | flops 30000001024 | tf_op jit(solution)/shard_map/route_kernel/pallas_call | solution.py:38
  72.6 1.6 %collective-permute-start.17 = (bf16[2,144,512]{2,1,0:T(8,128)(2,1)S(1)}, bf16[2,144,512]{2,1,0:T(8,128)(2,1)S(1)}, u32[]{:S(2)}, u32[]{:S(2)}) collective-permute-start(bf16[2,144,512]{2,1,0:T(8,128)(2,1)S(1)} %get-tuple-element.36), channel_id=1, source_target_pairs={{0,2},{1,3},{2,0},{3,1},{4,6},{5,7},{6,4},{7,5},{8,10},{9,11},{10,... | collective-permute-start | bytes 884744 | tf_op jit(solution)/shard_map/ppermute | solution.py:31
  74.2 1.1 collective-permute-start.18
  75.2 1.4 %collective-permute-start.19 = (bf16[2,144,512]{2,1,0:T(8,128)(2,1)S(1)}, bf16[2,144,512]{2,1,0:T(8,128)(2,1)S(1)}, u32[]{:S(2)}, u32[]{:S(2)}) collective-permute-start(bf16[2,144,512]{2,1,0:T(8,128)(2,1)S(1)} %get-tuple-element.38), channel_id=1, source_target_pairs={{0,6},{1,7},{2,4},{3,5},{4,2},{5,3},{6,0},{7,1},{8,14},{9,15},{10,... | collective-permute-start | bytes 884744 | tf_op jit(solution)/shard_map/ppermute | solution.py:31
  76.6 0.9 sums_kernel.3
  77.5 1.8 %collective-permute-start.24 = (bf16[1616,128]{1,0:T(8,128)(2,1)S(1)}, bf16[1616,128]{1,0:T(8,128)(2,1)S(1)}, u32[]{:S(2)}, u32[]{:S(2)}) collective-permute-start(bf16[1616,128]{1,0:T(8,128)(2,1)S(1)} %get-tuple-element.47), channel_id=1, source_target_pairs={{0,8},{8,0},{16,24},{24,16},{1,9},{9,1},{17,25},{25,17},{2,10},{10... | collective-permute-start | bytes 1241096 | tf_op jit(solution)/shard_map/ppermute | solution.py:31
  79.3 3.3 %sums_kernel.2 = (bf16[1616,128]{1,0:T(8,128)(2,1)S(1)}, bf16[1616,128]{1,0:T(8,128)(2,1)S(1)}) custom-call(s32[2]{0:T(128)S(1)} %copy-done.4, s32[8]{0:T(128)S(1)} %copy-done.2, s32[8]{0:T(128)S(1)} %copy-done.3, bf16[4,1616,512]{2,1,0:T(8,128)(2,1)S(1)} %get-tuple-element.31.weights.refs_0_, bf16[4,1616,512]{2,1,0:T(8,128)(2,1)S(1)} %get-tuple-element.43.refs_1_, ...), custom_call_target="tpu_custom_call" | custom-call | flops 4000000000 | tf_op jit(solution)/shard_map/sums_kernel/pallas_call | solution.py:38
  82.6 0.3 collective-permute-start.23
  83.0 5.2 %collective-permute-done.18.refs_2_ = bf16[2,144,512]{2,1,0:T(8,128)(2,1)S(1)} collective-permute-done((bf16[2,144,512]{2,1,0:T(8,128)(2,1)S(1)}, bf16[2,144,512]{2,1,0:T(8,128)(2,1)S(1)}, u32[]{:S(2)}, u32[]{:S(2)}) %collective-permute-start.18) | collective-permute-done | bytes 294944 | tf_op jit(solution)/shard_map/ppermute | solution.py:31
  88.1 1.8 %collective-permute-done.19.refs_3_ = bf16[2,144,512]{2,1,0:T(8,128)(2,1)S(1)} collective-permute-done((bf16[2,144,512]{2,1,0:T(8,128)(2,1)S(1)}, bf16[2,144,512]{2,1,0:T(8,128)(2,1)S(1)}, u32[]{:S(2)}, u32[]{:S(2)}) %collective-permute-start.19) | collective-permute-done | bytes 294944 | tf_op jit(solution)/shard_map/ppermute | solution.py:31
  90.3 1.8 %collective-permute-start.20 = (bf16[128,256]{1,0:T(8,128)(2,1)S(1)}, bf16[128,256]{1,0:T(8,128)(2,1)S(1)}, u32[]{:S(2)}, u32[]{:S(2)}) collective-permute-start(bf16[128,256]{1,0:T(8,128)(2,1)S(1)} %get-tuple-element.40), channel_id=1, source_target_pairs={{0,8},{8,0},{16,24},{24,16},{1,9},{9,1},{17,25},{25,17},{2,10},{10... | collective-permute-start | bytes 196616 | tf_op jit(solution)/shard_map/ppermute | solution.py:31
  92.1 1.5 %collective-permute-start.21 = (bf16[128,256]{1,0:T(8,128)(2,1)S(1)}, bf16[128,256]{1,0:T(8,128)(2,1)S(1)}, u32[]{:S(2)}, u32[]{:S(2)}) collective-permute-start(bf16[128,256]{1,0:T(8,128)(2,1)S(1)} %get-tuple-element.41), channel_id=1, source_target_pairs={{0,16},{8,24},{16,0},{24,8},{1,17},{9,25},{17,1},{25,9},{2,18},{10... | collective-permute-start | bytes 196616 | tf_op jit(solution)/shard_map/ppermute | solution.py:31
  93.6 1.2 %collective-permute-start.22 = (bf16[128,256]{1,0:T(8,128)(2,1)S(1)}, bf16[128,256]{1,0:T(8,128)(2,1)S(1)}, u32[]{:S(2)}, u32[]{:S(2)}) collective-permute-start(bf16[128,256]{1,0:T(8,128)(2,1)S(1)} %get-tuple-element.42), channel_id=1, source_target_pairs={{0,24},{8,16},{16,8},{24,0},{1,25},{9,17},{17,9},{25,1},{2,26},{10... | collective-permute-start | bytes 196616 | tf_op jit(solution)/shard_map/ppermute | solution.py:31
  94.8 5.9 %collective-permute-done.20.refs_1_ = bf16[128,256]{1,0:T(8,128)(2,1)S(1)} collective-permute-done((bf16[128,256]{1,0:T(8,128)(2,1)S(1)}, bf16[128,256]{1,0:T(8,128)(2,1)S(1)}, u32[]{:S(2)}, u32[]{:S(2)}) %collective-permute-start.20) | collective-permute-done | bytes 65568 | tf_op jit(solution)/shard_map/ppermute | solution.py:31
  100.7 3.8 %collective-permute-done.22.refs_3_ = bf16[128,256]{1,0:T(8,128)(2,1)S(1)} collective-permute-done((bf16[128,256]{1,0:T(8,128)(2,1)S(1)}, bf16[128,256]{1,0:T(8,128)(2,1)S(1)}, u32[]{:S(2)}, u32[]{:S(2)}) %collective-permute-start.22) | collective-permute-done | bytes 65568 | tf_op jit(solution)/shard_map/ppermute | solution.py:31
  104.5 1.3 %place_kernel.1 = bf16[128,1024]{1,0:T(8,128)(2,1)} custom-call(s32[2]{0:T(128)S(1)} %copy-done.4, bf16[128,256]{1,0:T(8,128)(2,1)S(1)} %get-tuple-element.39.refs_0_, bf16[128,256]{1,0:T(8,128)(2,1)S(1)} %collective-permute-done.20.refs_1_, bf16[128,256]{1,0:T(8,128)(2,1)S(1)} %collective-permute-done.21.refs_2_, ...), custom_call_target="tpu_custom_call" | custom-call | flops 1000000000 | tf_op jit(solution)/shard_map/place_kernel/pallas_call | solution.py:38
  105.8 2.0 %merge_kernel.1 = bf16[1601,2,128]{2,1,0:T(2,128)(2,1)} custom-call(bf16[1616,128]{1,0:T(8,128)(2,1)S(1)} %get-tuple-element.44.refs_0_, bf16[1616,128]{1,0:T(8,128)(2,1)S(1)} %get-tuple-element.45.refs_1_, bf16[1616,128]{1,0:T(8,128)(2,1)S(1)} %collective-permute-done.23.refs_2_, bf16[1616,128]{1,0:T(8,128)(2,1)S(1)} %collective-permute-done.24.refs_3_), custom_call_target="tpu_custom_call" | custom-call | flops 2000000000 | tf_op jit(solution)/shard_map/merge_kernel/pallas_call | solution.py:38
  (31 shorter events, 1.6 us)
Async XLA Ops:
  1.9 43.2 %copy-start.4 = (s32[2]{0:T(128)S(1)}, s32[2]{0:T(128)}, u32[]{:S(2)}) copy-start(s32[2]{0:T(128)} %pad_add_fusion.who) | copy-start | bytes 28
  4.8 36.5 %copy-start.1 = (bf16[2,272,128]{2,1,0:T(8,128)(2,1)S(1)}, bf16[2,272,128]{2,1,0:T(8,128)(2,1)}, u32[]{:S(2)}) copy-start(bf16[2,272,128]{2,1,0:T(8,128)(2,1)} %get-tuple-element.29.refs_0_) | copy-start | bytes 417796
  4.8 8.7 %collective-permute-start = (bf16[2,272,128]{2,1,0:T(8,128)(2,1)}, bf16[2,272,128]{2,1,0:T(8,128)(2,1)S(1)}, u32[]{:S(2)}, u32[]{:S(2)}) collective-permute-start(bf16[2,272,128]{2,1,0:T(8,128)(2,1)} %get-tuple-element.25), channel_id=1, source_target_pairs={{0,8},{8,0},{16,24},{24,16},{1,9},{9,1},{17,25},{25,17},{2,10},{10... | collective-permute-start | bytes 417800 | tf_op jit(solution)/shard_map/ppermute | solution.py:31
  7.9 13.7 %collective-permute-start.1 = (bf16[2,272,128]{2,1,0:T(8,128)(2,1)}, bf16[2,272,128]{2,1,0:T(8,128)(2,1)S(1)}, u32[]{:S(2)}, u32[]{:S(2)}) collective-permute-start(bf16[2,272,128]{2,1,0:T(8,128)(2,1)} %get-tuple-element.26), channel_id=1, source_target_pairs={{0,16},{8,24},{16,0},{24,8},{1,17},{9,25},{17,1},{25,9},{2,18},{10... | collective-permute-start | bytes 417800 | tf_op jit(solution)/shard_map/ppermute | solution.py:31
  10.5 11.1 %collective-permute-start.2 = (bf16[2,272,128]{2,1,0:T(8,128)(2,1)}, bf16[2,272,128]{2,1,0:T(8,128)(2,1)S(1)}, u32[]{:S(2)}, u32[]{:S(2)}) collective-permute-start(bf16[2,272,128]{2,1,0:T(8,128)(2,1)} %get-tuple-element.27), channel_id=1, source_target_pairs={{0,24},{8,16},{16,8},{24,0},{1,25},{9,17},{17,9},{25,1},{2,26},{10... | collective-permute-start | bytes 417800 | tf_op jit(solution)/shard_map/ppermute | solution.py:31
  11.7 34.4 %copy-start.2 = (s32[8]{0:T(128)S(1)}, s32[8]{0:T(128)}, u32[]{:S(2)}) copy-start(s32[8]{0:T(128)} %counts.11) | copy-start | bytes 100
  11.7 34.4 %copy-start.3 = (s32[8]{0:T(128)S(1)}, s32[8]{0:T(128)}, u32[]{:S(2)}) copy-start(s32[8]{0:T(128)} %perm.11) | copy-start | bytes 100
  21.6 19.5 %collective-permute-start.3 = (bf16[2,1616,128]{2,1,0:T(8,128)(2,1)S(1)}, bf16[2,1616,128]{2,1,0:T(8,128)(2,1)S(1)}, u32[]{:S(2)}, u32[]{:S(2)}) collective-permute-start(bf16[2,1616,128]{2,1,0:T(8,128)(2,1)S(1)} %pad_kernel.1.own.refs_4_), channel_id=1, source_target_pairs={{0,8},{8,0},{16,24},{24,16},{1,9},{9,1},{17,25},{25,17},{2,10},{10... | collective-permute-start | bytes 2482184 | tf_op jit(solution)/shard_map/ppermute | solution.py:31
  23.8 0.9 copy-start
  24.9 10.2 %collective-permute-start.6 = (bf16[4,2,128,128]{3,2,1,0:T(8,128)(2,1)S(1)}, bf16[4,2,128,128]{3,2,1,0:T(8,128)(2,1)S(1)}, u32[]{:S(2)}, u32[]{:S(2)}) collective-permute-start(bf16[4,2,128,128]{3,2,1,0:T(8,128)(2,1)S(1)} %stack_kernel.2.refs_0_), channel_id=1, source_target_pairs={{0,6},{1,7},{2,4},{3,5},{4,2},{5,3},{6,0},{7,1},{8,14},{9,15},{10,... | collective-permute-start | bytes 786440 | tf_op jit(solution)/shard_map/ppermute | solution.py:31
  27.4 10.7 %collective-permute-start.5 = (bf16[4,2,128,128]{3,2,1,0:T(8,128)(2,1)S(1)}, bf16[4,2,128,128]{3,2,1,0:T(8,128)(2,1)S(1)}, u32[]{:S(2)}, u32[]{:S(2)}) collective-permute-start(bf16[4,2,128,128]{3,2,1,0:T(8,128)(2,1)S(1)} %stack_kernel.2.refs_0_), channel_id=1, source_target_pairs={{0,4},{1,5},{2,6},{3,7},{4,0},{5,1},{6,2},{7,3},{8,12},{9,13},{10,... | collective-permute-start | bytes 786440 | tf_op jit(solution)/shard_map/ppermute | solution.py:31
  27.9 10.3 %collective-permute-start.4 = (bf16[4,2,128,128]{3,2,1,0:T(8,128)(2,1)S(1)}, bf16[4,2,128,128]{3,2,1,0:T(8,128)(2,1)S(1)}, u32[]{:S(2)}, u32[]{:S(2)}) collective-permute-start(bf16[4,2,128,128]{3,2,1,0:T(8,128)(2,1)S(1)} %stack_kernel.2.refs_0_), channel_id=1, source_target_pairs={{0,2},{1,3},{2,0},{3,1},{4,6},{5,7},{6,4},{7,5},{8,10},{9,11},{10,... | collective-permute-start | bytes 786440 | tf_op jit(solution)/shard_map/ppermute | solution.py:31
  41.2 4.9 %collective-permute-start.7 = (bf16[4,4,2,128,128]{4,3,2,1,0:T(8,128)(2,1)S(1)}, bf16[4,4,2,128,128]{4,3,2,1,0:T(8,128)(2,1)S(1)}, u32[]{:S(2)}, u32[]{:S(2)}) collective-permute-start(bf16[4,4,2,128,128]{4,3,2,1,0:T(8,128)(2,1)S(1)} %join_kernel.2.refs_0_.refs_3_), channel_id=1, source_target_pairs={{0,1},{1,0},{2,3},{3,2},{4,5},{5,4},{6,7},{7,6},{8,9},{9,8},{10,11... | collective-permute-start | bytes 3145736 | tf_op jit(solution)/shard_map/ppermute | solution.py:31
  41.6 10.8 %collective-permute-start.10 = (bf16[4,2,144,128]{3,2,1,0:T(8,128)(2,1)S(1)}, bf16[4,2,144,128]{3,2,1,0:T(8,128)(2,1)S(1)}, u32[]{:S(2)}, u32[]{:S(2)}) collective-permute-start(bf16[4,2,144,128]{3,2,1,0:T(8,128)(2,1)S(1)} %stack_kernel.3.refs_0_), channel_id=1, source_target_pairs={{0,6},{1,7},{2,4},{3,5},{4,2},{5,3},{6,0},{7,1},{8,14},{9,15},{10,... | collective-permute-start | bytes 884744 | tf_op jit(solution)/shard_map/ppermute | solution.py:31
  44.1 14.2 %collective-permute-start.9 = (bf16[4,2,144,128]{3,2,1,0:T(8,128)(2,1)S(1)}, bf16[4,2,144,128]{3,2,1,0:T(8,128)(2,1)S(1)}, u32[]{:S(2)}, u32[]{:S(2)}) collective-permute-start(bf16[4,2,144,128]{3,2,1,0:T(8,128)(2,1)S(1)} %stack_kernel.3.refs_0_), channel_id=1, source_target_pairs={{0,4},{1,5},{2,6},{3,7},{4,0},{5,1},{6,2},{7,3},{8,12},{9,13},{10,... | collective-permute-start | bytes 884744 | tf_op jit(solution)/shard_map/ppermute | solution.py:31
  44.6 13.7 %collective-permute-start.8 = (bf16[4,2,144,128]{3,2,1,0:T(8,128)(2,1)S(1)}, bf16[4,2,144,128]{3,2,1,0:T(8,128)(2,1)S(1)}, u32[]{:S(2)}, u32[]{:S(2)}) collective-permute-start(bf16[4,2,144,128]{3,2,1,0:T(8,128)(2,1)S(1)} %stack_kernel.3.refs_0_), channel_id=1, source_target_pairs={{0,2},{1,3},{2,0},{3,1},{4,6},{5,7},{6,4},{7,5},{8,10},{9,11},{10,... | collective-permute-start | bytes 884744 | tf_op jit(solution)/shard_map/ppermute | solution.py:31
  58.6 6.5 %collective-permute-start.11 = (bf16[4,4,2,144,128]{4,3,2,1,0:T(8,128)(2,1)S(1)}, bf16[4,4,2,144,128]{4,3,2,1,0:T(8,128)(2,1)S(1)}, u32[]{:S(2)}, u32[]{:S(2)}) collective-permute-start(bf16[4,4,2,144,128]{4,3,2,1,0:T(8,128)(2,1)S(1)} %join_kernel.3.refs_0_.refs_5_), channel_id=1, source_target_pairs={{0,1},{1,0},{2,3},{3,2},{4,5},{5,4},{6,7},{7,6},{8,9},{9,8},{10,11... | collective-permute-start | bytes 3538952 | tf_op jit(solution)/shard_map/ppermute | solution.py:31
  58.7 2.9 %collective-permute-start.12 = (f32[2,2,2,1,512]{4,3,2,1,0:T(1,128)S(1)}, f32[2,2,2,1,512]{4,3,2,1,0:T(1,128)S(1)}, u32[]{:S(2)}, u32[]{:S(2)}) collective-permute-start(f32[2,2,2,1,512]{4,3,2,1,0:T(1,128)S(1)} %get-tuple-element.30.refs_4_.stats), channel_id=1, source_target_pairs={{0,1},{1,0},{2,3},{3,2},{4,5},{5,4},{6,7},{7,6},{8,9},{9,8},{10,11... | collective-permute-start | bytes 49160 | tf_op jit(solution)/shard_map/ppermute | solution.py:31
  61.6 7.4 %collective-permute-start.16 = (f32[2,2,2,2,1,512]{5,4,3,2,1,0:T(1,128)S(1)}, f32[2,2,2,2,1,512]{5,4,3,2,1,0:T(1,128)S(1)}, u32[]{:S(2)}, u32[]{:S(2)}) collective-permute-start(f32[2,2,2,2,1,512]{5,4,3,2,1,0:T(1,128)S(1)} %pad_maximum_fusion.refs_2_.refs_0_), channel_id=1, source_target_pairs={{0,6},{1,7},{2,4},{3,5},{4,2},{5,3},{6,0},{7,1},{8,14},{9,15},{10,... | collective-permute-start | bytes 98312 | tf_op jit(solution)/shard_map/ppermute | solution.py:31
  63.3 5.7 %collective-permute-start.15 = (f32[2,2,2,2,1,512]{5,4,3,2,1,0:T(1,128)S(1)}, f32[2,2,2,2,1,512]{5,4,3,2,1,0:T(1,128)S(1)}, u32[]{:S(2)}, u32[]{:S(2)}) collective-permute-start(f32[2,2,2,2,1,512]{5,4,3,2,1,0:T(1,128)S(1)} %pad_maximum_fusion.refs_2_.refs_0_), channel_id=1, source_target_pairs={{0,4},{1,5},{2,6},{3,7},{4,0},{5,1},{6,2},{7,3},{8,12},{9,13},{10,... | collective-permute-start | bytes 98312 | tf_op jit(solution)/shard_map/ppermute | solution.py:31
  64.6 4.4 %collective-permute-start.14 = (f32[2,2,2,2,1,512]{5,4,3,2,1,0:T(1,128)S(1)}, f32[2,2,2,2,1,512]{5,4,3,2,1,0:T(1,128)S(1)}, u32[]{:S(2)}, u32[]{:S(2)}) collective-permute-start(f32[2,2,2,2,1,512]{5,4,3,2,1,0:T(1,128)S(1)} %pad_maximum_fusion.refs_2_.refs_0_), channel_id=1, source_target_pairs={{0,2},{1,3},{2,0},{3,1},{4,6},{5,7},{6,4},{7,5},{8,10},{9,11},{10,... | collective-permute-start | bytes 98312 | tf_op jit(solution)/shard_map/ppermute | solution.py:31
  67.8 2.8 %collective-permute-start.13 = (bf16[2,2,144,512]{3,2,1,0:T(8,128)(2,1)S(1)}, bf16[2,2,144,512]{3,2,1,0:T(8,128)(2,1)S(1)}, u32[]{:S(2)}, u32[]{:S(2)}) collective-permute-start(bf16[2,2,144,512]{3,2,1,0:T(8,128)(2,1)S(1)} %get-tuple-element.34.own), channel_id=1, source_target_pairs={{0,1},{1,0},{2,3},{3,2},{4,5},{5,4},{6,7},{7,6},{8,9},{9,8},{10,11... | collective-permute-start | bytes 1769480 | tf_op jit(solution)/shard_map/ppermute | solution.py:31
  72.6 10.4 %collective-permute-start.17 = (bf16[2,144,512]{2,1,0:T(8,128)(2,1)S(1)}, bf16[2,144,512]{2,1,0:T(8,128)(2,1)S(1)}, u32[]{:S(2)}, u32[]{:S(2)}) collective-permute-start(bf16[2,144,512]{2,1,0:T(8,128)(2,1)S(1)} %get-tuple-element.36), channel_id=1, source_target_pairs={{0,2},{1,3},{2,0},{3,1},{4,6},{5,7},{6,4},{7,5},{8,10},{9,11},{10,... | collective-permute-start | bytes 884744 | tf_op jit(solution)/shard_map/ppermute | solution.py:31
  74.2 13.9 %collective-permute-start.18 = (bf16[2,144,512]{2,1,0:T(8,128)(2,1)S(1)}, bf16[2,144,512]{2,1,0:T(8,128)(2,1)S(1)}, u32[]{:S(2)}, u32[]{:S(2)}) collective-permute-start(bf16[2,144,512]{2,1,0:T(8,128)(2,1)S(1)} %get-tuple-element.37), channel_id=1, source_target_pairs={{0,4},{1,5},{2,6},{3,7},{4,0},{5,1},{6,2},{7,3},{8,12},{9,13},{10,... | collective-permute-start | bytes 884744 | tf_op jit(solution)/shard_map/ppermute | solution.py:31
  75.2 14.7 %collective-permute-start.19 = (bf16[2,144,512]{2,1,0:T(8,128)(2,1)S(1)}, bf16[2,144,512]{2,1,0:T(8,128)(2,1)S(1)}, u32[]{:S(2)}, u32[]{:S(2)}) collective-permute-start(bf16[2,144,512]{2,1,0:T(8,128)(2,1)S(1)} %get-tuple-element.38), channel_id=1, source_target_pairs={{0,6},{1,7},{2,4},{3,5},{4,2},{5,3},{6,0},{7,1},{8,14},{9,15},{10,... | collective-permute-start | bytes 884744 | tf_op jit(solution)/shard_map/ppermute | solution.py:31
  77.5 28.3 %collective-permute-start.24 = (bf16[1616,128]{1,0:T(8,128)(2,1)S(1)}, bf16[1616,128]{1,0:T(8,128)(2,1)S(1)}, u32[]{:S(2)}, u32[]{:S(2)}) collective-permute-start(bf16[1616,128]{1,0:T(8,128)(2,1)S(1)} %get-tuple-element.47), channel_id=1, source_target_pairs={{0,8},{8,0},{16,24},{24,16},{1,9},{9,1},{17,25},{25,17},{2,10},{10... | collective-permute-start | bytes 1241096 | tf_op jit(solution)/shard_map/ppermute | solution.py:31
  82.6 23.2 %collective-permute-start.23 = (bf16[1616,128]{1,0:T(8,128)(2,1)S(1)}, bf16[1616,128]{1,0:T(8,128)(2,1)S(1)}, u32[]{:S(2)}, u32[]{:S(2)}) collective-permute-start(bf16[1616,128]{1,0:T(8,128)(2,1)S(1)} %get-tuple-element.46), channel_id=1, source_target_pairs={{0,8},{8,0},{16,24},{24,16},{1,9},{9,1},{17,25},{25,17},{2,10},{10... | collective-permute-start | bytes 1241096 | tf_op jit(solution)/shard_map/ppermute | solution.py:31
  90.3 10.4 %collective-permute-start.20 = (bf16[128,256]{1,0:T(8,128)(2,1)S(1)}, bf16[128,256]{1,0:T(8,128)(2,1)S(1)}, u32[]{:S(2)}, u32[]{:S(2)}) collective-permute-start(bf16[128,256]{1,0:T(8,128)(2,1)S(1)} %get-tuple-element.40), channel_id=1, source_target_pairs={{0,8},{8,0},{16,24},{24,16},{1,9},{9,1},{17,25},{25,17},{2,10},{10... | collective-permute-start | bytes 196616 | tf_op jit(solution)/shard_map/ppermute | solution.py:31
  92.1 8.6 %collective-permute-start.21 = (bf16[128,256]{1,0:T(8,128)(2,1)S(1)}, bf16[128,256]{1,0:T(8,128)(2,1)S(1)}, u32[]{:S(2)}, u32[]{:S(2)}) collective-permute-start(bf16[128,256]{1,0:T(8,128)(2,1)S(1)} %get-tuple-element.41), channel_id=1, source_target_pairs={{0,16},{8,24},{16,0},{24,8},{1,17},{9,25},{17,1},{25,9},{2,18},{10... | collective-permute-start | bytes 196616 | tf_op jit(solution)/shard_map/ppermute | solution.py:31
  93.6 10.9 %collective-permute-start.22 = (bf16[128,256]{1,0:T(8,128)(2,1)S(1)}, bf16[128,256]{1,0:T(8,128)(2,1)S(1)}, u32[]{:S(2)}, u32[]{:S(2)}) collective-permute-start(bf16[128,256]{1,0:T(8,128)(2,1)S(1)} %get-tuple-element.42), channel_id=1, source_target_pairs={{0,24},{8,16},{16,8},{24,0},{1,25},{9,17},{17,9},{25,1},{2,26},{10... | collective-permute-start | bytes 196616 | tf_op jit(solution)/shard_map/ppermute | solution.py:31

commit v5 on v4

v5 whole, which is shorter than its diff:
```python
import functools
import math

import jax
import jax.numpy as jnp
from jax import lax
from jax.experimental import pallas as pl
from jax.experimental.pallas import tpu as pltpu
from jax.sharding import PartitionSpec as P

HEAD_DIM = 128
MAX_TILES = 4
KEY_ROWS = 256
TEXT_CHUNKS = 4
TILE = 16
TERMS = 6
LOWEST = -1e30
SCALE = 1.0 / math.sqrt(HEAD_DIM)
SCALE_LOG2 = SCALE / math.log(2.0)
BF16 = jnp.bfloat16
F32 = jnp.float32

SMEM = pl.BlockSpec(memory_space=pltpu.SMEM)
VMEM = pl.BlockSpec(memory_space=pltpu.VMEM)
ANY = pl.BlockSpec(memory_space=pl.ANY)
HBM = pl.BlockSpec(memory_space=pltpu.HBM)


def whole_tiles(rows):
    return -(-rows // TILE) * TILE


def exchange(block, axis, distance):
    count = lax.axis_size(axis)
    return lax.ppermute(block, axis, [(i, i ^ distance) for i in range(count)])


def call(kernel, out_shape, in_specs, scratch, args, out_specs=None, grid=(), megabytes=16, cost=0):
    many = isinstance(out_shape, (list, tuple))
    if out_specs is None:
        out_specs = [VMEM] * len(out_shape) if many else VMEM
    return pl.pallas_call(
        kernel,
        out_shape=out_shape,
        in_specs=in_specs,
        out_specs=out_specs,
        grid=grid,
        name=getattr(kernel, "func", kernel).__name__,
        scratch_shapes=scratch,
        compiler_params=pltpu.CompilerParams(vmem_limit_bytes=megabytes << 20),
        cost_estimate=pl.CostEstimate(flops=cost * 10**9, bytes_accessed=0, transcendentals=0),
    )(*args)


def place_of(perm_ref, owner, owners):
    first = jnp.int32(0)
    for index in range(owners):
        first = first + jnp.where(perm_ref[index] == owner, index, 0)
    return first


def sample_at(count_ref, place, samples):
    end, sample, start = jnp.int32(0), jnp.int32(0), jnp.int32(0)
    for index in range(samples):
        end = end + count_ref[index]
        passed = place >= end
        sample = sample + passed.astype(jnp.int32)
        start = jnp.where(passed, end, start)
    return sample, start


def pack_kernel(heads, who, length, *refs):
    inputs, outs, buffers, sem = refs[:3], refs[3:-4], refs[-4:-1], refs[-1]
    copies = [pltpu.make_async_copy(a, b, sem.at[i]) for i, (a, b) in enumerate(zip(inputs, buffers))]
    for copy in copies:
        copy.start()
    for copy in copies:
        copy.wait()
    q_ref, o_ref, g_ref = buffers
    rows = q_ref.shape[0]
    seq = who[0]
    position = seq * rows + lax.broadcasted_iota(jnp.int32, (rows, HEAD_DIM), 0)
    keep = position < length[0]
    for j, out in enumerate(outs):
        place = lax.broadcasted_iota(jnp.int32, (out.shape[0] - 2 * heads * rows, HEAD_DIM), 0)
        deltas = jnp.zeros(place.shape, F32)
        for h in range(heads):
            columns = pl.ds(pl.multiple_of(((seq ^ j) * heads + h) * HEAD_DIM, HEAD_DIM), HEAD_DIM)
            grad = jnp.where(keep, g_ref[:, columns].astype(F32), 0.0)
            product = grad * o_ref[:, columns].astype(F32)
            delta = jnp.sum(jnp.transpose(product), axis=0, keepdims=True)
            out[h * rows:(h + 1) * rows] = q_ref[:, columns]
            out[(heads + h) * rows:(heads + h + 1) * rows] = grad.astype(BF16)
            deltas = jnp.where(place == j * heads + h, delta, deltas)
        out[2 * heads * rows:] = deltas.astype(BF16)


def stack_kernel(count, rows, extra, *refs):
    out, buffer, sem = refs[-3:]
    size = rows.stop - rows.start
    copies = [
        pltpu.make_async_copy(refs[i].at[rows], out.at[pl.ds(i * size, size)], sem.at[0, i]) for i in range(count)
    ]
    if extra:
        last = pl.ds(refs[0].shape[0] - extra, extra)
        copies += [pltpu.make_async_copy(refs[i].at[last], buffer.at[i], sem.at[1, i]) for i in range(count)]
    for copy in copies:
        copy.start()
    for copy in copies:
        copy.wait()
    if extra:
        out[count * size:] = sum(buffer[i].astype(F32) for i in range(count)).astype(BF16)


def join_kernel(count, *refs):
    out, sem = refs[-2], refs[-1]
    first = refs[0].shape[0]
    copies = []
    for i in range(count):
        second = refs[count + i].shape[0]
        copies.append(pltpu.make_async_copy(refs[i], out.at[i, pl.ds(0, first)], sem.at[0, i]))
        copies.append(pltpu.make_async_copy(refs[count + i], out.at[i, pl.ds(first, second)], sem.at[1, i]))
    for copy in copies:
        copy.start()
    for copy in copies:
        copy.wait()


def fetch(pieces, relative, target, sem):
    for distance, piece in enumerate(pieces):
        @pl.when(relative == distance)
        def _(piece=piece):
            pltpu.make_async_copy(piece, target, sem).start()


def fetch_pair(pieces, relative, target, sem):
    rows = pl.ds(0, target.shape[0])
    for core, piece in enumerate(pieces):
        @pl.when((relative & 1) == core)
        def _(piece=piece):
            pltpu.make_async_copy(piece.at[lax.shift_right_logical(relative, 1), rows], target, sem).start()


def spans_of(rows):
    full = rows // KEY_ROWS
    tail = rows - full * KEY_ROWS
    return [(i * KEY_ROWS, KEY_ROWS, KEY_ROWS) for i in range(full)] + [(full * KEY_ROWS, -(-tail // 16) * 16, tail)]


def dot_nt(a, b):
    return lax.dot_general(a, b, (((1,), (1,)), ((), ())), preferred_element_type=F32)


def dot_nn(a, b):
    return jnp.dot(a, b, preferred_element_type=F32)


def own_tiles(owners, slots, who, counts, perm):
    first = place_of(perm, who[1], owners)
    return [sample_at(counts, first + slot * owners, owners) for slot in range(slots)]


def pad_kernel(tiles, *refs):
    out = refs[-1]
    for slot in range(tiles.shape[0]):
        for low, size, used in spans_of(tiles.shape[1]):
            if size != used:
                out[slot, low:] = jnp.zeros((size, HEAD_DIM), BF16)
            out[slot, low:low + used] = tiles[slot, low:low + used]


def tiles_kernel(slots, rows, who, own, partner, keys, values, turned):
    for odd in range(2):
        @pl.when((who[0] & 1) == odd)
        def _(odd=odd):
            keys[...] = (own, partner)[odd][...]
            values[...] = (own, partner)[1 - odd][...]
    for slot in range(slots):
        for low, size, _ in spans_of(rows):
            turned[slot, :, low:low + size] = jnp.transpose(keys[slot, low:low + size].astype(F32)).astype(BF16)


def weights_kernel(owners, heads, blocks, slots, rows, who, counts, perm, keys, *refs):
    pieces = refs[:owners]
    notes, weights, text_buf, scores_buf, stats, sem = refs[owners:]
    step = pl.program_id(0)
    spans = spans_of(rows)
    groups = text_buf.shape[1] // (heads * HEAD_DIM)
    chunks = groups // blocks
    width = chunks * HEAD_DIM
    tiles = own_tiles(owners, slots, who, counts, perm)

    @pl.when(step == 0)
    def _():
        for slot in range(slots):
            @pl.when(tiles[slot][0] < owners)
            def _(slot=slot):
                fetch(pieces, tiles[slot][0] ^ who[1], text_buf.at[slot], sem.at[slot])

    for slot in range(slots):
        base = slot * heads * blocks

        @pl.when((step == base) & (tiles[slot][0] < owners))
        def _(slot=slot):
            pltpu.make_async_copy(pieces[0], text_buf.at[slot], sem.at[slot]).wait()

        @pl.when((step >= base) & (step < base + heads * blocks) & (tiles[slot][0] < owners))
        def _(slot=slot, base=base):
            head, block = (step - base) // blocks, (step - base) % blocks
            query = rows_of(text_buf.at[slot], heads, head, block, chunks)
            peak = jnp.full((8, width), -jnp.inf, F32)
            for low, size, used in spans:
                scores = dot_nt(keys[slot, low:low + size], query)
                if size != used:
                    row = lax.broadcasted_iota(jnp.int32, scores.shape, 0)
                    scores = jnp.where(row < used, scores, -jnp.inf)
                scores_buf[low:low + size] = scores
                peak = jnp.maximum(peak, jnp.max(scores.reshape(-1, 8, width), axis=0))
            top = jnp.max(peak, axis=0, keepdims=True) * SCALE_LOG2
            mass = jnp.zeros((8, width), F32)
            for low, size, used in spans:
                part = jnp.exp2(scores_buf[low:low + size] * SCALE_LOG2 - top)
                mass = mass + jnp.sum(part.reshape(-1, 8, width), axis=0)
                weights[0, low:low + size] = part.astype(BF16)
            stats[2 * head, pl.ds(block, 1)] = top
            stats[2 * head + 1, pl.ds(block, 1)] = jnp.sum(mass, axis=0, keepdims=True)

            @pl.when(step == base + heads * blocks - 1)
            def _():
                for done in range(blocks):
                    lines = [stats[index, done:done + 1] for index in range(2 * heads)]
                    full = note_rows(lines)
                    size = full.shape[0]
                    for chunk in range(chunks):
                        first = (slot * groups + done * chunks + chunk) * size
                        notes[first:first + size] = full[:, chunk * HEAD_DIM:(chunk + 1) * HEAD_DIM]


def in_parts(value):
    high = value.astype(BF16).astype(F32)
    middle = (value - high).astype(BF16).astype(F32)
    return [high, middle, value - high - middle]


def note_rows(lines):
    rows = [term for line in lines for term in in_parts(line)]
    index = lax.broadcasted_iota(jnp.int32, (whole_tiles(len(rows)), lines[0].shape[1]), 0)
    result = jnp.zeros(index.shape, F32)
    for place, row in enumerate(rows):
        result = jnp.where(index == place, row, result)
    return result.astype(BF16)


def read_notes(notes, head):
    notes = notes.astype(F32)
    rows = [notes[place:place + 1] for place in range(TERMS * head, TERMS * head + TERMS)]
    return rows[0] + rows[1] + rows[2], rows[3] + rows[4] + rows[5]


def rows_of(text, heads, head, block, chunks):
    first = block * chunks * heads + head
    starts = [pl.multiple_of((first + chunk * heads) * HEAD_DIM, HEAD_DIM) for chunk in range(chunks)]
    return jnp.concatenate([text[pl.ds(start, HEAD_DIM)] for start in starts], axis=0)


def slopes_kernel(owners, heads, blocks, slots, rows, who, counts, perm, notes, weights, values, keys_turned, *refs):
    pieces = refs[:2]
    slopes, turned, text_buf, deltas, sem = refs[-5:]
    step = pl.program_id(0)
    spans = spans_of(rows)
    groups = turned.shape[2] // HEAD_DIM
    chunks = groups // blocks
    text_rows = groups * heads * HEAD_DIM
    width = chunks * HEAD_DIM
    tiles = own_tiles(owners, slots, who, counts, perm)

    @pl.when(step == 0)
    def _():
        for slot in range(slots):
            @pl.when(tiles[slot][0] < owners)
            def _(slot=slot):
                fetch_pair(pieces, tiles[slot][0] ^ who[1], text_buf.at[slot], sem.at[slot])

            @pl.when(tiles[slot][0] >= owners)
            def _(slot=slot):
                turned[slot] = jnp.zeros(turned.shape[1:], BF16)

    for slot in range(slots):
        base = slot * heads * blocks

        @pl.when((step == base) & (tiles[slot][0] < owners))
        def _(slot=slot):
            pltpu.make_async_copy(pieces[0].at[0, pl.ds(0, text_buf.shape[1])], text_buf.at[slot], sem.at[slot]).wait()
            deltas[...] = text_buf[slot, text_rows:].astype(F32)
            size = turned.shape[1] - heads * HEAD_DIM
            for chunk in range(groups):
                first = (slot * groups + chunk) * size
                columns = slice(chunk * HEAD_DIM, (chunk + 1) * HEAD_DIM)
                turned[slot, heads * HEAD_DIM:, columns] = notes[first:first + size]

        @pl.when((step >= base) & (step < base + heads * blocks) & (tiles[slot][0] < owners))
        def _(slot=slot, base=base):
            head, block = (step - base) // blocks, (step - base) % blocks
            grad = rows_of(text_buf.at[slot], heads, head, block, chunks)
            first = block * chunks * heads + head
            delta = jnp.concatenate([deltas[pl.ds(first + chunk * heads, 1)] for chunk in range(chunks)], axis=1)
            for low, size, used in spans:
                slope = dot_nt(values[slot, low:low + size], grad)
                slopes[0, low:low + size] = (weights[0, low:low + size].astype(F32) * (slope - delta)).astype(BF16)
            total = dot_nn(keys_turned[slot, :, :slopes.shape[1]], slopes[0])
            columns = pl.ds(pl.multiple_of(block * width, width), width)
            turned[slot, pl.ds(pl.multiple_of(head * HEAD_DIM, HEAD_DIM), HEAD_DIM), columns] = total.astype(BF16)


def peak_and_mass(notes, owners, heads, groups, me, perm, start, tiles, head, chunk):
    found = []
    size = whole_tiles(TERMS * heads)
    for index in range(MAX_TILES):
        live = index < tiles
        place = jnp.where(live, start + index, start)
        other, slot = perm[place & (owners - 1)] ^ me, lax.div(place, owners)
        first = pl.multiple_of((slot * groups + chunk) * size, size)
        top, mass = read_notes(notes[other, pl.ds(first, size)], head)
        found.append((jnp.where(live, top, -jnp.inf), jnp.where(live, mass, 0.0)))
    top = functools.reduce(jnp.maximum, [peak for peak, _ in found])
    return top, sum(mass * jnp.exp2(peak - top) for peak, mass in found)


def factors_kernel(owners, heads, groups, slots, who, counts, perm, own, other, out, notes, sem):
    copies = []
    rows = notes.shape[1]
    for core, source in enumerate((own, other)):
        for chip in range(owners // 2):
            place = 2 * chip + core
            part = source.at[chip, pl.ds(source.shape[1] - rows, rows)]
            copies.append(pltpu.make_async_copy(part, notes.at[place], sem.at[place]))
    for copy in copies:
        copy.start()
    for copy in copies:
        copy.wait()
    size = whole_tiles(TERMS * heads)
    for slot, (sample, start) in enumerate(own_tiles(owners, slots, who, counts, perm)):
        @pl.when(sample < owners)
        def _(slot=slot, sample=sample, start=start):
            tiles = counts[jnp.minimum(sample, owners - 1)]
            for head in range(heads):
                for chunk in range(groups):
                    top, mass = peak_and_mass(
                        notes, owners, heads, groups, who[1], perm, start, tiles, head, chunk
                    )
                    first = (slot * groups + chunk) * size
                    peak = read_notes(notes[0, first:first + size], head)[0]
                    out[slot, head, chunk:chunk + 1] = jnp.exp2(peak - top) / mass


def sums_kernel(owners, heads, blocks, slots, slot, who, counts, perm, *refs):
    weights, slopes, factors = refs[:3]
    q_pieces, g_pieces = refs[3:3 + owners], refs[3 + owners:5 + owners]
    keep_out, send_out, q_buf, g_buf, sums, sem = refs[-6:]
    step = pl.program_id(0)
    odd, me = who[0] & 1, who[1]
    groups = q_buf.shape[0] // (heads * HEAD_DIM)
    chunks = groups // blocks
    width = chunks * HEAD_DIM
    sample = own_tiles(owners, slots, who, counts, perm)[slot][0]
    used = sample < owners

    @pl.when((step == 0) & used)
    def _():
        fetch(q_pieces, sample ^ me, q_buf, sem.at[0])
        fetch_pair(g_pieces, sample ^ me, g_buf, sem.at[1])
        pltpu.make_async_copy(q_pieces[0], q_buf, sem.at[0]).wait()
        pltpu.make_async_copy(g_pieces[0].at[0, pl.ds(0, g_buf.shape[0])], g_buf, sem.at[1]).wait()

    @pl.when(jnp.logical_not(used))
    def _():
        keep_out[...] = jnp.zeros(keep_out.shape, BF16)
        send_out[...] = jnp.zeros(send_out.shape, BF16)

    @pl.when(used)
    def _():
        head, block = step // blocks, step % blocks
        factor = jnp.concatenate(
            [factors[slot, head, pl.ds(block * chunks + chunk, 1)] for chunk in range(chunks)], axis=1
        )
        factor = jnp.transpose(jnp.broadcast_to(factor, (HEAD_DIM, width)))
        query = rows_of(q_buf, heads, head, block, chunks)
        grad = rows_of(g_buf, heads, head, block, chunks)
        query = (query.astype(F32) * factor * SCALE).astype(BF16)
        grad = (grad.astype(F32) * factor).astype(BF16)

        def add(which, source, right, fresh):
            for low in range(0, sums.shape[1], 2 * KEY_ROWS):
                span = slice(low, min(low + 2 * KEY_ROWS, sums.shape[1]))
                part = dot_nn(source[0, span], right)
                sums[which, span] = part if fresh else sums[which, span] + part

        for fresh in (True, False):
            @pl.when((step == 0) == fresh)
            def _(fresh=fresh):
                add(0, slopes, query, fresh)
                add(1, weights, grad, fresh)

        @pl.when(step == heads * blocks - 1)
        def _():
            keep_out[...] = sums[odd].astype(BF16)
            send_out[...] = sums[1 - odd].astype(BF16)


def route_kernel(owners, heads, blocks, slots, who, counts, perm, own, other, *refs):
    outs = refs[-(owners // 2):]
    me = who[1]
    width = own.shape[2] // blocks
    split = heads * HEAD_DIM
    found = []
    for near in range(2):
        first = place_of(perm, me ^ near, owners)
        for slot in range(slots):
            found.append((near, slot, sample_at(counts, first + slot * owners, owners)[0]))

    def one(block, carry):
        columns = pl.ds(pl.multiple_of(block * width, width), width)
        sources = [(own, other)[near].at[slot] for near, slot, _ in found]
        notes = [source[split:, columns] for source in sources]
        lines = [[] for _ in outs]
        for head in range(heads):
            rows = slice(head * HEAD_DIM, (head + 1) * HEAD_DIM)
            parts = [source[rows, columns].astype(F32) for source in sources]
            known = [read_notes(note, head) for note in notes]
            for distance, out in enumerate(outs):
                live = [sample == me ^ (2 * distance) for _, _, sample in found]
                tops = [jnp.where(hit, note[0], LOWEST) for hit, note in zip(live, known)]
                top = functools.reduce(jnp.maximum, tops)
                factors = [jnp.where(hit, jnp.exp2(peak - top), 0.0) for hit, peak in zip(live, tops)]
                mass = sum(note[1] * factor for note, factor in zip(known, factors))
                out[rows, columns] = sum(part * factor for part, factor in zip(parts, factors)).astype(BF16)
                lines[distance] += [top, mass]
        for distance, out in enumerate(outs):
            out[split:, columns] = note_rows(lines[distance])
        return carry

    lax.fori_loop(0, blocks, one, 0)


def gather_kernel(heads, parts, *refs):
    outs = refs[parts:]
    rows = outs[0].shape[0]
    split = heads * HEAD_DIM
    for piece, out in enumerate(outs):
        span = slice(piece * rows, (piece + 1) * rows)
        blocks = [ref[split:, span] for ref in refs[:parts]]
        for head in range(heads):
            lanes = slice(head * HEAD_DIM, (head + 1) * HEAD_DIM)
            notes = [read_notes(block, head) for block in blocks]
            top = functools.reduce(jnp.maximum, [note[0] for note in notes])
            factors = [jnp.exp2(note[0] - top) for note in notes]
            mass = sum(note[1] * factor for note, factor in zip(notes, factors))
            total = sum(ref[lanes, span].astype(F32) * factor for ref, factor in zip(refs[:parts], factors))
            out[:, lanes] = jnp.transpose(total * (SCALE / mass)).astype(BF16)


def place_kernel(who, *refs):
    out = refs[-1]
    for distance, ref in enumerate(refs[:-2]):
        width = ref.shape[1]
        start = pl.multiple_of((who[0] ^ distance) * width, width)
        out[:, pl.ds(start, width)] = ref[...]


def merge_kernel(slots, *refs):
    keep, got, out, done = refs[:slots], refs[slots:-2], refs[-2], refs[-1]
    done[...] = jnp.zeros(done.shape, BF16)
    for low, size, used in spans_of(out.shape[0]):
        row = lax.broadcasted_iota(jnp.int32, (slots * size, slots * size), 0)
        column = lax.broadcasted_iota(jnp.int32, (slots * size, slots * size), 1)
        source = lax.rem(row, slots) * size + lax.div(row, slots)
        order = (source == column).astype(BF16)
        total = [
            (keep[slot][low:low + size].astype(F32) + got[slot][low:low + size].astype(F32)).astype(BF16)
            for slot in range(slots)
        ]
        mixed = dot_nn(order, jnp.concatenate(total, axis=0)).astype(BF16).reshape(size, slots, HEAD_DIM)
        out[low:low + used] = mixed[:used]


def shards(queries, saved_output, grad_out, tile_kv, tile_count, owner_perm, text_len):
    rows_dev, features = queries.shape[1], queries.shape[2]
    groups, owners = lax.axis_size("seq"), lax.axis_size("dp")
    heads = features // HEAD_DIM // groups
    width = heads * HEAD_DIM
    chunks = min(TEXT_CHUNKS, groups)
    blocks = groups // chunks
    text_rows, block_rows = groups * rows_dev, chunks * rows_dev
    steps = heads * blocks
    slots, tile_rows = tile_kv.shape[0], tile_kv.shape[1]
    low, tail_rows, _ = spans_of(tile_rows)[-1]
    padded = low + tail_rows
    who = jnp.stack([lax.axis_index("seq"), lax.axis_index("dp")]).astype(jnp.int32)
    known = (who, tile_count, owner_perm)
    scale = blocks

    delta_rows = whole_tiles(groups * heads)
    piece_rows = 2 * heads * rows_dev + delta_rows
    note_size = whole_tiles(TERMS * heads)
    note_count = slots * groups * note_size
    packed = call(
        functools.partial(pack_kernel, heads),
        [jax.ShapeDtypeStruct((piece_rows, HEAD_DIM), BF16)] * groups,
        [SMEM, SMEM] + [HBM] * 3,
        [pltpu.VMEM((rows_dev, features), BF16)] * 3 + [pltpu.SemaphoreType.DMA((3,))],
        (who, text_len, queries[0], saved_output[0], grad_out[0]),
        megabytes=16,
        cost=1,
    )
    pieces = [packed[0]] + [exchange(packed[j], "seq", j) for j in range(1, groups)]
    tile_shape = jax.ShapeDtypeStruct((slots, padded, HEAD_DIM), BF16)
    own_tile = call(pad_kernel, tile_shape, [VMEM] + [ANY] * (groups - 1), [], (tile_kv, *pieces[1:]), cost=1)
    partner_tile = exchange(own_tile, "seq", 1)

    def near_of(first, extra, order):
        block = call(
            functools.partial(stack_kernel, groups, slice(first, first + heads * rows_dev), extra),
            jax.ShapeDtypeStruct((groups * heads * rows_dev + extra, HEAD_DIM), BF16),
            [HBM] + [ANY] * (groups - 1 + len(order)),
            [pltpu.VMEM((groups, delta_rows, HEAD_DIM), BF16), pltpu.SemaphoreType.DMA((2, groups))],
            (*pieces, *order),
            megabytes=8 * scale,
        )
        return near(block)

    def near(block):
        return [block] + [exchange(block, "dp", d) for d in range(2, owners, 2)]

    q_near = near_of(0, 0, [own_tile])
    g_near = near_of(heads * rows_dev, delta_rows, q_near[1:2])
    q_all = [block for piece in q_near for block in (piece, exchange(piece, "dp", 1))]

    turn_shape = jax.ShapeDtypeStruct((slots, HEAD_DIM, -(-padded // HEAD_DIM) * HEAD_DIM), BF16)
    keys, values, keys_turned = call(
        functools.partial(tiles_kernel, slots, tile_rows),
        [tile_shape, tile_shape, turn_shape],
        [SMEM] + [VMEM] * 2,
        [],
        (who, own_tile, partner_tile),
        cost=0,
    )
    stack_shape = jax.ShapeDtypeStruct((slots * steps, padded, block_rows), BF16)
    stack_spec = pl.BlockSpec((1, padded, block_rows), lambda i: (i, 0, 0))
    notes, weights = call(
        functools.partial(weights_kernel, owners, heads, blocks, slots, tile_rows),
        [jax.ShapeDtypeStruct((note_count, HEAD_DIM), BF16), stack_shape],
        [SMEM] * 3 + [VMEM] + [ANY] * owners,
        [
            pltpu.VMEM((slots,) + q_near[0].shape, BF16),
            pltpu.VMEM((padded, block_rows), F32),
            pltpu.VMEM((2 * heads, blocks, block_rows), F32),
            pltpu.SemaphoreType.DMA((slots,)),
        ],
        (*known, keys, *q_all),
        out_specs=[VMEM, stack_spec],
        grid=(slots * steps,),
        megabytes=16,
        cost=0,
    )
    notes_near = near(notes)
    joined = call(
        functools.partial(join_kernel, owners // 2),
        jax.ShapeDtypeStruct((owners // 2, g_near[0].shape[0] + note_count, HEAD_DIM), BF16),
        [ANY] * owners,
        [pltpu.SemaphoreType.DMA((2, owners // 2))],
        (*g_near, *notes_near),
        megabytes=12 * scale,
    )
    g_pair = (joined, exchange(joined, "dp", 1))
    slopes, part = call(
        functools.partial(slopes_kernel, owners, heads, blocks, slots, tile_rows),
        [stack_shape, jax.ShapeDtypeStruct((slots, width + note_size, text_rows), BF16)],
        [SMEM] * 3 + [VMEM, stack_spec] + [VMEM] * 2 + [ANY] * 2,
        [
            pltpu.VMEM((slots,) + g_near[0].shape, BF16),
            pltpu.VMEM((delta_rows, HEAD_DIM), F32),
            pltpu.SemaphoreType.DMA((slots,)),
        ],
        (*known, notes, weights, values, keys_turned, *g_pair),
        out_specs=[stack_spec, VMEM],
        grid=(slots * steps,),
        megabytes=20,
        cost=6,
    )
    factors = call(
        functools.partial(factors_kernel, owners, heads, groups, slots),
        jax.ShapeDtypeStruct((slots, heads, groups, HEAD_DIM), F32),
        [SMEM] * 3 + [ANY] * 2,
        [pltpu.VMEM((owners, note_count, HEAD_DIM), BF16), pltpu.SemaphoreType.DMA((owners,))],
        (*known, *g_pair),
        cost=30,
    )
    kept, got = [], []

    def tile_sums(slot, order):
        left_spec = pl.BlockSpec((1, padded, block_rows), lambda i: (slot * steps + i, 0, 0))
        keep, send = call(
            functools.partial(sums_kernel, owners, heads, blocks, slots, slot),
            [jax.ShapeDtypeStruct((padded, HEAD_DIM), BF16)] * 2,
            [SMEM] * 3 + [left_spec] * 2 + [VMEM] + [ANY] * (owners + 2 + len(order)),
            [
                pltpu.VMEM(q_near[0].shape, BF16),
                pltpu.VMEM(g_near[0].shape, BF16),
                pltpu.VMEM((2, padded, HEAD_DIM), F32),
                pltpu.SemaphoreType.DMA((2,)),
            ],
            (*known, weights, slopes, factors, *q_all, *g_pair, *order),
            out_specs=[VMEM] * 2,
            grid=(steps,),
            megabytes=8 * scale,
            cost=4,
        )
        kept.append(keep)
        got.append(exchange(send, "seq", 1))

    tile_sums(0, [])
    routed = call(
        functools.partial(route_kernel, owners, heads, blocks, slots),
        [jax.ShapeDtypeStruct((width + note_size, text_rows), BF16)] * (owners // 2),
        [SMEM] * 3 + [VMEM] * 2 + [ANY] * 2,
        [],
        (*known, part, exchange(part, "dp", 1), factors, kept[0]),
        megabytes=14,
        cost=30,
    )

    for slot in range(1, slots):
        tile_sums(slot, [routed[0]])

    sums = [routed[0]] + [exchange(routed[d], "dp", 2 * d) for d in range(1, owners // 2)]
    cut = call(
        functools.partial(gather_kernel, heads, len(sums)),
        [jax.ShapeDtypeStruct((rows_dev, width), BF16)] * groups,
        [VMEM] * len(sums),
        [],
        sums,
        megabytes=8 * scale,
        cost=30,
    )
    back = [cut[0]] + [exchange(cut[j], "seq", j) for j in range(1, groups)]
    grad_tiles, merged = call(
        functools.partial(merge_kernel, slots),
        [jax.ShapeDtypeStruct((tile_rows, slots, HEAD_DIM), BF16), jax.ShapeDtypeStruct((TILE, HEAD_DIM), BF16)],
        [VMEM] * (2 * slots),
        [],
        (*kept, *got),
        cost=2,
    )
    grad_queries = call(
        place_kernel,
        jax.ShapeDtypeStruct((rows_dev, features), BF16),
        [SMEM] + [VMEM] * groups + [ANY],
        [],
        (who, *back, merged),
        cost=1,
    )
    return (grad_queries[None], jnp.transpose(grad_tiles, (1, 0, 2)))


def solution(mesh):
    placed = (
        P("dp", "seq", None),
        P("dp", "seq", None),
        P("dp", "seq", None),
        P("dp", None, "seq"),
        P(),
        P(),
        P("dp"),
    )
    return jax.shard_map(
        shards,
        mesh=mesh,
        in_specs=placed,
        out_specs=(P("dp", "seq", None), P("dp", None, "seq")),
        check_vma=False,
    )
```

time: 109 us -> 98.2 us (0.901)
  waiting for transfers between devices: 51.2 us -> 35.8 us
  Pallas kernels: 21.4 us -> 26.7 us
  local copies, waits for them, and re-layouts: 2.18 us -> 4.11 us
  starting transfers between devices: 31 us -> 29.9 us
    ppermute x25 -> x27, waiting for transfers between devices: 51.2 us -> 35.8 us  [exchange(): return lax.ppermute(block, axis, [(i, i ^ distance) for i in range(count)])]
    pallas_call x16 -> x15, Pallas kernels: 21.4 us -> 26.7 us  [call(): pl.pallas_call(kernel, out_shape=out_shape, in_specs=in_specs, out_specs=...]
    unnamed x11, local copies, waits for them, and re-layouts: 2.18 us -> 4.11 us
    ppermute x25 -> x27, starting transfers between devices: 31 us -> 29.9 us  [exchange(): return lax.ppermute(block, axis, [(i, i ^ distance) for i in range(count)])]
  transfers between devices with their start and end apart: 25 -> 27, of which waited for: 15 -> 13; matrix products, arithmetic and copies ran while one was open for 1% -> 1% of each run, Pallas kernels for 13% -> 20%
where the time goes in v5:
time: 98.2 us; the launch traced here: 98 us
  waiting for transfers between devices  35.8 us (36%)
  starting transfers between devices  29.9 us (30%)
  Pallas kernels  26.7 us (27%)
  local copies, waits for them, and re-layouts  4.11 us (4%)
  between operations  1.45 us (1%)
    ppermute x27, waiting for transfers between devices, exchange(): return lax.ppermute(block, axis, [(i, i ^ distance) for i in range(count)])  35.8 us
    ppermute x27, starting transfers between devices, exchange(): return lax.ppermute(block, axis, [(i, i ^ distance) for i in range(count)])  29.9 us
    pallas_call x15, Pallas kernels, call(): pl.pallas_call(kernel, out_shape=out_shape, in_specs=in_specs, out_specs=...  26.7 us
    unnamed x11, local copies, waits for them, and re-layouts  4.11 us
  transfers between devices with their start and end apart: 27, of which 13 were waited for; matrix products, arithmetic and copies ran while one was open for 1% of the time, Pallas kernels for 20%

profile of v5, /device:TPU:0, one launch (start us, length us, event | category | flops | bytes accessed | tf_op | source)
XLA Modules:
  0.0 98.0 jit_solution(7529281308082083957)
XLA Ops:
  1.4 0.9 copy-done.2
  2.3 0.9 copy-done.3
  3.3 0.9 copy-done.4
  4.2 1.0 pack_kernel.1
  5.2 3.1 %collective-permute-start = (bf16[528,128]{1,0:T(8,128)(2,1)S(1)}, bf16[528,128]{1,0:T(8,128)(2,1)S(1)}, u32[]{:S(2)}, u32[]{:S(2)}) collective-permute-start(bf16[528,128]{1,0:T(8,128)(2,1)S(1)} %get-tuple-element.27), channel_id=1, source_target_pairs={{0,8},{8,0},{16,24},{24,16},{1,9},{9,1},{17,25},{25,17},{2,10},{10... | collective-permute-start | bytes 405512 | tf_op jit(solution)/shard_map/ppermute | solution.py:35
  8.3 2.6 %collective-permute-start.1 = (bf16[528,128]{1,0:T(8,128)(2,1)S(1)}, bf16[528,128]{1,0:T(8,128)(2,1)S(1)}, u32[]{:S(2)}, u32[]{:S(2)}) collective-permute-start(bf16[528,128]{1,0:T(8,128)(2,1)S(1)} %get-tuple-element.28), channel_id=1, source_target_pairs={{0,16},{8,24},{16,0},{24,8},{1,17},{9,25},{17,1},{25,9},{2,18},{10... | collective-permute-start | bytes 405512 | tf_op jit(solution)/shard_map/ppermute | solution.py:35
  10.9 1.3 %copy.9.tiles = bf16[2,1601,128]{2,1,0:T(8,128)(2,1)S(1)} copy(bf16[2,1601,128]{2,0,1:T(2,128)(2,1)} %param.10) | data formatting | bytes 1639424 | tf_op args[3]
  12.1 1.4 %collective-permute-done.refs_0_.refs_1_ = bf16[528,128]{1,0:T(8,128)(2,1)S(1)} collective-permute-done((bf16[528,128]{1,0:T(8,128)(2,1)S(1)}, bf16[528,128]{1,0:T(8,128)(2,1)S(1)}, u32[]{:S(2)}, u32[]{:S(2)}) %collective-permute-start) | collective-permute-done | bytes 135200 | tf_op jit(solution)/shard_map/ppermute | solution.py:35
  13.5 8.0 %collective-permute-done.1.refs_1_.refs_2_ = bf16[528,128]{1,0:T(8,128)(2,1)S(1)} collective-permute-done((bf16[528,128]{1,0:T(8,128)(2,1)S(1)}, bf16[528,128]{1,0:T(8,128)(2,1)S(1)}, u32[]{:S(2)}, u32[]{:S(2)}) %collective-permute-start.1) | collective-permute-done | bytes 135200 | tf_op jit(solution)/shard_map/ppermute | solution.py:35
  21.5 2.1 %collective-permute-start.3 = (bf16[2,1616,128]{2,1,0:T(8,128)(2,1)S(1)}, bf16[2,1616,128]{2,1,0:T(8,128)(2,1)S(1)}, u32[]{:S(2)}, u32[]{:S(2)}) collective-permute-start(bf16[2,1616,128]{2,1,0:T(8,128)(2,1)S(1)} %pad_kernel.1.own.refs_4_), channel_id=1, source_target_pairs={{0,8},{8,0},{16,24},{24,16},{1,9},{9,1},{17,25},{25,17},{2,10},{10... | collective-permute-start | bytes 2482184 | tf_op jit(solution)/shard_map/ppermute | solution.py:35
  23.6 0.4 stack_kernel.2.refs_0_.refs_3_
  24.0 2.5 %collective-permute-start.9 = (bf16[1024,128]{1,0:T(8,128)(2,1)S(1)}, bf16[1024,128]{1,0:T(8,128)(2,1)S(1)}, u32[]{:S(2)}, u32[]{:S(2)}) collective-permute-start(bf16[1024,128]{1,0:T(8,128)(2,1)S(1)} %stack_kernel.2.refs_0_.refs_3_), channel_id=1, source_target_pairs={{0,6},{1,7},{2,4},{3,5},{4,2},{5,3},{6,0},{7,1},{8,14},{9,15},{10,... | collective-permute-start | bytes 786440 | tf_op jit(solution)/shard_map/ppermute | solution.py:35
  26.5 0.5 collective-permute-start.5
  27.1 0.5 collective-permute-start.7
  27.6 6.6 %collective-permute-done.9.refs_6_.refs_9_ = bf16[1024,128]{1,0:T(8,128)(2,1)S(1)} collective-permute-done((bf16[1024,128]{1,0:T(8,128)(2,1)S(1)}, bf16[1024,128]{1,0:T(8,128)(2,1)S(1)}, u32[]{:S(2)}, u32[]{:S(2)}) %collective-permute-start.9) | collective-permute-done | bytes 262176 | tf_op jit(solution)/shard_map/ppermute | solution.py:35
  34.2 3.1 %collective-permute-done.5.refs_2_.refs_4_.refs_5_ = bf16[1024,128]{1,0:T(8,128)(2,1)S(1)} collective-permute-done((bf16[1024,128]{1,0:T(8,128)(2,1)S(1)}, bf16[1024,128]{1,0:T(8,128)(2,1)S(1)}, u32[]{:S(2)}, u32[]{:S(2)}) %collective-permute-start.5) | collective-permute-done | bytes 262176 | tf_op jit(solution)/shard_map/ppermute | solution.py:35
  37.3 0.4 stack_kernel.3.refs_0_
  37.8 1.5 %collective-permute-start.13 = (bf16[1040,128]{1,0:T(8,128)(2,1)S(1)}, bf16[1040,128]{1,0:T(8,128)(2,1)S(1)}, u32[]{:S(2)}, u32[]{:S(2)}) collective-permute-start(bf16[1040,128]{1,0:T(8,128)(2,1)S(1)} %stack_kernel.3.refs_0_), channel_id=1, source_target_pairs={{0,6},{1,7},{2,4},{3,5},{4,2},{5,3},{6,0},{7,1},{8,14},{9,15},{10,... | collective-permute-start | bytes 798728 | tf_op jit(solution)/shard_map/ppermute | solution.py:35
  39.2 0.5 collective-permute-start.6
  39.7 1.6 %collective-permute-start.12 = (bf16[1040,128]{1,0:T(8,128)(2,1)S(1)}, bf16[1040,128]{1,0:T(8,128)(2,1)S(1)}, u32[]{:S(2)}, u32[]{:S(2)}) collective-permute-start(bf16[1040,128]{1,0:T(8,128)(2,1)S(1)} %stack_kernel.3.refs_0_), channel_id=1, source_target_pairs={{0,4},{1,5},{2,6},{3,7},{4,0},{5,1},{6,2},{7,3},{8,12},{9,13},{10,... | collective-permute-start | bytes 798728 | tf_op jit(solution)/shard_map/ppermute | solution.py:35
  41.3 1.1 %collective-permute-start.11 = (bf16[1040,128]{1,0:T(8,128)(2,1)S(1)}, bf16[1040,128]{1,0:T(8,128)(2,1)S(1)}, u32[]{:S(2)}, u32[]{:S(2)}) collective-permute-start(bf16[1040,128]{1,0:T(8,128)(2,1)S(1)} %stack_kernel.3.refs_0_), channel_id=1, source_target_pairs={{0,2},{1,3},{2,0},{3,1},{4,6},{5,7},{6,4},{7,5},{8,10},{9,11},{10,... | collective-permute-start | bytes 798728 | tf_op jit(solution)/shard_map/ppermute | solution.py:35
  42.4 1.0 tiles_kernel.1
  43.4 6.0 %weights_kernel.1 = (bf16[128,128]{1,0:T(8,128)(2,1)S(1)}, bf16[4,1616,512]{2,1,0:T(8,128)(2,1)S(1)}) custom-call(s32[2]{0:T(128)S(1)} %pad_add_fusion.who, s32[8]{0:T(128)S(1)} %copy-done, s32[8]{0:T(128)S(1)} %copy-done.1, bf16[2,1616,128]{2,1,0:T(8,128)(2,1)S(1)} %get-tuple-element.30.keys, bf16[1024,128]{1,0:T(8,128)(2,1)S(1)} %stack_kernel.2.refs_0_.refs_3_, ...), custom_call_target="tpu_custom_call" | custom-call | tf_op jit(solution)/shard_map/weights_kernel/pallas_call | solution.py:42
  49.4 1.6 %collective-permute-start.16 = (bf16[128,128]{1,0:T(8,128)(2,1)S(1)}, bf16[128,128]{1,0:T(8,128)(2,1)S(1)}, u32[]{:S(2)}, u32[]{:S(2)}) collective-permute-start(bf16[128,128]{1,0:T(8,128)(2,1)S(1)} %get-tuple-element.32.refs_4_.notes), channel_id=1, source_target_pairs={{0,6},{1,7},{2,4},{3,5},{4,2},{5,3},{6,0},{7,1},{8,14},{9,15},{10,... | collective-permute-start | bytes 98312 | tf_op jit(solution)/shard_map/ppermute | solution.py:35
  51.1 1.9 %collective-permute-start.14 = (bf16[128,128]{1,0:T(8,128)(2,1)S(1)}, bf16[128,128]{1,0:T(8,128)(2,1)S(1)}, u32[]{:S(2)}, u32[]{:S(2)}) collective-permute-start(bf16[128,128]{1,0:T(8,128)(2,1)S(1)} %get-tuple-element.32.refs_4_.notes), channel_id=1, source_target_pairs={{0,2},{1,3},{2,0},{3,1},{4,6},{5,7},{6,4},{7,5},{8,10},{9,11},{10,... | collective-permute-start | bytes 98312 | tf_op jit(solution)/shard_map/ppermute | solution.py:35
  53.0 1.3 %collective-permute-done.16.refs_7_ = bf16[128,128]{1,0:T(8,128)(2,1)S(1)} collective-permute-done((bf16[128,128]{1,0:T(8,128)(2,1)S(1)}, bf16[128,128]{1,0:T(8,128)(2,1)S(1)}, u32[]{:S(2)}, u32[]{:S(2)}) %collective-permute-start.16) | collective-permute-done | bytes 32800 | tf_op jit(solution)/shard_map/ppermute | solution.py:35
  54.3 0.6 collective-permute-done.15.refs_6_
  55.0 0.3 join_kernel.1.refs_0_.own.refs_11_
  55.4 2.9 %collective-permute-done.17.refs_1_.other.refs_12_ = bf16[4,1168,128]{2,1,0:T(8,128)(2,1)S(1)} collective-permute-done((bf16[4,1168,128]{2,1,0:T(8,128)(2,1)S(1)}, bf16[4,1168,128]{2,1,0:T(8,128)(2,1)S(1)}, u32[]{:S(2)}, u32[]{:S(2)}) %collective-permute-start.17) | collective-permute-done | bytes 1196064 | tf_op jit(solution)/shard_map/ppermute | solution.py:35
  58.3 4.4 %slopes_kernel.1 = (bf16[4,1616,512]{2,1,0:T(8,128)(2,1)S(1)}, bf16[2,272,512]{2,1,0:T(8,128)(2,1)S(1)}) custom-call(s32[2]{0:T(128)S(1)} %pad_add_fusion.who, s32[8]{0:T(128)S(1)} %copy-done, s32[8]{0:T(128)S(1)} %copy-done.1, bf16[128,128]{1,0:T(8,128)(2,1)S(1)} %get-tuple-element.32.refs_4_.notes, ...), custom_call_target="tpu_custom_call" | custom-call | flops 6000000000 | tf_op jit(solution)/shard_map/slopes_kernel/pallas_call | solution.py:42
  62.8 1.4 %factors_kernel.1.refs_2_.refs_0_ = f32[2,2,4,128]{3,2,1,0:T(4,128)S(1)} custom-call(s32[2]{0:T(128)S(1)} %pad_add_fusion.who, s32[8]{0:T(128)S(1)} %copy-done, s32[8]{0:T(128)S(1)} %copy-done.1, bf16[4,1168,128]{2,1,0:T(8,128)(2,1)S(1)} %join_kernel.1.refs_0_.own.refs_11_, bf16[4,1168,128]{2,1,0:T(8,128)(2,1)S(1)} %collective-permute-done.17.refs_1_.other.refs_12_), custom_call_target="tpu_custom_call" | custom-call | flops 30000001024 | tf_op jit(solution)/shard_map/factors_kernel/pallas_call | solution.py:42
  64.3 3.3 %sums_kernel.2 = (bf16[1616,128]{1,0:T(8,128)(2,1)S(1)}, bf16[1616,128]{1,0:T(8,128)(2,1)S(1)}) custom-call(s32[2]{0:T(128)S(1)} %pad_add_fusion.who, s32[8]{0:T(128)S(1)} %copy-done, s32[8]{0:T(128)S(1)} %copy-done.1, bf16[4,1616,512]{2,1,0:T(8,128)(2,1)S(1)} %get-tuple-element.33.weights.refs_0_, bf16[4,1616,512]{2,1,0:T(8,128)(2,1)S(1)} %get-tuple-element.37.refs_1_, ...), custom_call_target="tpu_custom_call" | custom-call | flops 4000000000 | tf_op jit(solution)/shard_map/sums_kernel/pallas_call | solution.py:42
  67.6 1.8 %collective-permute-start.25 = (bf16[1616,128]{1,0:T(8,128)(2,1)S(1)}, bf16[1616,128]{1,0:T(8,128)(2,1)S(1)}, u32[]{:S(2)}, u32[]{:S(2)}) collective-permute-start(bf16[1616,128]{1,0:T(8,128)(2,1)S(1)} %get-tuple-element.48), channel_id=1, source_target_pairs={{0,8},{8,0},{16,24},{24,16},{1,9},{9,1},{17,25},{25,17},{2,10},{10... | collective-permute-start | bytes 1241096 | tf_op jit(solution)/shard_map/ppermute | solution.py:35
  69.4 1.4 %route_kernel.1 = (bf16[272,512]{1,0:T(8,128)(2,1)S(1)}, bf16[272,512]{1,0:T(8,128)(2,1)S(1)}, bf16[272,512]{1,0:T(8,128)(2,1)S(1)}, bf16[272,512]{1,0:T(8,128)(2,1)S(1)}) custom-call(s32[2]{0:T(128)S(1)} %pad_add_fusion.who, s32[8]{0:T(128)S(1)} %copy-done, s32[8]{0:T(128)S(1)} %copy-done.1, bf16[2,272,512]{2,1,0:T(8,128)(2,1)S(1)} %get-tuple-element.36.own, ...), custom_call_target="tpu_custom_call" | custom-call | flops 30000001024 | tf_op jit(solution)/shard_map/route_kernel/pallas_call | solution.py:42
  71.1 3.3 %collective-permute-start.20 = (bf16[272,512]{1,0:T(8,128)(2,1)S(1)}, bf16[272,512]{1,0:T(8,128)(2,1)S(1)}, u32[]{:S(2)}, u32[]{:S(2)}) collective-permute-start(bf16[272,512]{1,0:T(8,128)(2,1)S(1)} %get-tuple-element.41), channel_id=1, source_target_pairs={{0,4},{1,5},{2,6},{3,7},{4,0},{5,1},{6,2},{7,3},{8,12},{9,13},{10,... | collective-permute-start | bytes 835592 | tf_op jit(solution)/shard_map/ppermute | solution.py:35
  74.4 3.3 %sums_kernel.3 = (bf16[1616,128]{1,0:T(8,128)(2,1)S(1)}, bf16[1616,128]{1,0:T(8,128)(2,1)S(1)}) custom-call(s32[2]{0:T(128)S(1)} %pad_add_fusion.who, s32[8]{0:T(128)S(1)} %copy-done, s32[8]{0:T(128)S(1)} %copy-done.1, bf16[4,1616,512]{2,1,0:T(8,128)(2,1)S(1)} %get-tuple-element.33.weights.refs_0_, bf16[4,1616,512]{2,1,0:T(8,128)(2,1)S(1)} %get-tuple-element.37.refs_1_, ...), custom_call_target="tpu_custom_call" | custom-call | flops 4000000000 | tf_op jit(solution)/shard_map/sums_kernel/pallas_call | solution.py:42
  77.7 0.3 collective-permute-start.26
  78.0 2.4 %collective-permute-done.19.refs_1_ = bf16[272,512]{1,0:T(8,128)(2,1)S(1)} collective-permute-done((bf16[272,512]{1,0:T(8,128)(2,1)S(1)}, bf16[272,512]{1,0:T(8,128)(2,1)S(1)}, u32[]{:S(2)}, u32[]{:S(2)}) %collective-permute-start.19) | collective-permute-done | bytes 278560 | tf_op jit(solution)/shard_map/ppermute | solution.py:35
  80.4 5.8 %collective-permute-done.20.refs_2_ = bf16[272,512]{1,0:T(8,128)(2,1)S(1)} collective-permute-done((bf16[272,512]{1,0:T(8,128)(2,1)S(1)}, bf16[272,512]{1,0:T(8,128)(2,1)S(1)}, u32[]{:S(2)}, u32[]{:S(2)}) %collective-permute-start.20) | collective-permute-done | bytes 278560 | tf_op jit(solution)/shard_map/ppermute | solution.py:35
  86.2 0.8 collective-permute-done.21.refs_3_
  87.0 0.3 gather_kernel.1
  87.3 0.4 collective-permute-start.22
  87.7 2.9 %collective-permute-start.23 = (bf16[128,256]{1,0:T(8,128)(2,1)S(1)}, bf16[128,256]{1,0:T(8,128)(2,1)S(1)}, u32[]{:S(2)}, u32[]{:S(2)}) collective-permute-start(bf16[128,256]{1,0:T(8,128)(2,1)S(1)} %get-tuple-element.45), channel_id=1, source_target_pairs={{0,16},{8,24},{16,0},{24,8},{1,17},{9,25},{17,1},{25,9},{2,18},{10... | collective-permute-start | bytes 196616 | tf_op jit(solution)/shard_map/ppermute | solution.py:35
  90.6 1.2 %collective-permute-start.24 = (bf16[128,256]{1,0:T(8,128)(2,1)S(1)}, bf16[128,256]{1,0:T(8,128)(2,1)S(1)}, u32[]{:S(2)}, u32[]{:S(2)}) collective-permute-start(bf16[128,256]{1,0:T(8,128)(2,1)S(1)} %get-tuple-element.46), channel_id=1, source_target_pairs={{0,24},{8,16},{16,8},{24,0},{1,25},{9,17},{17,9},{25,1},{2,26},{10... | collective-permute-start | bytes 196616 | tf_op jit(solution)/shard_map/ppermute | solution.py:35
  91.8 2.0 %merge_kernel.1 = (bf16[1601,2,128]{2,1,0:T(2,128)(2,1)}, bf16[16,128]{1,0:T(8,128)(2,1)S(1)}) custom-call(bf16[1616,128]{1,0:T(8,128)(2,1)S(1)} %get-tuple-element.38.refs_1_.refs_0_, bf16[1616,128]{1,0:T(8,128)(2,1)S(1)} %get-tuple-element.47.refs_1_, bf16[1616,128]{1,0:T(8,128)(2,1)S(1)} %collective-permute-done.25.refs_2_, ...), custom_call_target="tpu_custom_call" | custom-call | flops 2000000000 | tf_op jit(solution)/shard_map/merge_kernel/pallas_call | solution.py:42
  93.8 1.1 %collective-permute-done.23.refs_2_ = bf16[128,256]{1,0:T(8,128)(2,1)S(1)} collective-permute-done((bf16[128,256]{1,0:T(8,128)(2,1)S(1)}, bf16[128,256]{1,0:T(8,128)(2,1)S(1)}, u32[]{:S(2)}, u32[]{:S(2)}) %collective-permute-start.23) | collective-permute-done | bytes 65568 | tf_op jit(solution)/shard_map/ppermute | solution.py:35
  94.9 1.8 %collective-permute-done.24.refs_3_ = bf16[128,256]{1,0:T(8,128)(2,1)S(1)} collective-permute-done((bf16[128,256]{1,0:T(8,128)(2,1)S(1)}, bf16[128,256]{1,0:T(8,128)(2,1)S(1)}, u32[]{:S(2)}, u32[]{:S(2)}) %collective-permute-start.24) | collective-permute-done | bytes 65568 | tf_op jit(solution)/shard_map/ppermute | solution.py:35
  96.7 1.3 %place_kernel.1 = bf16[128,1024]{1,0:T(8,128)(2,1)} custom-call(s32[2]{0:T(128)S(1)} %pad_add_fusion.who, bf16[128,256]{1,0:T(8,128)(2,1)S(1)} %get-tuple-element.43.refs_0_, bf16[128,256]{1,0:T(8,128)(2,1)S(1)} %collective-permute-done.22.refs_1_, bf16[128,256]{1,0:T(8,128)(2,1)S(1)} %collective-permute-done.23.refs_2_, ...), custom_call_target="tpu_custom_call" | custom-call | flops 1000000000 | tf_op jit(solution)/shard_map/place_kernel/pallas_call | solution.py:42
  (33 shorter events, 0.8 us)
Async XLA Ops:
  1.4 1.0 copy-start.2
  2.3 0.9 copy-start.3
  3.3 0.9 copy-start.4
  4.2 39.2 %copy-start = (s32[8]{0:T(128)S(1)}, s32[8]{0:T(128)}, u32[]{:S(2)}) copy-start(s32[8]{0:T(128)} %counts.11) | copy-start | bytes 100
  4.2 39.2 %copy-start.1 = (s32[8]{0:T(128)S(1)}, s32[8]{0:T(128)}, u32[]{:S(2)}) copy-start(s32[8]{0:T(128)} %perm.11) | copy-start | bytes 100
  5.2 8.3 %collective-permute-start = (bf16[528,128]{1,0:T(8,128)(2,1)S(1)}, bf16[528,128]{1,0:T(8,128)(2,1)S(1)}, u32[]{:S(2)}, u32[]{:S(2)}) collective-permute-start(bf16[528,128]{1,0:T(8,128)(2,1)S(1)} %get-tuple-element.27), channel_id=1, source_target_pairs={{0,8},{8,0},{16,24},{24,16},{1,9},{9,1},{17,25},{25,17},{2,10},{10... | collective-permute-start | bytes 405512 | tf_op jit(solution)/shard_map/ppermute | solution.py:35
  8.3 13.2 %collective-permute-start.1 = (bf16[528,128]{1,0:T(8,128)(2,1)S(1)}, bf16[528,128]{1,0:T(8,128)(2,1)S(1)}, u32[]{:S(2)}, u32[]{:S(2)}) collective-permute-start(bf16[528,128]{1,0:T(8,128)(2,1)S(1)} %get-tuple-element.28), channel_id=1, source_target_pairs={{0,16},{8,24},{16,0},{24,8},{1,17},{9,25},{17,1},{25,9},{2,18},{10... | collective-permute-start | bytes 405512 | tf_op jit(solution)/shard_map/ppermute | solution.py:35
  10.9 10.6 %collective-permute-start.2 = (bf16[528,128]{1,0:T(8,128)(2,1)S(1)}, bf16[528,128]{1,0:T(8,128)(2,1)S(1)}, u32[]{:S(2)}, u32[]{:S(2)}) collective-permute-start(bf16[528,128]{1,0:T(8,128)(2,1)S(1)} %get-tuple-element.29), channel_id=1, source_target_pairs={{0,24},{8,16},{16,8},{24,0},{1,25},{9,17},{17,9},{25,1},{2,26},{10... | collective-permute-start | bytes 405512 | tf_op jit(solution)/shard_map/ppermute | solution.py:35
  21.5 19.8 %collective-permute-start.3 = (bf16[2,1616,128]{2,1,0:T(8,128)(2,1)S(1)}, bf16[2,1616,128]{2,1,0:T(8,128)(2,1)S(1)}, u32[]{:S(2)}, u32[]{:S(2)}) collective-permute-start(bf16[2,1616,128]{2,1,0:T(8,128)(2,1)S(1)} %pad_kernel.1.own.refs_4_), channel_id=1, source_target_pairs={{0,8},{8,0},{16,24},{24,16},{1,9},{9,1},{17,25},{25,17},{2,10},{10... | collective-permute-start | bytes 2482184 | tf_op jit(solution)/shard_map/ppermute | solution.py:35
  24.0 10.2 %collective-permute-start.9 = (bf16[1024,128]{1,0:T(8,128)(2,1)S(1)}, bf16[1024,128]{1,0:T(8,128)(2,1)S(1)}, u32[]{:S(2)}, u32[]{:S(2)}) collective-permute-start(bf16[1024,128]{1,0:T(8,128)(2,1)S(1)} %stack_kernel.2.refs_0_.refs_3_), channel_id=1, source_target_pairs={{0,6},{1,7},{2,4},{3,5},{4,2},{5,3},{6,0},{7,1},{8,14},{9,15},{10,... | collective-permute-start | bytes 786440 | tf_op jit(solution)/shard_map/ppermute | solution.py:35
  26.5 10.8 %collective-permute-start.5 = (bf16[1024,128]{1,0:T(8,128)(2,1)S(1)}, bf16[1024,128]{1,0:T(8,128)(2,1)S(1)}, u32[]{:S(2)}, u32[]{:S(2)}) collective-permute-start(bf16[1024,128]{1,0:T(8,128)(2,1)S(1)} %stack_kernel.2.refs_0_.refs_3_), channel_id=1, source_target_pairs={{0,2},{1,3},{2,0},{3,1},{4,6},{5,7},{6,4},{7,5},{8,10},{9,11},{10,... | collective-permute-start | bytes 786440 | tf_op jit(solution)/shard_map/ppermute | solution.py:35
  27.1 12.1 %collective-permute-start.7 = (bf16[1024,128]{1,0:T(8,128)(2,1)S(1)}, bf16[1024,128]{1,0:T(8,128)(2,1)S(1)}, u32[]{:S(2)}, u32[]{:S(2)}) collective-permute-start(bf16[1024,128]{1,0:T(8,128)(2,1)S(1)} %stack_kernel.2.refs_0_.refs_3_), channel_id=1, source_target_pairs={{0,4},{1,5},{2,6},{3,7},{4,0},{5,1},{6,2},{7,3},{8,12},{9,13},{10,... | collective-permute-start | bytes 786440 | tf_op jit(solution)/shard_map/ppermute | solution.py:35
  27.6 11.6 %collective-permute-start.4 = (bf16[1024,128]{1,0:T(8,128)(2,1)S(1)}, bf16[1024,128]{1,0:T(8,128)(2,1)S(1)}, u32[]{:S(2)}, u32[]{:S(2)}) collective-permute-start(bf16[1024,128]{1,0:T(8,128)(2,1)S(1)} %stack_kernel.2.refs_0_.refs_3_), channel_id=1, source_target_pairs={{0,1},{1,0},{2,3},{3,2},{4,5},{5,4},{6,7},{7,6},{8,9},{9,8},{10,11... | collective-permute-start | bytes 786440 | tf_op jit(solution)/shard_map/ppermute | solution.py:35
  34.2 5.5 %collective-permute-start.10 = (bf16[1024,128]{1,0:T(8,128)(2,1)S(1)}, bf16[1024,128]{1,0:T(8,128)(2,1)S(1)}, u32[]{:S(2)}, u32[]{:S(2)}) collective-permute-start(bf16[1024,128]{1,0:T(8,128)(2,1)S(1)} %collective-permute-done.9.refs_6_.refs_9_), channel_id=1, source_target_pairs={{0,1},{1,0},{2,3},{3,2},{4,5},{5,4},{6,7},{7,6},{8,9},{9,8},{10,11... | collective-permute-start | bytes 786440 | tf_op jit(solution)/shard_map/ppermute | solution.py:35
  37.8 13.3 %collective-permute-start.13 = (bf16[1040,128]{1,0:T(8,128)(2,1)S(1)}, bf16[1040,128]{1,0:T(8,128)(2,1)S(1)}, u32[]{:S(2)}, u32[]{:S(2)}) collective-permute-start(bf16[1040,128]{1,0:T(8,128)(2,1)S(1)} %stack_kernel.3.refs_0_), channel_id=1, source_target_pairs={{0,6},{1,7},{2,4},{3,5},{4,2},{5,3},{6,0},{7,1},{8,14},{9,15},{10,... | collective-permute-start | bytes 798728 | tf_op jit(solution)/shard_map/ppermute | solution.py:35
  39.2 4.2 %collective-permute-start.8 = (bf16[1024,128]{1,0:T(8,128)(2,1)S(1)}, bf16[1024,128]{1,0:T(8,128)(2,1)S(1)}, u32[]{:S(2)}, u32[]{:S(2)}) collective-permute-start(bf16[1024,128]{1,0:T(8,128)(2,1)S(1)} %collective-permute-done.7.refs_4_.refs_7_), channel_id=1, source_target_pairs={{0,1},{1,0},{2,3},{3,2},{4,5},{5,4},{6,7},{7,6},{8,9},{9,8},{10,11... | collective-permute-start | bytes 786440 | tf_op jit(solution)/shard_map/ppermute | solution.py:35
  39.2 4.2 %collective-permute-start.6 = (bf16[1024,128]{1,0:T(8,128)(2,1)S(1)}, bf16[1024,128]{1,0:T(8,128)(2,1)S(1)}, u32[]{:S(2)}, u32[]{:S(2)}) collective-permute-start(bf16[1024,128]{1,0:T(8,128)(2,1)S(1)} %collective-permute-done.5.refs_2_.refs_4_.refs_5_), channel_id=1, source_target_pairs={{0,1},{1,0},{2,3},{3,2},{4,5},{5,4},{6,7},{7,6},{8,9},{9,8},{10,11... | collective-permute-start | bytes 786440 | tf_op jit(solution)/shard_map/ppermute | solution.py:35
  39.7 13.3 %collective-permute-start.12 = (bf16[1040,128]{1,0:T(8,128)(2,1)S(1)}, bf16[1040,128]{1,0:T(8,128)(2,1)S(1)}, u32[]{:S(2)}, u32[]{:S(2)}) collective-permute-start(bf16[1040,128]{1,0:T(8,128)(2,1)S(1)} %stack_kernel.3.refs_0_), channel_id=1, source_target_pairs={{0,4},{1,5},{2,6},{3,7},{4,0},{5,1},{6,2},{7,3},{8,12},{9,13},{10,... | collective-permute-start | bytes 798728 | tf_op jit(solution)/shard_map/ppermute | solution.py:35
  41.3 11.7 %collective-permute-start.11 = (bf16[1040,128]{1,0:T(8,128)(2,1)S(1)}, bf16[1040,128]{1,0:T(8,128)(2,1)S(1)}, u32[]{:S(2)}, u32[]{:S(2)}) collective-permute-start(bf16[1040,128]{1,0:T(8,128)(2,1)S(1)} %stack_kernel.3.refs_0_), channel_id=1, source_target_pairs={{0,2},{1,3},{2,0},{3,1},{4,6},{5,7},{6,4},{7,5},{8,10},{9,11},{10,... | collective-permute-start | bytes 798728 | tf_op jit(solution)/shard_map/ppermute | solution.py:35
  49.4 4.9 %collective-permute-start.16 = (bf16[128,128]{1,0:T(8,128)(2,1)S(1)}, bf16[128,128]{1,0:T(8,128)(2,1)S(1)}, u32[]{:S(2)}, u32[]{:S(2)}) collective-permute-start(bf16[128,128]{1,0:T(8,128)(2,1)S(1)} %get-tuple-element.32.refs_4_.notes), channel_id=1, source_target_pairs={{0,6},{1,7},{2,4},{3,5},{4,2},{5,3},{6,0},{7,1},{8,14},{9,15},{10,... | collective-permute-start | bytes 98312 | tf_op jit(solution)/shard_map/ppermute | solution.py:35
  51.0 3.9 %collective-permute-start.15 = (bf16[128,128]{1,0:T(8,128)(2,1)S(1)}, bf16[128,128]{1,0:T(8,128)(2,1)S(1)}, u32[]{:S(2)}, u32[]{:S(2)}) collective-permute-start(bf16[128,128]{1,0:T(8,128)(2,1)S(1)} %get-tuple-element.32.refs_4_.notes), channel_id=1, source_target_pairs={{0,4},{1,5},{2,6},{3,7},{4,0},{5,1},{6,2},{7,3},{8,12},{9,13},{10,... | collective-permute-start | bytes 98312 | tf_op jit(solution)/shard_map/ppermute | solution.py:35
  51.1 3.9 %collective-permute-start.14 = (bf16[128,128]{1,0:T(8,128)(2,1)S(1)}, bf16[128,128]{1,0:T(8,128)(2,1)S(1)}, u32[]{:S(2)}, u32[]{:S(2)}) collective-permute-start(bf16[128,128]{1,0:T(8,128)(2,1)S(1)} %get-tuple-element.32.refs_4_.notes), channel_id=1, source_target_pairs={{0,2},{1,3},{2,0},{3,1},{4,6},{5,7},{6,4},{7,5},{8,10},{9,11},{10,... | collective-permute-start | bytes 98312 | tf_op jit(solution)/shard_map/ppermute | solution.py:35
  55.4 2.9 %collective-permute-start.17 = (bf16[4,1168,128]{2,1,0:T(8,128)(2,1)S(1)}, bf16[4,1168,128]{2,1,0:T(8,128)(2,1)S(1)}, u32[]{:S(2)}, u32[]{:S(2)}) collective-permute-start(bf16[4,1168,128]{2,1,0:T(8,128)(2,1)S(1)} %join_kernel.1.refs_0_.own.refs_11_), channel_id=1, source_target_pairs={{0,1},{1,0},{2,3},{3,2},{4,5},{5,4},{6,7},{7,6},{8,9},{9,8},{10,11... | collective-permute-start | bytes 3588104 | tf_op jit(solution)/shard_map/ppermute | solution.py:35
  62.8 6.7 %collective-permute-start.18 = (bf16[2,272,512]{2,1,0:T(8,128)(2,1)S(1)}, bf16[2,272,512]{2,1,0:T(8,128)(2,1)S(1)}, u32[]{:S(2)}, u32[]{:S(2)}) collective-permute-start(bf16[2,272,512]{2,1,0:T(8,128)(2,1)S(1)} %get-tuple-element.36.own), channel_id=1, source_target_pairs={{0,1},{1,0},{2,3},{3,2},{4,5},{5,4},{6,7},{7,6},{8,9},{9,8},{10,11... | collective-permute-start | bytes 1671176 | tf_op jit(solution)/shard_map/ppermute | solution.py:35
  67.6 24.2 %collective-permute-start.25 = (bf16[1616,128]{1,0:T(8,128)(2,1)S(1)}, bf16[1616,128]{1,0:T(8,128)(2,1)S(1)}, u32[]{:S(2)}, u32[]{:S(2)}) collective-permute-start(bf16[1616,128]{1,0:T(8,128)(2,1)S(1)} %get-tuple-element.48), channel_id=1, source_target_pairs={{0,8},{8,0},{16,24},{24,16},{1,9},{9,1},{17,25},{25,17},{2,10},{10... | collective-permute-start | bytes 1241096 | tf_op jit(solution)/shard_map/ppermute | solution.py:35
  70.9 9.6 %collective-permute-start.19 = (bf16[272,512]{1,0:T(8,128)(2,1)S(1)}, bf16[272,512]{1,0:T(8,128)(2,1)S(1)}, u32[]{:S(2)}, u32[]{:S(2)}) collective-permute-start(bf16[272,512]{1,0:T(8,128)(2,1)S(1)} %get-tuple-element.40), channel_id=1, source_target_pairs={{0,2},{1,3},{2,0},{3,1},{4,6},{5,7},{6,4},{7,5},{8,10},{9,11},{10,... | collective-permute-start | bytes 835592 | tf_op jit(solution)/shard_map/ppermute | solution.py:35
  71.1 15.1 %collective-permute-start.20 = (bf16[272,512]{1,0:T(8,128)(2,1)S(1)}, bf16[272,512]{1,0:T(8,128)(2,1)S(1)}, u32[]{:S(2)}, u32[]{:S(2)}) collective-permute-start(bf16[272,512]{1,0:T(8,128)(2,1)S(1)} %get-tuple-element.41), channel_id=1, source_target_pairs={{0,4},{1,5},{2,6},{3,7},{4,0},{5,1},{6,2},{7,3},{8,12},{9,13},{10,... | collective-permute-start | bytes 835592 | tf_op jit(solution)/shard_map/ppermute | solution.py:35
  74.3 12.7 %collective-permute-start.21 = (bf16[272,512]{1,0:T(8,128)(2,1)S(1)}, bf16[272,512]{1,0:T(8,128)(2,1)S(1)}, u32[]{:S(2)}, u32[]{:S(2)}) collective-permute-start(bf16[272,512]{1,0:T(8,128)(2,1)S(1)} %get-tuple-element.42), channel_id=1, source_target_pairs={{0,6},{1,7},{2,4},{3,5},{4,2},{5,3},{6,0},{7,1},{8,14},{9,15},{10,... | collective-permute-start | bytes 835592 | tf_op jit(solution)/shard_map/ppermute | solution.py:35
  77.7 14.1 %collective-permute-start.26 = (bf16[1616,128]{1,0:T(8,128)(2,1)S(1)}, bf16[1616,128]{1,0:T(8,128)(2,1)S(1)}, u32[]{:S(2)}, u32[]{:S(2)}) collective-permute-start(bf16[1616,128]{1,0:T(8,128)(2,1)S(1)} %get-tuple-element.49), channel_id=1, source_target_pairs={{0,8},{8,0},{16,24},{24,16},{1,9},{9,1},{17,25},{25,17},{2,10},{10... | collective-permute-start | bytes 1241096 | tf_op jit(solution)/shard_map/ppermute | solution.py:35
  87.3 6.5 %collective-permute-start.22 = (bf16[128,256]{1,0:T(8,128)(2,1)S(1)}, bf16[128,256]{1,0:T(8,128)(2,1)S(1)}, u32[]{:S(2)}, u32[]{:S(2)}) collective-permute-start(bf16[128,256]{1,0:T(8,128)(2,1)S(1)} %get-tuple-element.44), channel_id=1, source_target_pairs={{0,8},{8,0},{16,24},{24,16},{1,9},{9,1},{17,25},{25,17},{2,10},{10... | collective-permute-start | bytes 196616 | tf_op jit(solution)/shard_map/ppermute | solution.py:35
  87.7 7.2 %collective-permute-start.23 = (bf16[128,256]{1,0:T(8,128)(2,1)S(1)}, bf16[128,256]{1,0:T(8,128)(2,1)S(1)}, u32[]{:S(2)}, u32[]{:S(2)}) collective-permute-start(bf16[128,256]{1,0:T(8,128)(2,1)S(1)} %get-tuple-element.45), channel_id=1, source_target_pairs={{0,16},{8,24},{16,0},{24,8},{1,17},{9,25},{17,1},{25,9},{2,18},{10... | collective-permute-start | bytes 196616 | tf_op jit(solution)/shard_map/ppermute | solution.py:35
  90.6 6.1 %collective-permute-start.24 = (bf16[128,256]{1,0:T(8,128)(2,1)S(1)}, bf16[128,256]{1,0:T(8,128)(2,1)S(1)}, u32[]{:S(2)}, u32[]{:S(2)}) collective-permute-start(bf16[128,256]{1,0:T(8,128)(2,1)S(1)} %get-tuple-element.46), channel_id=1, source_target_pairs={{0,24},{8,16},{16,8},{24,0},{1,25},{9,17},{17,9},{25,1},{2,26},{10... | collective-permute-start | bytes 196616 | tf_op jit(solution)/shard_map/ppermute | solution.py:35

commit v6 on v5

--- a/solution.py
+++ b/solution.py
@@ -14,6 +14,7 @@
 TEXT_CHUNKS = 4
 TILE = 16
 TERMS = 6
+MOST_IN_PLACE = 8 << 20
 LOWEST = -1e30
 SCALE = 1.0 / math.sqrt(HEAD_DIM)
 SCALE_LOG2 = SCALE / math.log(2.0)
@@ -114,16 +115,20 @@
 
 def join_kernel(count, *refs):
     out, sem = refs[-2], refs[-1]
-    first = refs[0].shape[0]
-    copies = []
-    for i in range(count):
-        second = refs[count + i].shape[0]
-        copies.append(pltpu.make_async_copy(refs[i], out.at[i, pl.ds(0, first)], sem.at[0, i]))
-        copies.append(pltpu.make_async_copy(refs[count + i], out.at[i, pl.ds(first, second)], sem.at[1, i]))
+    copies = [pltpu.make_async_copy(refs[i], out.at[i], sem.at[i]) for i in range(count)]
     for copy in copies:
         copy.start()
     for copy in copies:
         copy.wait()
+
+
+def by_distance(groups, refs):
+    found = {}
+    for index, group in enumerate(groups):
+        for place, chip in enumerate(group):
+            for core in range(2):
+                found[2 * chip + core] = refs[2 * index + core].at[place]
+    return [found[distance] for distance in range(len(found))]
 
 
 def fetch(pieces, relative, target, sem):
@@ -131,14 +136,6 @@
         @pl.when(relative == distance)
         def _(piece=piece):
             pltpu.make_async_copy(piece, target, sem).start()
-
-
-def fetch_pair(pieces, relative, target, sem):
-    rows = pl.ds(0, target.shape[0])
-    for core, piece in enumerate(pieces):
-        @pl.when((relative & 1) == core)
-        def _(piece=piece):
-            pltpu.make_async_copy(piece.at[lax.shift_right_logical(relative, 1), rows], target, sem).start()
 
 
 def spans_of(rows):
@@ -180,60 +177,69 @@
             turned[slot, :, low:low + size] = jnp.transpose(keys[slot, low:low + size].astype(F32)).astype(BF16)
 
 
-def weights_kernel(owners, heads, blocks, slots, rows, who, counts, perm, keys, *refs):
+def over_steps(body, steps, in_place):
+    if in_place:
+        lax.fori_loop(0, steps, lambda step, carry: (body(step, step), carry)[1], 0)
+    else:
+        body(pl.program_id(0), 0)
+
+
+def weights_kernel(owners, heads, blocks, slots, rows, in_place, who, counts, perm, keys, *refs):
     pieces = refs[:owners]
     notes, weights, text_buf, scores_buf, stats, sem = refs[owners:]
-    step = pl.program_id(0)
     spans = spans_of(rows)
     groups = text_buf.shape[1] // (heads * HEAD_DIM)
     chunks = groups // blocks
     width = chunks * HEAD_DIM
     tiles = own_tiles(owners, slots, who, counts, perm)
 
-    @pl.when(step == 0)
-    def _():
+    def body(step, index):
+        @pl.when(step == 0)
+        def _():
+            for slot in range(slots):
+                @pl.when(tiles[slot][0] < owners)
+                def _(slot=slot):
+                    fetch(pieces, tiles[slot][0] ^ who[1], text_buf.at[slot], sem.at[slot])
+
         for slot in range(slots):
-            @pl.when(tiles[slot][0] < owners)
+            base = slot * heads * blocks
+
+            @pl.when((step == base) & (tiles[slot][0] < owners))
             def _(slot=slot):
-                fetch(pieces, tiles[slot][0] ^ who[1], text_buf.at[slot], sem.at[slot])
-
-    for slot in range(slots):
-        base = slot * heads * blocks
-
-        @pl.when((step == base) & (tiles[slot][0] < owners))
-        def _(slot=slot):
-            pltpu.make_async_copy(pieces[0], text_buf.at[slot], sem.at[slot]).wait()
-
-        @pl.when((step >= base) & (step < base + heads * blocks) & (tiles[slot][0] < owners))
-        def _(slot=slot, base=base):
-            head, block = (step - base) // blocks, (step - base) % blocks
-            query = rows_of(text_buf.at[slot], heads, head, block, chunks)
-            peak = jnp.full((8, width), -jnp.inf, F32)
-            for low, size, used in spans:
-                scores = dot_nt(keys[slot, low:low + size], query)
-                if size != used:
-                    row = lax.broadcasted_iota(jnp.int32, scores.shape, 0)
-                    scores = jnp.where(row < used, scores, -jnp.inf)
-                scores_buf[low:low + size] = scores
-                peak = jnp.maximum(peak, jnp.max(scores.reshape(-1, 8, width), axis=0))
-            top = jnp.max(peak, axis=0, keepdims=True) * SCALE_LOG2
-            mass = jnp.zeros((8, width), F32)
-            for low, size, used in spans:
-                part = jnp.exp2(scores_buf[low:low + size] * SCALE_LOG2 - top)
-                mass = mass + jnp.sum(part.reshape(-1, 8, width), axis=0)
-                weights[0, low:low + size] = part.astype(BF16)
-            stats[2 * head, pl.ds(block, 1)] = top
-            stats[2 * head + 1, pl.ds(block, 1)] = jnp.sum(mass, axis=0, keepdims=True)
-
-            @pl.when(step == base + heads * blocks - 1)
-            def _():
-                for done in range(blocks):
-                    lines = [stats[index, done:done + 1] for index in range(2 * heads)]
-                    full = note_rows(lines)
-                    size = full.shape[0]
-                    for chunk in range(chunks):
-                        first = (slot * groups + done * chunks + chunk) * size
-                        notes[first:first + size] = full[:, chunk * HEAD_DIM:(chunk + 1) * HEAD_DIM]
+                pltpu.make_async_copy(pieces[0], text_buf.at[slot], sem.at[slot]).wait()
+
+            @pl.when((step >= base) & (step < base + heads * blocks) & (tiles[slot][0] < owners))
+            def _(slot=slot, base=base):
+                head, block = (step - base) // blocks, (step - base) % blocks
+                query = rows_of(text_buf.at[slot], heads, head, block, chunks)
+                peak = jnp.full((8, width), -jnp.inf, F32)
+                for low, size, used in spans:
+                    scores = dot_nt(keys[slot, low:low + size], query)
+                    if size != used:
+                        row = lax.broadcasted_iota(jnp.int32, scores.shape, 0)
+                        scores = jnp.where(row < used, scores, -jnp.inf)
+                    scores_buf[low:low + size] = scores
+                    peak = jnp.maximum(peak, jnp.max(scores.reshape(-1, 8, width), axis=0))
+                top = jnp.max(peak, axis=0, keepdims=True) * SCALE_LOG2
+                mass = jnp.zeros((8, width), F32)
+                for low, size, used in spans:
+                    part = jnp.exp2(scores_buf[low:low + size] * SCALE_LOG2 - top)
+                    mass = mass + jnp.sum(part.reshape(-1, 8, width), axis=0)
+                    weights[index, low:low + size] = part.astype(BF16)
+                stats[2 * head, pl.ds(block, 1)] = top
+                stats[2 * head + 1, pl.ds(block, 1)] = jnp.sum(mass, axis=0, keepdims=True)
+
+                @pl.when(step == base + heads * blocks - 1)
+                def _():
+                    for done in range(blocks):
+                        lines = [stats[line, done:done + 1] for line in range(2 * heads)]
+                        full = note_rows(lines)
+                        size = full.shape[0]
+                        for chunk in range(chunks):
+                            first = (slot * groups + done * chunks + chunk) * size
+                            notes[first:first + size] = full[:, chunk * HEAD_DIM:(chunk + 1) * HEAD_DIM]
+
+    over_steps(body, slots * heads * blocks, in_place)
 
 
 def in_parts(value):
@@ -263,10 +269,9 @@
     return jnp.concatenate([text[pl.ds(start, HEAD_DIM)] for start in starts], axis=0)
 
 
-def slopes_kernel(owners, heads, blocks, slots, rows, who, counts, perm, notes, weights, values, keys_turned, *refs):
-    pieces = refs[:2]
+def slopes_kernel(chip_groups, owners, heads, blocks, slots, rows, in_place, who, counts, perm, notes, weights, values, keys_turned, *refs):
+    pieces = by_distance(chip_groups, refs[:2 * len(chip_groups)])
     slopes, turned, text_buf, deltas, sem = refs[-5:]
-    step = pl.program_id(0)
     spans = spans_of(rows)
     groups = turned.shape[2] // HEAD_DIM
     chunks = groups // blocks
@@ -274,42 +279,45 @@
     width = chunks * HEAD_DIM
     tiles = own_tiles(owners, slots, who, counts, perm)
 
-    @pl.when(step == 0)
-    def _():
+    def body(step, index):
+        @pl.when(step == 0)
+        def _():
+            for slot in range(slots):
+                @pl.when(tiles[slot][0] < owners)
+                def _(slot=slot):
+                    fetch(pieces, tiles[slot][0] ^ who[1], text_buf.at[slot], sem.at[slot])
+
+                @pl.when(tiles[slot][0] >= owners)
+                def _(slot=slot):
+                    turned[slot] = jnp.zeros(turned.shape[1:], BF16)
+
         for slot in range(slots):
-            @pl.when(tiles[slot][0] < owners)
+            base = slot * heads * blocks
+
+            @pl.when((step == base) & (tiles[slot][0] < owners))
             def _(slot=slot):
-                fetch_pair(pieces, tiles[slot][0] ^ who[1], text_buf.at[slot], sem.at[slot])
-
-            @pl.when(tiles[slot][0] >= owners)
-            def _(slot=slot):
-                turned[slot] = jnp.zeros(turned.shape[1:], BF16)
-
-    for slot in range(slots):
-        base = slot * heads * blocks
-
-        @pl.when((step == base) & (tiles[slot][0] < owners))
-        def _(slot=slot):
-            pltpu.make_async_copy(pieces[0].at[0, pl.ds(0, text_buf.shape[1])], text_buf.at[slot], sem.at[slot]).wait()
-            deltas[...] = text_buf[slot, text_rows:].astype(F32)
-            size = turned.shape[1] - heads * HEAD_DIM
-            for chunk in range(groups):
-                first = (slot * groups + chunk) * size
-                columns = slice(chunk * HEAD_DIM, (chunk + 1) * HEAD_DIM)
-                turned[slot, heads * HEAD_DIM:, columns] = notes[first:first + size]
-
-        @pl.when((step >= base) & (step < base + heads * blocks) & (tiles[slot][0] < owners))
-        def _(slot=slot, base=base):
-            head, block = (step - base) // blocks, (step - base) % blocks
-            grad = rows_of(text_buf.at[slot], heads, head, block, chunks)
-            first = block * chunks * heads + head
-            delta = jnp.concatenate([deltas[pl.ds(first + chunk * heads, 1)] for chunk in range(chunks)], axis=1)
-            for low, size, used in spans:
-                slope = dot_nt(values[slot, low:low + size], grad)
-                slopes[0, low:low + size] = (weights[0, low:low + size].astype(F32) * (slope - delta)).astype(BF16)
-            total = dot_nn(keys_turned[slot, :, :slopes.shape[1]], slopes[0])
-            columns = pl.ds(pl.multiple_of(block * width, width), width)
-            turned[slot, pl.ds(pl.multiple_of(head * HEAD_DIM, HEAD_DIM), HEAD_DIM), columns] = total.astype(BF16)
+                pltpu.make_async_copy(pieces[0], text_buf.at[slot], sem.at[slot]).wait()
+                deltas[...] = text_buf[slot, text_rows:].astype(F32)
+                size = turned.shape[1] - heads * HEAD_DIM
+                for chunk in range(groups):
+                    first = (slot * groups + chunk) * size
+                    columns = slice(chunk * HEAD_DIM, (chunk + 1) * HEAD_DIM)
+                    turned[slot, heads * HEAD_DIM:, columns] = notes[first:first + size]
+
+            @pl.when((step >= base) & (step < base + heads * blocks) & (tiles[slot][0] < owners))
+            def _(slot=slot, base=base):
+                head, block = (step - base) // blocks, (step - base) % blocks
+                grad = rows_of(text_buf.at[slot], heads, head, block, chunks)
+                first = block * chunks * heads + head
+                delta = jnp.concatenate([deltas[pl.ds(first + chunk * heads, 1)] for chunk in range(chunks)], axis=1)
+                for low, size, used in spans:
+                    slope = dot_nt(values[slot, low:low + size], grad)
+                    slopes[index, low:low + size] = (weights[index, low:low + size].astype(F32) * (slope - delta)).astype(BF16)
+                total = dot_nn(keys_turned[slot, :, :slopes.shape[1]], slopes[index])
+                columns = pl.ds(pl.multiple_of(block * width, width), width)
+                turned[slot, pl.ds(pl.multiple_of(head * HEAD_DIM, HEAD_DIM), HEAD_DIM), columns] = total.astype(BF16)
+
+    over_steps(body, slots * heads * blocks, in_place)
 
 
 def peak_and_mass(notes, owners, heads, groups, me, perm, start, tiles, head, chunk):
@@ -326,18 +334,10 @@
     return top, sum(mass * jnp.exp2(peak - top) for peak, mass in found)
 
 
-def factors_kernel(owners, heads, groups, slots, who, counts, perm, own, other, out, notes, sem):
-    copies = []
-    rows = notes.shape[1]
-    for core, source in enumerate((own, other)):
-        for chip in range(owners // 2):
-            place = 2 * chip + core
-            part = source.at[chip, pl.ds(source.shape[1] - rows, rows)]
-            copies.append(pltpu.make_async_copy(part, notes.at[place], sem.at[place]))
-    for copy in copies:
-        copy.start()
-    for copy in copies:
-        copy.wait()
+def factors_kernel(owners, heads, groups, slots, who, counts, perm, own, other, out, notes):
+    for chip in range(owners // 2):
+        notes[2 * chip] = own[chip]
+        notes[2 * chip + 1] = other[chip]
     size = whole_tiles(TERMS * heads)
     for slot, (sample, start) in enumerate(own_tiles(owners, slots, who, counts, perm)):
         @pl.when(sample < owners)
@@ -353,58 +353,53 @@
                     out[slot, head, chunk:chunk + 1] = jnp.exp2(peak - top) / mass
 
 
-def sums_kernel(owners, heads, blocks, slots, slot, who, counts, perm, *refs):
-    weights, slopes, factors = refs[:3]
-    q_pieces, g_pieces = refs[3:3 + owners], refs[3 + owners:5 + owners]
-    keep_out, send_out, q_buf, g_buf, sums, sem = refs[-6:]
-    step = pl.program_id(0)
-    odd, me = who[0] & 1, who[1]
-    groups = q_buf.shape[0] // (heads * HEAD_DIM)
+def sums_kernel(owners, heads, blocks, slots, slot, in_place, who, counts, perm, *refs):
+    weights, slopes, factors, q_buf, g_buf = refs[:5]
+    keep_out, send_out, sums = refs[-3:]
+    odd = who[0] & 1
+    groups = q_buf.shape[1] // (heads * HEAD_DIM)
     chunks = groups // blocks
     width = chunks * HEAD_DIM
     sample = own_tiles(owners, slots, who, counts, perm)[slot][0]
     used = sample < owners
 
-    @pl.when((step == 0) & used)
-    def _():
-        fetch(q_pieces, sample ^ me, q_buf, sem.at[0])
-        fetch_pair(g_pieces, sample ^ me, g_buf, sem.at[1])
-        pltpu.make_async_copy(q_pieces[0], q_buf, sem.at[0]).wait()
-        pltpu.make_async_copy(g_pieces[0].at[0, pl.ds(0, g_buf.shape[0])], g_buf, sem.at[1]).wait()
-
-    @pl.when(jnp.logical_not(used))
-    def _():
-        keep_out[...] = jnp.zeros(keep_out.shape, BF16)
-        send_out[...] = jnp.zeros(send_out.shape, BF16)
-
-    @pl.when(used)
-    def _():
-        head, block = step // blocks, step % blocks
-        factor = jnp.concatenate(
-            [factors[slot, head, pl.ds(block * chunks + chunk, 1)] for chunk in range(chunks)], axis=1
-        )
-        factor = jnp.transpose(jnp.broadcast_to(factor, (HEAD_DIM, width)))
-        query = rows_of(q_buf, heads, head, block, chunks)
-        grad = rows_of(g_buf, heads, head, block, chunks)
-        query = (query.astype(F32) * factor * SCALE).astype(BF16)
-        grad = (grad.astype(F32) * factor).astype(BF16)
-
-        def add(which, source, right, fresh):
-            for low in range(0, sums.shape[1], 2 * KEY_ROWS):
-                span = slice(low, min(low + 2 * KEY_ROWS, sums.shape[1]))
-                part = dot_nn(source[0, span], right)
-                sums[which, span] = part if fresh else sums[which, span] + part
-
-        for fresh in (True, False):
-            @pl.when((step == 0) == fresh)
-            def _(fresh=fresh):
-                add(0, slopes, query, fresh)
-                add(1, weights, grad, fresh)
-
-        @pl.when(step == heads * blocks - 1)
+    def body(step, index):
+        @pl.when(jnp.logical_not(used))
         def _():
-            keep_out[...] = sums[odd].astype(BF16)
-            send_out[...] = sums[1 - odd].astype(BF16)
+            keep_out[...] = jnp.zeros(keep_out.shape, BF16)
+            send_out[...] = jnp.zeros(send_out.shape, BF16)
+
+        @pl.when(used)
+        def _():
+            head, block = step // blocks, step % blocks
+            factor = jnp.concatenate(
+                [factors[slot, head, pl.ds(block * chunks + chunk, 1)] for chunk in range(chunks)], axis=1
+            )
+            factor = jnp.transpose(jnp.broadcast_to(factor, (HEAD_DIM, width)))
+            query = rows_of(q_buf.at[slot], heads, head, block, chunks)
+            grad = rows_of(g_buf.at[slot], heads, head, block, chunks)
+            query = (query.astype(F32) * factor * SCALE).astype(BF16)
+            grad = (grad.astype(F32) * factor).astype(BF16)
+
+            def add(which, source, right, fresh):
+                for low in range(0, sums.shape[1], 2 * KEY_ROWS):
+                    span = slice(low, min(low + 2 * KEY_ROWS, sums.shape[1]))
+                    part = dot_nn(source[index, span], right)
+                    sums[which, span] = part if fresh else sums[which, span] + part
+
+            for fresh in (True, False):
+                @pl.when((step == 0) == fresh)
+                def _(fresh=fresh):
+                    add(0, slopes, query, fresh)
+                    add(1, weights, grad, fresh)
+
+            @pl.when(step == heads * blocks - 1)
+            def _():
+                keep_out[...] = sums[odd].astype(BF16)
+                send_out[...] = sums[1 - odd].astype(BF16)
+
+    steps = heads * blocks
+    over_steps(lambda step, index: body(step, slot * steps + index if in_place else index), steps, in_place)
 
 
 def route_kernel(owners, heads, blocks, slots, who, counts, perm, own, other, *refs):
@@ -545,73 +540,83 @@
         cost=0,
     )
     stack_shape = jax.ShapeDtypeStruct((slots * steps, padded, block_rows), BF16)
-    stack_spec = pl.BlockSpec((1, padded, block_rows), lambda i: (i, 0, 0))
-    notes, weights = call(
-        functools.partial(weights_kernel, owners, heads, blocks, slots, tile_rows),
-        [jax.ShapeDtypeStruct((note_count, HEAD_DIM), BF16), stack_shape],
+    in_place = 2 * math.prod(stack_shape.shape) <= MOST_IN_PLACE
+    stack_spec = VMEM if in_place else pl.BlockSpec((1, padded, block_rows), lambda i: (i, 0, 0))
+    notes, weights, q_own = call(
+        functools.partial(weights_kernel, owners, heads, blocks, slots, tile_rows, in_place),
+        [
+            jax.ShapeDtypeStruct((note_count, HEAD_DIM), BF16),
+            stack_shape,
+            jax.ShapeDtypeStruct((slots,) + q_near[0].shape, BF16),
+        ],
         [SMEM] * 3 + [VMEM] + [ANY] * owners,
         [
-            pltpu.VMEM((slots,) + q_near[0].shape, BF16),
             pltpu.VMEM((padded, block_rows), F32),
             pltpu.VMEM((2 * heads, blocks, block_rows), F32),
             pltpu.SemaphoreType.DMA((slots,)),
         ],
         (*known, keys, *q_all),
-        out_specs=[VMEM, stack_spec],
-        grid=(slots * steps,),
+        out_specs=[VMEM, stack_spec, VMEM],
+        grid=() if in_place else (slots * steps,),
         megabytes=16,
         cost=0,
     )
+    def over_core(blocks_near, order):
+        joined = call(
+            functools.partial(join_kernel, len(blocks_near)),
+            jax.ShapeDtypeStruct((len(blocks_near),) + blocks_near[0].shape, BF16),
+            [ANY] * (len(blocks_near) + len(order)),
+            [pltpu.SemaphoreType.DMA((len(blocks_near),))],
+            (*blocks_near, *order),
+            megabytes=12 * scale,
+        )
+        return [joined, exchange(joined, "dp", 1)]
+
     notes_near = near(notes)
-    joined = call(
-        functools.partial(join_kernel, owners // 2),
-        jax.ShapeDtypeStruct((owners // 2, g_near[0].shape[0] + note_count, HEAD_DIM), BF16),
-        [ANY] * owners,
-        [pltpu.SemaphoreType.DMA((2, owners // 2))],
-        (*g_near, *notes_near),
-        megabytes=12 * scale,
-    )
-    g_pair = (joined, exchange(joined, "dp", 1))
-    slopes, part = call(
-        functools.partial(slopes_kernel, owners, heads, blocks, slots, tile_rows),
-        [stack_shape, jax.ShapeDtypeStruct((slots, width + note_size, text_rows), BF16)],
-        [SMEM] * 3 + [VMEM, stack_spec] + [VMEM] * 2 + [ANY] * 2,
+    direct = [chip for chip in range(1, owners // 2) if chip & (chip - 1) == 0]
+    chip_groups = [[chip for chip in range(owners // 2) if chip not in direct], direct]
+    g_pairs = []
+    for group in chip_groups:
+        g_pairs += over_core([g_near[chip] for chip in group], [notes])
+    slopes, part, g_own = call(
+        functools.partial(slopes_kernel, chip_groups, owners, heads, blocks, slots, tile_rows, in_place),
         [
-            pltpu.VMEM((slots,) + g_near[0].shape, BF16),
+            stack_shape,
+            jax.ShapeDtypeStruct((slots, width + note_size, text_rows), BF16),
+            jax.ShapeDtypeStruct((slots,) + g_near[0].shape, BF16),
+        ],
+        [SMEM] * 3 + [VMEM, stack_spec] + [VMEM] * 2 + [ANY] * len(g_pairs),
+        [
             pltpu.VMEM((delta_rows, HEAD_DIM), F32),
             pltpu.SemaphoreType.DMA((slots,)),
         ],
-        (*known, notes, weights, values, keys_turned, *g_pair),
-        out_specs=[stack_spec, VMEM],
-        grid=(slots * steps,),
+        (*known, notes, weights, values, keys_turned, *g_pairs),
+        out_specs=[stack_spec, VMEM, VMEM],
+        grid=() if in_place else (slots * steps,),
         megabytes=20,
         cost=6,
     )
+    notes_pair = over_core(notes_near, [part])
     factors = call(
         functools.partial(factors_kernel, owners, heads, groups, slots),
         jax.ShapeDtypeStruct((slots, heads, groups, HEAD_DIM), F32),
-        [SMEM] * 3 + [ANY] * 2,
-        [pltpu.VMEM((owners, note_count, HEAD_DIM), BF16), pltpu.SemaphoreType.DMA((owners,))],
-        (*known, *g_pair),
+        [SMEM] * 3 + [VMEM] * 2,
+        [pltpu.VMEM((owners, note_count, HEAD_DIM), BF16)],
+        (*known, *notes_pair),
         cost=30,
     )
     kept, got = [], []
 
     def tile_sums(slot, order):
-        left_spec = pl.BlockSpec((1, padded, block_rows), lambda i: (slot * steps + i, 0, 0))
+        left_spec = VMEM if in_place else pl.BlockSpec((1, padded, block_rows), lambda i: (slot * steps + i, 0, 0))
         keep, send = call(
-            functools.partial(sums_kernel, owners, heads, blocks, slots, slot),
+            functools.partial(sums_kernel, owners, heads, blocks, slots, slot, in_place),
             [jax.ShapeDtypeStruct((padded, HEAD_DIM), BF16)] * 2,
-            [SMEM] * 3 + [left_spec] * 2 + [VMEM] + [ANY] * (owners + 2 + len(order)),
-            [
-                pltpu.VMEM(q_near[0].shape, BF16),
-                pltpu.VMEM(g_near[0].shape, BF16),
-                pltpu.VMEM((2, padded, HEAD_DIM), F32),
-                pltpu.SemaphoreType.DMA((2,)),
-            ],
-            (*known, weights, slopes, factors, *q_all, *g_pair, *order),
+            [SMEM] * 3 + [left_spec] * 2 + [VMEM] * 3 + [ANY] * len(order),
+            [pltpu.VMEM((2, padded, HEAD_DIM), F32)],
+            (*known, weights, slopes, factors, q_own, g_own, *order),
             out_specs=[VMEM] * 2,
-            grid=(steps,),
+            grid=() if in_place else (steps,),
             megabytes=8 * scale,
             cost=4,
         )

time: 98.2 us -> 93.5 us (0.952)
  Pallas kernels: 26.7 us -> 18.8 us
  starting transfers between devices: 29.9 us -> 33.2 us
    pallas_call x15 -> x17, Pallas kernels: 26.7 us -> 18.8 us  [call(): pl.pallas_call(kernel, out_shape=out_shape, in_specs=in_specs, out_specs=...]
    ppermute x27 -> x29, starting transfers between devices: 29.9 us -> 33.2 us  [exchange(): return lax.ppermute(block, axis, [(i, i ^ distance) for i in range(count)])]
    ppermute x27 -> x29, waiting for transfers between devices: 35.8 us -> 35.6 us  [exchange(): return lax.ppermute(block, axis, [(i, i ^ distance) for i in range(count)])]
  transfers between devices with their start and end apart: 27 -> 29, of which waited for: 13 -> 13; matrix products, arithmetic and copies ran while one was open for 1% -> 1% of each run, Pallas kernels for 20% -> 18%
where the time goes in v6:
time: 93.5 us; the launch traced here: 93.2 us
  waiting for transfers between devices  35.6 us (38%)
  starting transfers between devices  33.2 us (36%)
  Pallas kernels  18.8 us (20%)
  local copies, waits for them, and re-layouts  4.11 us (4%)
  between operations  1.47 us (2%)
    ppermute x29, waiting for transfers between devices, exchange(): return lax.ppermute(block, axis, [(i, i ^ distance) for i in range(count)])  35.6 us
    ppermute x29, starting transfers between devices, exchange(): return lax.ppermute(block, axis, [(i, i ^ distance) for i in range(count)])  33.2 us
    pallas_call x17, Pallas kernels, call(): pl.pallas_call(kernel, out_shape=out_shape, in_specs=in_specs, out_specs=...  18.8 us
    unnamed x11, local copies, waits for them, and re-layouts  4.11 us
  transfers between devices with their start and end apart: 29, of which 13 were waited for; matrix products, arithmetic and copies ran while one was open for 1% of the time, Pallas kernels for 18%

profile of v6, /device:TPU:0, one launch (start us, length us, event | category | flops | bytes accessed | tf_op | source)
XLA Modules:
  0.0 93.2 jit_solution(9071812787454991298)
XLA Ops:
  1.4 0.9 %copy-done.2 = bf16[1,128,1024]{2,1,0:T(8,128)(2,1)S(1)} copy-done((bf16[1,128,1024]{2,1,0:T(8,128)(2,1)S(1)}, bf16[1,128,1024]{2,1,0:T(8,128)(2,1)}, u32[]{:S(2)}) %copy-start.2) | copy-done | bytes 262168
  2.3 0.9 %copy-done.3 = bf16[1,128,1024]{2,1,0:T(8,128)(2,1)S(1)} copy-done((bf16[1,128,1024]{2,1,0:T(8,128)(2,1)S(1)}, bf16[1,128,1024]{2,1,0:T(8,128)(2,1)}, u32[]{:S(2)}) %copy-start.3) | copy-done | bytes 262168
  3.3 0.9 %copy-done.4 = bf16[1,128,1024]{2,1,0:T(8,128)(2,1)S(1)} copy-done((bf16[1,128,1024]{2,1,0:T(8,128)(2,1)S(1)}, bf16[1,128,1024]{2,1,0:T(8,128)(2,1)}, u32[]{:S(2)}) %copy-start.4) | copy-done | bytes 262168
  4.2 1.0 %pack_kernel.1 = (bf16[528,128]{1,0:T(8,128)(2,1)S(1)}, bf16[528,128]{1,0:T(8,128)(2,1)S(1)}, bf16[528,128]{1,0:T(8,128)(2,1)S(1)}, bf16[528,128]{1,0:T(8,128)(2,1)S(1)}) custom-call(s32[2]{0:T(128)S(1)} %pad_add_fusion.who, s32[1]{0:T(128)S(6)} %copy.10.length, bf16[128,1024]{1,0:T(8,128)(2,1)S(1)} %bitcast.7, bf16[128,1024]{1,0:T(8,128)(2,1)S(1)} %bitcast.8, ...), custom_call_target="tpu_custom_call" | custom-call | flops 1000000000 | tf_op jit(solution)/shard_map/pack_kernel/pallas_call | solution.py:43
  5.2 3.1 %collective-permute-start = (bf16[528,128]{1,0:T(8,128)(2,1)S(1)}, bf16[528,128]{1,0:T(8,128)(2,1)S(1)}, u32[]{:S(2)}, u32[]{:S(2)}) collective-permute-start(bf16[528,128]{1,0:T(8,128)(2,1)S(1)} %get-tuple-element.29), channel_id=1, source_target_pairs={{0,8},{8,0},{16,24},{24,16},{1,9},{9,1},{17,25},{25,17},{2,10},{10... | collective-permute-start | bytes 405512 | tf_op jit(solution)/shard_map/ppermute | solution.py:36
  8.3 2.6 %collective-permute-start.1 = (bf16[528,128]{1,0:T(8,128)(2,1)S(1)}, bf16[528,128]{1,0:T(8,128)(2,1)S(1)}, u32[]{:S(2)}, u32[]{:S(2)}) collective-permute-start(bf16[528,128]{1,0:T(8,128)(2,1)S(1)} %get-tuple-element.30), channel_id=1, source_target_pairs={{0,16},{8,24},{16,0},{24,8},{1,17},{9,25},{17,1},{25,9},{2,18},{10... | collective-permute-start | bytes 405512 | tf_op jit(solution)/shard_map/ppermute | solution.py:36
  10.9 1.3 %copy.9.tiles = bf16[2,1601,128]{2,1,0:T(8,128)(2,1)S(1)} copy(bf16[2,1601,128]{2,0,1:T(2,128)(2,1)} %param.10) | data formatting | bytes 1639424 | tf_op args[3]
  12.1 1.4 %collective-permute-done.refs_0_.refs_1_ = bf16[528,128]{1,0:T(8,128)(2,1)S(1)} collective-permute-done((bf16[528,128]{1,0:T(8,128)(2,1)S(1)}, bf16[528,128]{1,0:T(8,128)(2,1)S(1)}, u32[]{:S(2)}, u32[]{:S(2)}) %collective-permute-start) | collective-permute-done | bytes 135200 | tf_op jit(solution)/shard_map/ppermute | solution.py:36
  13.5 8.0 %collective-permute-done.1.refs_1_.refs_2_ = bf16[528,128]{1,0:T(8,128)(2,1)S(1)} collective-permute-done((bf16[528,128]{1,0:T(8,128)(2,1)S(1)}, bf16[528,128]{1,0:T(8,128)(2,1)S(1)}, u32[]{:S(2)}, u32[]{:S(2)}) %collective-permute-start.1) | collective-permute-done | bytes 135200 | tf_op jit(solution)/shard_map/ppermute | solution.py:36
  21.5 2.1 %collective-permute-start.3 = (bf16[2,1616,128]{2,1,0:T(8,128)(2,1)S(1)}, bf16[2,1616,128]{2,1,0:T(8,128)(2,1)S(1)}, u32[]{:S(2)}, u32[]{:S(2)}) collective-permute-start(bf16[2,1616,128]{2,1,0:T(8,128)(2,1)S(1)} %pad_kernel.1.own.refs_4_), channel_id=1, source_target_pairs={{0,8},{8,0},{16,24},{24,16},{1,9},{9,1},{17,25},{25,17},{2,10},{10... | collective-permute-start | bytes 2482184 | tf_op jit(solution)/shard_map/ppermute | solution.py:36
  23.6 0.4 stack_kernel.2.refs_0_
  24.0 1.6 %collective-permute-start.5 = (bf16[1024,128]{1,0:T(8,128)(2,1)S(1)}, bf16[1024,128]{1,0:T(8,128)(2,1)S(1)}, u32[]{:S(2)}, u32[]{:S(2)}) collective-permute-start(bf16[1024,128]{1,0:T(8,128)(2,1)S(1)} %stack_kernel.2.refs_0_), channel_id=1, source_target_pairs={{0,2},{1,3},{2,0},{3,1},{4,6},{5,7},{6,4},{7,5},{8,10},{9,11},{10,... | collective-permute-start | bytes 786440 | tf_op jit(solution)/shard_map/ppermute | solution.py:36
  25.6 1.5 %collective-permute-start.9 = (bf16[1024,128]{1,0:T(8,128)(2,1)S(1)}, bf16[1024,128]{1,0:T(8,128)(2,1)S(1)}, u32[]{:S(2)}, u32[]{:S(2)}) collective-permute-start(bf16[1024,128]{1,0:T(8,128)(2,1)S(1)} %stack_kernel.2.refs_0_), channel_id=1, source_target_pairs={{0,6},{1,7},{2,4},{3,5},{4,2},{5,3},{6,0},{7,1},{8,14},{9,15},{10,... | collective-permute-start | bytes 786440 | tf_op jit(solution)/shard_map/ppermute | solution.py:36
  27.1 0.5 collective-permute-start.7
  27.6 5.8 %collective-permute-done.5.refs_2_.refs_4_ = bf16[1024,128]{1,0:T(8,128)(2,1)S(1)} collective-permute-done((bf16[1024,128]{1,0:T(8,128)(2,1)S(1)}, bf16[1024,128]{1,0:T(8,128)(2,1)S(1)}, u32[]{:S(2)}, u32[]{:S(2)}) %collective-permute-start.5) | collective-permute-done | bytes 262176 | tf_op jit(solution)/shard_map/ppermute | solution.py:36
  33.3 0.4 stack_kernel.3.refs_0_
  33.8 3.6 %collective-permute-done.9.refs_6_ = bf16[1024,128]{1,0:T(8,128)(2,1)S(1)} collective-permute-done((bf16[1024,128]{1,0:T(8,128)(2,1)S(1)}, bf16[1024,128]{1,0:T(8,128)(2,1)S(1)}, u32[]{:S(2)}, u32[]{:S(2)}) %collective-permute-start.9) | collective-permute-done | bytes 262176 | tf_op jit(solution)/shard_map/ppermute | solution.py:36
  37.4 1.5 %collective-permute-start.13 = (bf16[1040,128]{1,0:T(8,128)(2,1)S(1)}, bf16[1040,128]{1,0:T(8,128)(2,1)S(1)}, u32[]{:S(2)}, u32[]{:S(2)}) collective-permute-start(bf16[1040,128]{1,0:T(8,128)(2,1)S(1)} %stack_kernel.3.refs_0_), channel_id=1, source_target_pairs={{0,2},{1,3},{2,0},{3,1},{4,6},{5,7},{6,4},{7,5},{8,10},{9,11},{10,... | collective-permute-start | bytes 798728 | tf_op jit(solution)/shard_map/ppermute | solution.py:36
  38.9 0.5 collective-permute-start.14
  39.4 3.4 %collective-permute-start.11 = (bf16[1040,128]{1,0:T(8,128)(2,1)S(1)}, bf16[1040,128]{1,0:T(8,128)(2,1)S(1)}, u32[]{:S(2)}, u32[]{:S(2)}) collective-permute-start(bf16[1040,128]{1,0:T(8,128)(2,1)S(1)} %stack_kernel.3.refs_0_), channel_id=1, source_target_pairs={{0,6},{1,7},{2,4},{3,5},{4,2},{5,3},{6,0},{7,1},{8,14},{9,15},{10,... | collective-permute-start | bytes 798728 | tf_op jit(solution)/shard_map/ppermute | solution.py:36
  42.8 0.5 collective-permute-start.8
  43.3 1.0 %tiles_kernel.1 = (bf16[2,1616,128]{2,1,0:T(8,128)(2,1)S(1)}, bf16[2,1616,128]{2,1,0:T(8,128)(2,1)S(1)}, bf16[2,128,1664]{2,1,0:T(8,128)(2,1)S(1)}) custom-call(s32[2]{0:T(128)S(1)} %pad_add_fusion.who, bf16[2,1616,128]{2,1,0:T(8,128)(2,1)S(1)} %pad_kernel.1.own.refs_4_, bf16[2,1616,128]{2,1,0:T(8,128)(2,1)S(1)} %collective-permute-done.3.partner), custom_call_target="tpu_custom_call" | custom-call | tf_op jit(solution)/shard_map/tiles_kernel/pallas_call | solution.py:43
  44.7 3.2 %weights_kernel.1 = (bf16[128,128]{1,0:T(8,128)(2,1)S(1)}, bf16[4,1616,512]{2,1,0:T(8,128)(2,1)S(1)}, bf16[2,1024,128]{2,1,0:T(8,128)(2,1)S(1)}) custom-call(s32[2]{0:T(128)S(1)} %pad_add_fusion.who, s32[8]{0:T(128)S(1)} %copy-done, s32[8]{0:T(128)S(1)} %copy-done.1, bf16[2,1616,128]{2,1,0:T(8,128)(2,1)S(1)} %get-tuple-element.32.keys, ...), custom_call_target="tpu_custom_call" | custom-call | tf_op jit(solution)/shard_map/weights_kernel/pallas_call | solution.py:43
  47.9 2.2 %collective-permute-done.14.refs_1_ = bf16[1040,128]{1,0:T(8,128)(2,1)S(1)} collective-permute-done((bf16[1040,128]{1,0:T(8,128)(2,1)S(1)}, bf16[1040,128]{1,0:T(8,128)(2,1)S(1)}, u32[]{:S(2)}, u32[]{:S(2)}) %collective-permute-start.14) | collective-permute-done | bytes 266272 | tf_op jit(solution)/shard_map/ppermute | solution.py:36
  50.4 0.5 collective-permute-start.12
  51.0 1.8 %collective-permute-start.17 = (bf16[128,128]{1,0:T(8,128)(2,1)S(1)}, bf16[128,128]{1,0:T(8,128)(2,1)S(1)}, u32[]{:S(2)}, u32[]{:S(2)}) collective-permute-start(bf16[128,128]{1,0:T(8,128)(2,1)S(1)} %get-tuple-element.34.refs_2_.notes.refs_0_), channel_id=1, source_target_pairs={{0,2},{1,3},{2,0},{3,1},{4,6},{5,7},{6,4},{7,5},{8,10},{9,11},{10,... | collective-permute-start | bytes 98312 | tf_op jit(solution)/shard_map/ppermute | solution.py:36
  53.0 1.5 %collective-permute-start.19 = (bf16[128,128]{1,0:T(8,128)(2,1)S(1)}, bf16[128,128]{1,0:T(8,128)(2,1)S(1)}, u32[]{:S(2)}, u32[]{:S(2)}) collective-permute-start(bf16[128,128]{1,0:T(8,128)(2,1)S(1)} %get-tuple-element.34.refs_2_.notes.refs_0_), channel_id=1, source_target_pairs={{0,6},{1,7},{2,4},{3,5},{4,2},{5,3},{6,0},{7,1},{8,14},{9,15},{10,... | collective-permute-start | bytes 98312 | tf_op jit(solution)/shard_map/ppermute | solution.py:36
  54.4 2.6 %slopes_kernel.1 = (bf16[4,1616,512]{2,1,0:T(8,128)(2,1)S(1)}, bf16[2,272,512]{2,1,0:T(8,128)(2,1)S(1)}, bf16[2,1040,128]{2,1,0:T(8,128)(2,1)S(1)}) custom-call(s32[2]{0:T(128)S(1)} %pad_add_fusion.who, s32[8]{0:T(128)S(1)} %copy-done, s32[8]{0:T(128)S(1)} %copy-done.1, bf16[128,128]{1,0:T(8,128)(2,1)S(1)} %get-tuple-element.34.refs_2_.notes.refs_0_, ...), custom_call_target="tpu_custom_call" | custom-call | flops 6000000000 | tf_op jit(solution)/shard_map/slopes_kernel/pallas_call | solution.py:43
  57.0 0.7 collective-permute-done.19.refs_3_
  58.0 0.5 collective-permute-start.16
  58.5 0.8 collective-permute-done.20.other
  59.4 0.9 factors_kernel.1.refs_2_.refs_0_
  60.3 3.1 %sums_kernel.2 = (bf16[1616,128]{1,0:T(8,128)(2,1)S(1)}, bf16[1616,128]{1,0:T(8,128)(2,1)S(1)}) custom-call(s32[2]{0:T(128)S(1)} %pad_add_fusion.who, s32[8]{0:T(128)S(1)} %copy-done, s32[8]{0:T(128)S(1)} %copy-done.1, bf16[4,1616,512]{2,1,0:T(8,128)(2,1)S(1)} %get-tuple-element.35.weights.refs_0_, bf16[4,1616,512]{2,1,0:T(8,128)(2,1)S(1)} %get-tuple-element.39.refs_1_, ...), custom_call_target="tpu_custom_call" | custom-call | flops 4000000000 | tf_op jit(solution)/shard_map/sums_kernel/pallas_call | solution.py:43
  63.4 0.8 collective-permute-start.27
  64.2 1.4 %route_kernel.1 = (bf16[272,512]{1,0:T(8,128)(2,1)S(1)}, bf16[272,512]{1,0:T(8,128)(2,1)S(1)}, bf16[272,512]{1,0:T(8,128)(2,1)S(1)}, bf16[272,512]{1,0:T(8,128)(2,1)S(1)}) custom-call(s32[2]{0:T(128)S(1)} %pad_add_fusion.who, s32[8]{0:T(128)S(1)} %copy-done, s32[8]{0:T(128)S(1)} %copy-done.1, bf16[2,272,512]{2,1,0:T(8,128)(2,1)S(1)} %get-tuple-element.38.refs_4_.own, ...), custom_call_target="tpu_custom_call" | custom-call | flops 30000001024 | tf_op jit(solution)/shard_map/route_kernel/pallas_call | solution.py:43
  65.6 2.4 %collective-permute-start.21 = (bf16[272,512]{1,0:T(8,128)(2,1)S(1)}, bf16[272,512]{1,0:T(8,128)(2,1)S(1)}, u32[]{:S(2)}, u32[]{:S(2)}) collective-permute-start(bf16[272,512]{1,0:T(8,128)(2,1)S(1)} %get-tuple-element.44), channel_id=1, source_target_pairs={{0,2},{1,3},{2,0},{3,1},{4,6},{5,7},{6,4},{7,5},{8,10},{9,11},{10,... | collective-permute-start | bytes 835592 | tf_op jit(solution)/shard_map/ppermute | solution.py:36
  68.1 1.5 %collective-permute-start.23 = (bf16[272,512]{1,0:T(8,128)(2,1)S(1)}, bf16[272,512]{1,0:T(8,128)(2,1)S(1)}, u32[]{:S(2)}, u32[]{:S(2)}) collective-permute-start(bf16[272,512]{1,0:T(8,128)(2,1)S(1)} %get-tuple-element.46), channel_id=1, source_target_pairs={{0,6},{1,7},{2,4},{3,5},{4,2},{5,3},{6,0},{7,1},{8,14},{9,15},{10,... | collective-permute-start | bytes 835592 | tf_op jit(solution)/shard_map/ppermute | solution.py:36
  69.6 0.8 sums_kernel.3
  70.4 2.1 %collective-permute-start.28 = (bf16[1616,128]{1,0:T(8,128)(2,1)S(1)}, bf16[1616,128]{1,0:T(8,128)(2,1)S(1)}, u32[]{:S(2)}, u32[]{:S(2)}) collective-permute-start(bf16[1616,128]{1,0:T(8,128)(2,1)S(1)} %get-tuple-element.53), channel_id=1, source_target_pairs={{0,8},{8,0},{16,24},{24,16},{1,9},{9,1},{17,25},{25,17},{2,10},{10... | collective-permute-start | bytes 1241096 | tf_op jit(solution)/shard_map/ppermute | solution.py:36
  72.5 3.0 %collective-permute-done.21.refs_1_ = bf16[272,512]{1,0:T(8,128)(2,1)S(1)} collective-permute-done((bf16[272,512]{1,0:T(8,128)(2,1)S(1)}, bf16[272,512]{1,0:T(8,128)(2,1)S(1)}, u32[]{:S(2)}, u32[]{:S(2)}) %collective-permute-start.21) | collective-permute-done | bytes 278560 | tf_op jit(solution)/shard_map/ppermute | solution.py:36
  75.5 7.0 %collective-permute-done.22.refs_2_ = bf16[272,512]{1,0:T(8,128)(2,1)S(1)} collective-permute-done((bf16[272,512]{1,0:T(8,128)(2,1)S(1)}, bf16[272,512]{1,0:T(8,128)(2,1)S(1)}, u32[]{:S(2)}, u32[]{:S(2)}) %collective-permute-start.22) | collective-permute-done | bytes 278560 | tf_op jit(solution)/shard_map/ppermute | solution.py:36
  82.8 1.8 %collective-permute-start.24 = (bf16[128,256]{1,0:T(8,128)(2,1)S(1)}, bf16[128,256]{1,0:T(8,128)(2,1)S(1)}, u32[]{:S(2)}, u32[]{:S(2)}) collective-permute-start(bf16[128,256]{1,0:T(8,128)(2,1)S(1)} %get-tuple-element.48), channel_id=1, source_target_pairs={{0,8},{8,0},{16,24},{24,16},{1,9},{9,1},{17,25},{25,17},{2,10},{10... | collective-permute-start | bytes 196616 | tf_op jit(solution)/shard_map/ppermute | solution.py:36
  84.6 1.2 %collective-permute-start.25 = (bf16[128,256]{1,0:T(8,128)(2,1)S(1)}, bf16[128,256]{1,0:T(8,128)(2,1)S(1)}, u32[]{:S(2)}, u32[]{:S(2)}) collective-permute-start(bf16[128,256]{1,0:T(8,128)(2,1)S(1)} %get-tuple-element.49), channel_id=1, source_target_pairs={{0,16},{8,24},{16,0},{24,8},{1,17},{9,25},{17,1},{25,9},{2,18},{10... | collective-permute-start | bytes 196616 | tf_op jit(solution)/shard_map/ppermute | solution.py:36
  85.8 1.5 %collective-permute-start.26 = (bf16[128,256]{1,0:T(8,128)(2,1)S(1)}, bf16[128,256]{1,0:T(8,128)(2,1)S(1)}, u32[]{:S(2)}, u32[]{:S(2)}) collective-permute-start(bf16[128,256]{1,0:T(8,128)(2,1)S(1)} %get-tuple-element.50), channel_id=1, source_target_pairs={{0,24},{8,16},{16,8},{24,0},{1,25},{9,17},{17,9},{25,1},{2,26},{10... | collective-permute-start | bytes 196616 | tf_op jit(solution)/shard_map/ppermute | solution.py:36
  87.3 2.0 %merge_kernel.1 = (bf16[1601,2,128]{2,1,0:T(2,128)(2,1)}, bf16[16,128]{1,0:T(8,128)(2,1)S(1)}) custom-call(bf16[1616,128]{1,0:T(8,128)(2,1)S(1)} %get-tuple-element.42.refs_1_.refs_0_, bf16[1616,128]{1,0:T(8,128)(2,1)S(1)} %get-tuple-element.51.refs_1_, bf16[1616,128]{1,0:T(8,128)(2,1)S(1)} %collective-permute-done.27.refs_2_, ...), custom_call_target="tpu_custom_call" | custom-call | flops 2000000000 | tf_op jit(solution)/shard_map/merge_kernel/pallas_call | solution.py:43
  89.3 1.2 %collective-permute-done.25.refs_2_ = bf16[128,256]{1,0:T(8,128)(2,1)S(1)} collective-permute-done((bf16[128,256]{1,0:T(8,128)(2,1)S(1)}, bf16[128,256]{1,0:T(8,128)(2,1)S(1)}, u32[]{:S(2)}, u32[]{:S(2)}) %collective-permute-start.25) | collective-permute-done | bytes 65568 | tf_op jit(solution)/shard_map/ppermute | solution.py:36
  90.5 1.5 %collective-permute-done.26.refs_3_ = bf16[128,256]{1,0:T(8,128)(2,1)S(1)} collective-permute-done((bf16[128,256]{1,0:T(8,128)(2,1)S(1)}, bf16[128,256]{1,0:T(8,128)(2,1)S(1)}, u32[]{:S(2)}, u32[]{:S(2)}) %collective-permute-start.26) | collective-permute-done | bytes 65568 | tf_op jit(solution)/shard_map/ppermute | solution.py:36
  91.9 1.3 %place_kernel.1 = bf16[128,1024]{1,0:T(8,128)(2,1)} custom-call(s32[2]{0:T(128)S(1)} %pad_add_fusion.who, bf16[128,256]{1,0:T(8,128)(2,1)S(1)} %get-tuple-element.47.refs_0_, bf16[128,256]{1,0:T(8,128)(2,1)S(1)} %collective-permute-done.24.refs_1_, bf16[128,256]{1,0:T(8,128)(2,1)S(1)} %collective-permute-done.25.refs_2_, ...), custom_call_target="tpu_custom_call" | custom-call | flops 1000000000 | tf_op jit(solution)/shard_map/place_kernel/pallas_call | solution.py:43
  (39 shorter events, 1.6 us)
Async XLA Ops:
  1.4 1.0 %copy-start.2 = (bf16[1,128,1024]{2,1,0:T(8,128)(2,1)S(1)}, bf16[1,128,1024]{2,1,0:T(8,128)(2,1)}, u32[]{:S(2)}) copy-start(bf16[1,128,1024]{2,1,0:T(8,128)(2,1)} %param.7) | copy-start | bytes 786436
  2.3 0.9 %copy-start.3 = (bf16[1,128,1024]{2,1,0:T(8,128)(2,1)S(1)}, bf16[1,128,1024]{2,1,0:T(8,128)(2,1)}, u32[]{:S(2)}) copy-start(bf16[1,128,1024]{2,1,0:T(8,128)(2,1)} %param.8) | copy-start | bytes 786436
  3.3 0.9 %copy-start.4 = (bf16[1,128,1024]{2,1,0:T(8,128)(2,1)S(1)}, bf16[1,128,1024]{2,1,0:T(8,128)(2,1)}, u32[]{:S(2)}) copy-start(bf16[1,128,1024]{2,1,0:T(8,128)(2,1)} %param.9) | copy-start | bytes 786436
  4.2 40.5 %copy-start = (s32[8]{0:T(128)S(1)}, s32[8]{0:T(128)}, u32[]{:S(2)}) copy-start(s32[8]{0:T(128)} %counts.11) | copy-start | bytes 100
  4.2 40.5 %copy-start.1 = (s32[8]{0:T(128)S(1)}, s32[8]{0:T(128)}, u32[]{:S(2)}) copy-start(s32[8]{0:T(128)} %perm.11) | copy-start | bytes 100
  5.2 8.3 %collective-permute-start = (bf16[528,128]{1,0:T(8,128)(2,1)S(1)}, bf16[528,128]{1,0:T(8,128)(2,1)S(1)}, u32[]{:S(2)}, u32[]{:S(2)}) collective-permute-start(bf16[528,128]{1,0:T(8,128)(2,1)S(1)} %get-tuple-element.29), channel_id=1, source_target_pairs={{0,8},{8,0},{16,24},{24,16},{1,9},{9,1},{17,25},{25,17},{2,10},{10... | collective-permute-start | bytes 405512 | tf_op jit(solution)/shard_map/ppermute | solution.py:36
  8.3 13.2 %collective-permute-start.1 = (bf16[528,128]{1,0:T(8,128)(2,1)S(1)}, bf16[528,128]{1,0:T(8,128)(2,1)S(1)}, u32[]{:S(2)}, u32[]{:S(2)}) collective-permute-start(bf16[528,128]{1,0:T(8,128)(2,1)S(1)} %get-tuple-element.30), channel_id=1, source_target_pairs={{0,16},{8,24},{16,0},{24,8},{1,17},{9,25},{17,1},{25,9},{2,18},{10... | collective-permute-start | bytes 405512 | tf_op jit(solution)/shard_map/ppermute | solution.py:36
  10.9 10.6 %collective-permute-start.2 = (bf16[528,128]{1,0:T(8,128)(2,1)S(1)}, bf16[528,128]{1,0:T(8,128)(2,1)S(1)}, u32[]{:S(2)}, u32[]{:S(2)}) collective-permute-start(bf16[528,128]{1,0:T(8,128)(2,1)S(1)} %get-tuple-element.31), channel_id=1, source_target_pairs={{0,24},{8,16},{16,8},{24,0},{1,25},{9,17},{17,9},{25,1},{2,26},{10... | collective-permute-start | bytes 405512 | tf_op jit(solution)/shard_map/ppermute | solution.py:36
  21.5 21.2 %collective-permute-start.3 = (bf16[2,1616,128]{2,1,0:T(8,128)(2,1)S(1)}, bf16[2,1616,128]{2,1,0:T(8,128)(2,1)S(1)}, u32[]{:S(2)}, u32[]{:S(2)}) collective-permute-start(bf16[2,1616,128]{2,1,0:T(8,128)(2,1)S(1)} %pad_kernel.1.own.refs_4_), channel_id=1, source_target_pairs={{0,8},{8,0},{16,24},{24,16},{1,9},{9,1},{17,25},{25,17},{2,10},{10... | collective-permute-start | bytes 2482184 | tf_op jit(solution)/shard_map/ppermute | solution.py:36
  24.0 9.3 %collective-permute-start.5 = (bf16[1024,128]{1,0:T(8,128)(2,1)S(1)}, bf16[1024,128]{1,0:T(8,128)(2,1)S(1)}, u32[]{:S(2)}, u32[]{:S(2)}) collective-permute-start(bf16[1024,128]{1,0:T(8,128)(2,1)S(1)} %stack_kernel.2.refs_0_), channel_id=1, source_target_pairs={{0,2},{1,3},{2,0},{3,1},{4,6},{5,7},{6,4},{7,5},{8,10},{9,11},{10,... | collective-permute-start | bytes 786440 | tf_op jit(solution)/shard_map/ppermute | solution.py:36
  25.6 11.8 %collective-permute-start.9 = (bf16[1024,128]{1,0:T(8,128)(2,1)S(1)}, bf16[1024,128]{1,0:T(8,128)(2,1)S(1)}, u32[]{:S(2)}, u32[]{:S(2)}) collective-permute-start(bf16[1024,128]{1,0:T(8,128)(2,1)S(1)} %stack_kernel.2.refs_0_), channel_id=1, source_target_pairs={{0,6},{1,7},{2,4},{3,5},{4,2},{5,3},{6,0},{7,1},{8,14},{9,15},{10,... | collective-permute-start | bytes 786440 | tf_op jit(solution)/shard_map/ppermute | solution.py:36
  27.1 11.8 %collective-permute-start.7 = (bf16[1024,128]{1,0:T(8,128)(2,1)S(1)}, bf16[1024,128]{1,0:T(8,128)(2,1)S(1)}, u32[]{:S(2)}, u32[]{:S(2)}) collective-permute-start(bf16[1024,128]{1,0:T(8,128)(2,1)S(1)} %stack_kernel.2.refs_0_), channel_id=1, source_target_pairs={{0,4},{1,5},{2,6},{3,7},{4,0},{5,1},{6,2},{7,3},{8,12},{9,13},{10,... | collective-permute-start | bytes 786440 | tf_op jit(solution)/shard_map/ppermute | solution.py:36
  27.6 11.8 %collective-permute-start.4 = (bf16[1024,128]{1,0:T(8,128)(2,1)S(1)}, bf16[1024,128]{1,0:T(8,128)(2,1)S(1)}, u32[]{:S(2)}, u32[]{:S(2)}) collective-permute-start(bf16[1024,128]{1,0:T(8,128)(2,1)S(1)} %stack_kernel.2.refs_0_), channel_id=1, source_target_pairs={{0,1},{1,0},{2,3},{3,2},{4,5},{5,4},{6,7},{7,6},{8,9},{9,8},{10,11... | collective-permute-start | bytes 786440 | tf_op jit(solution)/shard_map/ppermute | solution.py:36
  33.3 9.4 %collective-permute-start.6 = (bf16[1024,128]{1,0:T(8,128)(2,1)S(1)}, bf16[1024,128]{1,0:T(8,128)(2,1)S(1)}, u32[]{:S(2)}, u32[]{:S(2)}) collective-permute-start(bf16[1024,128]{1,0:T(8,128)(2,1)S(1)} %collective-permute-done.5.refs_2_.refs_4_), channel_id=1, source_target_pairs={{0,1},{1,0},{2,3},{3,2},{4,5},{5,4},{6,7},{7,6},{8,9},{9,8},{10,11... | collective-permute-start | bytes 786440 | tf_op jit(solution)/shard_map/ppermute | solution.py:36
  37.4 10.5 %collective-permute-start.13 = (bf16[1040,128]{1,0:T(8,128)(2,1)S(1)}, bf16[1040,128]{1,0:T(8,128)(2,1)S(1)}, u32[]{:S(2)}, u32[]{:S(2)}) collective-permute-start(bf16[1040,128]{1,0:T(8,128)(2,1)S(1)} %stack_kernel.3.refs_0_), channel_id=1, source_target_pairs={{0,2},{1,3},{2,0},{3,1},{4,6},{5,7},{6,4},{7,5},{8,10},{9,11},{10,... | collective-permute-start | bytes 798728 | tf_op jit(solution)/shard_map/ppermute | solution.py:36
  38.9 11.3 %collective-permute-start.14 = (bf16[1040,128]{1,0:T(8,128)(2,1)S(1)}, bf16[1040,128]{1,0:T(8,128)(2,1)S(1)}, u32[]{:S(2)}, u32[]{:S(2)}) collective-permute-start(bf16[1040,128]{1,0:T(8,128)(2,1)S(1)} %stack_kernel.3.refs_0_), channel_id=1, source_target_pairs={{0,4},{1,5},{2,6},{3,7},{4,0},{5,1},{6,2},{7,3},{8,12},{9,13},{10,... | collective-permute-start | bytes 798728 | tf_op jit(solution)/shard_map/ppermute | solution.py:36
  39.4 10.9 %collective-permute-start.11 = (bf16[1040,128]{1,0:T(8,128)(2,1)S(1)}, bf16[1040,128]{1,0:T(8,128)(2,1)S(1)}, u32[]{:S(2)}, u32[]{:S(2)}) collective-permute-start(bf16[1040,128]{1,0:T(8,128)(2,1)S(1)} %stack_kernel.3.refs_0_), channel_id=1, source_target_pairs={{0,6},{1,7},{2,4},{3,5},{4,2},{5,3},{6,0},{7,1},{8,14},{9,15},{10,... | collective-permute-start | bytes 798728 | tf_op jit(solution)/shard_map/ppermute | solution.py:36
  42.8 1.5 %collective-permute-start.10 = (bf16[1024,128]{1,0:T(8,128)(2,1)S(1)}, bf16[1024,128]{1,0:T(8,128)(2,1)S(1)}, u32[]{:S(2)}, u32[]{:S(2)}) collective-permute-start(bf16[1024,128]{1,0:T(8,128)(2,1)S(1)} %collective-permute-done.9.refs_6_), channel_id=1, source_target_pairs={{0,1},{1,0},{2,3},{3,2},{4,5},{5,4},{6,7},{7,6},{8,9},{9,8},{10,11... | collective-permute-start | bytes 786440 | tf_op jit(solution)/shard_map/ppermute | solution.py:36
  42.8 1.9 %collective-permute-start.8 = (bf16[1024,128]{1,0:T(8,128)(2,1)S(1)}, bf16[1024,128]{1,0:T(8,128)(2,1)S(1)}, u32[]{:S(2)}, u32[]{:S(2)}) collective-permute-start(bf16[1024,128]{1,0:T(8,128)(2,1)S(1)} %collective-permute-done.7.refs_4_), channel_id=1, source_target_pairs={{0,1},{1,0},{2,3},{3,2},{4,5},{5,4},{6,7},{7,6},{8,9},{9,8},{10,11... | collective-permute-start | bytes 786440 | tf_op jit(solution)/shard_map/ppermute | solution.py:36
  50.2 4.2 %collective-permute-start.15 = (bf16[2,1040,128]{2,1,0:T(8,128)(2,1)S(1)}, bf16[2,1040,128]{2,1,0:T(8,128)(2,1)S(1)}, u32[]{:S(2)}, u32[]{:S(2)}) collective-permute-start(bf16[2,1040,128]{2,1,0:T(8,128)(2,1)S(1)} %join_kernel.4.refs_2_), channel_id=1, source_target_pairs={{0,1},{1,0},{2,3},{3,2},{4,5},{5,4},{6,7},{7,6},{8,9},{9,8},{10,11... | collective-permute-start | bytes 1597448 | tf_op jit(solution)/shard_map/ppermute | solution.py:36
  50.4 4.0 %collective-permute-start.12 = (bf16[2,1040,128]{2,1,0:T(8,128)(2,1)S(1)}, bf16[2,1040,128]{2,1,0:T(8,128)(2,1)S(1)}, u32[]{:S(2)}, u32[]{:S(2)}) collective-permute-start(bf16[2,1040,128]{2,1,0:T(8,128)(2,1)S(1)} %join_kernel.3.refs_0_), channel_id=1, source_target_pairs={{0,1},{1,0},{2,3},{3,2},{4,5},{5,4},{6,7},{7,6},{8,9},{9,8},{10,11... | collective-permute-start | bytes 1597448 | tf_op jit(solution)/shard_map/ppermute | solution.py:36
  51.0 6.1 %collective-permute-start.17 = (bf16[128,128]{1,0:T(8,128)(2,1)S(1)}, bf16[128,128]{1,0:T(8,128)(2,1)S(1)}, u32[]{:S(2)}, u32[]{:S(2)}) collective-permute-start(bf16[128,128]{1,0:T(8,128)(2,1)S(1)} %get-tuple-element.34.refs_2_.notes.refs_0_), channel_id=1, source_target_pairs={{0,2},{1,3},{2,0},{3,1},{4,6},{5,7},{6,4},{7,5},{8,10},{9,11},{10,... | collective-permute-start | bytes 98312 | tf_op jit(solution)/shard_map/ppermute | solution.py:36
  52.8 4.3 %collective-permute-start.18 = (bf16[128,128]{1,0:T(8,128)(2,1)S(1)}, bf16[128,128]{1,0:T(8,128)(2,1)S(1)}, u32[]{:S(2)}, u32[]{:S(2)}) collective-permute-start(bf16[128,128]{1,0:T(8,128)(2,1)S(1)} %get-tuple-element.34.refs_2_.notes.refs_0_), channel_id=1, source_target_pairs={{0,4},{1,5},{2,6},{3,7},{4,0},{5,1},{6,2},{7,3},{8,12},{9,13},{10,... | collective-permute-start | bytes 98312 | tf_op jit(solution)/shard_map/ppermute | solution.py:36
  53.0 4.8 %collective-permute-start.19 = (bf16[128,128]{1,0:T(8,128)(2,1)S(1)}, bf16[128,128]{1,0:T(8,128)(2,1)S(1)}, u32[]{:S(2)}, u32[]{:S(2)}) collective-permute-start(bf16[128,128]{1,0:T(8,128)(2,1)S(1)} %get-tuple-element.34.refs_2_.notes.refs_0_), channel_id=1, source_target_pairs={{0,6},{1,7},{2,4},{3,5},{4,2},{5,3},{6,0},{7,1},{8,14},{9,15},{10,... | collective-permute-start | bytes 98312 | tf_op jit(solution)/shard_map/ppermute | solution.py:36
  58.0 1.4 %collective-permute-start.20 = (bf16[4,128,128]{2,1,0:T(8,128)(2,1)S(1)}, bf16[4,128,128]{2,1,0:T(8,128)(2,1)S(1)}, u32[]{:S(2)}, u32[]{:S(2)}) collective-permute-start(bf16[4,128,128]{2,1,0:T(8,128)(2,1)S(1)} %join_kernel.5.own), channel_id=1, source_target_pairs={{0,1},{1,0},{2,3},{3,2},{4,5},{5,4},{6,7},{7,6},{8,9},{9,8},{10,11... | collective-permute-start | bytes 393224 | tf_op jit(solution)/shard_map/ppermute | solution.py:36
  58.0 6.1 %collective-permute-start.16 = (bf16[2,272,512]{2,1,0:T(8,128)(2,1)S(1)}, bf16[2,272,512]{2,1,0:T(8,128)(2,1)S(1)}, u32[]{:S(2)}, u32[]{:S(2)}) collective-permute-start(bf16[2,272,512]{2,1,0:T(8,128)(2,1)S(1)} %get-tuple-element.38.refs_4_.own), channel_id=1, source_target_pairs={{0,1},{1,0},{2,3},{3,2},{4,5},{5,4},{6,7},{7,6},{8,9},{9,8},{10,11... | collective-permute-start | bytes 1671176 | tf_op jit(solution)/shard_map/ppermute | solution.py:36
  63.4 23.9 %collective-permute-start.27 = (bf16[1616,128]{1,0:T(8,128)(2,1)S(1)}, bf16[1616,128]{1,0:T(8,128)(2,1)S(1)}, u32[]{:S(2)}, u32[]{:S(2)}) collective-permute-start(bf16[1616,128]{1,0:T(8,128)(2,1)S(1)} %get-tuple-element.52), channel_id=1, source_target_pairs={{0,8},{8,0},{16,24},{24,16},{1,9},{9,1},{17,25},{25,17},{2,10},{10... | collective-permute-start | bytes 1241096 | tf_op jit(solution)/shard_map/ppermute | solution.py:36
  65.6 9.9 %collective-permute-start.21 = (bf16[272,512]{1,0:T(8,128)(2,1)S(1)}, bf16[272,512]{1,0:T(8,128)(2,1)S(1)}, u32[]{:S(2)}, u32[]{:S(2)}) collective-permute-start(bf16[272,512]{1,0:T(8,128)(2,1)S(1)} %get-tuple-element.44), channel_id=1, source_target_pairs={{0,2},{1,3},{2,0},{3,1},{4,6},{5,7},{6,4},{7,5},{8,10},{9,11},{10,... | collective-permute-start | bytes 835592 | tf_op jit(solution)/shard_map/ppermute | solution.py:36
  68.1 14.4 %collective-permute-start.22 = (bf16[272,512]{1,0:T(8,128)(2,1)S(1)}, bf16[272,512]{1,0:T(8,128)(2,1)S(1)}, u32[]{:S(2)}, u32[]{:S(2)}) collective-permute-start(bf16[272,512]{1,0:T(8,128)(2,1)S(1)} %get-tuple-element.45), channel_id=1, source_target_pairs={{0,4},{1,5},{2,6},{3,7},{4,0},{5,1},{6,2},{7,3},{8,12},{9,13},{10,... | collective-permute-start | bytes 835592 | tf_op jit(solution)/shard_map/ppermute | solution.py:36
  68.1 14.4 %collective-permute-start.23 = (bf16[272,512]{1,0:T(8,128)(2,1)S(1)}, bf16[272,512]{1,0:T(8,128)(2,1)S(1)}, u32[]{:S(2)}, u32[]{:S(2)}) collective-permute-start(bf16[272,512]{1,0:T(8,128)(2,1)S(1)} %get-tuple-element.46), channel_id=1, source_target_pairs={{0,6},{1,7},{2,4},{3,5},{4,2},{5,3},{6,0},{7,1},{8,14},{9,15},{10,... | collective-permute-start | bytes 835592 | tf_op jit(solution)/shard_map/ppermute | solution.py:36
  70.4 16.8 %collective-permute-start.28 = (bf16[1616,128]{1,0:T(8,128)(2,1)S(1)}, bf16[1616,128]{1,0:T(8,128)(2,1)S(1)}, u32[]{:S(2)}, u32[]{:S(2)}) collective-permute-start(bf16[1616,128]{1,0:T(8,128)(2,1)S(1)} %get-tuple-element.53), channel_id=1, source_target_pairs={{0,8},{8,0},{16,24},{24,16},{1,9},{9,1},{17,25},{25,17},{2,10},{10... | collective-permute-start | bytes 1241096 | tf_op jit(solution)/shard_map/ppermute | solution.py:36
  82.8 6.5 %collective-permute-start.24 = (bf16[128,256]{1,0:T(8,128)(2,1)S(1)}, bf16[128,256]{1,0:T(8,128)(2,1)S(1)}, u32[]{:S(2)}, u32[]{:S(2)}) collective-permute-start(bf16[128,256]{1,0:T(8,128)(2,1)S(1)} %get-tuple-element.48), channel_id=1, source_target_pairs={{0,8},{8,0},{16,24},{24,16},{1,9},{9,1},{17,25},{25,17},{2,10},{10... | collective-permute-start | bytes 196616 | tf_op jit(solution)/shard_map/ppermute | solution.py:36
  84.6 5.9 %collective-permute-start.25 = (bf16[128,256]{1,0:T(8,128)(2,1)S(1)}, bf16[128,256]{1,0:T(8,128)(2,1)S(1)}, u32[]{:S(2)}, u32[]{:S(2)}) collective-permute-start(bf16[128,256]{1,0:T(8,128)(2,1)S(1)} %get-tuple-element.49), channel_id=1, source_target_pairs={{0,16},{8,24},{16,0},{24,8},{1,17},{9,25},{17,1},{25,9},{2,18},{10... | collective-permute-start | bytes 196616 | tf_op jit(solution)/shard_map/ppermute | solution.py:36
  85.8 6.1 %collective-permute-start.26 = (bf16[128,256]{1,0:T(8,128)(2,1)S(1)}, bf16[128,256]{1,0:T(8,128)(2,1)S(1)}, u32[]{:S(2)}, u32[]{:S(2)}) collective-permute-start(bf16[128,256]{1,0:T(8,128)(2,1)S(1)} %get-tuple-element.50), channel_id=1, source_target_pairs={{0,24},{8,16},{16,8},{24,0},{1,25},{9,17},{17,9},{25,1},{2,26},{10... | collective-permute-start | bytes 196616 | tf_op jit(solution)/shard_map/ppermute | solution.py:36

commit v7 on v6

--- a/solution.py
+++ b/solution.py
@@ -131,11 +131,17 @@
     return [found[distance] for distance in range(len(found))]
 
 
-def fetch(pieces, relative, target, sem):
-    for distance, piece in enumerate(pieces):
+def fetch(pieces, relative, targets, sems):
+    for distance, blocks in enumerate(pieces):
         @pl.when(relative == distance)
-        def _(piece=piece):
-            pltpu.make_async_copy(piece, target, sem).start()
+        def _(blocks=blocks):
+            for block, target, sem in zip(blocks, targets, sems):
+                pltpu.make_async_copy(block, target, sem).start()
+
+
+def await_fetch(pieces, targets, sems):
+    for block, target, sem in zip(pieces[0], targets, sems):
+        pltpu.make_async_copy(block, target, sem).wait()
 
 
 def spans_of(rows):
@@ -185,7 +191,7 @@
 
 
 def weights_kernel(owners, heads, blocks, slots, rows, in_place, who, counts, perm, keys, *refs):
-    pieces = refs[:owners]
+    pieces = [[piece] for piece in refs[:owners]]
     notes, weights, text_buf, scores_buf, stats, sem = refs[owners:]
     spans = spans_of(rows)
     groups = text_buf.shape[1] // (heads * HEAD_DIM)
@@ -193,53 +199,80 @@
     width = chunks * HEAD_DIM
     tiles = own_tiles(owners, slots, who, counts, perm)
 
-    def body(step, index):
-        @pl.when(step == 0)
-        def _():
-            for slot in range(slots):
-                @pl.when(tiles[slot][0] < owners)
-                def _(slot=slot):
-                    fetch(pieces, tiles[slot][0] ^ who[1], text_buf.at[slot], sem.at[slot])
-
-        for slot in range(slots):
-            base = slot * heads * blocks
-
-            @pl.when((step == base) & (tiles[slot][0] < owners))
-            def _(slot=slot):
-                pltpu.make_async_copy(pieces[0], text_buf.at[slot], sem.at[slot]).wait()
-
-            @pl.when((step >= base) & (step < base + heads * blocks) & (tiles[slot][0] < owners))
-            def _(slot=slot, base=base):
-                head, block = (step - base) // blocks, (step - base) % blocks
-                query = rows_of(text_buf.at[slot], heads, head, block, chunks)
-                peak = jnp.full((8, width), -jnp.inf, F32)
-                for low, size, used in spans:
-                    scores = dot_nt(keys[slot, low:low + size], query)
-                    if size != used:
-                        row = lax.broadcasted_iota(jnp.int32, scores.shape, 0)
-                        scores = jnp.where(row < used, scores, -jnp.inf)
-                    scores_buf[low:low + size] = scores
-                    peak = jnp.maximum(peak, jnp.max(scores.reshape(-1, 8, width), axis=0))
-                top = jnp.max(peak, axis=0, keepdims=True) * SCALE_LOG2
-                mass = jnp.zeros((8, width), F32)
-                for low, size, used in spans:
-                    part = jnp.exp2(scores_buf[low:low + size] * SCALE_LOG2 - top)
-                    mass = mass + jnp.sum(part.reshape(-1, 8, width), axis=0)
-                    weights[index, low:low + size] = part.astype(BF16)
+    def score(slot, query, buffer, span, peak):
+        low, size, used = span
+        scores = dot_nt(keys[slot, low:low + size], query)
+        if size != used:
+            row = lax.broadcasted_iota(jnp.int32, scores.shape, 0)
+            scores = jnp.where(row < used, scores, -jnp.inf)
+        scores_buf[buffer, low:low + size] = scores
+        return jnp.maximum(peak, jnp.max(scores.reshape(-1, 8, width), axis=0))
+
+    def weigh(index, buffer, span, top, mass):
+        low, size, _ = span
+        part = jnp.exp2(scores_buf[buffer, low:low + size] * SCALE_LOG2 - top)
+        weights[index, low:low + size] = part.astype(BF16)
+        return mass + jnp.sum(part.reshape(-1, 8, width), axis=0)
+
+    lowest = jnp.full((8, width), -jnp.inf, F32)
+    nothing = jnp.zeros((8, width), F32)
+
+    def tile_weights(slot, items):
+        before = None
+        for buffer, item in enumerate(items + [None]):
+            peak, mass = lowest, nothing
+            if item is not None:
+                query = rows_of(text_buf.at[slot], heads, item[1], item[2], chunks)
+            for span in spans:
+                if item is not None:
+                    peak = score(slot, query, buffer % 2, span, peak)
+                if before is not None:
+                    mass = weigh(before[0][0], (buffer + 1) % 2, span, before[1], mass)
+            if before is not None:
+                (_, head, block), top = before
                 stats[2 * head, pl.ds(block, 1)] = top
                 stats[2 * head + 1, pl.ds(block, 1)] = jnp.sum(mass, axis=0, keepdims=True)
-
-                @pl.when(step == base + heads * blocks - 1)
-                def _():
-                    for done in range(blocks):
-                        lines = [stats[line, done:done + 1] for line in range(2 * heads)]
-                        full = note_rows(lines)
-                        size = full.shape[0]
-                        for chunk in range(chunks):
-                            first = (slot * groups + done * chunks + chunk) * size
-                            notes[first:first + size] = full[:, chunk * HEAD_DIM:(chunk + 1) * HEAD_DIM]
-
-    over_steps(body, slots * heads * blocks, in_place)
+            before = (item, jnp.max(peak, axis=0, keepdims=True) * SCALE_LOG2)
+
+    def write_notes(slot):
+        for done in range(blocks):
+            lines = [stats[line, done:done + 1] for line in range(2 * heads)]
+            full = note_rows(lines)
+            size = full.shape[0]
+            for chunk in range(chunks):
+                begin = (slot * groups + done * chunks + chunk) * size
+                notes[begin:begin + size] = full[:, chunk * HEAD_DIM:(chunk + 1) * HEAD_DIM]
+
+    def start_fetches():
+        for slot in range(slots):
+            @pl.when(tiles[slot][0] < owners)
+            def _(slot=slot):
+                fetch(pieces, tiles[slot][0] ^ who[1], [text_buf.at[slot]], [sem.at[slot]])
+
+    def wait_fetch(slot):
+        await_fetch(pieces, [text_buf.at[slot]], [sem.at[slot]])
+
+    steps = heads * blocks
+    if in_place:
+        start_fetches()
+        for slot in range(slots):
+            @pl.when(tiles[slot][0] < owners)
+            def _(slot=slot):
+                wait_fetch(slot)
+                tile_weights(slot, [(slot * steps + i, i // blocks, i % blocks) for i in range(steps)])
+                write_notes(slot)
+        return
+
+    step = pl.program_id(0)
+    pl.when(step == 0)(start_fetches)
+    for slot in range(slots):
+        base = slot * steps
+
+        @pl.when((step >= base) & (step < base + steps) & (tiles[slot][0] < owners))
+        def _(slot=slot, base=base):
+            pl.when(step == base)(lambda: wait_fetch(slot))
+            tile_weights(slot, [(0, (step - base) // blocks, (step - base) % blocks)])
+            pl.when(step == base + steps - 1)(lambda: write_notes(slot))
 
 
 def in_parts(value):
@@ -270,7 +303,7 @@
 
 
 def slopes_kernel(chip_groups, owners, heads, blocks, slots, rows, in_place, who, counts, perm, notes, weights, values, keys_turned, *refs):
-    pieces = by_distance(chip_groups, refs[:2 * len(chip_groups)])
+    pieces = [[piece] for piece in by_distance(chip_groups, refs[:2 * len(chip_groups)])]
     slopes, turned, text_buf, deltas, sem = refs[-5:]
     spans = spans_of(rows)
     groups = turned.shape[2] // HEAD_DIM
@@ -285,7 +318,7 @@
             for slot in range(slots):
                 @pl.when(tiles[slot][0] < owners)
                 def _(slot=slot):
-                    fetch(pieces, tiles[slot][0] ^ who[1], text_buf.at[slot], sem.at[slot])
+                    fetch(pieces, tiles[slot][0] ^ who[1], [text_buf.at[slot]], [sem.at[slot]])
 
                 @pl.when(tiles[slot][0] >= owners)
                 def _(slot=slot):
@@ -296,7 +329,7 @@
 
             @pl.when((step == base) & (tiles[slot][0] < owners))
             def _(slot=slot):
-                pltpu.make_async_copy(pieces[0], text_buf.at[slot], sem.at[slot]).wait()
+                await_fetch(pieces, [text_buf.at[slot]], [sem.at[slot]])
                 deltas[...] = text_buf[slot, text_rows:].astype(F32)
                 size = turned.shape[1] - heads * HEAD_DIM
                 for chunk in range(groups):
@@ -363,6 +396,18 @@
     sample = own_tiles(owners, slots, who, counts, perm)[slot][0]
     used = sample < owners
 
+    def scaled(step):
+        head, block = step // blocks, step % blocks
+        factor = jnp.concatenate(
+            [factors[slot, head, pl.ds(block * chunks + chunk, 1)] for chunk in range(chunks)], axis=1
+        )
+        factor = jnp.transpose(jnp.broadcast_to(factor, (HEAD_DIM, width)))
+        query = rows_of(q_buf.at[slot], heads, head, block, chunks)
+        grad = rows_of(g_buf.at[slot], heads, head, block, chunks)
+        query = (query.astype(F32) * factor * SCALE).astype(BF16)
+        grad = (grad.astype(F32) * factor).astype(BF16)
+        return query, grad
+
     def body(step, index):
         @pl.when(jnp.logical_not(used))
         def _():
@@ -371,15 +416,7 @@
 
         @pl.when(used)
         def _():
-            head, block = step // blocks, step % blocks
-            factor = jnp.concatenate(
-                [factors[slot, head, pl.ds(block * chunks + chunk, 1)] for chunk in range(chunks)], axis=1
-            )
-            factor = jnp.transpose(jnp.broadcast_to(factor, (HEAD_DIM, width)))
-            query = rows_of(q_buf.at[slot], heads, head, block, chunks)
-            grad = rows_of(g_buf.at[slot], heads, head, block, chunks)
-            query = (query.astype(F32) * factor * SCALE).astype(BF16)
-            grad = (grad.astype(F32) * factor).astype(BF16)
+            query, grad = scaled(step)
 
             def add(which, source, right, fresh):
                 for low in range(0, sums.shape[1], 2 * KEY_ROWS):
@@ -399,7 +436,25 @@
                 send_out[...] = sums[1 - odd].astype(BF16)
 
     steps = heads * blocks
-    over_steps(lambda step, index: body(step, slot * steps + index if in_place else index), steps, in_place)
+    if not in_place:
+        over_steps(body, steps, in_place)
+        return
+
+    @pl.when(jnp.logical_not(used))
+    def _():
+        keep_out[...] = jnp.zeros(keep_out.shape, BF16)
+        send_out[...] = jnp.zeros(send_out.shape, BF16)
+
+    @pl.when(used)
+    def _():
+        rights = [scaled(step) for step in range(steps)]
+        for low in range(0, sums.shape[1], KEY_ROWS):
+            span = slice(low, min(low + KEY_ROWS, sums.shape[1]))
+            for which, source in ((0, slopes), (1, weights)):
+                total = sum(dot_nn(source[slot * steps + step, span], rights[step][which]) for step in range(steps))
+                sums[which, span] = total.astype(BF16)
+        keep_out[...] = sums[odd]
+        send_out[...] = sums[1 - odd]
 
 
 def route_kernel(owners, heads, blocks, slots, who, counts, perm, own, other, *refs):
@@ -551,7 +606,7 @@
         ],
         [SMEM] * 3 + [VMEM] + [ANY] * owners,
         [
-            pltpu.VMEM((padded, block_rows), F32),
+            pltpu.VMEM((2, padded, block_rows), F32),
             pltpu.VMEM((2 * heads, blocks, block_rows), F32),
             pltpu.SemaphoreType.DMA((slots,)),
         ],
@@ -613,7 +668,7 @@
             functools.partial(sums_kernel, owners, heads, blocks, slots, slot, in_place),
             [jax.ShapeDtypeStruct((padded, HEAD_DIM), BF16)] * 2,
             [SMEM] * 3 + [left_spec] * 2 + [VMEM] * 3 + [ANY] * len(order),
-            [pltpu.VMEM((2, padded, HEAD_DIM), F32)],
+            [pltpu.VMEM((2, padded, HEAD_DIM), BF16 if in_place else F32)],
             (*known, weights, slopes, factors, q_own, g_own, *order),
             out_specs=[VMEM] * 2,
             grid=() if in_place else (steps,),

time: 93.5 us -> 93.1 us (level)
  transfers between devices with their start and end apart: 29 -> 29, of which waited for: 13 -> 13; matrix products, arithmetic and copies ran while one was open for 1% -> 1% of each run, Pallas kernels for 18% -> 17%
where the time goes in v7:
time: 93.1 us; the launch traced here: 92.8 us
  waiting for transfers between devices  35.9 us (39%)
  starting transfers between devices  33.1 us (36%)
  Pallas kernels  18.1 us (19%)
  local copies, waits for them, and re-layouts  4.11 us (4%)
  between operations  1.46 us (2%)
    ppermute x29, waiting for transfers between devices, exchange(): return lax.ppermute(block, axis, [(i, i ^ distance) for i in range(count)])  35.9 us
    ppermute x29, starting transfers between devices, exchange(): return lax.ppermute(block, axis, [(i, i ^ distance) for i in range(count)])  33.1 us
    pallas_call x17, Pallas kernels, call(): pl.pallas_call(kernel, out_shape=out_shape, in_specs=in_specs, out_specs=...  18.1 us
    unnamed x11, local copies, waits for them, and re-layouts  4.11 us
  transfers between devices with their start and end apart: 29, of which 13 were waited for; matrix products, arithmetic and copies ran while one was open for 1% of the time, Pallas kernels for 17%

profile of v7, /device:TPU:0, one launch (start us, length us, event | category | flops | bytes accessed | tf_op | source)
XLA Modules:
  0.0 92.8 jit_solution(6814018859805064447)
XLA Ops:
  1.4 0.9 %copy-done.2 = bf16[1,128,1024]{2,1,0:T(8,128)(2,1)S(1)} copy-done((bf16[1,128,1024]{2,1,0:T(8,128)(2,1)S(1)}, bf16[1,128,1024]{2,1,0:T(8,128)(2,1)}, u32[]{:S(2)}) %copy-start.2) | copy-done | bytes 262168
  2.3 0.9 %copy-done.3 = bf16[1,128,1024]{2,1,0:T(8,128)(2,1)S(1)} copy-done((bf16[1,128,1024]{2,1,0:T(8,128)(2,1)S(1)}, bf16[1,128,1024]{2,1,0:T(8,128)(2,1)}, u32[]{:S(2)}) %copy-start.3) | copy-done | bytes 262168
  3.3 0.9 %copy-done.4 = bf16[1,128,1024]{2,1,0:T(8,128)(2,1)S(1)} copy-done((bf16[1,128,1024]{2,1,0:T(8,128)(2,1)S(1)}, bf16[1,128,1024]{2,1,0:T(8,128)(2,1)}, u32[]{:S(2)}) %copy-start.4) | copy-done | bytes 262168
  4.2 1.0 %pack_kernel.1 = (bf16[528,128]{1,0:T(8,128)(2,1)S(1)}, bf16[528,128]{1,0:T(8,128)(2,1)S(1)}, bf16[528,128]{1,0:T(8,128)(2,1)S(1)}, bf16[528,128]{1,0:T(8,128)(2,1)S(1)}) custom-call(s32[2]{0:T(128)S(1)} %pad_add_fusion.who, s32[1]{0:T(128)S(6)} %copy.10.length, bf16[128,1024]{1,0:T(8,128)(2,1)S(1)} %bitcast.7, bf16[128,1024]{1,0:T(8,128)(2,1)S(1)} %bitcast.8, ...), custom_call_target="tpu_custom_call" | custom-call | flops 1000000000 | tf_op jit(solution)/shard_map/pack_kernel/pallas_call | solution.py:43
  5.2 3.1 %collective-permute-start = (bf16[528,128]{1,0:T(8,128)(2,1)S(1)}, bf16[528,128]{1,0:T(8,128)(2,1)S(1)}, u32[]{:S(2)}, u32[]{:S(2)}) collective-permute-start(bf16[528,128]{1,0:T(8,128)(2,1)S(1)} %get-tuple-element.29), channel_id=1, source_target_pairs={{0,8},{8,0},{16,24},{24,16},{1,9},{9,1},{17,25},{25,17},{2,10},{10... | collective-permute-start | bytes 405512 | tf_op jit(solution)/shard_map/ppermute | solution.py:36
  8.3 2.6 %collective-permute-start.1 = (bf16[528,128]{1,0:T(8,128)(2,1)S(1)}, bf16[528,128]{1,0:T(8,128)(2,1)S(1)}, u32[]{:S(2)}, u32[]{:S(2)}) collective-permute-start(bf16[528,128]{1,0:T(8,128)(2,1)S(1)} %get-tuple-element.30), channel_id=1, source_target_pairs={{0,16},{8,24},{16,0},{24,8},{1,17},{9,25},{17,1},{25,9},{2,18},{10... | collective-permute-start | bytes 405512 | tf_op jit(solution)/shard_map/ppermute | solution.py:36
  10.9 1.3 %copy.9.tiles = bf16[2,1601,128]{2,1,0:T(8,128)(2,1)S(1)} copy(bf16[2,1601,128]{2,0,1:T(2,128)(2,1)} %param.10) | data formatting | bytes 1639424 | tf_op args[3]
  12.1 1.4 %collective-permute-done.refs_0_.refs_1_ = bf16[528,128]{1,0:T(8,128)(2,1)S(1)} collective-permute-done((bf16[528,128]{1,0:T(8,128)(2,1)S(1)}, bf16[528,128]{1,0:T(8,128)(2,1)S(1)}, u32[]{:S(2)}, u32[]{:S(2)}) %collective-permute-start) | collective-permute-done | bytes 135200 | tf_op jit(solution)/shard_map/ppermute | solution.py:36
  13.5 8.0 %collective-permute-done.1.refs_1_.refs_2_ = bf16[528,128]{1,0:T(8,128)(2,1)S(1)} collective-permute-done((bf16[528,128]{1,0:T(8,128)(2,1)S(1)}, bf16[528,128]{1,0:T(8,128)(2,1)S(1)}, u32[]{:S(2)}, u32[]{:S(2)}) %collective-permute-start.1) | collective-permute-done | bytes 135200 | tf_op jit(solution)/shard_map/ppermute | solution.py:36
  21.5 2.1 %collective-permute-start.3 = (bf16[2,1616,128]{2,1,0:T(8,128)(2,1)S(1)}, bf16[2,1616,128]{2,1,0:T(8,128)(2,1)S(1)}, u32[]{:S(2)}, u32[]{:S(2)}) collective-permute-start(bf16[2,1616,128]{2,1,0:T(8,128)(2,1)S(1)} %pad_kernel.1.own.refs_4_), channel_id=1, source_target_pairs={{0,8},{8,0},{16,24},{24,16},{1,9},{9,1},{17,25},{25,17},{2,10},{10... | collective-permute-start | bytes 2482184 | tf_op jit(solution)/shard_map/ppermute | solution.py:36
  23.6 0.4 stack_kernel.2.refs_0_
  24.0 1.6 %collective-permute-start.5 = (bf16[1024,128]{1,0:T(8,128)(2,1)S(1)}, bf16[1024,128]{1,0:T(8,128)(2,1)S(1)}, u32[]{:S(2)}, u32[]{:S(2)}) collective-permute-start(bf16[1024,128]{1,0:T(8,128)(2,1)S(1)} %stack_kernel.2.refs_0_), channel_id=1, source_target_pairs={{0,2},{1,3},{2,0},{3,1},{4,6},{5,7},{6,4},{7,5},{8,10},{9,11},{10,... | collective-permute-start | bytes 786440 | tf_op jit(solution)/shard_map/ppermute | solution.py:36
  25.6 1.5 %collective-permute-start.9 = (bf16[1024,128]{1,0:T(8,128)(2,1)S(1)}, bf16[1024,128]{1,0:T(8,128)(2,1)S(1)}, u32[]{:S(2)}, u32[]{:S(2)}) collective-permute-start(bf16[1024,128]{1,0:T(8,128)(2,1)S(1)} %stack_kernel.2.refs_0_), channel_id=1, source_target_pairs={{0,6},{1,7},{2,4},{3,5},{4,2},{5,3},{6,0},{7,1},{8,14},{9,15},{10,... | collective-permute-start | bytes 786440 | tf_op jit(solution)/shard_map/ppermute | solution.py:36
  27.1 0.5 collective-permute-start.7
  27.6 5.8 %collective-permute-done.5.refs_2_.refs_4_ = bf16[1024,128]{1,0:T(8,128)(2,1)S(1)} collective-permute-done((bf16[1024,128]{1,0:T(8,128)(2,1)S(1)}, bf16[1024,128]{1,0:T(8,128)(2,1)S(1)}, u32[]{:S(2)}, u32[]{:S(2)}) %collective-permute-start.5) | collective-permute-done | bytes 262176 | tf_op jit(solution)/shard_map/ppermute | solution.py:36
  33.3 0.4 stack_kernel.3.refs_0_
  33.8 3.6 %collective-permute-done.9.refs_6_ = bf16[1024,128]{1,0:T(8,128)(2,1)S(1)} collective-permute-done((bf16[1024,128]{1,0:T(8,128)(2,1)S(1)}, bf16[1024,128]{1,0:T(8,128)(2,1)S(1)}, u32[]{:S(2)}, u32[]{:S(2)}) %collective-permute-start.9) | collective-permute-done | bytes 262176 | tf_op jit(solution)/shard_map/ppermute | solution.py:36
  37.4 1.5 %collective-permute-start.13 = (bf16[1040,128]{1,0:T(8,128)(2,1)S(1)}, bf16[1040,128]{1,0:T(8,128)(2,1)S(1)}, u32[]{:S(2)}, u32[]{:S(2)}) collective-permute-start(bf16[1040,128]{1,0:T(8,128)(2,1)S(1)} %stack_kernel.3.refs_0_), channel_id=1, source_target_pairs={{0,2},{1,3},{2,0},{3,1},{4,6},{5,7},{6,4},{7,5},{8,10},{9,11},{10,... | collective-permute-start | bytes 798728 | tf_op jit(solution)/shard_map/ppermute | solution.py:36
  38.9 0.5 collective-permute-start.14
  39.4 3.4 %collective-permute-start.11 = (bf16[1040,128]{1,0:T(8,128)(2,1)S(1)}, bf16[1040,128]{1,0:T(8,128)(2,1)S(1)}, u32[]{:S(2)}, u32[]{:S(2)}) collective-permute-start(bf16[1040,128]{1,0:T(8,128)(2,1)S(1)} %stack_kernel.3.refs_0_), channel_id=1, source_target_pairs={{0,6},{1,7},{2,4},{3,5},{4,2},{5,3},{6,0},{7,1},{8,14},{9,15},{10,... | collective-permute-start | bytes 798728 | tf_op jit(solution)/shard_map/ppermute | solution.py:36
  42.8 0.5 collective-permute-start.8
  43.3 1.0 %tiles_kernel.1 = (bf16[2,1616,128]{2,1,0:T(8,128)(2,1)S(1)}, bf16[2,1616,128]{2,1,0:T(8,128)(2,1)S(1)}, bf16[2,128,1664]{2,1,0:T(8,128)(2,1)S(1)}) custom-call(s32[2]{0:T(128)S(1)} %pad_add_fusion.who, bf16[2,1616,128]{2,1,0:T(8,128)(2,1)S(1)} %pad_kernel.1.own.refs_4_, bf16[2,1616,128]{2,1,0:T(8,128)(2,1)S(1)} %collective-permute-done.3.partner), custom_call_target="tpu_custom_call" | custom-call | tf_op jit(solution)/shard_map/tiles_kernel/pallas_call | solution.py:43
  44.7 3.0 %weights_kernel.1 = (bf16[128,128]{1,0:T(8,128)(2,1)S(1)}, bf16[4,1616,512]{2,1,0:T(8,128)(2,1)S(1)}, bf16[2,1024,128]{2,1,0:T(8,128)(2,1)S(1)}) custom-call(s32[2]{0:T(128)S(1)} %pad_add_fusion.who, s32[8]{0:T(128)S(1)} %copy-done, s32[8]{0:T(128)S(1)} %copy-done.1, bf16[2,1616,128]{2,1,0:T(8,128)(2,1)S(1)} %get-tuple-element.32.keys, ...), custom_call_target="tpu_custom_call" | custom-call | tf_op jit(solution)/shard_map/weights_kernel/pallas_call | solution.py:43
  47.7 2.4 %collective-permute-done.14.refs_1_ = bf16[1040,128]{1,0:T(8,128)(2,1)S(1)} collective-permute-done((bf16[1040,128]{1,0:T(8,128)(2,1)S(1)}, bf16[1040,128]{1,0:T(8,128)(2,1)S(1)}, u32[]{:S(2)}, u32[]{:S(2)}) %collective-permute-start.14) | collective-permute-done | bytes 266272 | tf_op jit(solution)/shard_map/ppermute | solution.py:36
  50.4 0.5 collective-permute-start.12
  51.0 1.8 %collective-permute-start.17 = (bf16[128,128]{1,0:T(8,128)(2,1)S(1)}, bf16[128,128]{1,0:T(8,128)(2,1)S(1)}, u32[]{:S(2)}, u32[]{:S(2)}) collective-permute-start(bf16[128,128]{1,0:T(8,128)(2,1)S(1)} %get-tuple-element.34.refs_2_.notes.refs_0_), channel_id=1, source_target_pairs={{0,2},{1,3},{2,0},{3,1},{4,6},{5,7},{6,4},{7,5},{8,10},{9,11},{10,... | collective-permute-start | bytes 98312 | tf_op jit(solution)/shard_map/ppermute | solution.py:36
  53.0 1.5 %collective-permute-start.19 = (bf16[128,128]{1,0:T(8,128)(2,1)S(1)}, bf16[128,128]{1,0:T(8,128)(2,1)S(1)}, u32[]{:S(2)}, u32[]{:S(2)}) collective-permute-start(bf16[128,128]{1,0:T(8,128)(2,1)S(1)} %get-tuple-element.34.refs_2_.notes.refs_0_), channel_id=1, source_target_pairs={{0,6},{1,7},{2,4},{3,5},{4,2},{5,3},{6,0},{7,1},{8,14},{9,15},{10,... | collective-permute-start | bytes 98312 | tf_op jit(solution)/shard_map/ppermute | solution.py:36
  54.4 2.6 %slopes_kernel.1 = (bf16[4,1616,512]{2,1,0:T(8,128)(2,1)S(1)}, bf16[2,272,512]{2,1,0:T(8,128)(2,1)S(1)}, bf16[2,1040,128]{2,1,0:T(8,128)(2,1)S(1)}) custom-call(s32[2]{0:T(128)S(1)} %pad_add_fusion.who, s32[8]{0:T(128)S(1)} %copy-done, s32[8]{0:T(128)S(1)} %copy-done.1, bf16[128,128]{1,0:T(8,128)(2,1)S(1)} %get-tuple-element.34.refs_2_.notes.refs_0_, ...), custom_call_target="tpu_custom_call" | custom-call | flops 6000000000 | tf_op jit(solution)/shard_map/slopes_kernel/pallas_call | solution.py:43
  57.0 0.7 collective-permute-done.19.refs_3_
  58.0 0.5 collective-permute-start.16
  58.5 0.8 collective-permute-done.20.other
  59.4 0.7 factors_kernel.1.refs_2_.refs_0_
  60.1 2.9 %sums_kernel.2 = (bf16[1616,128]{1,0:T(8,128)(2,1)S(1)}, bf16[1616,128]{1,0:T(8,128)(2,1)S(1)}) custom-call(s32[2]{0:T(128)S(1)} %pad_add_fusion.who, s32[8]{0:T(128)S(1)} %copy-done, s32[8]{0:T(128)S(1)} %copy-done.1, bf16[4,1616,512]{2,1,0:T(8,128)(2,1)S(1)} %get-tuple-element.35.weights.refs_0_, bf16[4,1616,512]{2,1,0:T(8,128)(2,1)S(1)} %get-tuple-element.39.refs_1_, ...), custom_call_target="tpu_custom_call" | custom-call | flops 4000000000 | tf_op jit(solution)/shard_map/sums_kernel/pallas_call | solution.py:43
  63.0 0.9 collective-permute-start.27
  63.9 1.4 %route_kernel.1 = (bf16[272,512]{1,0:T(8,128)(2,1)S(1)}, bf16[272,512]{1,0:T(8,128)(2,1)S(1)}, bf16[272,512]{1,0:T(8,128)(2,1)S(1)}, bf16[272,512]{1,0:T(8,128)(2,1)S(1)}) custom-call(s32[2]{0:T(128)S(1)} %pad_add_fusion.who, s32[8]{0:T(128)S(1)} %copy-done, s32[8]{0:T(128)S(1)} %copy-done.1, bf16[2,272,512]{2,1,0:T(8,128)(2,1)S(1)} %get-tuple-element.38.refs_4_.own, ...), custom_call_target="tpu_custom_call" | custom-call | flops 30000001024 | tf_op jit(solution)/shard_map/route_kernel/pallas_call | solution.py:43
  65.4 2.4 %collective-permute-start.21 = (bf16[272,512]{1,0:T(8,128)(2,1)S(1)}, bf16[272,512]{1,0:T(8,128)(2,1)S(1)}, u32[]{:S(2)}, u32[]{:S(2)}) collective-permute-start(bf16[272,512]{1,0:T(8,128)(2,1)S(1)} %get-tuple-element.44), channel_id=1, source_target_pairs={{0,2},{1,3},{2,0},{3,1},{4,6},{5,7},{6,4},{7,5},{8,10},{9,11},{10,... | collective-permute-start | bytes 835592 | tf_op jit(solution)/shard_map/ppermute | solution.py:36
  67.7 1.5 %collective-permute-start.23 = (bf16[272,512]{1,0:T(8,128)(2,1)S(1)}, bf16[272,512]{1,0:T(8,128)(2,1)S(1)}, u32[]{:S(2)}, u32[]{:S(2)}) collective-permute-start(bf16[272,512]{1,0:T(8,128)(2,1)S(1)} %get-tuple-element.46), channel_id=1, source_target_pairs={{0,6},{1,7},{2,4},{3,5},{4,2},{5,3},{6,0},{7,1},{8,14},{9,15},{10,... | collective-permute-start | bytes 835592 | tf_op jit(solution)/shard_map/ppermute | solution.py:36
  69.3 0.7 sums_kernel.3
  70.0 2.0 %collective-permute-start.28 = (bf16[1616,128]{1,0:T(8,128)(2,1)S(1)}, bf16[1616,128]{1,0:T(8,128)(2,1)S(1)}, u32[]{:S(2)}, u32[]{:S(2)}) collective-permute-start(bf16[1616,128]{1,0:T(8,128)(2,1)S(1)} %get-tuple-element.53), channel_id=1, source_target_pairs={{0,8},{8,0},{16,24},{24,16},{1,9},{9,1},{17,25},{25,17},{2,10},{10... | collective-permute-start | bytes 1241096 | tf_op jit(solution)/shard_map/ppermute | solution.py:36
  72.0 3.2 %collective-permute-done.21.refs_1_ = bf16[272,512]{1,0:T(8,128)(2,1)S(1)} collective-permute-done((bf16[272,512]{1,0:T(8,128)(2,1)S(1)}, bf16[272,512]{1,0:T(8,128)(2,1)S(1)}, u32[]{:S(2)}, u32[]{:S(2)}) %collective-permute-start.21) | collective-permute-done | bytes 278560 | tf_op jit(solution)/shard_map/ppermute | solution.py:36
  75.2 6.8 %collective-permute-done.22.refs_2_ = bf16[272,512]{1,0:T(8,128)(2,1)S(1)} collective-permute-done((bf16[272,512]{1,0:T(8,128)(2,1)S(1)}, bf16[272,512]{1,0:T(8,128)(2,1)S(1)}, u32[]{:S(2)}, u32[]{:S(2)}) %collective-permute-start.22) | collective-permute-done | bytes 278560 | tf_op jit(solution)/shard_map/ppermute | solution.py:36
  82.3 1.8 %collective-permute-start.24 = (bf16[128,256]{1,0:T(8,128)(2,1)S(1)}, bf16[128,256]{1,0:T(8,128)(2,1)S(1)}, u32[]{:S(2)}, u32[]{:S(2)}) collective-permute-start(bf16[128,256]{1,0:T(8,128)(2,1)S(1)} %get-tuple-element.48), channel_id=1, source_target_pairs={{0,8},{8,0},{16,24},{24,16},{1,9},{9,1},{17,25},{25,17},{2,10},{10... | collective-permute-start | bytes 196616 | tf_op jit(solution)/shard_map/ppermute | solution.py:36
  84.1 1.3 %collective-permute-start.25 = (bf16[128,256]{1,0:T(8,128)(2,1)S(1)}, bf16[128,256]{1,0:T(8,128)(2,1)S(1)}, u32[]{:S(2)}, u32[]{:S(2)}) collective-permute-start(bf16[128,256]{1,0:T(8,128)(2,1)S(1)} %get-tuple-element.49), channel_id=1, source_target_pairs={{0,16},{8,24},{16,0},{24,8},{1,17},{9,25},{17,1},{25,9},{2,18},{10... | collective-permute-start | bytes 196616 | tf_op jit(solution)/shard_map/ppermute | solution.py:36
  85.4 1.4 %collective-permute-start.26 = (bf16[128,256]{1,0:T(8,128)(2,1)S(1)}, bf16[128,256]{1,0:T(8,128)(2,1)S(1)}, u32[]{:S(2)}, u32[]{:S(2)}) collective-permute-start(bf16[128,256]{1,0:T(8,128)(2,1)S(1)} %get-tuple-element.50), channel_id=1, source_target_pairs={{0,24},{8,16},{16,8},{24,0},{1,25},{9,17},{17,9},{25,1},{2,26},{10... | collective-permute-start | bytes 196616 | tf_op jit(solution)/shard_map/ppermute | solution.py:36
  86.8 2.0 %merge_kernel.1 = (bf16[1601,2,128]{2,1,0:T(2,128)(2,1)}, bf16[16,128]{1,0:T(8,128)(2,1)S(1)}) custom-call(bf16[1616,128]{1,0:T(8,128)(2,1)S(1)} %get-tuple-element.42.refs_1_.refs_0_, bf16[1616,128]{1,0:T(8,128)(2,1)S(1)} %get-tuple-element.51.refs_1_, bf16[1616,128]{1,0:T(8,128)(2,1)S(1)} %collective-permute-done.27.refs_2_, ...), custom_call_target="tpu_custom_call" | custom-call | flops 2000000000 | tf_op jit(solution)/shard_map/merge_kernel/pallas_call | solution.py:43
  88.8 1.2 %collective-permute-done.25.refs_2_ = bf16[128,256]{1,0:T(8,128)(2,1)S(1)} collective-permute-done((bf16[128,256]{1,0:T(8,128)(2,1)S(1)}, bf16[128,256]{1,0:T(8,128)(2,1)S(1)}, u32[]{:S(2)}, u32[]{:S(2)}) %collective-permute-start.25) | collective-permute-done | bytes 65568 | tf_op jit(solution)/shard_map/ppermute | solution.py:36
  90.0 1.6 %collective-permute-done.26.refs_3_ = bf16[128,256]{1,0:T(8,128)(2,1)S(1)} collective-permute-done((bf16[128,256]{1,0:T(8,128)(2,1)S(1)}, bf16[128,256]{1,0:T(8,128)(2,1)S(1)}, u32[]{:S(2)}, u32[]{:S(2)}) %collective-permute-start.26) | collective-permute-done | bytes 65568 | tf_op jit(solution)/shard_map/ppermute | solution.py:36
  91.6 1.3 %place_kernel.1 = bf16[128,1024]{1,0:T(8,128)(2,1)} custom-call(s32[2]{0:T(128)S(1)} %pad_add_fusion.who, bf16[128,256]{1,0:T(8,128)(2,1)S(1)} %get-tuple-element.47.refs_0_, bf16[128,256]{1,0:T(8,128)(2,1)S(1)} %collective-permute-done.24.refs_1_, bf16[128,256]{1,0:T(8,128)(2,1)S(1)} %collective-permute-done.25.refs_2_, ...), custom_call_target="tpu_custom_call" | custom-call | flops 1000000000 | tf_op jit(solution)/shard_map/place_kernel/pallas_call | solution.py:43
  (39 shorter events, 1.6 us)
Async XLA Ops:
  1.4 1.0 %copy-start.2 = (bf16[1,128,1024]{2,1,0:T(8,128)(2,1)S(1)}, bf16[1,128,1024]{2,1,0:T(8,128)(2,1)}, u32[]{:S(2)}) copy-start(bf16[1,128,1024]{2,1,0:T(8,128)(2,1)} %param.7) | copy-start | bytes 786436
  2.3 0.9 %copy-start.3 = (bf16[1,128,1024]{2,1,0:T(8,128)(2,1)S(1)}, bf16[1,128,1024]{2,1,0:T(8,128)(2,1)}, u32[]{:S(2)}) copy-start(bf16[1,128,1024]{2,1,0:T(8,128)(2,1)} %param.8) | copy-start | bytes 786436
  3.3 0.9 %copy-start.4 = (bf16[1,128,1024]{2,1,0:T(8,128)(2,1)S(1)}, bf16[1,128,1024]{2,1,0:T(8,128)(2,1)}, u32[]{:S(2)}) copy-start(bf16[1,128,1024]{2,1,0:T(8,128)(2,1)} %param.9) | copy-start | bytes 786436
  4.2 40.5 %copy-start = (s32[8]{0:T(128)S(1)}, s32[8]{0:T(128)}, u32[]{:S(2)}) copy-start(s32[8]{0:T(128)} %counts.11) | copy-start | bytes 100
  4.2 40.5 %copy-start.1 = (s32[8]{0:T(128)S(1)}, s32[8]{0:T(128)}, u32[]{:S(2)}) copy-start(s32[8]{0:T(128)} %perm.11) | copy-start | bytes 100
  5.2 8.3 %collective-permute-start = (bf16[528,128]{1,0:T(8,128)(2,1)S(1)}, bf16[528,128]{1,0:T(8,128)(2,1)S(1)}, u32[]{:S(2)}, u32[]{:S(2)}) collective-permute-start(bf16[528,128]{1,0:T(8,128)(2,1)S(1)} %get-tuple-element.29), channel_id=1, source_target_pairs={{0,8},{8,0},{16,24},{24,16},{1,9},{9,1},{17,25},{25,17},{2,10},{10... | collective-permute-start | bytes 405512 | tf_op jit(solution)/shard_map/ppermute | solution.py:36
  8.3 13.2 %collective-permute-start.1 = (bf16[528,128]{1,0:T(8,128)(2,1)S(1)}, bf16[528,128]{1,0:T(8,128)(2,1)S(1)}, u32[]{:S(2)}, u32[]{:S(2)}) collective-permute-start(bf16[528,128]{1,0:T(8,128)(2,1)S(1)} %get-tuple-element.30), channel_id=1, source_target_pairs={{0,16},{8,24},{16,0},{24,8},{1,17},{9,25},{17,1},{25,9},{2,18},{10... | collective-permute-start | bytes 405512 | tf_op jit(solution)/shard_map/ppermute | solution.py:36
  10.9 10.6 %collective-permute-start.2 = (bf16[528,128]{1,0:T(8,128)(2,1)S(1)}, bf16[528,128]{1,0:T(8,128)(2,1)S(1)}, u32[]{:S(2)}, u32[]{:S(2)}) collective-permute-start(bf16[528,128]{1,0:T(8,128)(2,1)S(1)} %get-tuple-element.31), channel_id=1, source_target_pairs={{0,24},{8,16},{16,8},{24,0},{1,25},{9,17},{17,9},{25,1},{2,26},{10... | collective-permute-start | bytes 405512 | tf_op jit(solution)/shard_map/ppermute | solution.py:36
  21.5 21.2 %collective-permute-start.3 = (bf16[2,1616,128]{2,1,0:T(8,128)(2,1)S(1)}, bf16[2,1616,128]{2,1,0:T(8,128)(2,1)S(1)}, u32[]{:S(2)}, u32[]{:S(2)}) collective-permute-start(bf16[2,1616,128]{2,1,0:T(8,128)(2,1)S(1)} %pad_kernel.1.own.refs_4_), channel_id=1, source_target_pairs={{0,8},{8,0},{16,24},{24,16},{1,9},{9,1},{17,25},{25,17},{2,10},{10... | collective-permute-start | bytes 2482184 | tf_op jit(solution)/shard_map/ppermute | solution.py:36
  24.0 9.3 %collective-permute-start.5 = (bf16[1024,128]{1,0:T(8,128)(2,1)S(1)}, bf16[1024,128]{1,0:T(8,128)(2,1)S(1)}, u32[]{:S(2)}, u32[]{:S(2)}) collective-permute-start(bf16[1024,128]{1,0:T(8,128)(2,1)S(1)} %stack_kernel.2.refs_0_), channel_id=1, source_target_pairs={{0,2},{1,3},{2,0},{3,1},{4,6},{5,7},{6,4},{7,5},{8,10},{9,11},{10,... | collective-permute-start | bytes 786440 | tf_op jit(solution)/shard_map/ppermute | solution.py:36
  25.6 11.8 %collective-permute-start.9 = (bf16[1024,128]{1,0:T(8,128)(2,1)S(1)}, bf16[1024,128]{1,0:T(8,128)(2,1)S(1)}, u32[]{:S(2)}, u32[]{:S(2)}) collective-permute-start(bf16[1024,128]{1,0:T(8,128)(2,1)S(1)} %stack_kernel.2.refs_0_), channel_id=1, source_target_pairs={{0,6},{1,7},{2,4},{3,5},{4,2},{5,3},{6,0},{7,1},{8,14},{9,15},{10,... | collective-permute-start | bytes 786440 | tf_op jit(solution)/shard_map/ppermute | solution.py:36
  27.1 11.8 %collective-permute-start.7 = (bf16[1024,128]{1,0:T(8,128)(2,1)S(1)}, bf16[1024,128]{1,0:T(8,128)(2,1)S(1)}, u32[]{:S(2)}, u32[]{:S(2)}) collective-permute-start(bf16[1024,128]{1,0:T(8,128)(2,1)S(1)} %stack_kernel.2.refs_0_), channel_id=1, source_target_pairs={{0,4},{1,5},{2,6},{3,7},{4,0},{5,1},{6,2},{7,3},{8,12},{9,13},{10,... | collective-permute-start | bytes 786440 | tf_op jit(solution)/shard_map/ppermute | solution.py:36
  27.6 11.8 %collective-permute-start.4 = (bf16[1024,128]{1,0:T(8,128)(2,1)S(1)}, bf16[1024,128]{1,0:T(8,128)(2,1)S(1)}, u32[]{:S(2)}, u32[]{:S(2)}) collective-permute-start(bf16[1024,128]{1,0:T(8,128)(2,1)S(1)} %stack_kernel.2.refs_0_), channel_id=1, source_target_pairs={{0,1},{1,0},{2,3},{3,2},{4,5},{5,4},{6,7},{7,6},{8,9},{9,8},{10,11... | collective-permute-start | bytes 786440 | tf_op jit(solution)/shard_map/ppermute | solution.py:36
  33.3 9.4 %collective-permute-start.6 = (bf16[1024,128]{1,0:T(8,128)(2,1)S(1)}, bf16[1024,128]{1,0:T(8,128)(2,1)S(1)}, u32[]{:S(2)}, u32[]{:S(2)}) collective-permute-start(bf16[1024,128]{1,0:T(8,128)(2,1)S(1)} %collective-permute-done.5.refs_2_.refs_4_), channel_id=1, source_target_pairs={{0,1},{1,0},{2,3},{3,2},{4,5},{5,4},{6,7},{7,6},{8,9},{9,8},{10,11... | collective-permute-start | bytes 786440 | tf_op jit(solution)/shard_map/ppermute | solution.py:36
  37.4 10.3 %collective-permute-start.13 = (bf16[1040,128]{1,0:T(8,128)(2,1)S(1)}, bf16[1040,128]{1,0:T(8,128)(2,1)S(1)}, u32[]{:S(2)}, u32[]{:S(2)}) collective-permute-start(bf16[1040,128]{1,0:T(8,128)(2,1)S(1)} %stack_kernel.3.refs_0_), channel_id=1, source_target_pairs={{0,2},{1,3},{2,0},{3,1},{4,6},{5,7},{6,4},{7,5},{8,10},{9,11},{10,... | collective-permute-start | bytes 798728 | tf_op jit(solution)/shard_map/ppermute | solution.py:36
  38.9 11.3 %collective-permute-start.14 = (bf16[1040,128]{1,0:T(8,128)(2,1)S(1)}, bf16[1040,128]{1,0:T(8,128)(2,1)S(1)}, u32[]{:S(2)}, u32[]{:S(2)}) collective-permute-start(bf16[1040,128]{1,0:T(8,128)(2,1)S(1)} %stack_kernel.3.refs_0_), channel_id=1, source_target_pairs={{0,4},{1,5},{2,6},{3,7},{4,0},{5,1},{6,2},{7,3},{8,12},{9,13},{10,... | collective-permute-start | bytes 798728 | tf_op jit(solution)/shard_map/ppermute | solution.py:36
  39.4 10.9 %collective-permute-start.11 = (bf16[1040,128]{1,0:T(8,128)(2,1)S(1)}, bf16[1040,128]{1,0:T(8,128)(2,1)S(1)}, u32[]{:S(2)}, u32[]{:S(2)}) collective-permute-start(bf16[1040,128]{1,0:T(8,128)(2,1)S(1)} %stack_kernel.3.refs_0_), channel_id=1, source_target_pairs={{0,6},{1,7},{2,4},{3,5},{4,2},{5,3},{6,0},{7,1},{8,14},{9,15},{10,... | collective-permute-start | bytes 798728 | tf_op jit(solution)/shard_map/ppermute | solution.py:36
  42.8 1.5 %collective-permute-start.10 = (bf16[1024,128]{1,0:T(8,128)(2,1)S(1)}, bf16[1024,128]{1,0:T(8,128)(2,1)S(1)}, u32[]{:S(2)}, u32[]{:S(2)}) collective-permute-start(bf16[1024,128]{1,0:T(8,128)(2,1)S(1)} %collective-permute-done.9.refs_6_), channel_id=1, source_target_pairs={{0,1},{1,0},{2,3},{3,2},{4,5},{5,4},{6,7},{7,6},{8,9},{9,8},{10,11... | collective-permute-start | bytes 786440 | tf_op jit(solution)/shard_map/ppermute | solution.py:36
  42.8 1.9 %collective-permute-start.8 = (bf16[1024,128]{1,0:T(8,128)(2,1)S(1)}, bf16[1024,128]{1,0:T(8,128)(2,1)S(1)}, u32[]{:S(2)}, u32[]{:S(2)}) collective-permute-start(bf16[1024,128]{1,0:T(8,128)(2,1)S(1)} %collective-permute-done.7.refs_4_), channel_id=1, source_target_pairs={{0,1},{1,0},{2,3},{3,2},{4,5},{5,4},{6,7},{7,6},{8,9},{9,8},{10,11... | collective-permute-start | bytes 786440 | tf_op jit(solution)/shard_map/ppermute | solution.py:36
  50.2 4.2 %collective-permute-start.15 = (bf16[2,1040,128]{2,1,0:T(8,128)(2,1)S(1)}, bf16[2,1040,128]{2,1,0:T(8,128)(2,1)S(1)}, u32[]{:S(2)}, u32[]{:S(2)}) collective-permute-start(bf16[2,1040,128]{2,1,0:T(8,128)(2,1)S(1)} %join_kernel.4.refs_2_), channel_id=1, source_target_pairs={{0,1},{1,0},{2,3},{3,2},{4,5},{5,4},{6,7},{7,6},{8,9},{9,8},{10,11... | collective-permute-start | bytes 1597448 | tf_op jit(solution)/shard_map/ppermute | solution.py:36
  50.4 4.0 %collective-permute-start.12 = (bf16[2,1040,128]{2,1,0:T(8,128)(2,1)S(1)}, bf16[2,1040,128]{2,1,0:T(8,128)(2,1)S(1)}, u32[]{:S(2)}, u32[]{:S(2)}) collective-permute-start(bf16[2,1040,128]{2,1,0:T(8,128)(2,1)S(1)} %join_kernel.3.refs_0_), channel_id=1, source_target_pairs={{0,1},{1,0},{2,3},{3,2},{4,5},{5,4},{6,7},{7,6},{8,9},{9,8},{10,11... | collective-permute-start | bytes 1597448 | tf_op jit(solution)/shard_map/ppermute | solution.py:36
  51.0 6.1 %collective-permute-start.17 = (bf16[128,128]{1,0:T(8,128)(2,1)S(1)}, bf16[128,128]{1,0:T(8,128)(2,1)S(1)}, u32[]{:S(2)}, u32[]{:S(2)}) collective-permute-start(bf16[128,128]{1,0:T(8,128)(2,1)S(1)} %get-tuple-element.34.refs_2_.notes.refs_0_), channel_id=1, source_target_pairs={{0,2},{1,3},{2,0},{3,1},{4,6},{5,7},{6,4},{7,5},{8,10},{9,11},{10,... | collective-permute-start | bytes 98312 | tf_op jit(solution)/shard_map/ppermute | solution.py:36
  52.8 4.3 %collective-permute-start.18 = (bf16[128,128]{1,0:T(8,128)(2,1)S(1)}, bf16[128,128]{1,0:T(8,128)(2,1)S(1)}, u32[]{:S(2)}, u32[]{:S(2)}) collective-permute-start(bf16[128,128]{1,0:T(8,128)(2,1)S(1)} %get-tuple-element.34.refs_2_.notes.refs_0_), channel_id=1, source_target_pairs={{0,4},{1,5},{2,6},{3,7},{4,0},{5,1},{6,2},{7,3},{8,12},{9,13},{10,... | collective-permute-start | bytes 98312 | tf_op jit(solution)/shard_map/ppermute | solution.py:36
  53.0 4.8 %collective-permute-start.19 = (bf16[128,128]{1,0:T(8,128)(2,1)S(1)}, bf16[128,128]{1,0:T(8,128)(2,1)S(1)}, u32[]{:S(2)}, u32[]{:S(2)}) collective-permute-start(bf16[128,128]{1,0:T(8,128)(2,1)S(1)} %get-tuple-element.34.refs_2_.notes.refs_0_), channel_id=1, source_target_pairs={{0,6},{1,7},{2,4},{3,5},{4,2},{5,3},{6,0},{7,1},{8,14},{9,15},{10,... | collective-permute-start | bytes 98312 | tf_op jit(solution)/shard_map/ppermute | solution.py:36
  58.0 1.4 %collective-permute-start.20 = (bf16[4,128,128]{2,1,0:T(8,128)(2,1)S(1)}, bf16[4,128,128]{2,1,0:T(8,128)(2,1)S(1)}, u32[]{:S(2)}, u32[]{:S(2)}) collective-permute-start(bf16[4,128,128]{2,1,0:T(8,128)(2,1)S(1)} %join_kernel.5.own), channel_id=1, source_target_pairs={{0,1},{1,0},{2,3},{3,2},{4,5},{5,4},{6,7},{7,6},{8,9},{9,8},{10,11... | collective-permute-start | bytes 393224 | tf_op jit(solution)/shard_map/ppermute | solution.py:36
  58.0 5.9 %collective-permute-start.16 = (bf16[2,272,512]{2,1,0:T(8,128)(2,1)S(1)}, bf16[2,272,512]{2,1,0:T(8,128)(2,1)S(1)}, u32[]{:S(2)}, u32[]{:S(2)}) collective-permute-start(bf16[2,272,512]{2,1,0:T(8,128)(2,1)S(1)} %get-tuple-element.38.refs_4_.own), channel_id=1, source_target_pairs={{0,1},{1,0},{2,3},{3,2},{4,5},{5,4},{6,7},{7,6},{8,9},{9,8},{10,11... | collective-permute-start | bytes 1671176 | tf_op jit(solution)/shard_map/ppermute | solution.py:36
  63.0 23.7 %collective-permute-start.27 = (bf16[1616,128]{1,0:T(8,128)(2,1)S(1)}, bf16[1616,128]{1,0:T(8,128)(2,1)S(1)}, u32[]{:S(2)}, u32[]{:S(2)}) collective-permute-start(bf16[1616,128]{1,0:T(8,128)(2,1)S(1)} %get-tuple-element.52), channel_id=1, source_target_pairs={{0,8},{8,0},{16,24},{24,16},{1,9},{9,1},{17,25},{25,17},{2,10},{10... | collective-permute-start | bytes 1241096 | tf_op jit(solution)/shard_map/ppermute | solution.py:36
  65.4 9.8 %collective-permute-start.21 = (bf16[272,512]{1,0:T(8,128)(2,1)S(1)}, bf16[272,512]{1,0:T(8,128)(2,1)S(1)}, u32[]{:S(2)}, u32[]{:S(2)}) collective-permute-start(bf16[272,512]{1,0:T(8,128)(2,1)S(1)} %get-tuple-element.44), channel_id=1, source_target_pairs={{0,2},{1,3},{2,0},{3,1},{4,6},{5,7},{6,4},{7,5},{8,10},{9,11},{10,... | collective-permute-start | bytes 835592 | tf_op jit(solution)/shard_map/ppermute | solution.py:36
  67.7 14.2 %collective-permute-start.22 = (bf16[272,512]{1,0:T(8,128)(2,1)S(1)}, bf16[272,512]{1,0:T(8,128)(2,1)S(1)}, u32[]{:S(2)}, u32[]{:S(2)}) collective-permute-start(bf16[272,512]{1,0:T(8,128)(2,1)S(1)} %get-tuple-element.45), channel_id=1, source_target_pairs={{0,4},{1,5},{2,6},{3,7},{4,0},{5,1},{6,2},{7,3},{8,12},{9,13},{10,... | collective-permute-start | bytes 835592 | tf_op jit(solution)/shard_map/ppermute | solution.py:36
  67.7 14.2 %collective-permute-start.23 = (bf16[272,512]{1,0:T(8,128)(2,1)S(1)}, bf16[272,512]{1,0:T(8,128)(2,1)S(1)}, u32[]{:S(2)}, u32[]{:S(2)}) collective-permute-start(bf16[272,512]{1,0:T(8,128)(2,1)S(1)} %get-tuple-element.46), channel_id=1, source_target_pairs={{0,6},{1,7},{2,4},{3,5},{4,2},{5,3},{6,0},{7,1},{8,14},{9,15},{10,... | collective-permute-start | bytes 835592 | tf_op jit(solution)/shard_map/ppermute | solution.py:36
  70.0 16.8 %collective-permute-start.28 = (bf16[1616,128]{1,0:T(8,128)(2,1)S(1)}, bf16[1616,128]{1,0:T(8,128)(2,1)S(1)}, u32[]{:S(2)}, u32[]{:S(2)}) collective-permute-start(bf16[1616,128]{1,0:T(8,128)(2,1)S(1)} %get-tuple-element.53), channel_id=1, source_target_pairs={{0,8},{8,0},{16,24},{24,16},{1,9},{9,1},{17,25},{25,17},{2,10},{10... | collective-permute-start | bytes 1241096 | tf_op jit(solution)/shard_map/ppermute | solution.py:36
  82.3 6.5 %collective-permute-start.24 = (bf16[128,256]{1,0:T(8,128)(2,1)S(1)}, bf16[128,256]{1,0:T(8,128)(2,1)S(1)}, u32[]{:S(2)}, u32[]{:S(2)}) collective-permute-start(bf16[128,256]{1,0:T(8,128)(2,1)S(1)} %get-tuple-element.48), channel_id=1, source_target_pairs={{0,8},{8,0},{16,24},{24,16},{1,9},{9,1},{17,25},{25,17},{2,10},{10... | collective-permute-start | bytes 196616 | tf_op jit(solution)/shard_map/ppermute | solution.py:36
  84.1 5.9 %collective-permute-start.25 = (bf16[128,256]{1,0:T(8,128)(2,1)S(1)}, bf16[128,256]{1,0:T(8,128)(2,1)S(1)}, u32[]{:S(2)}, u32[]{:S(2)}) collective-permute-start(bf16[128,256]{1,0:T(8,128)(2,1)S(1)} %get-tuple-element.49), channel_id=1, source_target_pairs={{0,16},{8,24},{16,0},{24,8},{1,17},{9,25},{17,1},{25,9},{2,18},{10... | collective-permute-start | bytes 196616 | tf_op jit(solution)/shard_map/ppermute | solution.py:36
  85.4 6.1 %collective-permute-start.26 = (bf16[128,256]{1,0:T(8,128)(2,1)S(1)}, bf16[128,256]{1,0:T(8,128)(2,1)S(1)}, u32[]{:S(2)}, u32[]{:S(2)}) collective-permute-start(bf16[128,256]{1,0:T(8,128)(2,1)S(1)} %get-tuple-element.50), channel_id=1, source_target_pairs={{0,24},{8,16},{16,8},{24,0},{1,25},{9,17},{17,9},{25,1},{2,26},{10... | collective-permute-start | bytes 196616 | tf_op jit(solution)/shard_map/ppermute | solution.py:36
